TPU v7x, 32 devices: a whole 2x2x4 slice. The times are simulated.
32 devices in a mesh: row: 4 (over x, core), col: 8 (over z, y).
Axes of the slice: x: 2, y: 2, z: 4, core: 2. Of those that a mesh axis runs over, the one named last changes fastest.
Arguments:
- interactions: bfloat16 [4096, 2048], P('col', 'row'), may hold values from -1 to 1
- regular: float32 [4096], P('col'), may hold values from 0.2 to 2
Outputs:
- factored: float32 [4, 1024, 4096], P(None, 'row', 'col')
All inputs are finite; a program needn't handle non-finite values.
Results may differ from a plain program's by a relative error of at most 0.0003.
Values may be sent and summed in bfloat16 or wider, within the bound.
No kernel may reach another device: no remote copies, remote signals or barrier semaphores. Data moves between devices by JAX's collectives and lax.ppermute only.
A program may use at most 128 MiB of HBM per device.

v0:
```python
import jax
import jax.numpy as jnp
from jax import lax
from jax.sharding import PartitionSpec as P

PANEL = 1024
SPAN = 4


def from_root(value, axis, source):
    kept = jnp.where(lax.axis_index(axis) == source, value, 0).astype(value.dtype)
    return lax.psum(kept, axis)


def body(interactions, regular):
    row_count = lax.axis_size("row")
    row_index = lax.axis_index("row")
    col_index = lax.axis_index("col")
    block_width = interactions.shape[0]
    user_count = interactions.shape[1]
    band_rows = PANEL // row_count
    per_owner = SPAN * band_rows
    panel_blocks = PANEL // block_width
    highest = lax.Precision.HIGHEST
    everyone = lax.all_gather(interactions, "col", axis=0, tiled=True)
    grouped = everyone.reshape(SPAN, row_count, band_rows, user_count)
    term_block = jnp.einsum(
        "kotu,ju->oktj", grouped, interactions, preferred_element_type=jnp.float32
    )
    grid_tile = lax.psum_scatter(
        term_block.reshape(per_owner * lax.axis_size("row"), block_width),
        "row",
        scatter_dimension=0,
        tiled=True,
    ).reshape(SPAN, band_rows, block_width)
    row_items = (
        jnp.arange(SPAN, dtype=jnp.int32)[:, None] * PANEL
        + row_index * band_rows
        + jnp.arange(band_rows, dtype=jnp.int32)[None, :]
    )
    col_items = col_index * block_width + jnp.arange(block_width, dtype=jnp.int32)
    on_diagonal = row_items[:, :, None] == col_items[None, None, :]
    grid_tile = grid_tile + jnp.where(on_diagonal, regular[None, None, :], jnp.float32(0.0))
    row_band = lax.all_gather(grid_tile, "col", axis=2, tiled=True)
    corner = row_band[0, :, :PANEL]
    diagonal = lax.all_gather(corner, "row", axis=0, tiled=True)
    lower_factor = jnp.linalg.cholesky(diagonal)
    inverse = lax.linalg.triangular_solve(
        lower_factor, jnp.eye(PANEL, dtype=jnp.float32), left_side=True, lower=True
    )
    col_slot = col_index * block_width // PANEL
    first_owner = col_index * block_width % PANEL // band_rows
    lower_rows = row_band[1:, :, :PANEL].reshape((SPAN - 1) * band_rows, PANEL)
    left_own = jnp.dot(lower_rows, inverse.T, precision=highest)
    offered = lax.dynamic_slice_in_dim(
        left_own, jnp.maximum(col_slot - 1, 0) * band_rows, band_rows, 0
    )
    pieces = []
    for half_index in range(block_width // band_rows):
        pieces.append(from_root(offered, "row", first_owner + half_index))
    left_cols = jnp.concatenate(pieces, 0)
    current = grid_tile[1:].reshape((SPAN - 1) * band_rows, block_width)
    trailing = current - jnp.einsum("ia,ja->ij", left_own, left_cols, precision=highest)
    column_slot = jnp.minimum(col_index, panel_blocks - 1)
    lower_tile = lax.dynamic_slice(
        lower_factor, (row_index * band_rows, column_slot * block_width), (band_rows, block_width)
    )
    left_tile = lax.dynamic_slice_in_dim(left_own, column_slot * block_width, block_width, 1)
    in_panel = col_index < panel_blocks
    first_part = jnp.where(in_panel, lower_tile, jnp.zeros_like(lower_tile))
    other_parts = jnp.where(in_panel, left_tile, trailing).reshape(SPAN - 1, band_rows, block_width)
    return jnp.concatenate([first_part[None], other_parts], 0)


def solution(mesh):
    return jax.shard_map(
        body,
        mesh=mesh,
        in_specs=(P("col", "row"), P("col")),
        out_specs=P(None, "row", "col"),
        check_vma=False,
    )
```

profile of v0, /device:TPU:17, one launch (start us, length us, event | category | flops | bytes accessed | tf_op | source)
XLA Modules:
  0.0 865.0 jit_solution(3083761101344396939)
XLA Ops:
  7.3 75.5 %all-gather.5.cloned.1.call-done = bf16[4096,512]{1,0:T(8,128)(2,1)} async-done(((bf16[512,512]{1,0:T(8,128)(2,1)}), bf16[4096,512]{1,0:T(8,128)(2,1)}) %all-gather.5.cloned.1.call-update) | async-done | bytes 4194320 | tf_op jit(solution)/shard_map/all_gather | solution.py:25
  82.8 4.9 convolution_bitcast_fusion
  87.7 4.3 copy.4
  92.1 71.2 %reduce-scatter.2.cloned.1.call-done = f32[1024,512]{1,0:T(8,128)} async-done(((f32[4096,512]{1,0:T(8,128)}), f32[1024,512]{1,0:T(8,128)}) %reduce-scatter.2.cloned.1.call-update) | async-done | bytes 2097168 | tf_op jit(solution)/shard_map/reduce_scatter | solution.py:30
  163.3 1.9 copy.5
  165.3 1.6 select_add_fusion
  166.9 226.4 %all-gather.7.cloned.1.call-done = f32[4,256,4096]{1,2,0:T(8,128)} async-done(((f32[4,256,512]{1,2,0:T(8,128)}), f32[4,256,4096]{1,2,0:T(8,128)}) %all-gather.7.cloned.1.call-update) | async-done | bytes 16777232 | tf_op jit(solution)/shard_map/all_gather | solution.py:44
  393.4 2.3 slice.246
  397.2 2.4 fusion.29
  399.6 2.1 slice.247
  401.7 2.4 copy.7
  404.1 26.1 %all-gather.9.cloned.1.call-done = f32[1,1024,1024]{1,2,0:T(8,128)} async-done(((f32[1,256,1024]{1,2,0:T(8,128)}), f32[1,1024,1024]{1,2,0:T(8,128)}) %all-gather.9.cloned.1.call-update) | async-done | bytes 4194320 | tf_op jit(solution)/shard_map/all_gather | solution.py:46
  430.2 5.8 copy.6
  436.0 4.4 fusion
  440.5 1.9 copy-done.2
  442.4 11.7 %cholesky.223 = f32[128,128]{1,0:T(8,128)S(1)} custom-call(f32[128,128]{1,0:T(8,128)S(1)} %cholesky.580), custom_call_target="Cholesky" | custom-call | tf_op jit(solution)/shard_map/jit(cholesky)/cholesky | solution.py:47
  454.2 9.8 %custom-call.62 = f32[1,128,128]{1,2,0:T(8,128)S(1)} custom-call(f32[1,128,128]{2,1,0:T(8,128)S(1)} %get-tuple-element.75), custom_call_target="InvertDiagBlocksLowerTriangular" | custom-call | tf_op jit(solution)/shard_map/jit(cholesky)/cholesky | solution.py:47
  464.0 2.5 cholesky.255
  466.5 2.3 constant_dynamic-update-slice_fusion.29
  468.8 1.5 convolution_subtract_fusion.5
  470.4 11.9 %cholesky.244 = f32[128,128]{1,0:T(8,128)S(1)} custom-call(f32[128,128]{1,0:T(8,128)S(1)} %cholesky.584), custom_call_target="Cholesky" | custom-call | tf_op jit(solution)/shard_map/jit(cholesky)/cholesky | solution.py:47
  482.9 9.8 %custom-call.63 = f32[1,128,128]{1,2,0:T(8,128)S(1)} custom-call(f32[1,128,128]{2,1,0:T(8,128)S(1)} %get-tuple-element.72), custom_call_target="InvertDiagBlocksLowerTriangular" | custom-call | tf_op jit(solution)/shard_map/jit(cholesky)/cholesky | solution.py:47
  493.9 2.1 convolution_subtract_fusion.6
  496.1 11.7 %cholesky.468 = f32[128,128]{1,0:T(8,128)S(1)} custom-call(f32[128,128]{1,0:T(8,128)S(1)} %cholesky.589), custom_call_target="Cholesky" | custom-call | tf_op jit(solution)/shard_map/jit(cholesky)/cholesky | solution.py:47
  509.1 9.8 %custom-call.64 = f32[1,128,128]{1,2,0:T(8,128)S(1)} custom-call(f32[1,128,128]{2,1,0:T(8,128)S(1)} %get-tuple-element.69), custom_call_target="InvertDiagBlocksLowerTriangular" | custom-call | tf_op jit(solution)/shard_map/jit(cholesky)/cholesky | solution.py:47
  520.1 2.3 convolution_subtract_fusion.7
  522.4 11.9 %cholesky.487 = f32[128,128]{1,0:T(8,128)S(1)} custom-call(f32[128,128]{1,0:T(8,128)S(1)} %cholesky.594), custom_call_target="Cholesky" | custom-call | tf_op jit(solution)/shard_map/jit(cholesky)/cholesky | solution.py:47
  535.7 9.8 %custom-call.65 = f32[1,128,128]{1,2,0:T(8,128)S(1)} custom-call(f32[1,128,128]{2,1,0:T(8,128)S(1)} %get-tuple-element.66), custom_call_target="InvertDiagBlocksLowerTriangular" | custom-call | tf_op jit(solution)/shard_map/jit(cholesky)/cholesky | solution.py:47
  546.6 2.3 convolution_subtract_fusion.8
  548.9 11.7 %cholesky.506 = f32[128,128]{1,0:T(8,128)S(1)} custom-call(f32[128,128]{1,0:T(8,128)S(1)} %cholesky.599), custom_call_target="Cholesky" | custom-call | tf_op jit(solution)/shard_map/jit(cholesky)/cholesky | solution.py:47
  561.9 10.2 %custom-call.66 = f32[1,128,128]{1,2,0:T(8,128)S(1)} custom-call(f32[1,128,128]{2,1,0:T(8,128)S(1)} %get-tuple-element.63), custom_call_target="InvertDiagBlocksLowerTriangular" | custom-call | tf_op jit(solution)/shard_map/jit(cholesky)/cholesky | solution.py:47
  573.1 2.3 convolution_subtract_fusion.9
  575.4 11.7 %cholesky.526 = f32[128,128]{1,0:T(8,128)S(1)} custom-call(f32[128,128]{1,0:T(8,128)S(1)} %cholesky.604), custom_call_target="Cholesky" | custom-call | tf_op jit(solution)/shard_map/jit(cholesky)/cholesky | solution.py:47
  588.4 9.8 %custom-call.67 = f32[1,128,128]{1,2,0:T(8,128)S(1)} custom-call(f32[1,128,128]{2,1,0:T(8,128)S(1)} %get-tuple-element.60), custom_call_target="InvertDiagBlocksLowerTriangular" | custom-call | tf_op jit(solution)/shard_map/jit(cholesky)/cholesky | solution.py:47
  599.2 2.0 convolution_subtract_fusion.10
  601.2 11.9 %cholesky.546 = f32[128,128]{1,0:T(8,128)S(1)} custom-call(f32[128,128]{1,0:T(8,128)S(1)} %cholesky.609), custom_call_target="Cholesky" | custom-call | tf_op jit(solution)/shard_map/jit(cholesky)/cholesky | solution.py:47
  614.4 9.8 %custom-call.68 = f32[1,128,128]{1,2,0:T(8,128)S(1)} custom-call(f32[1,128,128]{2,1,0:T(8,128)S(1)} %get-tuple-element.57), custom_call_target="InvertDiagBlocksLowerTriangular" | custom-call | tf_op jit(solution)/shard_map/jit(cholesky)/cholesky | solution.py:47
  625.1 1.8 convolution_subtract_fusion.11
  626.9 11.7 %cholesky.564 = f32[128,128]{1,0:T(8,128)S(1)} custom-call(f32[128,128]{1,0:T(8,128)S(1)} %convolution_subtract_fusion.11), custom_call_target="Cholesky" | custom-call | tf_op jit(solution)/shard_map/jit(cholesky)/cholesky | solution.py:47
  645.7 6.6 fusion.1
  652.4 28.3 %while.1 = (s32[]{:T(128)}, f32[1024,1024]{1,0:T(8,128)}, s32[8,2]{0,1:T(2,128)S(1)}, f32[8,128,128]{2,1,0:T(8,128)}, s32[]{:T(128)}) while((s32[]{:T(128)}, f32[1024,1024]{1,0:T(8,128)}, s32[8,2]{0,1:T(2,128)S(1)}, f32[8,128,128]{2,1,0:T(8,128)}, s32[]{:T(128)}) %tuple.59), condition=%wide.while_cond, body=%wide.while_body.sunk | while | flops 2 | bytes 132205 | solution.py:48
  653.0 2.9 bitcast_dynamic-update-slice_fusion.2
  656.6 2.9 bitcast_dynamic-update-slice_fusion.2
  660.1 2.9 bitcast_dynamic-update-slice_fusion.2
  663.6 2.9 bitcast_dynamic-update-slice_fusion.2
  667.2 2.9 bitcast_dynamic-update-slice_fusion.2
  670.7 2.9 bitcast_dynamic-update-slice_fusion.2
  674.3 2.9 bitcast_dynamic-update-slice_fusion.2
  677.8 2.8 bitcast_dynamic-update-slice_fusion.2
  680.6 79.6 %custom-call.69 = f32[8,128,128]{1,2,0:T(8,128)S(1)} custom-call(f32[8,128,128]{2,1,0:T(8,128)} %get-tuple-element.12), custom_call_target="InvertDiagBlocksLowerTriangular" | custom-call | tf_op jit(solution)/shard_map/triangular_solve | solution.py:48
  761.8 1.7 convolution_subtract_fusion.4
  764.2 1.6 convolution_subtract_fusion
  766.6 2.0 fusion.23
  769.3 2.2 fusion.26
  772.3 2.6 convolution_subtract_fusion.2
  775.6 2.8 convolution_subtract_fusion.1
  779.1 4.0 convolution_subtract_fusion.3
  783.7 10.6 %fusion.81 = f32[768,1024]{1,0:T(8,128)S(1)} fusion(f32[768,1024]{1,0:T(8,128)S(1)} %bitcast.129, f32[1024,1024]{1,0:T(8,128)S(1)} %convolution_dynamic-update-slice_fusion), kind=kOutput, calls=%fused_computation.177 | convolution fusion | flops 9663676416 | bytes 10485760 | tf_op jit(solution)/shard_map/dot_general | solution.py:54
  794.3 1.7 copy-done.3
  796.0 1.6 dynamic-slice_select_fusion.1
  799.6 1.9 copy.8
  802.5 46.3 %all-reduce.4.cloned.1.call-done = (f32[256,1024]{1,0:T(8,128)}, f32[256,1024]{1,0:T(8,128)}) async-done(((f32[256,1024]{1,0:T(8,128)}, f32[256,1024]{1,0:T(8,128)}), (f32[256,1024]{1,0:T(8,128)}, f32[256,1024]{1,0:T(8,128)})) %all-reduce.4.cloned.1.call-update) | async-done | bytes 2097168 | tf_op jit(solution)/shard_map/psum | solution.py:12
  848.8 7.9 fusion.20
  856.7 1.5 pad_maximum_fusion
  (81 shorter events, 32.7 us)
Async XLA Ops:
  6.5 76.2 %all-gather.5.cloned.1.call-start = ((), (), s32[]{:S(2)}) async-start(), calls=%async_computation.1 | async-start | bytes 4718592 | tf_op jit(solution)/shard_map/all_gather | solution.py:25
  7.3 156.1 %reduce-scatter.2.cloned.1.call-start = ((), (), s32[]{:S(2)}) async-start(), calls=%async_computation.2 | async-start | bytes 10485760 | tf_op jit(solution)/shard_map/reduce_scatter | solution.py:30
  92.0 73.3 %copy-start.5 = (f32[512]{0:T(512)S(1)}, f32[512]{0:T(512)}, u32[]{:S(2)}) copy-start(f32[512]{0:T(512)} %param.3) | copy-start | bytes 6148
  92.0 301.4 %all-gather.7.cloned.1.call-start = ((), (), s32[]{:S(2)}) async-start(), calls=%async_computation.3 | async-start | bytes 18874368 | tf_op jit(solution)/shard_map/all_gather | solution.py:44
  166.9 263.3 %all-gather.9.cloned.1.call-start = ((), (), s32[]{:S(2)}) async-start(), calls=%async_computation.4 | async-start | bytes 5242880 | tf_op jit(solution)/shard_map/all_gather | solution.py:46
  395.6 453.2 %all-reduce.4.cloned.1.call-start = ((), (), s32[]{:S(2)}) async-start(), calls=%async_computation.5 | async-start | bytes 4194304 | tf_op jit(solution)/shard_map/psum | solution.py:12
  440.5 1.9 copy-start.2
  760.3 3.9 copy-start.1
  778.5 5.2 copy-start.4
  794.3 1.7 copy-start.3
  796.0 2.3 copy-start
Sparse Core Ops, SparseCore 0:
  9.5 73.2 all-gather.4
  92.1 71.1 reduce-scatter.1
  167.0 226.3 all-gather.6
  395.8 34.3 all-gather.8
  797.7 51.0 all-reduce.3
where the time goes:
time: 872 us; the launch traced here: 865 us
  waiting for transfers between devices  446 us (51%)
  other arithmetic  273 us (31%)
  matrix products  69.7 us (8%)
  local copies, waits for them, and re-layouts  57.1 us (7%)
  between operations  18.9 us (2%)
    all_gather x1, waiting for transfers between devices, body(): row_band = lax.all_gather(grid_tile, 'col', axis=2, tiled=True)  226 us
    another operation x30, other arithmetic, body(): lower_factor = jnp.linalg.cholesky(diagonal)  173 us
    another operation x3, other arithmetic, body(): lax.linalg.triangular_solve(lower_factor, jnp.eye(PANEL, dtype=jnp.float3...  86.2 us
    all_gather x1, waiting for transfers between devices, body(): everyone = lax.all_gather(interactions, 'col', axis=0, tiled=True)  75.5 us
    reduce_scatter x1, waiting for transfers between devices, body(): lax.psum_scatter(term_block.reshape(per_owner * lax.axis_size('row'), blo...  71.2 us
    psum x1, waiting for transfers between devices, from_root(): return lax.psum(kept, axis)  46.3 us
    another operation x24, local copies, waits for them, and re-layouts  28.3 us
    all_gather x1, waiting for transfers between devices, body(): diagonal = lax.all_gather(corner, 'row', axis=0, tiled=True)  26.1 us
  transfers between devices with their start and end apart: 5, of which 5 were waited for; matrix products, arithmetic and copies ran while one was open for 1% of the time, Pallas kernels for 0%

commit v1 on v0

v1 whole, which is shorter than its diff:
```python
import functools
import jax
import jax.numpy as jnp
from jax import lax
from jax.experimental import pallas as pl
from jax.experimental.pallas import tpu as pltpu
from jax.sharding import PartitionSpec as P

PANEL = 1024
SPAN = 4
BLOCK = 128
WIDE = 256
SUB = 8
NBLOCKS = PANEL // BLOCK
PARTS = 16
VMEM = pltpu.VMEM
f32 = jnp.float32
bf16 = jnp.bfloat16


def dot_nt(a, b):
    return lax.dot_general(a, b, (((1,), (1,)), ((), ())), preferred_element_type=f32)


def split(value):
    high = value.astype(bf16)
    return high, (value - high.astype(f32)).astype(bf16)


def dot_nt3(a, b):
    return dot_nt(a[0], b[0]) + (dot_nt(a[0], b[1]) + dot_nt(a[1], b[0]))


def dot_nn3(a, b):
    def dot(x, y):
        return jnp.dot(x, y, preferred_element_type=f32)

    return dot(a[0], b[0]) + (dot(a[0], b[1]) + dot(a[1], b[0]))


def lanes(value, lane):
    return jnp.broadcast_to(value[:, lane : lane + 1], (SUB, BLOCK))


def sublanes(value, row):
    return jnp.broadcast_to(value[row : row + 1, :], (SUB, BLOCK))


def factor_block(block_ref, inverse_ref):
    tiles_count = BLOCK // SUB
    row_in_tile = lax.broadcasted_iota(jnp.int32, (SUB, BLOCK), 0)
    lane = lax.broadcasted_iota(jnp.int32, (SUB, BLOCK), 1)
    sides = [block_ref[pl.ds(SUB * t, SUB), :] for t in range(tiles_count)]
    inverses = [(lane == row_in_tile + SUB * t).astype(f32) for t in range(tiles_count)]
    uppers = []
    for step in range(tiles_count):
        base = SUB * step
        side, inverse = sides[step], inverses[step]
        columns = [lanes(side, base + b) for b in range(SUB)]
        entry = {(a, b): sublanes(columns[b], a) for b in range(SUB) for a in range(b, SUB)}
        ahead = [lanes(sides[step + 1], base + b) for b in range(SUB)] if step + 1 < tiles_count else None
        tops = [sublanes(side, a) for a in range(SUB)]
        insides = [sublanes(inverse, a) for a in range(SUB)]
        scale = []
        for m in range(SUB):
            root = lax.rsqrt(entry[m, m])
            scale.append(root)
            for a in range(m + 1, SUB):
                entry[a, m] = entry[a, m] * root
            for b in range(m + 1, SUB):
                for a in range(b, SUB):
                    entry[a, b] = entry[a, b] - entry[a, m] * entry[b, m]
            tops[m] = tops[m] * root
            insides[m] = insides[m] * root
            for a in range(m + 1, SUB):
                tops[a] = tops[a] - entry[a, m] * tops[m]
                insides[a] = insides[a] - entry[a, m] * insides[m]
            if ahead is not None:
                ahead[m] = ahead[m] * root
                for b in range(m + 1, SUB):
                    ahead[b] = ahead[b] - entry[b, m] * ahead[m]
        upper, lower_inverse = tops[0], insides[0]
        for m in range(1, SUB):
            upper = jnp.where(row_in_tile == m, tops[m], upper)
            lower_inverse = jnp.where(row_in_tile == m, insides[m], lower_inverse)
        uppers.append(jnp.where(lane >= row_in_tile + base, upper, 0.0))
        inverse_ref[pl.ds(base, SUB), :] = lower_inverse
        if ahead is not None:
            for m in range(SUB):
                sides[step + 1] = sides[step + 1] - ahead[m] * tops[m]
                inverses[step + 1] = inverses[step + 1] - ahead[m] * insides[m]
        if step + 2 < tiles_count:
            weights_top, weights_in = [None] * SUB, [None] * SUB
            for m in reversed(range(SUB)):
                top, inside = tops[m], insides[m]
                for b in range(m + 1, SUB):
                    top = top - entry[b, m] * weights_top[b]
                    inside = inside - entry[b, m] * weights_in[b]
                weights_top[m], weights_in[m] = top * scale[m], inside * scale[m]
            for t in range(step + 2, tiles_count):
                for m in range(SUB):
                    column = lanes(sides[t], base + m)
                    if m == 0:
                        top_sum, in_sum = column * weights_top[m], column * weights_in[m]
                    else:
                        top_sum = top_sum + column * weights_top[m]
                        in_sum = in_sum + column * weights_in[m]
                sides[t] = sides[t] - top_sum
                inverses[t] = inverses[t] - in_sum
    block_ref[...] = jnp.concatenate(uppers, 0).T


def place_pieces(place_ref, first, pieces, helds, sem):
    copies = []
    for i, (piece, held_ref) in enumerate(zip(pieces, helds)):
        rows, users = piece.shape
        row = pl.multiple_of(place_ref[first + 2 * i], rows)
        user = pl.multiple_of(place_ref[first + 2 * i + 1], users)
        copy = pltpu.make_async_copy(
            piece, held_ref.at[pl.ds(row, rows), pl.ds(user, users)], sem.at[i]
        )
        copy.start()
        copies.append(copy)
    return copies


def panel_kernel(views, count, width, place_ref, *refs):
    pieces, refs = refs[:count], refs[count:]
    outs, (high_ref, low_ref, inv_high_ref, inv_low_ref, lower_ref, block_ref, inverse_ref, items_ref, parts_ref, sem, out_sem) = refs[:4], refs[4:]
    held = [parts_ref if is_part else items_ref for _, _, _, is_part in views]
    views = [pieces[which].at[pl.ds(start, rows)] for which, start, rows, _ in views]
    for copy in place_pieces(place_ref, 0, views, held, sem):
        copy.wait()
    on_diagonal = lax.broadcasted_iota(jnp.int32, (BLOCK, BLOCK), 0) == lax.broadcasted_iota(
        jnp.int32, (BLOCK, BLOCK), 1
    )

    def before(k):
        start = k * BLOCK
        here = pl.ds(start, BLOCK)
        column = dot_nt(items_ref[pl.ds(start, PANEL - start), :], items_ref[here, :])
        if k > 0:
            high, low = high_ref[pl.ds(start, PANEL - start), :start], low_ref[pl.ds(start, PANEL - start), :start]
            column = column - dot_nt3((high, low), (high[:BLOCK], low[:BLOCK]))
        part, lane = PARTS * (start // width), start % width
        parts = parts_ref[pl.ds(part, PARTS), pl.ds(lane, BLOCK)].astype(f32)
        regular = parts[0:1] + parts[1:2] + parts[2:3]
        block_ref[...] = column[:BLOCK] + jnp.where(on_diagonal, regular, 0.0)
        if k + 1 < NBLOCKS:
            lower_ref[pl.ds(start + BLOCK, PANEL - start - BLOCK), :] = column[BLOCK:]

    def after(k):
        start = k * BLOCK
        here = pl.ds(start, BLOCK)
        diagonal = block_ref[...]
        inverse = split(inverse_ref[...])
        inv_high_ref[here, :], inv_low_ref[here, :] = inverse
        high_ref[here, here], low_ref[here, here] = split(diagonal)
        if k > 0:
            above = jnp.zeros((start, BLOCK), bf16)
            high_ref[pl.ds(0, start), here], low_ref[pl.ds(0, start), here] = above, above
        if k + 1 < NBLOCKS:
            rest = pl.ds(start + BLOCK, PANEL - start - BLOCK)
            high_ref[rest, here], low_ref[rest, here] = split(dot_nt3(split(lower_ref[rest, :]), inverse))

    def leave(k):
        column = pl.ds(k * BLOCK, BLOCK)
        return [
            pltpu.make_async_copy(high_ref.at[:, column], outs[0].at[:, column], out_sem.at[0, k]),
            pltpu.make_async_copy(low_ref.at[:, column], outs[1].at[:, column], out_sem.at[1, k]),
            pltpu.make_async_copy(inv_high_ref.at[column, :], outs[2].at[column, :], out_sem.at[2, k]),
            pltpu.make_async_copy(inv_low_ref.at[column, :], outs[3].at[column, :], out_sem.at[3, k]),
        ]

    before(0)

    def turn(k, carry):
        factor_block(block_ref, inverse_ref)
        for which in range(NBLOCKS):

            @pl.when(k == which)
            def _():
                after(which)
                for copy in leave(which):
                    copy.start()
                if which + 1 < NBLOCKS:
                    before(which + 1)

        return carry

    lax.fori_loop(0, NBLOCKS, turn, 0)
    for k in range(NBLOCKS):
        for copy in leave(k):
            copy.wait()


def room(users):
    return (2 * PANEL * users + 32 * 1024 * 1024) // 2**20 * 2**20


def factor_panel(place, pieces, views, width, users):
    outs = [
        ((PANEL, PANEL), bf16),
        ((PANEL, PANEL), bf16),
        ((PANEL, BLOCK), bf16),
        ((PANEL, BLOCK), bf16),
    ]
    held = [
        ((PANEL, BLOCK), f32),
        ((BLOCK, BLOCK), f32),
        ((BLOCK, BLOCK), f32),
        ((PANEL, users), bf16),
        ((PANEL // width * PARTS, users), bf16),
    ]
    return pl.pallas_call(
        functools.partial(panel_kernel, views, len(pieces), width),
        out_shape=[pltpu.HBM(*out) for out in outs],
        in_specs=[pl.BlockSpec(memory_space=pltpu.SMEM)]
        + [pl.BlockSpec(memory_space=pl.ANY)] * len(pieces),
        out_specs=[pl.BlockSpec(memory_space=pltpu.HBM)] * len(outs),
        scratch_shapes=[VMEM(*one) for one in outs + held]
        + [pltpu.SemaphoreType.DMA((len(views),)), pltpu.SemaphoreType.DMA((len(outs), NBLOCKS))],
        compiler_params=pltpu.CompilerParams(vmem_limit_bytes=room(users)),
        cost_estimate=pl.CostEstimate(flops=4 * 10**10, bytes_accessed=16 * 2**20, transcendentals=1024),
        name="factor_panel",
    )(place, *pieces)


def tile_kernel(counts, views, place_ref, regular_ref, *refs):
    factors, refs = refs[:4], refs[4:]
    pieces, refs = refs[: sum(counts)], refs[sum(counts) :]
    out_ref, refs = refs[0], refs[1:]
    high_ref, low_ref, inv_high_ref, inv_low_ref, left_high_ref, left_low_ref, wide_high_ref, wide_low_ref = refs[:8]
    panel_ref, rows_ref, cols_ref, sem, factor_sem = refs[8:]
    targets = [panel_ref] * counts[0] + [rows_ref] * counts[1] + [cols_ref] * counts[2]
    held = [targets[which] for which, *_ in views]
    views = [pieces[which].at[pl.ds(start, rows)] for which, start, rows in views]
    fetches = [
        pltpu.make_async_copy(factor, ref, factor_sem.at[i])
        for i, (factor, ref) in enumerate(zip(factors, (high_ref, low_ref, inv_high_ref, inv_low_ref)))
    ]
    for fetch in fetches:
        fetch.start()
    copies = place_pieces(place_ref, 2, views, held, sem)
    for fetch in fetches:
        fetch.wait()
    row_index, col_index = place_ref[0], place_ref[1]
    width, band = cols_ref.shape[0], rows_ref.shape[0] // SPAN
    row_count = (SPAN - 1) * band
    lower_items = rows_ref.at[pl.ds(band, row_count), :]
    panel_blocks = PANEL // width
    in_panel = col_index < panel_blocks
    slot = jnp.minimum(col_index, panel_blocks - 1)
    at = pl.ds(pl.multiple_of(slot * width, width), width)
    below, right = pl.ds(0, row_count), pl.ds(row_count, width)

    for start in range(0, PANEL, WIDE):
        first, second = pl.ds(start, BLOCK), pl.ds(start + BLOCK, BLOCK)
        between = dot_nn3((high_ref[second, first], low_ref[second, first]), (inv_high_ref[first, :], inv_low_ref[first, :]))
        corner = split(-dot_nn3((inv_high_ref[second, :], inv_low_ref[second, :]), split(between)))
        for wide_ref, inv_ref, part in ((wide_high_ref, inv_high_ref, corner[0]), (wide_low_ref, inv_low_ref, corner[1])):
            wide_ref[first, pl.ds(0, BLOCK)] = inv_ref[first, :]
            wide_ref[first, pl.ds(BLOCK, BLOCK)] = jnp.zeros((BLOCK, BLOCK), bf16)
            wide_ref[second, pl.ds(0, BLOCK)] = part
            wide_ref[second, pl.ds(BLOCK, BLOCK)] = inv_ref[second, :]

    def solve(items_ref, mine):
        for start in range(0, PANEL, WIDE):
            here = pl.ds(start, WIDE)
            column = dot_nt(items_ref[...], panel_ref[here, :])
            if start > 0:
                column = column - dot_nt3(
                    (left_high_ref[mine, :start], left_low_ref[mine, :start]), (high_ref[here, :start], low_ref[here, :start])
                )
            column = dot_nt3(split(column), (wide_high_ref[here, :], wide_low_ref[here, :]))
            left_high_ref[mine, here], left_low_ref[mine, here] = split(column)

    for copy, target in zip(copies, held):
        if target is not rows_ref:
            copy.wait()
    solve(cols_ref, right)
    for copy, target in zip(copies, held):
        if target is rows_ref:
            copy.wait()
    solve(lower_items, below)

    @pl.when(in_panel)
    def _():
        mine = pl.ds(pl.multiple_of(row_index * band, band), band)
        out_ref[pl.ds(0, band), :] = high_ref[mine, at].astype(f32) + low_ref[mine, at].astype(f32)
        out_ref[pl.ds(band, row_count), :] = left_high_ref[below, at].astype(f32) + left_low_ref[below, at].astype(f32)

    @pl.when(jnp.logical_not(in_panel))
    def _():
        out_ref[pl.ds(0, band), :] = jnp.zeros((band, width), f32)
        items = lax.broadcasted_iota(jnp.int32, (band, width), 0) + row_index * band
        columns = lax.broadcasted_iota(jnp.int32, (band, width), 1) + col_index * width
        for part in range(SPAN - 1):
            mine = pl.ds(part * band, band)
            tile = dot_nt(lower_items[mine, :], cols_ref[...])
            tile = tile + jnp.where(items + (part + 1) * PANEL == columns, regular_ref[...], 0.0)
            out_ref[pl.ds((part + 1) * band, band), :] = tile - dot_nt3(
                (left_high_ref[mine, :], left_low_ref[mine, :]), (left_high_ref[right, :], left_low_ref[right, :])
            )


def finish_tile(place, regular, factors, panel, rows, cols, views, band, users):
    spec = pl.BlockSpec(memory_space=VMEM)
    width = regular.shape[1]
    rows, cols = ([pltpu.with_memory_space_constraint(x, pltpu.HBM) for x in group] for group in (rows, cols))
    factors = [pltpu.with_memory_space_constraint(x, pltpu.HBM) for x in factors]
    pieces = panel + rows + cols
    out = ((SPAN * band, width), f32)
    below = (SPAN - 1) * band + width
    held = [
        ((below, PANEL), bf16),
        ((below, PANEL), bf16),
        ((PANEL, WIDE), bf16),
        ((PANEL, WIDE), bf16),
        ((PANEL, users), bf16),
        ((SPAN * band, users), bf16),
        ((width, users), bf16),
    ]
    return pl.pallas_call(
        functools.partial(tile_kernel, (len(panel), len(rows), len(cols)), views),
        out_shape=jax.ShapeDtypeStruct(*out),
        in_specs=[pl.BlockSpec(memory_space=pltpu.SMEM)]
        + [spec]
        + [pl.BlockSpec(memory_space=pltpu.HBM)] * len(factors)
        + [pl.BlockSpec(memory_space=pl.ANY)] * len(panel)
        + [pl.BlockSpec(memory_space=pltpu.HBM)] * (len(rows) + len(cols)),
        out_specs=spec,
        scratch_shapes=[VMEM(factor.shape, factor.dtype) for factor in factors]
        + [VMEM(*one) for one in held]
        + [pltpu.SemaphoreType.DMA((len(views),)), pltpu.SemaphoreType.DMA((len(factors),))],
        compiler_params=pltpu.CompilerParams(vmem_limit_bytes=room(users)),
        cost_estimate=pl.CostEstimate(flops=20 * 10**9, bytes_accessed=24 * 2**20, transcendentals=0),
        name="finish_tile",
    )(place, regular, *factors, *pieces)


CORES = 2


def body(interactions, regular):
    row_count, col_count = lax.axis_size("row"), lax.axis_size("col")
    row_index, col_index = lax.axis_index("row"), lax.axis_index("col")
    width, users = interactions.shape
    band = PANEL // row_count
    ways = PANEL // width
    assert row_count == CORES * ways and col_count == SPAN * ways and users >= width
    slot, way = col_index // ways, col_index % ways
    pair, core = row_index // CORES, row_index % CORES
    all_users = row_count * users

    def exchange(value, move, only=None):
        perm = []
        for source_row in range(row_count):
            for source_col in range(col_count):
                place = (source_row // CORES, source_row % CORES, source_col // ways, source_col % ways)
                if only is None or only(*place):
                    to = move(*place)
                    target = (to[0] * CORES + to[1]) * col_count + to[2] * ways + to[3]
                    perm.append((source_row * col_count + source_col, target))
        return lax.ppermute(value, ("row", "col"), perm)

    def after(value, *others):
        return lax.optimization_barrier((value, *others))[0]

    high = lax.reduce_precision(regular, 8, 7)
    middle = lax.reduce_precision(regular - high, 8, 7)
    parts = jnp.stack([high, middle, regular - high - middle]).astype(bf16)
    parts = jnp.pad(parts, ((0, PARTS - 3), (0, users - width)))

    half = width // 2
    shared = [interactions[:half], jnp.concatenate([interactions[half:], parts], 0)]
    reach = SPAN // 2
    while reach:
        got = [
            exchange(part, lambda p, h, s, w: (p, h, s + reach, w), lambda p, h, s, w: s % (2 * reach) == 0)
            for part in shared
        ]
        shared = [jnp.where(slot % (2 * reach) == reach, new, old) for new, old in zip(got, shared)]
        reach //= 2

    halves = interactions.reshape(CORES, band, users)
    offers = [lax.dynamic_index_in_dim(halves, core ^ flip, 0, False) for flip in range(CORES)]

    def numbers(values):
        return jnp.stack([jnp.asarray(v, jnp.int32) for v in values])

    panel, panel_views, panel_place, part_views, part_place = [], [], [], [], []
    cols, cols_place = [interactions], [0, row_index * users]
    rows, rows_views, rows_place = [], [], []

    def over_core(value):
        return exchange(value, lambda p, h, s, w: (p, 1 - h, s, w))

    def over_pair(value):
        return exchange(value, lambda p, h, s, w: (1 - p, h, s, w))

    def over_way(value, only=None):
        return exchange(value, lambda p, h, s, w: (p, h, s, 1 - w), only)

    if ways == 2:
        swapped = jnp.concatenate(
            [exchange(offers[flip], lambda p, h, s, w: (w, h ^ flip, s, p)) for flip in range(CORES)], 0
        )
        shared = [after(part, swapped) for part in shared]
        pair_side = [over_pair(part) for part in shared]
        way_side = [over_way(part) for part in shared]
        diagonal = [over_way(pair_side[0]), over_pair(way_side[1])]
        for from_pair, from_way, pieces in (
            (pair, way, shared),
            (1 - pair, way, pair_side),
            (pair, 1 - way, way_side),
            (1 - pair, 1 - way, diagonal),
        ):
            for which, piece in enumerate(pieces):
                for from_core, value in ((core, piece), (1 - core, over_core(piece))):
                    if which and value is piece and (pieces is shared or pieces is way_side):
                        part_views.append((len(panel), half, PARTS, True))
                        part_place += [from_way * PARTS, 0]
                    panel_views.append((len(panel), 0, half, False))
                    panel_place += [from_way * width + which * half, (from_pair * CORES + from_core) * users]
                    panel.append(value)
        crossed = [*pair_side, *way_side, *diagonal]
        held = after(interactions, *crossed)
        for flip in range(1, row_count):
            cols.append(lax.ppermute(held, "row", [(r, r ^ flip) for r in range(row_count)]))
            cols_place += [0, (row_index ^ flip) * users]
        for turn in range(SPAN):
            piece = swapped
            if turn:
                piece = exchange(
                    swapped if turn == 1 else after(swapped, *got),
                    lambda p, h, s, w: (p, h, (s - turn) % SPAN, w),
                    lambda p, h, s, w: s > 0,
                )
            twin = over_way(after(piece, *crossed), lambda p, h, s, w: (s + turn) % SPAN > 0)
            for from_way, value in ((way, piece), (1 - way, twin)):
                for flip in range(CORES):
                    rows_views.append((len(rows), flip * band, band))
                    rows_place += [(slot + turn) % SPAN * band, (from_way * CORES + (core ^ flip)) * users]
                rows.append(value)
    else:
        groups = [[s * ways + w for w in range(ways)] for s in range(SPAN)]
        shared = lax.all_gather(jnp.concatenate(shared, 0), "col", axis=0, axis_index_groups=groups)
        parts = shared[:, width:].reshape(ways * PARTS, users)
        shared = shared[:, :width].reshape(PANEL, users)
        panel, panel_place = [lax.all_gather(shared, "row", axis=1, tiled=True), parts], [0, 0]
        panel_views = [(0, 0, PANEL, False)]
        part_views, part_place = [(1, 0, ways * PARTS, True)], [0, 0]
        cols, cols_place = [lax.all_gather(interactions, "row", axis=1, tiled=True)], [0, 0]
        quarters, quarter_users = [], []
        for turn in range(ways):
            for flip in range(CORES):
                quarters.append(exchange(offers[flip], lambda p, h, s, w: (w, h ^ flip, s, (p + turn) % ways)))
                quarter_users.append(((way - turn) % ways * CORES + (core ^ flip)) * users)
        groups = [[s * ways + w for s in range(SPAN)] for w in range(ways)]
        rows = [lax.all_gather(jnp.concatenate(quarters, 0), "col", axis=0, tiled=True, axis_index_groups=groups)]
        for from_slot in range(1, SPAN):
            for which, from_users in enumerate(quarter_users):
                rows_views.append((0, (from_slot * len(quarters) + which) * band, band))
                rows_place += [from_slot * band, from_users]

    factors = factor_panel(
        numbers(panel_place + part_place), panel, panel_views + part_views, width, all_users
    )
    views = [view[:3] for view in panel_views]
    views += [(len(panel) + i, start, count) for i, start, count in rows_views]
    views += [(len(panel) + len(rows) + i, 0, width) for i in range(len(cols))]
    tile = finish_tile(
        numbers([row_index, col_index] + panel_place + rows_place + cols_place),
        regular[None, :], factors, panel, rows, cols, views, band, all_users,
    )
    return tile.reshape(SPAN, band, width)


def solution(mesh):
    return jax.shard_map(
        body,
        mesh=mesh,
        in_specs=(P("col", "row"), P("col")),
        out_specs=P(None, "row", "col"),
        check_vma=False,
    )
```

time: 872 us -> 169 us (0.19)
  waiting for transfers between devices: 446 us -> 24.7 us
  other arithmetic: 273 us -> 1.93 us
  Pallas kernels: 0 us -> 72.3 us
  matrix products: 69.7 us -> 0 us
  starting transfers between devices: 0.17 us -> 55.6 us
  local copies, waits for them, and re-layouts: 57.1 us -> 11.1 us
  between operations: 18.9 us -> 0.6 us
    all_gather x3 -> x0, waiting for transfers between devices: 328 us -> none  [the longest x1 226 us: body(): row_band = lax.all_gather(grid_tile, 'col', axis=2, tiled=True)]
    another operation x33 -> x2, other arithmetic: 259 us -> 0.71 us  [the longest x30 173 us: body(): lower_factor = jnp.linalg.cholesky(diagonal)]
    pallas_call x0 -> x2, Pallas kernels: none -> 72.3 us  [the longest x1 46.9 us: factor_panel(): pl.pallas_call(functools.partial(panel_kernel, views, len(pieces), width)...]
    reduce_scatter x1 -> x0, waiting for transfers between devices: 71.2 us -> none  [body(): lax.psum_scatter(term_block.reshape(per_owner * lax.axis_size('row'), blo...]
    ppermute x0 -> x30, starting transfers between devices: none -> 55.6 us  [the longest x27 52.1 us: exchange(): return lax.ppermute(value, ('row', 'col'), perm)]
    another operation x29 -> x0, matrix products: 46.4 us -> none  [the longest x15 23.3 us: body(): lax.linalg.triangular_solve(lower_factor, jnp.eye(PANEL, dtype=jnp.float3...]
    psum x1 -> x0, waiting for transfers between devices: 46.3 us -> none  [from_root(): return lax.psum(kept, axis)]
    another operation x33 -> x5, local copies, waits for them, and re-layouts: 30.8 us -> 0.29 us  [the longest x2 0.28 us: numbers(): return jnp.stack([jnp.asarray(v, jnp.int32) for v in values])]
  transfers between devices with their start and end apart: 5 -> 30, of which waited for: 5 -> 6; matrix products, arithmetic and copies ran while one was open for 1% -> 3% of each run, Pallas kernels for 0% -> 28%
where the time goes in v1:
time: 169 us; the launch traced here: 166 us
  Pallas kernels  72.3 us (43%)
  starting transfers between devices  55.6 us (33%)
  waiting for transfers between devices  24.7 us (15%)
  local copies, waits for them, and re-layouts  11.1 us (7%)
  other arithmetic  1.93 us (1%)
    ppermute x27, starting transfers between devices, exchange(): return lax.ppermute(value, ('row', 'col'), perm)  52.1 us
    pallas_call x1, Pallas kernels, factor_panel(): pl.pallas_call(functools.partial(panel_kernel, views, len(pieces), width)...  46.9 us
    pallas_call x1, Pallas kernels, finish_tile(): pl.pallas_call(functools.partial(tile_kernel, (len(panel), len(rows), len...  25.4 us
    ppermute x27, waiting for transfers between devices, exchange(): return lax.ppermute(value, ('row', 'col'), perm)  24.7 us
    unnamed x31, local copies, waits for them, and re-layouts  7.98 us
    ppermute x3, starting transfers between devices, body(): lax.ppermute(held, 'row', [(r, r ^ flip) for r in range(row_count)])  3.45 us
  transfers between devices with their start and end apart: 30, of which 6 were waited for; matrix products, arithmetic and copies ran while one was open for 3% of the time, Pallas kernels for 28%

profile of v1, /device:TPU:17, one launch (start us, length us, event | category | flops | bytes accessed | tf_op | source)
XLA Modules:
  0.0 166.2 jit_solution(12079087516118634640)
XLA Ops:
  0.0 1.0 slice.6
  1.0 1.3 collective-permute-start
  2.3 1.1 dynamic-slice_bitcast_fusion
  3.4 0.7 collective-permute-start.2
  4.1 0.7 reduce-precision_convert_fusion.1
  4.8 6.1 %collective-permute-done = bf16[256,512]{1,0:T(8,128)(2,1)S(1)} collective-permute-done((bf16[256,512]{1,0:T(8,128)(2,1)S(1)}, bf16[256,512]{1,0:T(8,128)(2,1)S(1)}, u32[]{:S(2)}, u32[]{:S(2)}) %collective-permute-start) | collective-permute-done | bytes 262176 | tf_op jit(solution)/shard_map/ppermute | solution.py:365
  10.9 1.1 fusion.6
  12.0 1.3 collective-permute-start.5
  13.3 1.6 collective-permute-start.3
  15.0 1.3 collective-permute-start.1
  16.3 0.7 constant_dynamic-update-slice_fusion.1
  17.0 4.4 %collective-permute-done.5 = bf16[272,512]{1,0:T(8,128)(2,1)S(1)} collective-permute-done((bf16[272,512]{1,0:T(8,128)(2,1)S(1)}, bf16[272,512]{1,0:T(8,128)(2,1)S(1)}, u32[]{:S(2)}, u32[]{:S(2)}) %collective-permute-start.5) | collective-permute-done | bytes 278560 | tf_op jit(solution)/shard_map/ppermute | solution.py:365
  21.4 0.1 broadcast_select_fusion
  21.5 1.3 collective-permute-start.6
  22.8 0.0 collective-permute-done.3
  22.8 0.8 constant_dynamic-update-slice_fusion.refs_20_
  23.6 1.9 %collective-permute-start.21 = (bf16[512,512]{1,0:T(8,128)(2,1)}, bf16[512,512]{1,0:T(8,128)(2,1)S(1)}, u32[]{:S(2)}, u32[]{:S(2)}) collective-permute-start(bf16[512,512]{1,0:T(8,128)(2,1)} %constant_dynamic-update-slice_fusion.refs_20_), channel_id=1, source_target_pairs={{2,0},{3,1},{4,2},{5,3},{6,4},{7,5},{10,8},{11,9},{12,10},{13,11},... | collective-permute-start | bytes 1572872 | tf_op jit(solution)/shard_map/ppermute | solution.py:365
  25.6 1.3 collective-permute-start.12
  26.9 1.2 collective-permute-start.8
  28.1 5.1 %collective-permute-start.4 = (bf16[256,512]{1,0:T(8,128)(2,1)S(1)}, bf16[256,512]{1,0:T(8,128)(2,1)S(1)}, u32[]{:S(2)}, u32[]{:S(2)}) collective-permute-start(bf16[256,512]{1,0:T(8,128)(2,1)S(1)} %broadcast_select_fusion.3.refs_0_.refs_4_), channel_id=1, source_target_pairs={{0,8},{1,9},{2,10},{3,11},{4,12},{5,13},{6,14},{7,15},{8,0},{9,1},... | collective-permute-start | bytes 786440 | tf_op jit(solution)/shard_map/ppermute | solution.py:365
  33.2 0.1 collective-permute-start.14
  33.3 3.3 %collective-permute-start.13 = (bf16[256,512]{1,0:T(8,128)(2,1)S(1)}, bf16[256,512]{1,0:T(8,128)(2,1)S(1)}, u32[]{:S(2)}, u32[]{:S(2)}) collective-permute-start(bf16[256,512]{1,0:T(8,128)(2,1)S(1)} %collective-permute-done.12.refs_8_.refs_12_), channel_id=1, source_target_pairs={{0,8},{1,9},{2,10},{3,11},{4,12},{5,13},{6,14},{7,15},{8,0},{9,1},... | collective-permute-start | bytes 786440 | tf_op jit(solution)/shard_map/ppermute | solution.py:365
  36.6 0.0 collective-permute-done.8.refs_4_.refs_8_
  36.6 2.3 %collective-permute-start.10 = (bf16[272,512]{1,0:T(8,128)(2,1)S(1)}, bf16[272,512]{1,0:T(8,128)(2,1)S(1)}, u32[]{:S(2)}, u32[]{:S(2)}) collective-permute-start(bf16[272,512]{1,0:T(8,128)(2,1)S(1)} %broadcast_select_fusion.1.refs_2_.refs_6_), channel_id=1, source_target_pairs={{0,16},{1,17},{2,18},{3,19},{4,20},{5,21},{6,22},{7,23},{8,24},{9,... | collective-permute-start | bytes 835592 | tf_op jit(solution)/shard_map/ppermute | solution.py:365
  39.0 2.2 %collective-permute-start.16 = (bf16[256,512]{1,0:T(8,128)(2,1)S(1)}, bf16[256,512]{1,0:T(8,128)(2,1)S(1)}, u32[]{:S(2)}, u32[]{:S(2)}) collective-permute-start(bf16[256,512]{1,0:T(8,128)(2,1)S(1)} %collective-permute-done.8.refs_4_.refs_8_), channel_id=1, source_target_pairs={{0,1},{1,0},{2,3},{3,2},{4,5},{5,4},{6,7},{7,6},{8,9},{9,8},{10,11... | collective-permute-start | bytes 786440 | tf_op jit(solution)/shard_map/ppermute | solution.py:365
  41.2 0.6 collective-permute-done.14.refs_10_.refs_14_
  41.8 0.1 collective-permute-start.18
  41.9 3.7 %collective-permute-start.25 = (bf16[512,512]{1,0:T(8,128)(2,1)}, bf16[512,512]{1,0:T(8,128)(2,1)S(1)}, u32[]{:S(2)}, u32[]{:S(2)}) collective-permute-start(bf16[512,512]{1,0:T(8,128)(2,1)} %constant_dynamic-update-slice_fusion.refs_20_), channel_id=1, source_target_pairs={{2,4},{3,5},{4,6},{5,7},{6,0},{7,1},{10,12},{11,13},{12,14},{13,15... | collective-permute-start | bytes 1572872 | tf_op jit(solution)/shard_map/ppermute | solution.py:365
  45.6 1.3 collective-permute-start.23
  46.9 0.7 collective-permute-done.16.refs_12_.refs_16_
  47.6 1.6 collective-permute-start.7
  49.2 0.0 collective-permute-done.10.refs_6_.refs_10_
  49.2 0.1 collective-permute-start.9
  49.3 2.2 %collective-permute-done.18.refs_14_.refs_18_ = bf16[272,512]{1,0:T(8,128)(2,1)S(1)} collective-permute-done((bf16[272,512]{1,0:T(8,128)(2,1)S(1)}, bf16[272,512]{1,0:T(8,128)(2,1)S(1)}, u32[]{:S(2)}, u32[]{:S(2)}) %collective-permute-start.18) | collective-permute-done | bytes 278560 | tf_op jit(solution)/shard_map/ppermute | solution.py:365
  51.6 1.0 collective-permute-start.17
  52.5 0.7 copy-done.1
  53.2 0.0 collective-permute-done.9.refs_5_.refs_9_
  53.2 0.7 copy-done.3
  53.9 4.1 %collective-permute-start.20 = (bf16[512,512]{1,0:T(8,128)(2,1)}, bf16[512,512]{1,0:T(8,128)(2,1)}, u32[]{:S(2)}, u32[]{:S(2)}) collective-permute-start(bf16[512,512]{1,0:T(8,128)(2,1)} %constant_dynamic-update-slice_fusion.refs_20_), channel_id=1, source_target_pairs={{2,3},{3,2},{4,5},{5,4},{6,7},{7,6},{10,11},{11,10},{12,13},{13,12... | collective-permute-start | bytes 1572872 | tf_op jit(solution)/shard_map/ppermute | solution.py:365
  58.0 1.7 %collective-permute-start.29 = (bf16[512,512]{1,0:T(8,128)(2,1)}, bf16[512,512]{1,0:T(8,128)(2,1)}, u32[]{:S(2)}, u32[]{:S(2)}) collective-permute-start(bf16[512,512]{1,0:T(8,128)(2,1)} %refs_28_.1), channel_id=1, source_target_pairs={{0,24},{8,16},{16,8},{24,0},{1,25},{9,17},{17,9},{25,1},{2,26},{10... | collective-permute-start | bytes 1572872 | tf_op jit(solution)/shard_map/ppermute | solution.py:430
  59.7 0.7 copy-done.5
  60.4 0.2 collective-permute-start.15
  60.7 8.6 %collective-permute-start.11 = (bf16[272,512]{1,0:T(8,128)(2,1)S(1)}, bf16[272,512]{1,0:T(8,128)(2,1)S(1)}, u32[]{:S(2)}, u32[]{:S(2)}) collective-permute-start(bf16[272,512]{1,0:T(8,128)(2,1)S(1)} %collective-permute-done.10.refs_6_.refs_10_), channel_id=1, source_target_pairs={{0,8},{1,9},{2,10},{3,11},{4,12},{5,13},{6,14},{7,15},{8,0},{9,1},... | collective-permute-start | bytes 835592 | tf_op jit(solution)/shard_map/ppermute | solution.py:365
  69.2 10.4 %collective-permute-done.23.refs_24_ = bf16[512,512]{1,0:T(8,128)(2,1)S(1)} collective-permute-done((bf16[512,512]{1,0:T(8,128)(2,1)}, bf16[512,512]{1,0:T(8,128)(2,1)S(1)}, u32[]{:S(2)}, u32[]{:S(2)}) %collective-permute-start.23) | collective-permute-done | bytes 524320 | tf_op jit(solution)/shard_map/ppermute | solution.py:365
  79.7 0.8 copy-done.9
  80.5 0.5 collective-permute-start.19
  81.0 0.1 stack.89.place_ref
  81.1 0.2 stack.86.place_ref
  81.3 0.0 copy-start
  81.3 1.5 collective-permute-start.28
  82.7 0.3 collective-permute-start.27
  83.0 2.1 %collective-permute-start.26 = (bf16[512,512]{1,0:T(8,128)(2,1)}, bf16[512,512]{1,0:T(8,128)(2,1)S(1)}, u32[]{:S(2)}, u32[]{:S(2)}) collective-permute-start(bf16[512,512]{1,0:T(8,128)(2,1)} %copy-done.8), channel_id=1, source_target_pairs={{0,1},{1,0},{4,5},{5,4},{6,7},{7,6},{8,9},{9,8},{12,13},{13,12},{1... | collective-permute-start | bytes 1572872 | tf_op jit(solution)/shard_map/ppermute | solution.py:365
  85.2 0.7 collective-permute-start.24
  85.9 3.3 %collective-permute-start.22 = (bf16[512,512]{1,0:T(8,128)(2,1)}, bf16[512,512]{1,0:T(8,128)(2,1)S(1)}, u32[]{:S(2)}, u32[]{:S(2)}) collective-permute-start(bf16[512,512]{1,0:T(8,128)(2,1)} %copy-done.7), channel_id=1, source_target_pairs={{0,1},{1,0},{2,3},{3,2},{4,5},{5,4},{8,9},{9,8},{10,11},{11,10},{1... | collective-permute-start | bytes 1572872 | tf_op jit(solution)/shard_map/ppermute | solution.py:365
  89.2 0.9 copy-done.2
  90.2 0.9 copy-done.4
  91.1 0.9 copy-done.6
  92.1 46.9 %factor_panel.1 = (bf16[1024,1024]{1,0:T(8,128)(2,1)}, bf16[1024,1024]{1,0:T(8,128)(2,1)}, bf16[1024,128]{1,0:T(8,128)(2,1)}, bf16[1024,128]{1,0:T(8,128)(2,1)}) custom-call(s32[36]{0:T(128)S(1)} %stack.89.place_ref, bf16[256,512]{1,0:T(8,128)(2,1)S(1)} %broadcast_select_fusion.3.refs_0_.refs_4_, ...), custom_call_target="tpu_custom_call" | custom-call | flops 40000000000 | bytes 16777216 | tf_op jit(solution)/shard_map/factor_panel/pallas_call | solution.py:215
  139.1 0.7 copy-done.10
  139.8 0.2 copy-done.11
  140.0 0.2 copy-done.12
  140.2 0.2 copy-done.13
  140.4 0.2 copy-done.14
  140.6 25.4 %finish_tile.1 = f32[1024,512]{1,0:T(8,128)} custom-call(s32[74]{0:T(128)S(1)} %stack.86.place_ref, f32[1,512]{1,0:T(1,128)S(1)} %bitcast.31, bf16[1024,1024]{1,0:T(8,128)(2,1)} %get-tuple-element.19.refs_0_, bf16[1024,1024]{1,0:T(8,128)(2,1)} %get-tuple-element.20.refs_1_, bf16[1024,128]{1,0:T(8,128)(2,1)} %get-tuple-element.21.refs_2_, ...), custom_call_target="tpu_custom_call" | custom-call | flops 20000000000 | bytes 25165824 | tf_op jit(solution)/shard_map/finish_tile/pallas_call | solution.py:324
  (44 shorter events, 0.2 us)
Async XLA Ops:
  1.0 10.0 %collective-permute-start = (bf16[256,512]{1,0:T(8,128)(2,1)S(1)}, bf16[256,512]{1,0:T(8,128)(2,1)S(1)}, u32[]{:S(2)}, u32[]{:S(2)}) collective-permute-start(bf16[256,512]{1,0:T(8,128)(2,1)S(1)} %slice.6), channel_id=1, source_target_pairs={{0,4},{1,5},{8,12},{9,13},{16,20},{17,21},{24,28},{25,29}} | collective-permute-start | bytes 786440 | tf_op jit(solution)/shard_map/ppermute | solution.py:365
  3.4 12.9 %collective-permute-start.2 = (bf16[256,512]{1,0:T(8,128)(2,1)S(1)}, bf16[256,512]{1,0:T(8,128)(2,1)S(1)}, u32[]{:S(2)}, u32[]{:S(2)}) collective-permute-start(bf16[256,512]{1,0:T(8,128)(2,1)S(1)} %get-tuple-element.32), channel_id=1, source_target_pairs={{0,0},{1,16},{2,2},{3,18},{4,4},{5,20},{6,6},{7,22},{8,8},{9,24},{... | collective-permute-start | bytes 786440 | tf_op jit(solution)/shard_map/ppermute | solution.py:365
  12.0 9.4 %collective-permute-start.5 = (bf16[272,512]{1,0:T(8,128)(2,1)S(1)}, bf16[272,512]{1,0:T(8,128)(2,1)S(1)}, u32[]{:S(2)}, u32[]{:S(2)}) collective-permute-start(bf16[272,512]{1,0:T(8,128)(2,1)S(1)} %pad_maximum_fusion), channel_id=1, source_target_pairs={{0,4},{1,5},{8,12},{9,13},{16,20},{17,21},{24,28},{25,29}} | collective-permute-start | bytes 835592 | tf_op jit(solution)/shard_map/ppermute | solution.py:365
  13.3 9.5 %collective-permute-start.3 = (bf16[256,512]{1,0:T(8,128)(2,1)S(1)}, bf16[256,512]{1,0:T(8,128)(2,1)S(1)}, u32[]{:S(2)}, u32[]{:S(2)}) collective-permute-start(bf16[256,512]{1,0:T(8,128)(2,1)S(1)} %get-tuple-element.31), channel_id=1, source_target_pairs={{0,8},{1,24},{2,10},{3,26},{4,12},{5,28},{6,14},{7,30},{8,0},{9,16... | collective-permute-start | bytes 786440 | tf_op jit(solution)/shard_map/ppermute | solution.py:365
  15.0 10.6 %collective-permute-start.1 = (bf16[256,512]{1,0:T(8,128)(2,1)S(1)}, bf16[256,512]{1,0:T(8,128)(2,1)S(1)}, u32[]{:S(2)}, u32[]{:S(2)}) collective-permute-start(bf16[256,512]{1,0:T(8,128)(2,1)S(1)} %get-tuple-element.30), channel_id=1, source_target_pairs={{0,2},{1,3},{4,6},{5,7},{8,10},{9,11},{12,14},{13,15},{16,18},{17,... | collective-permute-start | bytes 786440 | tf_op jit(solution)/shard_map/ppermute | solution.py:365
  21.5 11.7 %collective-permute-start.6 = (bf16[272,512]{1,0:T(8,128)(2,1)S(1)}, bf16[272,512]{1,0:T(8,128)(2,1)S(1)}, u32[]{:S(2)}, u32[]{:S(2)}) collective-permute-start(bf16[272,512]{1,0:T(8,128)(2,1)S(1)} %broadcast_select_fusion), channel_id=1, source_target_pairs={{0,2},{1,3},{4,6},{5,7},{8,10},{9,11},{12,14},{13,15},{16,18},{17,... | collective-permute-start | bytes 835592 | tf_op jit(solution)/shard_map/ppermute | solution.py:365
  23.6 18.3 %collective-permute-start.21 = (bf16[512,512]{1,0:T(8,128)(2,1)}, bf16[512,512]{1,0:T(8,128)(2,1)S(1)}, u32[]{:S(2)}, u32[]{:S(2)}) collective-permute-start(bf16[512,512]{1,0:T(8,128)(2,1)} %constant_dynamic-update-slice_fusion.refs_20_), channel_id=1, source_target_pairs={{2,0},{3,1},{4,2},{5,3},{6,4},{7,5},{10,8},{11,9},{12,10},{13,11},... | collective-permute-start | bytes 1572872 | tf_op jit(solution)/shard_map/ppermute | solution.py:365
  25.6 7.7 %collective-permute-start.12 = (bf16[256,512]{1,0:T(8,128)(2,1)S(1)}, bf16[256,512]{1,0:T(8,128)(2,1)S(1)}, u32[]{:S(2)}, u32[]{:S(2)}) collective-permute-start(bf16[256,512]{1,0:T(8,128)(2,1)S(1)} %broadcast_select_fusion.3.refs_0_.refs_4_), channel_id=1, source_target_pairs={{0,1},{1,0},{2,3},{3,2},{4,5},{5,4},{6,7},{7,6},{8,9},{9,8},{10,11... | collective-permute-start | bytes 786440 | tf_op jit(solution)/shard_map/ppermute | solution.py:365
  26.9 9.8 %collective-permute-start.8 = (bf16[256,512]{1,0:T(8,128)(2,1)S(1)}, bf16[256,512]{1,0:T(8,128)(2,1)S(1)}, u32[]{:S(2)}, u32[]{:S(2)}) collective-permute-start(bf16[256,512]{1,0:T(8,128)(2,1)S(1)} %broadcast_select_fusion.3.refs_0_.refs_4_), channel_id=1, source_target_pairs={{0,16},{1,17},{2,18},{3,19},{4,20},{5,21},{6,22},{7,23},{8,24},{9,... | collective-permute-start | bytes 786440 | tf_op jit(solution)/shard_map/ppermute | solution.py:365
  28.1 10.9 %collective-permute-start.4 = (bf16[256,512]{1,0:T(8,128)(2,1)S(1)}, bf16[256,512]{1,0:T(8,128)(2,1)S(1)}, u32[]{:S(2)}, u32[]{:S(2)}) collective-permute-start(bf16[256,512]{1,0:T(8,128)(2,1)S(1)} %broadcast_select_fusion.3.refs_0_.refs_4_), channel_id=1, source_target_pairs={{0,8},{1,9},{2,10},{3,11},{4,12},{5,13},{6,14},{7,15},{8,0},{9,1},... | collective-permute-start | bytes 786440 | tf_op jit(solution)/shard_map/ppermute | solution.py:365
  33.2 8.6 %collective-permute-start.14 = (bf16[272,512]{1,0:T(8,128)(2,1)S(1)}, bf16[272,512]{1,0:T(8,128)(2,1)S(1)}, u32[]{:S(2)}, u32[]{:S(2)}) collective-permute-start(bf16[272,512]{1,0:T(8,128)(2,1)S(1)} %broadcast_select_fusion.1.refs_2_.refs_6_), channel_id=1, source_target_pairs={{0,1},{1,0},{2,3},{3,2},{4,5},{5,4},{6,7},{7,6},{8,9},{9,8},{10,11... | collective-permute-start | bytes 835592 | tf_op jit(solution)/shard_map/ppermute | solution.py:365
  33.3 12.2 %collective-permute-start.13 = (bf16[256,512]{1,0:T(8,128)(2,1)S(1)}, bf16[256,512]{1,0:T(8,128)(2,1)S(1)}, u32[]{:S(2)}, u32[]{:S(2)}) collective-permute-start(bf16[256,512]{1,0:T(8,128)(2,1)S(1)} %collective-permute-done.12.refs_8_.refs_12_), channel_id=1, source_target_pairs={{0,8},{1,9},{2,10},{3,11},{4,12},{5,13},{6,14},{7,15},{8,0},{9,1},... | collective-permute-start | bytes 786440 | tf_op jit(solution)/shard_map/ppermute | solution.py:365
  36.6 12.6 %collective-permute-start.10 = (bf16[272,512]{1,0:T(8,128)(2,1)S(1)}, bf16[272,512]{1,0:T(8,128)(2,1)S(1)}, u32[]{:S(2)}, u32[]{:S(2)}) collective-permute-start(bf16[272,512]{1,0:T(8,128)(2,1)S(1)} %broadcast_select_fusion.1.refs_2_.refs_6_), channel_id=1, source_target_pairs={{0,16},{1,17},{2,18},{3,19},{4,20},{5,21},{6,22},{7,23},{8,24},{9,... | collective-permute-start | bytes 835592 | tf_op jit(solution)/shard_map/ppermute | solution.py:365
  39.0 8.7 %collective-permute-start.16 = (bf16[256,512]{1,0:T(8,128)(2,1)S(1)}, bf16[256,512]{1,0:T(8,128)(2,1)S(1)}, u32[]{:S(2)}, u32[]{:S(2)}) collective-permute-start(bf16[256,512]{1,0:T(8,128)(2,1)S(1)} %collective-permute-done.8.refs_4_.refs_8_), channel_id=1, source_target_pairs={{0,1},{1,0},{2,3},{3,2},{4,5},{5,4},{6,7},{7,6},{8,9},{9,8},{10,11... | collective-permute-start | bytes 786440 | tf_op jit(solution)/shard_map/ppermute | solution.py:365
  41.8 9.8 %collective-permute-start.18 = (bf16[272,512]{1,0:T(8,128)(2,1)S(1)}, bf16[272,512]{1,0:T(8,128)(2,1)S(1)}, u32[]{:S(2)}, u32[]{:S(2)}) collective-permute-start(bf16[272,512]{1,0:T(8,128)(2,1)S(1)} %collective-permute-done.14.refs_10_.refs_14_), channel_id=1, source_target_pairs={{0,16},{1,17},{2,18},{3,19},{4,20},{5,21},{6,22},{7,23},{8,24},{9,... | collective-permute-start | bytes 835592 | tf_op jit(solution)/shard_map/ppermute | solution.py:365
  41.9 27.4 %copy-start.7 = (bf16[512,512]{1,0:T(8,128)(2,1)}, bf16[512,512]{1,0:T(8,128)(2,1)S(1)}, u32[]{:S(2)}) copy-start(bf16[512,512]{1,0:T(8,128)(2,1)S(1)} %collective-permute-done.21.refs_22_) | copy-start | bytes 1572868
  41.9 18.8 %collective-permute-start.25 = (bf16[512,512]{1,0:T(8,128)(2,1)}, bf16[512,512]{1,0:T(8,128)(2,1)S(1)}, u32[]{:S(2)}, u32[]{:S(2)}) collective-permute-start(bf16[512,512]{1,0:T(8,128)(2,1)} %constant_dynamic-update-slice_fusion.refs_20_), channel_id=1, source_target_pairs={{2,4},{3,5},{4,6},{5,7},{6,0},{7,1},{10,12},{11,13},{12,14},{13,15... | collective-permute-start | bytes 1572872 | tf_op jit(solution)/shard_map/ppermute | solution.py:365
  45.6 34.1 %collective-permute-start.23 = (bf16[512,512]{1,0:T(8,128)(2,1)}, bf16[512,512]{1,0:T(8,128)(2,1)S(1)}, u32[]{:S(2)}, u32[]{:S(2)}) collective-permute-start(bf16[512,512]{1,0:T(8,128)(2,1)} %constant_dynamic-update-slice_fusion.refs_20_), channel_id=1, source_target_pairs={{2,6},{3,7},{4,0},{5,1},{6,2},{7,3},{10,14},{11,15},{12,8},{13,9},... | collective-permute-start | bytes 1572872 | tf_op jit(solution)/shard_map/ppermute | solution.py:365
  47.6 10.4 %collective-permute-start.7 = (bf16[272,512]{1,0:T(8,128)(2,1)S(1)}, bf16[272,512]{1,0:T(8,128)(2,1)S(1)}, u32[]{:S(2)}, u32[]{:S(2)}) collective-permute-start(bf16[272,512]{1,0:T(8,128)(2,1)S(1)} %broadcast_select_fusion.1.refs_2_.refs_6_), channel_id=1, source_target_pairs={{0,8},{1,9},{2,10},{3,11},{4,12},{5,13},{6,14},{7,15},{8,0},{9,1},... | collective-permute-start | bytes 835592 | tf_op jit(solution)/shard_map/ppermute | solution.py:365
  49.2 4.0 %collective-permute-start.9 = (bf16[256,512]{1,0:T(8,128)(2,1)S(1)}, bf16[256,512]{1,0:T(8,128)(2,1)S(1)}, u32[]{:S(2)}, u32[]{:S(2)}) collective-permute-start(bf16[256,512]{1,0:T(8,128)(2,1)S(1)} %collective-permute-done.8.refs_4_.refs_8_), channel_id=1, source_target_pairs={{0,8},{1,9},{2,10},{3,11},{4,12},{5,13},{6,14},{7,15},{8,0},{9,1},... | collective-permute-start | bytes 786440 | tf_op jit(solution)/shard_map/ppermute | solution.py:365
  51.6 8.2 %collective-permute-start.17 = (bf16[256,512]{1,0:T(8,128)(2,1)S(1)}, bf16[256,512]{1,0:T(8,128)(2,1)S(1)}, u32[]{:S(2)}, u32[]{:S(2)}) collective-permute-start(bf16[256,512]{1,0:T(8,128)(2,1)S(1)} %collective-permute-done.16.refs_12_.refs_16_), channel_id=1, source_target_pairs={{0,8},{1,9},{2,10},{3,11},{4,12},{5,13},{6,14},{7,15},{8,0},{9,1},... | collective-permute-start | bytes 786440 | tf_op jit(solution)/shard_map/ppermute | solution.py:365
  52.5 0.7 copy-start.1
  53.2 0.7 copy-start.3
  53.9 31.3 %collective-permute-start.20 = (bf16[512,512]{1,0:T(8,128)(2,1)}, bf16[512,512]{1,0:T(8,128)(2,1)}, u32[]{:S(2)}, u32[]{:S(2)}) collective-permute-start(bf16[512,512]{1,0:T(8,128)(2,1)} %constant_dynamic-update-slice_fusion.refs_20_), channel_id=1, source_target_pairs={{2,3},{3,2},{4,5},{5,4},{6,7},{7,6},{10,11},{11,10},{12,13},{13,12... | collective-permute-start | bytes 1572872 | tf_op jit(solution)/shard_map/ppermute | solution.py:365
  58.0 27.9 %collective-permute-start.29 = (bf16[512,512]{1,0:T(8,128)(2,1)}, bf16[512,512]{1,0:T(8,128)(2,1)}, u32[]{:S(2)}, u32[]{:S(2)}) collective-permute-start(bf16[512,512]{1,0:T(8,128)(2,1)} %refs_28_.1), channel_id=1, source_target_pairs={{0,24},{8,16},{16,8},{24,0},{1,25},{9,17},{17,9},{25,1},{2,26},{10... | collective-permute-start | bytes 1572872 | tf_op jit(solution)/shard_map/ppermute | solution.py:430
  59.7 0.7 copy-start.5
  60.4 20.8 %collective-permute-start.15 = (bf16[272,512]{1,0:T(8,128)(2,1)S(1)}, bf16[272,512]{1,0:T(8,128)(2,1)S(1)}, u32[]{:S(2)}, u32[]{:S(2)}) collective-permute-start(bf16[272,512]{1,0:T(8,128)(2,1)S(1)} %collective-permute-done.14.refs_10_.refs_14_), channel_id=1, source_target_pairs={{0,8},{1,9},{2,10},{3,11},{4,12},{5,13},{6,14},{7,15},{8,0},{9,1},... | collective-permute-start | bytes 835592 | tf_op jit(solution)/shard_map/ppermute | solution.py:365
  60.7 19.0 %copy-start.8 = (bf16[512,512]{1,0:T(8,128)(2,1)}, bf16[512,512]{1,0:T(8,128)(2,1)S(1)}, u32[]{:S(2)}) copy-start(bf16[512,512]{1,0:T(8,128)(2,1)S(1)} %collective-permute-done.25.refs_26_) | copy-start | bytes 1572868
  60.7 22.1 %collective-permute-start.11 = (bf16[272,512]{1,0:T(8,128)(2,1)S(1)}, bf16[272,512]{1,0:T(8,128)(2,1)S(1)}, u32[]{:S(2)}, u32[]{:S(2)}) collective-permute-start(bf16[272,512]{1,0:T(8,128)(2,1)S(1)} %collective-permute-done.10.refs_6_.refs_10_), channel_id=1, source_target_pairs={{0,8},{1,9},{2,10},{3,11},{4,12},{5,13},{6,14},{7,15},{8,0},{9,1},... | collective-permute-start | bytes 835592 | tf_op jit(solution)/shard_map/ppermute | solution.py:365
  79.7 0.8 copy-start.9
  80.5 2.6 %collective-permute-start.19 = (bf16[272,512]{1,0:T(8,128)(2,1)S(1)}, bf16[272,512]{1,0:T(8,128)(2,1)S(1)}, u32[]{:S(2)}, u32[]{:S(2)}) collective-permute-start(bf16[272,512]{1,0:T(8,128)(2,1)S(1)} %collective-permute-done.18.refs_14_.refs_18_), channel_id=1, source_target_pairs={{0,8},{1,9},{2,10},{3,11},{4,12},{5,13},{6,14},{7,15},{8,0},{9,1},... | collective-permute-start | bytes 835592 | tf_op jit(solution)/shard_map/ppermute | solution.py:365
  81.3 59.3 %copy-start = (f32[512]{0:T(512)S(1)}, f32[512]{0:T(512)}, u32[]{:S(2)}) copy-start(f32[512]{0:T(512)} %param.3) | copy-start | bytes 6148
  81.3 57.7 %collective-permute-start.28 = (bf16[512,512]{1,0:T(8,128)(2,1)}, bf16[512,512]{1,0:T(8,128)(2,1)S(1)}, u32[]{:S(2)}, u32[]{:S(2)}) collective-permute-start(bf16[512,512]{1,0:T(8,128)(2,1)} %refs_28_.1), channel_id=1, source_target_pairs={{0,16},{8,24},{16,0},{24,8},{1,17},{9,25},{17,1},{25,9},{2,18},{10... | collective-permute-start | bytes 1572872 | tf_op jit(solution)/shard_map/ppermute | solution.py:430
  82.7 56.3 %collective-permute-start.27 = (bf16[512,512]{1,0:T(8,128)(2,1)}, bf16[512,512]{1,0:T(8,128)(2,1)S(1)}, u32[]{:S(2)}, u32[]{:S(2)}) collective-permute-start(bf16[512,512]{1,0:T(8,128)(2,1)} %refs_28_.1), channel_id=1, source_target_pairs={{0,8},{8,0},{16,24},{24,16},{1,9},{9,1},{17,25},{25,17},{2,10},{10... | collective-permute-start | bytes 1572872 | tf_op jit(solution)/shard_map/ppermute | solution.py:430
  83.0 56.0 %collective-permute-start.26 = (bf16[512,512]{1,0:T(8,128)(2,1)}, bf16[512,512]{1,0:T(8,128)(2,1)S(1)}, u32[]{:S(2)}, u32[]{:S(2)}) collective-permute-start(bf16[512,512]{1,0:T(8,128)(2,1)} %copy-done.8), channel_id=1, source_target_pairs={{0,1},{1,0},{4,5},{5,4},{6,7},{7,6},{8,9},{9,8},{12,13},{13,12},{1... | collective-permute-start | bytes 1572872 | tf_op jit(solution)/shard_map/ppermute | solution.py:365
  85.2 53.9 %collective-permute-start.24 = (bf16[512,512]{1,0:T(8,128)(2,1)}, bf16[512,512]{1,0:T(8,128)(2,1)S(1)}, u32[]{:S(2)}, u32[]{:S(2)}) collective-permute-start(bf16[512,512]{1,0:T(8,128)(2,1)} %copy-done.9), channel_id=1, source_target_pairs={{0,1},{1,0},{2,3},{3,2},{6,7},{7,6},{8,9},{9,8},{10,11},{11,10},{1... | collective-permute-start | bytes 1572872 | tf_op jit(solution)/shard_map/ppermute | solution.py:365
  85.9 53.2 %collective-permute-start.22 = (bf16[512,512]{1,0:T(8,128)(2,1)}, bf16[512,512]{1,0:T(8,128)(2,1)S(1)}, u32[]{:S(2)}, u32[]{:S(2)}) collective-permute-start(bf16[512,512]{1,0:T(8,128)(2,1)} %copy-done.7), channel_id=1, source_target_pairs={{0,1},{1,0},{2,3},{3,2},{4,5},{5,4},{8,9},{9,8},{10,11},{11,10},{1... | collective-permute-start | bytes 1572872 | tf_op jit(solution)/shard_map/ppermute | solution.py:365
  89.2 1.0 copy-start.2
  90.2 0.9 copy-start.4
  91.1 0.9 copy-start.6
  139.0 0.8 copy-start.10
  139.0 1.0 copy-start.11
  139.0 1.2 copy-start.12
  139.1 1.3 copy-start.13
  139.1 1.5 copy-start.14

commit v2 on v1

--- a/solution.py
+++ b/solution.py
@@ -1,4 +1,5 @@
 import functools
+import math
 import jax
 import jax.numpy as jnp
 from jax import lax
@@ -111,17 +112,16 @@
 
 
 def place_pieces(place_ref, first, pieces, helds, sem):
-    copies = []
+    waits = []
     for i, (piece, held_ref) in enumerate(zip(pieces, helds)):
         rows, users = piece.shape
-        row = pl.multiple_of(place_ref[first + 2 * i], rows)
+        row = place_ref[first + 2 * i]
         user = pl.multiple_of(place_ref[first + 2 * i + 1], users)
-        copy = pltpu.make_async_copy(
-            piece, held_ref.at[pl.ds(row, rows), pl.ds(user, users)], sem.at[i]
-        )
-        copy.start()
-        copies.append(copy)
-    return copies
+        to = held_ref.at[pl.ds(pl.multiple_of(jnp.maximum(row, 0), rows), rows), pl.ds(user, users)]
+        copy = pltpu.make_async_copy(piece, to, sem.at[i])
+        pl.when(row >= 0)(copy.start)
+        waits.append(functools.partial(pl.when(row >= 0), copy.wait))
+    return waits
 
 
 def panel_kernel(views, count, width, place_ref, *refs):
@@ -129,8 +129,8 @@
     outs, (high_ref, low_ref, inv_high_ref, inv_low_ref, lower_ref, block_ref, inverse_ref, items_ref, parts_ref, sem, out_sem) = refs[:4], refs[4:]
     held = [parts_ref if is_part else items_ref for _, _, _, is_part in views]
     views = [pieces[which].at[pl.ds(start, rows)] for which, start, rows, _ in views]
-    for copy in place_pieces(place_ref, 0, views, held, sem):
-        copy.wait()
+    for wait in place_pieces(place_ref, 0, views, held, sem):
+        wait()
     on_diagonal = lax.broadcasted_iota(jnp.int32, (BLOCK, BLOCK), 0) == lax.broadcasted_iota(
         jnp.int32, (BLOCK, BLOCK), 1
     )
@@ -194,8 +194,8 @@
             copy.wait()
 
 
-def room(users):
-    return (2 * PANEL * users + 32 * 1024 * 1024) // 2**20 * 2**20
+def room(*arrays):
+    return sum(math.prod(shape) * jnp.dtype(dtype).itemsize for shape, dtype in arrays) + 8 * 2**20
 
 
 def factor_panel(place, pieces, views, width, users):
@@ -220,7 +220,7 @@
         out_specs=[pl.BlockSpec(memory_space=pltpu.HBM)] * len(outs),
         scratch_shapes=[VMEM(*one) for one in outs + held]
         + [pltpu.SemaphoreType.DMA((len(views),)), pltpu.SemaphoreType.DMA((len(outs), NBLOCKS))],
-        compiler_params=pltpu.CompilerParams(vmem_limit_bytes=room(users)),
+        compiler_params=pltpu.CompilerParams(vmem_limit_bytes=room(*outs, *held)),
         cost_estimate=pl.CostEstimate(flops=4 * 10**10, bytes_accessed=16 * 2**20, transcendentals=1024),
         name="factor_panel",
     )(place, *pieces)
@@ -241,13 +241,12 @@
     ]
     for fetch in fetches:
         fetch.start()
-    copies = place_pieces(place_ref, 2, views, held, sem)
+    waits = place_pieces(place_ref, 2, views, held, sem)
     for fetch in fetches:
         fetch.wait()
     row_index, col_index = place_ref[0], place_ref[1]
-    width, band = cols_ref.shape[0], rows_ref.shape[0] // SPAN
+    width, band = cols_ref.shape[0], rows_ref.shape[0] // (SPAN - 1)
     row_count = (SPAN - 1) * band
-    lower_items = rows_ref.at[pl.ds(band, row_count), :]
     panel_blocks = PANEL // width
     in_panel = col_index < panel_blocks
     slot = jnp.minimum(col_index, panel_blocks - 1)
@@ -275,14 +274,14 @@
             column = dot_nt3(split(column), (wide_high_ref[here, :], wide_low_ref[here, :]))
             left_high_ref[mine, here], left_low_ref[mine, here] = split(column)
 
-    for copy, target in zip(copies, held):
+    for wait, target in zip(waits, held):
         if target is not rows_ref:
-            copy.wait()
+            wait()
     solve(cols_ref, right)
-    for copy, target in zip(copies, held):
+    for wait, target in zip(waits, held):
         if target is rows_ref:
-            copy.wait()
-    solve(lower_items, below)
+            wait()
+    solve(rows_ref, below)
 
     @pl.when(in_panel)
     def _():
@@ -297,7 +296,7 @@
         columns = lax.broadcasted_iota(jnp.int32, (band, width), 1) + col_index * width
         for part in range(SPAN - 1):
             mine = pl.ds(part * band, band)
-            tile = dot_nt(lower_items[mine, :], cols_ref[...])
+            tile = dot_nt(rows_ref[mine, :], cols_ref[...])
             tile = tile + jnp.where(items + (part + 1) * PANEL == columns, regular_ref[...], 0.0)
             out_ref[pl.ds((part + 1) * band, band), :] = tile - dot_nt3(
                 (left_high_ref[mine, :], left_low_ref[mine, :]), (left_high_ref[right, :], left_low_ref[right, :])
@@ -307,7 +306,6 @@
 def finish_tile(place, regular, factors, panel, rows, cols, views, band, users):
     spec = pl.BlockSpec(memory_space=VMEM)
     width = regular.shape[1]
-    rows, cols = ([pltpu.with_memory_space_constraint(x, pltpu.HBM) for x in group] for group in (rows, cols))
     factors = [pltpu.with_memory_space_constraint(x, pltpu.HBM) for x in factors]
     pieces = panel + rows + cols
     out = ((SPAN * band, width), f32)
@@ -318,7 +316,7 @@
         ((PANEL, WIDE), bf16),
         ((PANEL, WIDE), bf16),
         ((PANEL, users), bf16),
-        ((SPAN * band, users), bf16),
+        (((SPAN - 1) * band, users), bf16),
         ((width, users), bf16),
     ]
     return pl.pallas_call(
@@ -327,13 +325,12 @@
         in_specs=[pl.BlockSpec(memory_space=pltpu.SMEM)]
         + [spec]
         + [pl.BlockSpec(memory_space=pltpu.HBM)] * len(factors)
-        + [pl.BlockSpec(memory_space=pl.ANY)] * len(panel)
-        + [pl.BlockSpec(memory_space=pltpu.HBM)] * (len(rows) + len(cols)),
+        + [pl.BlockSpec(memory_space=pl.ANY)] * len(pieces),
         out_specs=spec,
         scratch_shapes=[VMEM(factor.shape, factor.dtype) for factor in factors]
         + [VMEM(*one) for one in held]
         + [pltpu.SemaphoreType.DMA((len(views),)), pltpu.SemaphoreType.DMA((len(factors),))],
-        compiler_params=pltpu.CompilerParams(vmem_limit_bytes=room(users)),
+        compiler_params=pltpu.CompilerParams(vmem_limit_bytes=room(out, *held, *((factor.shape, factor.dtype) for factor in factors))),
         cost_estimate=pl.CostEstimate(flops=20 * 10**9, bytes_accessed=24 * 2**20, transcendentals=0),
         name="finish_tile",
     )(place, regular, *factors, *pieces)
@@ -372,19 +369,28 @@
     parts = jnp.stack([high, middle, regular - high - middle]).astype(bf16)
     parts = jnp.pad(parts, ((0, PARTS - 3), (0, users - width)))
 
+    halves = interactions.reshape(CORES, band, users)
+    offers = [lax.dynamic_index_in_dim(halves, core ^ flip, 0, False) for flip in range(CORES)]
+
     half = width // 2
-    shared = [interactions[:half], jnp.concatenate([interactions[half:], parts], 0)]
+    shared = jnp.concatenate([interactions, parts], 0)
+    quarters, quarter_users = [], []
     reach = SPAN // 2
     while reach:
-        got = [
-            exchange(part, lambda p, h, s, w: (p, h, s + reach, w), lambda p, h, s, w: s % (2 * reach) == 0)
-            for part in shared
-        ]
-        shared = [jnp.where(slot % (2 * reach) == reach, new, old) for new, old in zip(got, shared)]
+        got = exchange(
+            shared, lambda p, h, s, w: (p, h, s + reach, w), lambda p, h, s, w: s % (2 * reach) == 0
+        )
+        if reach == SPAN // 2:
+            for turn in reversed(range(ways)):
+                for flip in range(CORES):
+                    quarters.append(
+                        exchange(offers[flip], lambda p, h, s, w: (w, h ^ flip, s, (p + turn) % ways))
+                    )
+                    quarter_users.append(((way - turn) % ways * CORES + (core ^ flip)) * users)
+            got = after(got, *quarters[:CORES])
+        shared = jnp.where(slot % (2 * reach) == reach, got, shared)
         reach //= 2
-
-    halves = interactions.reshape(CORES, band, users)
-    offers = [lax.dynamic_index_in_dim(halves, core ^ flip, 0, False) for flip in range(CORES)]
+    quarters = jnp.concatenate(quarters, 0)
 
     def numbers(values):
         return jnp.stack([jnp.asarray(v, jnp.int32) for v in values])
@@ -403,66 +409,63 @@
         return exchange(value, lambda p, h, s, w: (p, h, s, 1 - w), only)
 
     if ways == 2:
-        swapped = jnp.concatenate(
-            [exchange(offers[flip], lambda p, h, s, w: (w, h ^ flip, s, p)) for flip in range(CORES)], 0
-        )
-        shared = [after(part, swapped) for part in shared]
-        pair_side = [over_pair(part) for part in shared]
-        way_side = [over_way(part) for part in shared]
-        diagonal = [over_way(pair_side[0]), over_pair(way_side[1])]
-        for from_pair, from_way, pieces in (
-            (pair, way, shared),
-            (1 - pair, way, pair_side),
-            (pair, 1 - way, way_side),
-            (1 - pair, 1 - way, diagonal),
+        twin_items = over_core(interactions)
+        shared = after(shared, quarters, twin_items)
+        pair_side, way_side = over_pair(shared), over_way(shared)
+        own_twin = over_core(shared)
+        diagonal = [over_way(after(pair_side, own_twin)[:half]), over_pair(after(way_side, own_twin)[half:])]
+        for from_pair, from_way, first_row, piece in (
+            (pair, way, 0, shared),
+            (1 - pair, way, 0, pair_side),
+            (pair, 1 - way, 0, way_side),
+            (1 - pair, 1 - way, 0, diagonal[0]),
+            (1 - pair, 1 - way, half, diagonal[1]),
         ):
-            for which, piece in enumerate(pieces):
-                for from_core, value in ((core, piece), (1 - core, over_core(piece))):
-                    if which and value is piece and (pieces is shared or pieces is way_side):
-                        part_views.append((len(panel), half, PARTS, True))
-                        part_place += [from_way * PARTS, 0]
-                    panel_views.append((len(panel), 0, half, False))
-                    panel_place += [from_way * width + which * half, (from_pair * CORES + from_core) * users]
-                    panel.append(value)
-        crossed = [*pair_side, *way_side, *diagonal]
+            twin = own_twin if piece is shared else over_core(piece)
+            for from_core, value in ((core, piece), (1 - core, twin)):
+                if value is shared or value is way_side:
+                    part_views.append((len(panel), width, PARTS, True))
+                    part_place += [from_way * PARTS, 0]
+                count = min(value.shape[0], half if value.shape[0] < width else width)
+                panel_views.append((len(panel), 0, count, False))
+                panel_place += [from_way * width + first_row, (from_pair * CORES + from_core) * users]
+                panel.append(value)
+        crossed = [pair_side, way_side, *diagonal]
         held = after(interactions, *crossed)
-        for flip in range(1, row_count):
-            cols.append(lax.ppermute(held, "row", [(r, r ^ flip) for r in range(row_count)]))
-            cols_place += [0, (row_index ^ flip) * users]
-        for turn in range(SPAN):
-            piece = swapped
-            if turn:
-                piece = exchange(
-                    swapped if turn == 1 else after(swapped, *got),
-                    lambda p, h, s, w: (p, h, (s - turn) % SPAN, w),
-                    lambda p, h, s, w: s > 0,
-                )
-            twin = over_way(after(piece, *crossed), lambda p, h, s, w: (s + turn) % SPAN > 0)
-            for from_way, value in ((way, piece), (1 - way, twin)):
-                for flip in range(CORES):
-                    rows_views.append((len(rows), flip * band, band))
-                    rows_place += [(slot + turn) % SPAN * band, (from_way * CORES + (core ^ flip)) * users]
-                rows.append(value)
+        cols += [twin_items, over_pair(held), exchange(held, lambda p, h, s, w: (1 - p, 1 - h, s, w))]
+        cols_place += [0, (row_index ^ 1) * users, 0, (row_index ^ 2) * users, 0, (row_index ^ 3) * users]
+        first = exchange(quarters, lambda p, h, s, w: (p, h, s - 1, w), lambda p, h, s, w: s > 0)
+        relayed, ready = lax.optimization_barrier((first, quarters, *crossed))[:2]
+        second = exchange(relayed, lambda p, h, s, w: (p, h, s - 1, w), lambda p, h, s, w: 0 < s < SPAN - 1)
+        ring = exchange(ready, lambda p, h, s, w: (p, h, (s + 1) % SPAN, w), lambda p, h, s, w: s > 0)
+        leap = exchange(ready, lambda p, h, s, w: (p, h, s + 2, w), lambda p, h, s, w: s == 1)
+        rows = [quarters, first, second, ring, leap]
+        from_slots = [
+            slot,
+            jnp.where(slot < 3, slot + 1, 0),
+            jnp.where(slot < 2, slot + 2, 0),
+            jnp.where(slot == 1, 0, (slot + 3) % SPAN),
+            jnp.where(slot == 3, 1, 0),
+        ]
+        for from_slot, piece in enumerate(rows):
+            for which, from_users in enumerate(quarter_users):
+                rows_views.append((from_slot, which * band, band))
+                rows_place += [(from_slots[from_slot] - 1) * band, from_users]
     else:
         groups = [[s * ways + w for w in range(ways)] for s in range(SPAN)]
-        shared = lax.all_gather(jnp.concatenate(shared, 0), "col", axis=0, axis_index_groups=groups)
+        shared = lax.all_gather(shared, "col", axis=0, axis_index_groups=groups)
         parts = shared[:, width:].reshape(ways * PARTS, users)
         shared = shared[:, :width].reshape(PANEL, users)
         panel, panel_place = [lax.all_gather(shared, "row", axis=1, tiled=True), parts], [0, 0]
         panel_views = [(0, 0, PANEL, False)]
         part_views, part_place = [(1, 0, ways * PARTS, True)], [0, 0]
         cols, cols_place = [lax.all_gather(interactions, "row", axis=1, tiled=True)], [0, 0]
-        quarters, quarter_users = [], []
-        for turn in range(ways):
-            for flip in range(CORES):
-                quarters.append(exchange(offers[flip], lambda p, h, s, w: (w, h ^ flip, s, (p + turn) % ways)))
-                quarter_users.append(((way - turn) % ways * CORES + (core ^ flip)) * users)
         groups = [[s * ways + w for s in range(SPAN)] for w in range(ways)]
-        rows = [lax.all_gather(jnp.concatenate(quarters, 0), "col", axis=0, tiled=True, axis_index_groups=groups)]
+        rows = [lax.all_gather(quarters, "col", axis=0, tiled=True, axis_index_groups=groups)]
         for from_slot in range(1, SPAN):
             for which, from_users in enumerate(quarter_users):
-                rows_views.append((0, (from_slot * len(quarters) + which) * band, band))
-                rows_place += [from_slot * band, from_users]
+                rows_views.append((0, (from_slot * len(quarter_users) + which) * band, band))
+                rows_place += [(from_slot - 1) * band, from_users]
 
     factors = factor_panel(
         numbers(panel_place + part_place), panel, panel_views + part_views, width, all_users

time: 169 us -> 152 us (0.90)
  starting transfers between devices: 55.6 us -> 36.1 us
  waiting for transfers between devices: 24.7 us -> 34.1 us
  local copies, waits for them, and re-layouts: 11.1 us -> 5.68 us
    ppermute x27 -> x22, starting transfers between devices: 52.1 us -> 36.1 us  [exchange(): return lax.ppermute(value, ('row', 'col'), perm)]
    ppermute x27 -> x22, waiting for transfers between devices: 24.7 us -> 34.1 us  [exchange(): return lax.ppermute(value, ('row', 'col'), perm)]
    unnamed x31 -> x17, local copies, waits for them, and re-layouts: 7.98 us -> 3.67 us
    ppermute x3 -> x0, starting transfers between devices: 3.45 us -> none  [body(): lax.ppermute(held, 'row', [(r, r ^ flip) for r in range(row_count)])]
  transfers between devices with their start and end apart: 30 -> 22, of which waited for: 6 -> 8; matrix products, arithmetic and copies ran while one was open for 3% -> 2% of each run, Pallas kernels for 28% -> 32%
where the time goes in v2:
time: 152 us; the launch traced here: 151 us
  Pallas kernels  72.5 us (48%)
  starting transfers between devices  36.1 us (24%)
  waiting for transfers between devices  34.1 us (22%)
  local copies, waits for them, and re-layouts  5.68 us (4%)
  other arithmetic  2.04 us (1%)
    pallas_call x1, Pallas kernels, factor_panel(): pl.pallas_call(functools.partial(panel_kernel, views, len(pieces), width)...  48.1 us
    ppermute x22, starting transfers between devices, exchange(): return lax.ppermute(value, ('row', 'col'), perm)  36.1 us
    ppermute x22, waiting for transfers between devices, exchange(): return lax.ppermute(value, ('row', 'col'), perm)  34.1 us
    pallas_call x1, Pallas kernels, finish_tile(): pl.pallas_call(functools.partial(tile_kernel, (len(panel), len(rows), len...  24.4 us
    unnamed x17, local copies, waits for them, and re-layouts  3.67 us
  transfers between devices with their start and end apart: 22, of which 8 were waited for; matrix products, arithmetic and copies ran while one was open for 2% of the time, Pallas kernels for 32%

profile of v2, /device:TPU:17, one launch (start us, length us, event | category | flops | bytes accessed | tf_op | source)
XLA Modules:
  0.0 150.8 jit_solution(5315461422392983138)
XLA Ops:
  0.0 0.7 reduce-precision_convert_fusion.1
  0.8 1.1 pad_maximum_fusion
  1.9 1.3 collective-permute-start
  3.2 0.7 dynamic-slice_bitcast_fusion
  4.0 1.8 %collective-permute-start.2 = (bf16[256,512]{1,0:T(8,128)(2,1)S(1)}, bf16[256,512]{1,0:T(8,128)(2,1)S(1)}, u32[]{:S(2)}, u32[]{:S(2)}) collective-permute-start(bf16[256,512]{1,0:T(8,128)(2,1)S(1)} %get-tuple-element.27), channel_id=1, source_target_pairs={{0,9},{1,25},{2,11},{3,27},{4,13},{5,29},{6,15},{7,31},{8,1},{9,17... | collective-permute-start | bytes 786440 | tf_op jit(solution)/shard_map/ppermute | solution.py:362
  5.8 1.2 collective-permute-start.1
  7.0 5.9 %collective-permute-done.2 = bf16[256,512]{1,0:T(8,128)(2,1)S(1)} collective-permute-done((bf16[256,512]{1,0:T(8,128)(2,1)S(1)}, bf16[256,512]{1,0:T(8,128)(2,1)S(1)}, u32[]{:S(2)}, u32[]{:S(2)}) %collective-permute-start.2) | collective-permute-done | bytes 262176 | tf_op jit(solution)/shard_map/ppermute | solution.py:362
  12.9 5.5 %collective-permute-done.1 = bf16[256,512]{1,0:T(8,128)(2,1)S(1)} collective-permute-done((bf16[256,512]{1,0:T(8,128)(2,1)}, bf16[256,512]{1,0:T(8,128)(2,1)S(1)}, u32[]{:S(2)}, u32[]{:S(2)}) %collective-permute-start.1) | collective-permute-done | bytes 262176 | tf_op jit(solution)/shard_map/ppermute | solution.py:362
  18.4 0.0 collective-permute-done
  18.4 0.1 broadcast_select_fusion
  18.6 3.4 %collective-permute-start.3 = (bf16[528,512]{1,0:T(8,128)(2,1)S(1)}, bf16[528,512]{1,0:T(8,128)(2,1)}, u32[]{:S(2)}, u32[]{:S(2)}) collective-permute-start(bf16[528,512]{1,0:T(8,128)(2,1)S(1)} %broadcast_select_fusion), channel_id=1, source_target_pairs={{0,2},{1,3},{4,6},{5,7},{8,10},{9,11},{12,14},{13,15},{16,18},{17,... | collective-permute-start | bytes 1622024 | tf_op jit(solution)/shard_map/ppermute | solution.py:362
  22.0 3.6 %collective-permute-start.4 = (bf16[256,512]{1,0:T(8,128)(2,1)}, bf16[256,512]{1,0:T(8,128)(2,1)}, u32[]{:S(2)}, u32[]{:S(2)}) collective-permute-start(bf16[256,512]{1,0:T(8,128)(2,1)} %get-tuple-element.28), channel_id=1, source_target_pairs={{0,0},{1,16},{2,2},{3,18},{4,4},{5,20},{6,6},{7,22},{8,8},{9,24},{... | collective-permute-start | bytes 786440 | tf_op jit(solution)/shard_map/ppermute | solution.py:362
  25.6 0.7 collective-permute-start.5
  26.3 0.0 collective-permute-start.6
  26.4 0.0 collective-permute-done.4
  26.4 1.0 constant_dynamic-update-slice_fusion.1
  27.3 0.6 collective-permute-done.5
  27.9 1.0 constant_dynamic-update-slice_fusion.refs_14_
  28.9 3.5 %collective-permute-done.3 = bf16[528,512]{1,0:T(8,128)(2,1)} collective-permute-done((bf16[528,512]{1,0:T(8,128)(2,1)S(1)}, bf16[528,512]{1,0:T(8,128)(2,1)}, u32[]{:S(2)}, u32[]{:S(2)}) %collective-permute-start.3) | collective-permute-done | bytes 540704 | tf_op jit(solution)/shard_map/ppermute | solution.py:362
  32.4 0.1 broadcast_select_fusion.1.refs_0_.refs_4_
  32.4 0.0 collective-permute-done.6.refs_20_
  32.4 0.0 copy-start.5
  32.5 0.8 copy-done.5
  33.3 8.6 %collective-permute-start.10 = (bf16[528,512]{1,0:T(8,128)(2,1)S(1)}, bf16[528,512]{1,0:T(8,128)(2,1)S(1)}, u32[]{:S(2)}, u32[]{:S(2)}) collective-permute-start(bf16[528,512]{1,0:T(8,128)(2,1)S(1)} %broadcast_select_fusion.1.refs_0_.refs_4_), channel_id=1, source_target_pairs={{0,1},{1,0},{2,3},{3,2},{4,5},{5,4},{6,7},{7,6},{8,9},{9,8},{10,11... | collective-permute-start | bytes 1622024 | tf_op jit(solution)/shard_map/ppermute | solution.py:362
  41.9 0.0 collective-permute-start.7
  41.9 0.0 collective-permute-start.8
  41.9 1.9 %collective-permute-start.16 = (bf16[1024,512]{1,0:T(8,128)(2,1)S(1)}, bf16[1024,512]{1,0:T(8,128)(2,1)}, u32[]{:S(2)}, u32[]{:S(2)}) collective-permute-start(bf16[1024,512]{1,0:T(8,128)(2,1)S(1)} %constant_dynamic-update-slice_fusion.refs_14_), channel_id=1, source_target_pairs={{2,0},{3,1},{4,2},{5,3},{6,4},{7,5},{10,8},{11,9},{12,10},{13,11},... | collective-permute-start | bytes 3145736 | tf_op jit(solution)/shard_map/ppermute | solution.py:362
  43.8 10.7 %collective-permute-done.10.refs_4_.refs_8_ = bf16[528,512]{1,0:T(8,128)(2,1)S(1)} collective-permute-done((bf16[528,512]{1,0:T(8,128)(2,1)S(1)}, bf16[528,512]{1,0:T(8,128)(2,1)S(1)}, u32[]{:S(2)}, u32[]{:S(2)}) %collective-permute-start.10) | collective-permute-done | bytes 540704 | tf_op jit(solution)/shard_map/ppermute | solution.py:362
  54.5 0.0 collective-permute-done.7.refs_1_.refs_5_
  54.5 0.8 copy-done.2
  55.3 1.7 %collective-permute-start.14 = (bf16[272,512]{1,0:T(8,128)(2,1)S(1)}, bf16[272,512]{1,0:T(8,128)(2,1)S(1)}, u32[]{:S(2)}, u32[]{:S(2)}) collective-permute-start(bf16[272,512]{1,0:T(8,128)(2,1)S(1)} %slice.7), channel_id=1, source_target_pairs={{0,16},{1,17},{2,18},{3,19},{4,20},{5,21},{6,22},{7,23},{8,24},{9,... | collective-permute-start | bytes 835592 | tf_op jit(solution)/shard_map/ppermute | solution.py:362
  57.0 0.5 collective-permute-start.11
  57.5 0.0 collective-permute-done.8.refs_2_.refs_6_
  57.5 0.0 collective-permute-start.9
  57.5 0.3 collective-permute-start.12
  57.8 6.2 %collective-permute-done.14.refs_8_.refs_12_ = bf16[272,512]{1,0:T(8,128)(2,1)S(1)} collective-permute-done((bf16[272,512]{1,0:T(8,128)(2,1)S(1)}, bf16[272,512]{1,0:T(8,128)(2,1)S(1)}, u32[]{:S(2)}, u32[]{:S(2)}) %collective-permute-start.14) | collective-permute-done | bytes 278560 | tf_op jit(solution)/shard_map/ppermute | solution.py:362
  64.0 0.6 collective-permute-start.15
  64.6 0.5 collective-permute-done.12.refs_6_.refs_10_
  65.1 1.3 collective-permute-start.13
  66.4 0.1 stack.89.place_ref
  66.5 0.2 stack.86.place_ref
  66.7 0.0 copy-start.1
  66.7 1.2 collective-permute-done.16.refs_15_
  67.9 2.9 %collective-permute-start.21 = (bf16[512,512]{1,0:T(8,128)(2,1)S(1)}, bf16[512,512]{1,0:T(8,128)(2,1)S(1)}, u32[]{:S(2)}, u32[]{:S(2)}) collective-permute-start(bf16[512,512]{1,0:T(8,128)(2,1)S(1)} %copy-done), channel_id=1, source_target_pairs={{0,24},{1,25},{2,26},{3,27},{4,28},{5,29},{6,30},{7,31},{8,16},{9,... | collective-permute-start | bytes 1572872 | tf_op jit(solution)/shard_map/ppermute | solution.py:362
  70.8 0.0 collective-permute-done.13.refs_7_.refs_11_
  70.8 0.0 collective-permute-start.20
  70.8 0.0 collective-permute-done.11.refs_5_.refs_9_
  70.9 0.7 collective-permute-start.19
  71.6 0.0 collective-permute-done.9.refs_3_.refs_7_
  71.6 1.9 %collective-permute-start.18 = (bf16[1024,512]{1,0:T(8,128)(2,1)S(1)}, bf16[1024,512]{1,0:T(8,128)(2,1)S(1)}, u32[]{:S(2)}, u32[]{:S(2)}) collective-permute-start(bf16[1024,512]{1,0:T(8,128)(2,1)S(1)} %constant_dynamic-update-slice_fusion.refs_14_), channel_id=1, source_target_pairs={{2,4},{3,5},{4,6},{5,7},{6,0},{7,1},{10,12},{11,13},{12,14},{13,15... | collective-permute-start | bytes 3145736 | tf_op jit(solution)/shard_map/ppermute | solution.py:362
  73.5 0.0 collective-permute-done.15.refs_9_.refs_13_
  73.5 3.5 %collective-permute-start.17 = (bf16[1024,512]{1,0:T(8,128)(2,1)}, bf16[1024,512]{1,0:T(8,128)(2,1)S(1)}, u32[]{:S(2)}, u32[]{:S(2)}) collective-permute-start(bf16[1024,512]{1,0:T(8,128)(2,1)} %collective-permute-done.16.refs_15_), channel_id=1, source_target_pairs={{2,0},{3,1},{4,2},{5,3},{10,8},{11,9},{12,10},{13,11},{18,16},{19,... | collective-permute-start | bytes 3145736 | tf_op jit(solution)/shard_map/ppermute | solution.py:362
  77.0 0.0 copy-start.3
  77.0 1.0 copy-done.3
  78.1 48.1 %factor_panel.1 = (bf16[1024,1024]{1,0:T(8,128)(2,1)}, bf16[1024,1024]{1,0:T(8,128)(2,1)}, bf16[1024,128]{1,0:T(8,128)(2,1)}, bf16[1024,128]{1,0:T(8,128)(2,1)}) custom-call(s32[24]{0:T(128)S(1)} %stack.89.place_ref, bf16[528,512]{1,0:T(8,128)(2,1)S(1)} %broadcast_select_fusion.1.refs_0_.refs_4_, bf16[528,512]{1,0:T(8,128)(2,1)S(1)} %copy-done.3, ...), custom_call_target="tpu_custom_call" | custom-call | flops 40000000000 | bytes 16777216 | tf_op jit(solution)/shard_map/factor_panel/pallas_call | solution.py:215
  126.2 0.0 collective-permute-done.21.refs_22_
  126.2 0.0 collective-permute-done.20.refs_21_
  126.2 0.0 collective-permute-done.17.refs_16_
  126.2 0.0 collective-permute-done.19.refs_18_
  126.2 0.0 collective-permute-done.18.refs_17_
  126.2 0.0 copy-done.1
  126.2 0.0 copy-done.4
  126.2 0.0 copy-done.6
  126.2 24.4 %finish_tile.1 = f32[1024,512]{1,0:T(8,128)} custom-call(s32[70]{0:T(128)S(1)} %stack.86.place_ref, f32[1,512]{1,0:T(1,128)S(1)} %bitcast.32, bf16[1024,1024]{1,0:T(8,128)(2,1)} %get-tuple-element.20.refs_0_, bf16[1024,1024]{1,0:T(8,128)(2,1)} %get-tuple-element.21.refs_1_, bf16[1024,128]{1,0:T(8,128)(2,1)} %get-tuple-element.22.refs_2_, ...), custom_call_target="tpu_custom_call" | custom-call | flops 20000000000 | bytes 25165824 | tf_op jit(solution)/shard_map/finish_tile/pallas_call | solution.py:322
  (13 shorter events, 0.1 us)
Async XLA Ops:
  0.0 3.2 %copy-start = (bf16[512,512]{1,0:T(8,128)(2,1)S(1)}, bf16[512,512]{1,0:T(8,128)(2,1)}, u32[]{:S(2)}) copy-start(bf16[512,512]{1,0:T(8,128)(2,1)} %refs_19_.1) | copy-start | bytes 1572868
  1.9 16.5 %collective-permute-start = (bf16[528,512]{1,0:T(8,128)(2,1)S(1)}, bf16[528,512]{1,0:T(8,128)(2,1)S(1)}, u32[]{:S(2)}, u32[]{:S(2)}) collective-permute-start(bf16[528,512]{1,0:T(8,128)(2,1)S(1)} %pad_maximum_fusion), channel_id=1, source_target_pairs={{0,4},{1,5},{8,12},{9,13},{16,20},{17,21},{24,28},{25,29}} | collective-permute-start | bytes 1622024 | tf_op jit(solution)/shard_map/ppermute | solution.py:362
  4.0 8.9 %collective-permute-start.2 = (bf16[256,512]{1,0:T(8,128)(2,1)S(1)}, bf16[256,512]{1,0:T(8,128)(2,1)S(1)}, u32[]{:S(2)}, u32[]{:S(2)}) collective-permute-start(bf16[256,512]{1,0:T(8,128)(2,1)S(1)} %get-tuple-element.27), channel_id=1, source_target_pairs={{0,9},{1,25},{2,11},{3,27},{4,13},{5,29},{6,15},{7,31},{8,1},{9,17... | collective-permute-start | bytes 786440 | tf_op jit(solution)/shard_map/ppermute | solution.py:362
  5.8 12.7 %collective-permute-start.1 = (bf16[256,512]{1,0:T(8,128)(2,1)}, bf16[256,512]{1,0:T(8,128)(2,1)S(1)}, u32[]{:S(2)}, u32[]{:S(2)}) collective-permute-start(bf16[256,512]{1,0:T(8,128)(2,1)} %get-tuple-element.28), channel_id=1, source_target_pairs={{0,1},{1,17},{2,3},{3,19},{4,5},{5,21},{6,7},{7,23},{8,9},{9,25},{... | collective-permute-start | bytes 786440 | tf_op jit(solution)/shard_map/ppermute | solution.py:362
  18.6 13.8 %collective-permute-start.3 = (bf16[528,512]{1,0:T(8,128)(2,1)S(1)}, bf16[528,512]{1,0:T(8,128)(2,1)}, u32[]{:S(2)}, u32[]{:S(2)}) collective-permute-start(bf16[528,512]{1,0:T(8,128)(2,1)S(1)} %broadcast_select_fusion), channel_id=1, source_target_pairs={{0,2},{1,3},{4,6},{5,7},{8,10},{9,11},{12,14},{13,15},{16,18},{17,... | collective-permute-start | bytes 1622024 | tf_op jit(solution)/shard_map/ppermute | solution.py:362
  22.0 4.4 %collective-permute-start.4 = (bf16[256,512]{1,0:T(8,128)(2,1)}, bf16[256,512]{1,0:T(8,128)(2,1)}, u32[]{:S(2)}, u32[]{:S(2)}) collective-permute-start(bf16[256,512]{1,0:T(8,128)(2,1)} %get-tuple-element.28), channel_id=1, source_target_pairs={{0,0},{1,16},{2,2},{3,18},{4,4},{5,20},{6,6},{7,22},{8,8},{9,24},{... | collective-permute-start | bytes 786440 | tf_op jit(solution)/shard_map/ppermute | solution.py:362
  25.6 2.4 %collective-permute-start.5 = (bf16[256,512]{1,0:T(8,128)(2,1)S(1)}, bf16[256,512]{1,0:T(8,128)(2,1)}, u32[]{:S(2)}, u32[]{:S(2)}) collective-permute-start(bf16[256,512]{1,0:T(8,128)(2,1)S(1)} %get-tuple-element.27), channel_id=1, source_target_pairs={{0,8},{1,24},{2,10},{3,26},{4,12},{5,28},{6,14},{7,30},{8,0},{9,16... | collective-permute-start | bytes 786440 | tf_op jit(solution)/shard_map/ppermute | solution.py:362
  26.3 6.1 %collective-permute-start.6 = (bf16[512,512]{1,0:T(8,128)(2,1)S(1)}, bf16[512,512]{1,0:T(8,128)(2,1)S(1)}, u32[]{:S(2)}, u32[]{:S(2)}) collective-permute-start(bf16[512,512]{1,0:T(8,128)(2,1)S(1)} %copy-done), channel_id=1, source_target_pairs={{0,8},{1,9},{2,10},{3,11},{4,12},{5,13},{6,14},{7,15},{8,0},{9,1},... | collective-permute-start | bytes 1572872 | tf_op jit(solution)/shard_map/ppermute | solution.py:362
  32.4 0.8 copy-start.5
  33.3 21.3 %collective-permute-start.10 = (bf16[528,512]{1,0:T(8,128)(2,1)S(1)}, bf16[528,512]{1,0:T(8,128)(2,1)S(1)}, u32[]{:S(2)}, u32[]{:S(2)}) collective-permute-start(bf16[528,512]{1,0:T(8,128)(2,1)S(1)} %broadcast_select_fusion.1.refs_0_.refs_4_), channel_id=1, source_target_pairs={{0,1},{1,0},{2,3},{3,2},{4,5},{5,4},{6,7},{7,6},{8,9},{9,8},{10,11... | collective-permute-start | bytes 1622024 | tf_op jit(solution)/shard_map/ppermute | solution.py:362
  41.9 12.6 %collective-permute-start.7 = (bf16[528,512]{1,0:T(8,128)(2,1)S(1)}, bf16[528,512]{1,0:T(8,128)(2,1)S(1)}, u32[]{:S(2)}, u32[]{:S(2)}) collective-permute-start(bf16[528,512]{1,0:T(8,128)(2,1)S(1)} %broadcast_select_fusion.1.refs_0_.refs_4_), channel_id=1, source_target_pairs={{0,8},{1,9},{2,10},{3,11},{4,12},{5,13},{6,14},{7,15},{8,0},{9,1},... | collective-permute-start | bytes 1622024 | tf_op jit(solution)/shard_map/ppermute | solution.py:362
  41.9 15.6 %collective-permute-start.8 = (bf16[528,512]{1,0:T(8,128)(2,1)S(1)}, bf16[528,512]{1,0:T(8,128)(2,1)S(1)}, u32[]{:S(2)}, u32[]{:S(2)}) collective-permute-start(bf16[528,512]{1,0:T(8,128)(2,1)S(1)} %broadcast_select_fusion.1.refs_0_.refs_4_), channel_id=1, source_target_pairs={{0,16},{1,17},{2,18},{3,19},{4,20},{5,21},{6,22},{7,23},{8,24},{9,... | collective-permute-start | bytes 1622024 | tf_op jit(solution)/shard_map/ppermute | solution.py:362
  41.9 26.0 %collective-permute-start.16 = (bf16[1024,512]{1,0:T(8,128)(2,1)S(1)}, bf16[1024,512]{1,0:T(8,128)(2,1)}, u32[]{:S(2)}, u32[]{:S(2)}) collective-permute-start(bf16[1024,512]{1,0:T(8,128)(2,1)S(1)} %constant_dynamic-update-slice_fusion.refs_14_), channel_id=1, source_target_pairs={{2,0},{3,1},{4,2},{5,3},{6,4},{7,5},{10,8},{11,9},{12,10},{13,11},... | collective-permute-start | bytes 3145736 | tf_op jit(solution)/shard_map/ppermute | solution.py:362
  54.5 0.8 copy-start.2
  55.3 8.7 %collective-permute-start.14 = (bf16[272,512]{1,0:T(8,128)(2,1)S(1)}, bf16[272,512]{1,0:T(8,128)(2,1)S(1)}, u32[]{:S(2)}, u32[]{:S(2)}) collective-permute-start(bf16[272,512]{1,0:T(8,128)(2,1)S(1)} %slice.7), channel_id=1, source_target_pairs={{0,16},{1,17},{2,18},{3,19},{4,20},{5,21},{6,22},{7,23},{8,24},{9,... | collective-permute-start | bytes 835592 | tf_op jit(solution)/shard_map/ppermute | solution.py:362
  57.0 13.8 %collective-permute-start.11 = (bf16[528,512]{1,0:T(8,128)(2,1)S(1)}, bf16[528,512]{1,0:T(8,128)(2,1)}, u32[]{:S(2)}, u32[]{:S(2)}) collective-permute-start(bf16[528,512]{1,0:T(8,128)(2,1)S(1)} %collective-permute-done.10.refs_4_.refs_8_), channel_id=1, source_target_pairs={{0,8},{1,9},{2,10},{3,11},{4,12},{5,13},{6,14},{7,15},{8,0},{9,1},... | collective-permute-start | bytes 1622024 | tf_op jit(solution)/shard_map/ppermute | solution.py:362
  57.5 14.1 %collective-permute-start.9 = (bf16[528,512]{1,0:T(8,128)(2,1)S(1)}, bf16[528,512]{1,0:T(8,128)(2,1)}, u32[]{:S(2)}, u32[]{:S(2)}) collective-permute-start(bf16[528,512]{1,0:T(8,128)(2,1)S(1)} %collective-permute-done.8.refs_2_.refs_6_), channel_id=1, source_target_pairs={{0,8},{1,9},{2,10},{3,11},{4,12},{5,13},{6,14},{7,15},{8,0},{9,1},... | collective-permute-start | bytes 1622024 | tf_op jit(solution)/shard_map/ppermute | solution.py:362
  57.5 7.6 %collective-permute-start.12 = (bf16[256,512]{1,0:T(8,128)(2,1)S(1)}, bf16[256,512]{1,0:T(8,128)(2,1)}, u32[]{:S(2)}, u32[]{:S(2)}) collective-permute-start(bf16[256,512]{1,0:T(8,128)(2,1)S(1)} %slice.6), channel_id=1, source_target_pairs={{0,1},{1,0},{2,3},{3,2},{4,5},{5,4},{6,7},{7,6},{8,9},{9,8},{10,11... | collective-permute-start | bytes 786440 | tf_op jit(solution)/shard_map/ppermute | solution.py:362
  64.0 9.5 %collective-permute-start.15 = (bf16[272,512]{1,0:T(8,128)(2,1)S(1)}, bf16[272,512]{1,0:T(8,128)(2,1)}, u32[]{:S(2)}, u32[]{:S(2)}) collective-permute-start(bf16[272,512]{1,0:T(8,128)(2,1)S(1)} %collective-permute-done.14.refs_8_.refs_12_), channel_id=1, source_target_pairs={{0,8},{1,9},{2,10},{3,11},{4,12},{5,13},{6,14},{7,15},{8,0},{9,1},... | collective-permute-start | bytes 835592 | tf_op jit(solution)/shard_map/ppermute | solution.py:362
  65.1 5.7 %collective-permute-start.13 = (bf16[256,512]{1,0:T(8,128)(2,1)}, bf16[256,512]{1,0:T(8,128)(2,1)}, u32[]{:S(2)}, u32[]{:S(2)}) collective-permute-start(bf16[256,512]{1,0:T(8,128)(2,1)} %collective-permute-done.12.refs_6_.refs_10_), channel_id=1, source_target_pairs={{0,8},{1,9},{2,10},{3,11},{4,12},{5,13},{6,14},{7,15},{8,0},{9,1},... | collective-permute-start | bytes 786440 | tf_op jit(solution)/shard_map/ppermute | solution.py:362
  66.7 59.5 %copy-start.1 = (f32[512]{0:T(512)S(1)}, f32[512]{0:T(512)}, u32[]{:S(2)}) copy-start(f32[512]{0:T(512)} %param.3) | copy-start | bytes 6148
  67.9 58.3 %collective-permute-start.21 = (bf16[512,512]{1,0:T(8,128)(2,1)S(1)}, bf16[512,512]{1,0:T(8,128)(2,1)S(1)}, u32[]{:S(2)}, u32[]{:S(2)}) collective-permute-start(bf16[512,512]{1,0:T(8,128)(2,1)S(1)} %copy-done), channel_id=1, source_target_pairs={{0,24},{1,25},{2,26},{3,27},{4,28},{5,29},{6,30},{7,31},{8,16},{9,... | collective-permute-start | bytes 1572872 | tf_op jit(solution)/shard_map/ppermute | solution.py:362
  70.8 55.4 %collective-permute-start.20 = (bf16[512,512]{1,0:T(8,128)(2,1)S(1)}, bf16[512,512]{1,0:T(8,128)(2,1)S(1)}, u32[]{:S(2)}, u32[]{:S(2)}) collective-permute-start(bf16[512,512]{1,0:T(8,128)(2,1)S(1)} %copy-done), channel_id=1, source_target_pairs={{0,16},{1,17},{2,18},{3,19},{4,20},{5,21},{6,22},{7,23},{8,24},{9,... | collective-permute-start | bytes 1572872 | tf_op jit(solution)/shard_map/ppermute | solution.py:362
  70.9 55.3 %collective-permute-start.19 = (bf16[1024,512]{1,0:T(8,128)(2,1)S(1)}, bf16[1024,512]{1,0:T(8,128)(2,1)S(1)}, u32[]{:S(2)}, u32[]{:S(2)}) collective-permute-start(bf16[1024,512]{1,0:T(8,128)(2,1)S(1)} %constant_dynamic-update-slice_fusion.refs_14_), channel_id=1, source_target_pairs={{2,6},{3,7},{10,14},{11,15},{18,22},{19,23},{26,30},{27,31}} | collective-permute-start | bytes 3145736 | tf_op jit(solution)/shard_map/ppermute | solution.py:362
  71.6 54.6 %collective-permute-start.18 = (bf16[1024,512]{1,0:T(8,128)(2,1)S(1)}, bf16[1024,512]{1,0:T(8,128)(2,1)S(1)}, u32[]{:S(2)}, u32[]{:S(2)}) collective-permute-start(bf16[1024,512]{1,0:T(8,128)(2,1)S(1)} %constant_dynamic-update-slice_fusion.refs_14_), channel_id=1, source_target_pairs={{2,4},{3,5},{4,6},{5,7},{6,0},{7,1},{10,12},{11,13},{12,14},{13,15... | collective-permute-start | bytes 3145736 | tf_op jit(solution)/shard_map/ppermute | solution.py:362
  73.5 52.7 %collective-permute-start.17 = (bf16[1024,512]{1,0:T(8,128)(2,1)}, bf16[1024,512]{1,0:T(8,128)(2,1)S(1)}, u32[]{:S(2)}, u32[]{:S(2)}) collective-permute-start(bf16[1024,512]{1,0:T(8,128)(2,1)} %collective-permute-done.16.refs_15_), channel_id=1, source_target_pairs={{2,0},{3,1},{4,2},{5,3},{10,8},{11,9},{12,10},{13,11},{18,16},{19,... | collective-permute-start | bytes 3145736 | tf_op jit(solution)/shard_map/ppermute | solution.py:362
  77.0 1.1 copy-start.3
  78.1 48.2 %copy-start.4 = (bf16[528,512]{1,0:T(8,128)(2,1)S(1)}, bf16[528,512]{1,0:T(8,128)(2,1)}, u32[]{:S(2)}) copy-start(bf16[528,512]{1,0:T(8,128)(2,1)} %copy-done.2) | copy-start | bytes 1622020
  78.1 48.2 %copy-start.6 = (bf16[512,512]{1,0:T(8,128)(2,1)S(1)}, bf16[512,512]{1,0:T(8,128)(2,1)}, u32[]{:S(2)}) copy-start(bf16[512,512]{1,0:T(8,128)(2,1)} %copy-done.5) | copy-start | bytes 1572868

commit v3 on v2

--- a/solution.py
+++ b/solution.py
@@ -59,34 +59,43 @@
         side, inverse = sides[step], inverses[step]
         columns = [lanes(side, base + b) for b in range(SUB)]
         entry = {(a, b): sublanes(columns[b], a) for b in range(SUB) for a in range(b, SUB)}
-        ahead = [lanes(sides[step + 1], base + b) for b in range(SUB)] if step + 1 < tiles_count else None
-        tops = [sublanes(side, a) for a in range(SUB)]
-        insides = [sublanes(inverse, a) for a in range(SUB)]
-        scale = []
-        for m in range(SUB):
-            root = lax.rsqrt(entry[m, m])
-            scale.append(root)
-            for a in range(m + 1, SUB):
-                entry[a, m] = entry[a, m] * root
-            for b in range(m + 1, SUB):
-                for a in range(b, SUB):
-                    entry[a, b] = entry[a, b] - entry[a, m] * entry[b, m]
-            tops[m] = tops[m] * root
-            insides[m] = insides[m] * root
-            for a in range(m + 1, SUB):
-                tops[a] = tops[a] - entry[a, m] * tops[m]
-                insides[a] = insides[a] - entry[a, m] * insides[m]
-            if ahead is not None:
-                ahead[m] = ahead[m] * root
-                for b in range(m + 1, SUB):
-                    ahead[b] = ahead[b] - entry[b, m] * ahead[m]
+        vectors = [[sublanes(side, a) for a in range(SUB)], [sublanes(inverse, a) for a in range(SUB)]]
+        if step + 1 < tiles_count:
+            vectors.append([lanes(sides[step + 1], base + b) for b in range(SUB)])
+        scale = [None] * SUB
+        for m in range(0, SUB, 2):
+            n = m + 1
+            first, cross, second = entry[m, m], entry[n, m], entry[n, n]
+            root = lax.rsqrt(first)
+            det_root = lax.rsqrt(first * second - cross * cross)
+            scale[m], scale[n] = root, det_root * (first * root)
+            det_square = det_root * det_root
+            link = cross * root
+            entry[n, m] = link
+            rest = range(n + 1, SUB)
+            for x in rest:
+                entry[x, m] = entry[x, m] * root
+                entry[x, n] = entry[x, n] - entry[x, m] * link
+            weighted = {x: entry[x, n] * first for x in rest}
+            for y in rest:
+                for x in range(y, SUB):
+                    entry[x, y] = (entry[x, y] - entry[x, m] * entry[y, m]) - (weighted[x] * entry[y, n]) * det_square
+            for x in rest:
+                entry[x, n] = entry[x, n] * scale[n]
+            for vector in vectors:
+                vector[m] = vector[m] * root
+                vector[n] = (vector[n] - link * vector[m]) * scale[n]
+                for x in rest:
+                    vector[x] = (vector[x] - entry[x, m] * vector[m]) - entry[x, n] * vector[n]
+        tops, insides = vectors[:2]
         upper, lower_inverse = tops[0], insides[0]
         for m in range(1, SUB):
             upper = jnp.where(row_in_tile == m, tops[m], upper)
             lower_inverse = jnp.where(row_in_tile == m, insides[m], lower_inverse)
         uppers.append(jnp.where(lane >= row_in_tile + base, upper, 0.0))
         inverse_ref[pl.ds(base, SUB), :] = lower_inverse
-        if ahead is not None:
+        if step + 1 < tiles_count:
+            ahead = vectors[2]
             for m in range(SUB):
                 sides[step + 1] = sides[step + 1] - ahead[m] * tops[m]
                 inverses[step + 1] = inverses[step + 1] - ahead[m] * insides[m]
@@ -126,10 +135,15 @@
 
 def panel_kernel(views, count, width, place_ref, *refs):
     pieces, refs = refs[:count], refs[count:]
-    outs, (high_ref, low_ref, inv_high_ref, inv_low_ref, lower_ref, block_ref, inverse_ref, items_ref, parts_ref, sem, out_sem) = refs[:4], refs[4:]
+    outs, (high_ref, low_ref, inv_high_ref, inv_low_ref, lower_ref, coming_ref, *refs) = refs[:4], refs[4:]
+    block_ref, inverse_ref, items_ref, parts_ref, sem, out_sem = refs
     held = [parts_ref if is_part else items_ref for _, _, _, is_part in views]
     views = [pieces[which].at[pl.ds(start, rows)] for which, start, rows, _ in views]
-    for wait in place_pieces(place_ref, 0, views, held, sem):
+    waits = place_pieces(place_ref, 0, views, held, sem)
+    for k in range(1, NBLOCKS):
+        for ref in (high_ref, low_ref):
+            ref[pl.ds(0, k * BLOCK), pl.ds(k * BLOCK, BLOCK)] = jnp.zeros((k * BLOCK, BLOCK), bf16)
+    for wait in waits:
         wait()
     on_diagonal = lax.broadcasted_iota(jnp.int32, (BLOCK, BLOCK), 0) == lax.broadcasted_iota(
         jnp.int32, (BLOCK, BLOCK), 1
@@ -137,28 +151,32 @@
 
     def before(k):
         start = k * BLOCK
-        here = pl.ds(start, BLOCK)
-        column = dot_nt(items_ref[pl.ds(start, PANEL - start), :], items_ref[here, :])
-        if k > 0:
-            high, low = high_ref[pl.ds(start, PANEL - start), :start], low_ref[pl.ds(start, PANEL - start), :start]
-            column = column - dot_nt3((high, low), (high[:BLOCK], low[:BLOCK]))
+        here, rest = pl.ds(start, BLOCK), pl.ds(start, PANEL - start)
+        if k % 2 == 0:
+            both = pl.ds(start, 2 * BLOCK)
+            columns = dot_nt(items_ref[rest, :], items_ref[both, :])
+            if k > 0:
+                columns = columns - dot_nt3(
+                    (high_ref[rest, :start], low_ref[rest, :start]), (high_ref[both, :start], low_ref[both, :start])
+                )
+            column = columns[:, :BLOCK]
+            coming_ref[pl.ds(start + BLOCK, PANEL - start - BLOCK), :] = columns[BLOCK:, BLOCK:]
+        else:
+            last = pl.ds(start - BLOCK, BLOCK)
+            high, low = high_ref[rest, last], low_ref[rest, last]
+            column = coming_ref[rest, :] - dot_nt3((high, low), (high[:BLOCK], low[:BLOCK]))
         part, lane = PARTS * (start // width), start % width
         parts = parts_ref[pl.ds(part, PARTS), pl.ds(lane, BLOCK)].astype(f32)
-        regular = parts[0:1] + parts[1:2] + parts[2:3]
-        block_ref[...] = column[:BLOCK] + jnp.where(on_diagonal, regular, 0.0)
+        block_ref[...] = column[:BLOCK] + jnp.where(on_diagonal, parts[0:1] + parts[1:2] + parts[2:3], 0.0)
         if k + 1 < NBLOCKS:
             lower_ref[pl.ds(start + BLOCK, PANEL - start - BLOCK), :] = column[BLOCK:]
 
     def after(k):
         start = k * BLOCK
         here = pl.ds(start, BLOCK)
-        diagonal = block_ref[...]
         inverse = split(inverse_ref[...])
         inv_high_ref[here, :], inv_low_ref[here, :] = inverse
-        high_ref[here, here], low_ref[here, here] = split(diagonal)
-        if k > 0:
-            above = jnp.zeros((start, BLOCK), bf16)
-            high_ref[pl.ds(0, start), here], low_ref[pl.ds(0, start), here] = above, above
+        high_ref[here, here], low_ref[here, here] = split(block_ref[...])
         if k + 1 < NBLOCKS:
             rest = pl.ds(start + BLOCK, PANEL - start - BLOCK)
             high_ref[rest, here], low_ref[rest, here] = split(dot_nt3(split(lower_ref[rest, :]), inverse))
@@ -206,6 +224,7 @@
         ((PANEL, BLOCK), bf16),
     ]
     held = [
+        ((PANEL, BLOCK), f32),
         ((PANEL, BLOCK), f32),
         ((BLOCK, BLOCK), f32),
         ((BLOCK, BLOCK), f32),
@@ -242,8 +261,6 @@
     for fetch in fetches:
         fetch.start()
     waits = place_pieces(place_ref, 2, views, held, sem)
-    for fetch in fetches:
-        fetch.wait()
     row_index, col_index = place_ref[0], place_ref[1]
     width, band = cols_ref.shape[0], rows_ref.shape[0] // (SPAN - 1)
     row_count = (SPAN - 1) * band
@@ -252,6 +269,20 @@
     slot = jnp.minimum(col_index, panel_blocks - 1)
     at = pl.ds(pl.multiple_of(slot * width, width), width)
     below, right = pl.ds(0, row_count), pl.ds(row_count, width)
+
+    for wait in waits:
+        wait()
+    step = min(WIDE, width)
+    groups = [(cols_ref, at_row, pl.ds(row_count + at_row, step), step) for at_row in range(0, width, step)]
+    groups += [(rows_ref, at_row, pl.ds(at_row, band), band) for at_row in range(0, row_count, band)]
+
+    def grams(start):
+        block = panel_ref[pl.ds(start, WIDE), :]
+        return [dot_nt(ref[pl.ds(at_row, count), :], block) for ref, at_row, _, count in groups]
+
+    columns = grams(0)
+    for fetch in fetches:
+        fetch.wait()
 
     for start in range(0, PANEL, WIDE):
         first, second = pl.ds(start, BLOCK), pl.ds(start + BLOCK, BLOCK)
@@ -263,25 +294,19 @@
             wide_ref[second, pl.ds(0, BLOCK)] = part
             wide_ref[second, pl.ds(BLOCK, BLOCK)] = inv_ref[second, :]
 
-    def solve(items_ref, mine):
-        for start in range(0, PANEL, WIDE):
-            here = pl.ds(start, WIDE)
-            column = dot_nt(items_ref[...], panel_ref[here, :])
-            if start > 0:
-                column = column - dot_nt3(
+    for start in range(0, PANEL, WIDE):
+        here = pl.ds(start, WIDE)
+        if start > 0:
+            columns = [
+                column
+                - dot_nt3(
                     (left_high_ref[mine, :start], left_low_ref[mine, :start]), (high_ref[here, :start], low_ref[here, :start])
                 )
+                for column, (_, _, mine, _) in zip(grams(start), groups)
+            ]
+        for column, (_, _, mine, _) in zip(columns, groups):
             column = dot_nt3(split(column), (wide_high_ref[here, :], wide_low_ref[here, :]))
             left_high_ref[mine, here], left_low_ref[mine, here] = split(column)
-
-    for wait, target in zip(waits, held):
-        if target is not rows_ref:
-            wait()
-    solve(cols_ref, right)
-    for wait, target in zip(waits, held):
-        if target is rows_ref:
-            wait()
-    solve(rows_ref, below)
 
     @pl.when(in_panel)
     def _():
@@ -387,7 +412,6 @@
                         exchange(offers[flip], lambda p, h, s, w: (w, h ^ flip, s, (p + turn) % ways))
                     )
                     quarter_users.append(((way - turn) % ways * CORES + (core ^ flip)) * users)
-            got = after(got, *quarters[:CORES])
         shared = jnp.where(slot % (2 * reach) == reach, got, shared)
         reach //= 2
     quarters = jnp.concatenate(quarters, 0)

time: 152 us -> 142 us (0.934)
  Pallas kernels: 72.5 us -> 63.3 us
  waiting for transfers between devices: 34.1 us -> 31.8 us
    pallas_call x1, Pallas kernels: 48.1 us -> 41.1 us  [factor_panel(): pl.pallas_call(functools.partial(panel_kernel, views, len(pieces), width)...]
    ppermute x22, waiting for transfers between devices: 34.1 us -> 31.8 us  [exchange(): return lax.ppermute(value, ('row', 'col'), perm)]
    pallas_call x1, Pallas kernels: 24.4 us -> 22.2 us  [finish_tile(): pl.pallas_call(functools.partial(tile_kernel, (len(panel), len(rows), len...]
  transfers between devices with their start and end apart: 22 -> 22, of which waited for: 8 -> 6; matrix products, arithmetic and copies ran while one was open for 2% -> 3% of each run, Pallas kernels for 32% -> 29%
where the time goes in v3:
time: 142 us; the launch traced here: 140 us
  Pallas kernels  63.3 us (45%)
  starting transfers between devices  35.5 us (25%)
  waiting for transfers between devices  31.8 us (22%)
  local copies, waits for them, and re-layouts  6.64 us (5%)
  other arithmetic  2.04 us (1%)
    pallas_call x1, Pallas kernels, factor_panel(): pl.pallas_call(functools.partial(panel_kernel, views, len(pieces), width)...  41.1 us
    ppermute x22, starting transfers between devices, exchange(): return lax.ppermute(value, ('row', 'col'), perm)  35.5 us
    ppermute x22, waiting for transfers between devices, exchange(): return lax.ppermute(value, ('row', 'col'), perm)  31.8 us
    pallas_call x1, Pallas kernels, finish_tile(): pl.pallas_call(functools.partial(tile_kernel, (len(panel), len(rows), len...  22.2 us
    unnamed x17, local copies, waits for them, and re-layouts  4.62 us
  transfers between devices with their start and end apart: 22, of which 6 were waited for; matrix products, arithmetic and copies ran while one was open for 3% of the time, Pallas kernels for 29%

profile of v3, /device:TPU:17, one launch (start us, length us, event | category | flops | bytes accessed | tf_op | source)
XLA Modules:
  0.0 139.7 jit_solution(9221484368635582826)
XLA Ops:
  0.0 0.7 reduce-precision_convert_fusion.1
  0.8 1.1 pad_maximum_fusion
  1.9 1.3 collective-permute-start
  3.2 0.0 copy-done
  3.2 0.7 dynamic-slice_bitcast_fusion
  4.0 1.8 %collective-permute-start.3 = (bf16[256,512]{1,0:T(8,128)(2,1)S(1)}, bf16[256,512]{1,0:T(8,128)(2,1)}, u32[]{:S(2)}, u32[]{:S(2)}) collective-permute-start(bf16[256,512]{1,0:T(8,128)(2,1)S(1)} %get-tuple-element.25), channel_id=1, source_target_pairs={{0,9},{1,25},{2,11},{3,27},{4,13},{5,29},{6,15},{7,31},{8,1},{9,17... | collective-permute-start | bytes 786440 | tf_op jit(solution)/shard_map/ppermute | solution.py:387
  5.8 1.2 collective-permute-start.2
  7.0 10.8 %collective-permute-done = bf16[528,512]{1,0:T(8,128)(2,1)S(1)} collective-permute-done((bf16[528,512]{1,0:T(8,128)(2,1)S(1)}, bf16[528,512]{1,0:T(8,128)(2,1)S(1)}, u32[]{:S(2)}, u32[]{:S(2)}) %collective-permute-start) | collective-permute-done | bytes 540704 | tf_op jit(solution)/shard_map/ppermute | solution.py:387
  17.8 0.1 broadcast_select_fusion
  18.0 2.1 %collective-permute-start.1 = (bf16[528,512]{1,0:T(8,128)(2,1)S(1)}, bf16[528,512]{1,0:T(8,128)(2,1)}, u32[]{:S(2)}, u32[]{:S(2)}) collective-permute-start(bf16[528,512]{1,0:T(8,128)(2,1)S(1)} %broadcast_select_fusion), channel_id=1, source_target_pairs={{0,2},{1,3},{4,6},{5,7},{8,10},{9,11},{12,14},{13,15},{16,18},{17,... | collective-permute-start | bytes 1622024 | tf_op jit(solution)/shard_map/ppermute | solution.py:387
  20.1 3.6 %collective-permute-start.4 = (bf16[256,512]{1,0:T(8,128)(2,1)}, bf16[256,512]{1,0:T(8,128)(2,1)}, u32[]{:S(2)}, u32[]{:S(2)}) collective-permute-start(bf16[256,512]{1,0:T(8,128)(2,1)} %get-tuple-element.26), channel_id=1, source_target_pairs={{0,0},{1,16},{2,2},{3,18},{4,4},{5,20},{6,6},{7,22},{8,8},{9,24},{... | collective-permute-start | bytes 786440 | tf_op jit(solution)/shard_map/ppermute | solution.py:387
  23.7 1.5 %collective-permute-start.5 = (bf16[256,512]{1,0:T(8,128)(2,1)S(1)}, bf16[256,512]{1,0:T(8,128)(2,1)}, u32[]{:S(2)}, u32[]{:S(2)}) collective-permute-start(bf16[256,512]{1,0:T(8,128)(2,1)S(1)} %get-tuple-element.25), channel_id=1, source_target_pairs={{0,8},{1,24},{2,10},{3,26},{4,12},{5,28},{6,14},{7,30},{8,0},{9,16... | collective-permute-start | bytes 786440 | tf_op jit(solution)/shard_map/ppermute | solution.py:387
  25.2 0.0 collective-permute-done.2
  25.2 0.1 collective-permute-start.6
  25.3 0.0 collective-permute-done.3
  25.3 1.0 constant_dynamic-update-slice_fusion.2
  26.3 0.0 collective-permute-done.4
  26.3 1.0 constant_dynamic-update-slice_fusion.1
  27.3 0.0 collective-permute-done.5
  27.3 1.0 constant_dynamic-update-slice_fusion.refs_14_
  28.2 1.3 collective-permute-done.1
  29.5 0.1 broadcast_select_fusion.1.refs_0_.refs_4_
  29.6 0.0 collective-permute-done.6.refs_20_
  29.6 0.0 copy-start.5
  29.6 0.8 copy-done.5
  30.4 9.5 %collective-permute-start.10 = (bf16[528,512]{1,0:T(8,128)(2,1)S(1)}, bf16[528,512]{1,0:T(8,128)(2,1)S(1)}, u32[]{:S(2)}, u32[]{:S(2)}) collective-permute-start(bf16[528,512]{1,0:T(8,128)(2,1)S(1)} %broadcast_select_fusion.1.refs_0_.refs_4_), channel_id=1, source_target_pairs={{0,1},{1,0},{2,3},{3,2},{4,5},{5,4},{6,7},{7,6},{8,9},{9,8},{10,11... | collective-permute-start | bytes 1622024 | tf_op jit(solution)/shard_map/ppermute | solution.py:387
  39.9 0.0 collective-permute-start.7
  39.9 0.0 collective-permute-start.8
  39.9 1.9 %collective-permute-start.16 = (bf16[1024,512]{1,0:T(8,128)(2,1)S(1)}, bf16[1024,512]{1,0:T(8,128)(2,1)}, u32[]{:S(2)}, u32[]{:S(2)}) collective-permute-start(bf16[1024,512]{1,0:T(8,128)(2,1)S(1)} %constant_dynamic-update-slice_fusion.refs_14_), channel_id=1, source_target_pairs={{2,0},{3,1},{4,2},{5,3},{6,4},{7,5},{10,8},{11,9},{12,10},{13,11},... | collective-permute-start | bytes 3145736 | tf_op jit(solution)/shard_map/ppermute | solution.py:387
  41.9 9.8 %collective-permute-done.10.refs_4_.refs_8_ = bf16[528,512]{1,0:T(8,128)(2,1)S(1)} collective-permute-done((bf16[528,512]{1,0:T(8,128)(2,1)S(1)}, bf16[528,512]{1,0:T(8,128)(2,1)S(1)}, u32[]{:S(2)}, u32[]{:S(2)}) %collective-permute-start.10) | collective-permute-done | bytes 540704 | tf_op jit(solution)/shard_map/ppermute | solution.py:387
  51.7 0.0 collective-permute-done.7.refs_1_.refs_5_
  51.7 0.8 copy-done.2
  52.5 1.8 %collective-permute-start.14 = (bf16[272,512]{1,0:T(8,128)(2,1)S(1)}, bf16[272,512]{1,0:T(8,128)(2,1)S(1)}, u32[]{:S(2)}, u32[]{:S(2)}) collective-permute-start(bf16[272,512]{1,0:T(8,128)(2,1)S(1)} %slice.7), channel_id=1, source_target_pairs={{0,16},{1,17},{2,18},{3,19},{4,20},{5,21},{6,22},{7,23},{8,24},{9,... | collective-permute-start | bytes 835592 | tf_op jit(solution)/shard_map/ppermute | solution.py:387
  54.3 0.0 collective-permute-start.11
  54.3 0.0 collective-permute-done.8.refs_2_.refs_6_
  54.4 0.5 collective-permute-start.9
  54.9 0.1 collective-permute-start.12
  55.0 6.3 %collective-permute-done.14.refs_8_.refs_12_ = bf16[272,512]{1,0:T(8,128)(2,1)S(1)} collective-permute-done((bf16[272,512]{1,0:T(8,128)(2,1)S(1)}, bf16[272,512]{1,0:T(8,128)(2,1)S(1)}, u32[]{:S(2)}, u32[]{:S(2)}) %collective-permute-start.14) | collective-permute-done | bytes 278560 | tf_op jit(solution)/shard_map/ppermute | solution.py:387
  61.3 0.0 collective-permute-start.15
  61.3 1.7 %collective-permute-done.12.refs_6_.refs_10_ = bf16[256,512]{1,0:T(8,128)(2,1)} collective-permute-done((bf16[256,512]{1,0:T(8,128)(2,1)S(1)}, bf16[256,512]{1,0:T(8,128)(2,1)}, u32[]{:S(2)}, u32[]{:S(2)}) %collective-permute-start.12) | collective-permute-done | bytes 262176 | tf_op jit(solution)/shard_map/ppermute | solution.py:387
  63.0 0.8 collective-permute-start.13
  63.8 0.1 stack.89.place_ref
  63.9 0.2 stack.86.place_ref
  64.0 0.0 copy-start.1
  64.1 1.8 %collective-permute-done.16.refs_15_ = bf16[1024,512]{1,0:T(8,128)(2,1)} collective-permute-done((bf16[1024,512]{1,0:T(8,128)(2,1)S(1)}, bf16[1024,512]{1,0:T(8,128)(2,1)}, u32[]{:S(2)}, u32[]{:S(2)}) %collective-permute-start.16) | collective-permute-done | bytes 1048608 | tf_op jit(solution)/shard_map/ppermute | solution.py:387
  65.9 3.0 %collective-permute-start.21 = (bf16[512,512]{1,0:T(8,128)(2,1)S(1)}, bf16[512,512]{1,0:T(8,128)(2,1)S(1)}, u32[]{:S(2)}, u32[]{:S(2)}) collective-permute-start(bf16[512,512]{1,0:T(8,128)(2,1)S(1)} %copy-done), channel_id=1, source_target_pairs={{0,24},{1,25},{2,26},{3,27},{4,28},{5,29},{6,30},{7,31},{8,16},{9,... | collective-permute-start | bytes 1572872 | tf_op jit(solution)/shard_map/ppermute | solution.py:387
  68.8 0.0 collective-permute-done.13.refs_7_.refs_11_
  68.8 0.0 collective-permute-start.20
  68.9 0.0 collective-permute-done.11.refs_5_.refs_9_
  68.9 0.7 collective-permute-start.19
  69.6 0.0 collective-permute-done.9.refs_3_.refs_7_
  69.6 1.9 %collective-permute-start.18 = (bf16[1024,512]{1,0:T(8,128)(2,1)S(1)}, bf16[1024,512]{1,0:T(8,128)(2,1)S(1)}, u32[]{:S(2)}, u32[]{:S(2)}) collective-permute-start(bf16[1024,512]{1,0:T(8,128)(2,1)S(1)} %constant_dynamic-update-slice_fusion.refs_14_), channel_id=1, source_target_pairs={{2,4},{3,5},{4,6},{5,7},{6,0},{7,1},{10,12},{11,13},{12,14},{13,15... | collective-permute-start | bytes 3145736 | tf_op jit(solution)/shard_map/ppermute | solution.py:387
  71.6 0.0 collective-permute-done.15.refs_9_.refs_13_
  71.6 3.5 %collective-permute-start.17 = (bf16[1024,512]{1,0:T(8,128)(2,1)}, bf16[1024,512]{1,0:T(8,128)(2,1)S(1)}, u32[]{:S(2)}, u32[]{:S(2)}) collective-permute-start(bf16[1024,512]{1,0:T(8,128)(2,1)} %collective-permute-done.16.refs_15_), channel_id=1, source_target_pairs={{2,0},{3,1},{4,2},{5,3},{10,8},{11,9},{12,10},{13,11},{18,16},{19,... | collective-permute-start | bytes 3145736 | tf_op jit(solution)/shard_map/ppermute | solution.py:387
  75.1 0.0 copy-start.3
  75.1 1.0 copy-done.3
  76.1 41.1 %factor_panel.1 = (bf16[1024,1024]{1,0:T(8,128)(2,1)}, bf16[1024,1024]{1,0:T(8,128)(2,1)}, bf16[1024,128]{1,0:T(8,128)(2,1)}, bf16[1024,128]{1,0:T(8,128)(2,1)}) custom-call(s32[24]{0:T(128)S(1)} %stack.89.place_ref, bf16[528,512]{1,0:T(8,128)(2,1)S(1)} %broadcast_select_fusion.1.refs_0_.refs_4_, bf16[528,512]{1,0:T(8,128)(2,1)S(1)} %copy-done.3, ...), custom_call_target="tpu_custom_call" | custom-call | flops 40000000000 | bytes 16777216 | tf_op jit(solution)/shard_map/factor_panel/pallas_call | solution.py:234
  117.2 0.0 collective-permute-done.21.refs_22_
  117.2 0.0 collective-permute-done.20.refs_21_
  117.2 0.0 collective-permute-done.17.refs_16_
  117.2 0.0 collective-permute-done.19.refs_18_
  117.3 0.0 collective-permute-done.18.refs_17_
  117.3 0.0 copy-done.1
  117.3 22.2 %finish_tile.1 = f32[1024,512]{1,0:T(8,128)} custom-call(s32[70]{0:T(128)S(1)} %stack.86.place_ref, f32[1,512]{1,0:T(1,128)S(1)} %bitcast.32, bf16[1024,1024]{1,0:T(8,128)(2,1)} %get-tuple-element.18.refs_0_, bf16[1024,1024]{1,0:T(8,128)(2,1)} %get-tuple-element.19.refs_1_, bf16[1024,128]{1,0:T(8,128)(2,1)} %get-tuple-element.20.refs_2_, ...), custom_call_target="tpu_custom_call" | custom-call | flops 20000000000 | bytes 25165824 | tf_op jit(solution)/shard_map/finish_tile/pallas_call | solution.py:347
  (13 shorter events, 0.1 us)
Async XLA Ops:
  0.0 3.2 %copy-start = (bf16[512,512]{1,0:T(8,128)(2,1)S(1)}, bf16[512,512]{1,0:T(8,128)(2,1)}, u32[]{:S(2)}) copy-start(bf16[512,512]{1,0:T(8,128)(2,1)} %refs_19_.1) | copy-start | bytes 1572868
  1.9 15.9 %collective-permute-start = (bf16[528,512]{1,0:T(8,128)(2,1)S(1)}, bf16[528,512]{1,0:T(8,128)(2,1)S(1)}, u32[]{:S(2)}, u32[]{:S(2)}) collective-permute-start(bf16[528,512]{1,0:T(8,128)(2,1)S(1)} %pad_maximum_fusion), channel_id=1, source_target_pairs={{0,4},{1,5},{8,12},{9,13},{16,20},{17,21},{24,28},{25,29}} | collective-permute-start | bytes 1622024 | tf_op jit(solution)/shard_map/ppermute | solution.py:387
  4.0 21.3 %collective-permute-start.3 = (bf16[256,512]{1,0:T(8,128)(2,1)S(1)}, bf16[256,512]{1,0:T(8,128)(2,1)}, u32[]{:S(2)}, u32[]{:S(2)}) collective-permute-start(bf16[256,512]{1,0:T(8,128)(2,1)S(1)} %get-tuple-element.25), channel_id=1, source_target_pairs={{0,9},{1,25},{2,11},{3,27},{4,13},{5,29},{6,15},{7,31},{8,1},{9,17... | collective-permute-start | bytes 786440 | tf_op jit(solution)/shard_map/ppermute | solution.py:387
  5.8 19.4 %collective-permute-start.2 = (bf16[256,512]{1,0:T(8,128)(2,1)}, bf16[256,512]{1,0:T(8,128)(2,1)S(1)}, u32[]{:S(2)}, u32[]{:S(2)}) collective-permute-start(bf16[256,512]{1,0:T(8,128)(2,1)} %get-tuple-element.26), channel_id=1, source_target_pairs={{0,1},{1,17},{2,3},{3,19},{4,5},{5,21},{6,7},{7,23},{8,9},{9,25},{... | collective-permute-start | bytes 786440 | tf_op jit(solution)/shard_map/ppermute | solution.py:387
  18.0 11.6 %collective-permute-start.1 = (bf16[528,512]{1,0:T(8,128)(2,1)S(1)}, bf16[528,512]{1,0:T(8,128)(2,1)}, u32[]{:S(2)}, u32[]{:S(2)}) collective-permute-start(bf16[528,512]{1,0:T(8,128)(2,1)S(1)} %broadcast_select_fusion), channel_id=1, source_target_pairs={{0,2},{1,3},{4,6},{5,7},{8,10},{9,11},{12,14},{13,15},{16,18},{17,... | collective-permute-start | bytes 1622024 | tf_op jit(solution)/shard_map/ppermute | solution.py:387
  20.1 6.2 %collective-permute-start.4 = (bf16[256,512]{1,0:T(8,128)(2,1)}, bf16[256,512]{1,0:T(8,128)(2,1)}, u32[]{:S(2)}, u32[]{:S(2)}) collective-permute-start(bf16[256,512]{1,0:T(8,128)(2,1)} %get-tuple-element.26), channel_id=1, source_target_pairs={{0,0},{1,16},{2,2},{3,18},{4,4},{5,20},{6,6},{7,22},{8,8},{9,24},{... | collective-permute-start | bytes 786440 | tf_op jit(solution)/shard_map/ppermute | solution.py:387
  23.7 3.6 %collective-permute-start.5 = (bf16[256,512]{1,0:T(8,128)(2,1)S(1)}, bf16[256,512]{1,0:T(8,128)(2,1)}, u32[]{:S(2)}, u32[]{:S(2)}) collective-permute-start(bf16[256,512]{1,0:T(8,128)(2,1)S(1)} %get-tuple-element.25), channel_id=1, source_target_pairs={{0,8},{1,24},{2,10},{3,26},{4,12},{5,28},{6,14},{7,30},{8,0},{9,16... | collective-permute-start | bytes 786440 | tf_op jit(solution)/shard_map/ppermute | solution.py:387
  25.2 4.4 %collective-permute-start.6 = (bf16[512,512]{1,0:T(8,128)(2,1)S(1)}, bf16[512,512]{1,0:T(8,128)(2,1)S(1)}, u32[]{:S(2)}, u32[]{:S(2)}) collective-permute-start(bf16[512,512]{1,0:T(8,128)(2,1)S(1)} %copy-done), channel_id=1, source_target_pairs={{0,8},{1,9},{2,10},{3,11},{4,12},{5,13},{6,14},{7,15},{8,0},{9,1},... | collective-permute-start | bytes 1572872 | tf_op jit(solution)/shard_map/ppermute | solution.py:387
  29.6 0.8 copy-start.5
  30.4 21.3 %collective-permute-start.10 = (bf16[528,512]{1,0:T(8,128)(2,1)S(1)}, bf16[528,512]{1,0:T(8,128)(2,1)S(1)}, u32[]{:S(2)}, u32[]{:S(2)}) collective-permute-start(bf16[528,512]{1,0:T(8,128)(2,1)S(1)} %broadcast_select_fusion.1.refs_0_.refs_4_), channel_id=1, source_target_pairs={{0,1},{1,0},{2,3},{3,2},{4,5},{5,4},{6,7},{7,6},{8,9},{9,8},{10,11... | collective-permute-start | bytes 1622024 | tf_op jit(solution)/shard_map/ppermute | solution.py:387
  39.9 11.8 %collective-permute-start.7 = (bf16[528,512]{1,0:T(8,128)(2,1)S(1)}, bf16[528,512]{1,0:T(8,128)(2,1)S(1)}, u32[]{:S(2)}, u32[]{:S(2)}) collective-permute-start(bf16[528,512]{1,0:T(8,128)(2,1)S(1)} %broadcast_select_fusion.1.refs_0_.refs_4_), channel_id=1, source_target_pairs={{0,8},{1,9},{2,10},{3,11},{4,12},{5,13},{6,14},{7,15},{8,0},{9,1},... | collective-permute-start | bytes 1622024 | tf_op jit(solution)/shard_map/ppermute | solution.py:387
  39.9 14.4 %collective-permute-start.8 = (bf16[528,512]{1,0:T(8,128)(2,1)S(1)}, bf16[528,512]{1,0:T(8,128)(2,1)S(1)}, u32[]{:S(2)}, u32[]{:S(2)}) collective-permute-start(bf16[528,512]{1,0:T(8,128)(2,1)S(1)} %broadcast_select_fusion.1.refs_0_.refs_4_), channel_id=1, source_target_pairs={{0,16},{1,17},{2,18},{3,19},{4,20},{5,21},{6,22},{7,23},{8,24},{9,... | collective-permute-start | bytes 1622024 | tf_op jit(solution)/shard_map/ppermute | solution.py:387
  39.9 25.9 %collective-permute-start.16 = (bf16[1024,512]{1,0:T(8,128)(2,1)S(1)}, bf16[1024,512]{1,0:T(8,128)(2,1)}, u32[]{:S(2)}, u32[]{:S(2)}) collective-permute-start(bf16[1024,512]{1,0:T(8,128)(2,1)S(1)} %constant_dynamic-update-slice_fusion.refs_14_), channel_id=1, source_target_pairs={{2,0},{3,1},{4,2},{5,3},{6,4},{7,5},{10,8},{11,9},{12,10},{13,11},... | collective-permute-start | bytes 3145736 | tf_op jit(solution)/shard_map/ppermute | solution.py:387
  51.7 0.8 copy-start.2
  52.5 8.8 %collective-permute-start.14 = (bf16[272,512]{1,0:T(8,128)(2,1)S(1)}, bf16[272,512]{1,0:T(8,128)(2,1)S(1)}, u32[]{:S(2)}, u32[]{:S(2)}) collective-permute-start(bf16[272,512]{1,0:T(8,128)(2,1)S(1)} %slice.7), channel_id=1, source_target_pairs={{0,16},{1,17},{2,18},{3,19},{4,20},{5,21},{6,22},{7,23},{8,24},{9,... | collective-permute-start | bytes 835592 | tf_op jit(solution)/shard_map/ppermute | solution.py:387
  54.3 14.6 %collective-permute-start.11 = (bf16[528,512]{1,0:T(8,128)(2,1)S(1)}, bf16[528,512]{1,0:T(8,128)(2,1)}, u32[]{:S(2)}, u32[]{:S(2)}) collective-permute-start(bf16[528,512]{1,0:T(8,128)(2,1)S(1)} %collective-permute-done.10.refs_4_.refs_8_), channel_id=1, source_target_pairs={{0,8},{1,9},{2,10},{3,11},{4,12},{5,13},{6,14},{7,15},{8,0},{9,1},... | collective-permute-start | bytes 1622024 | tf_op jit(solution)/shard_map/ppermute | solution.py:387
  54.4 15.3 %collective-permute-start.9 = (bf16[528,512]{1,0:T(8,128)(2,1)S(1)}, bf16[528,512]{1,0:T(8,128)(2,1)}, u32[]{:S(2)}, u32[]{:S(2)}) collective-permute-start(bf16[528,512]{1,0:T(8,128)(2,1)S(1)} %collective-permute-done.8.refs_2_.refs_6_), channel_id=1, source_target_pairs={{0,8},{1,9},{2,10},{3,11},{4,12},{5,13},{6,14},{7,15},{8,0},{9,1},... | collective-permute-start | bytes 1622024 | tf_op jit(solution)/shard_map/ppermute | solution.py:387
  54.9 8.1 %collective-permute-start.12 = (bf16[256,512]{1,0:T(8,128)(2,1)S(1)}, bf16[256,512]{1,0:T(8,128)(2,1)}, u32[]{:S(2)}, u32[]{:S(2)}) collective-permute-start(bf16[256,512]{1,0:T(8,128)(2,1)S(1)} %slice.6), channel_id=1, source_target_pairs={{0,1},{1,0},{2,3},{3,2},{4,5},{5,4},{6,7},{7,6},{8,9},{9,8},{10,11... | collective-permute-start | bytes 786440 | tf_op jit(solution)/shard_map/ppermute | solution.py:387
  61.3 10.3 %collective-permute-start.15 = (bf16[272,512]{1,0:T(8,128)(2,1)S(1)}, bf16[272,512]{1,0:T(8,128)(2,1)}, u32[]{:S(2)}, u32[]{:S(2)}) collective-permute-start(bf16[272,512]{1,0:T(8,128)(2,1)S(1)} %collective-permute-done.14.refs_8_.refs_12_), channel_id=1, source_target_pairs={{0,8},{1,9},{2,10},{3,11},{4,12},{5,13},{6,14},{7,15},{8,0},{9,1},... | collective-permute-start | bytes 835592 | tf_op jit(solution)/shard_map/ppermute | solution.py:387
  63.0 5.9 %collective-permute-start.13 = (bf16[256,512]{1,0:T(8,128)(2,1)}, bf16[256,512]{1,0:T(8,128)(2,1)}, u32[]{:S(2)}, u32[]{:S(2)}) collective-permute-start(bf16[256,512]{1,0:T(8,128)(2,1)} %collective-permute-done.12.refs_6_.refs_10_), channel_id=1, source_target_pairs={{0,8},{1,9},{2,10},{3,11},{4,12},{5,13},{6,14},{7,15},{8,0},{9,1},... | collective-permute-start | bytes 786440 | tf_op jit(solution)/shard_map/ppermute | solution.py:387
  64.0 53.2 %copy-start.1 = (f32[512]{0:T(512)S(1)}, f32[512]{0:T(512)}, u32[]{:S(2)}) copy-start(f32[512]{0:T(512)} %param.3) | copy-start | bytes 6148
  65.9 51.4 %collective-permute-start.21 = (bf16[512,512]{1,0:T(8,128)(2,1)S(1)}, bf16[512,512]{1,0:T(8,128)(2,1)S(1)}, u32[]{:S(2)}, u32[]{:S(2)}) collective-permute-start(bf16[512,512]{1,0:T(8,128)(2,1)S(1)} %copy-done), channel_id=1, source_target_pairs={{0,24},{1,25},{2,26},{3,27},{4,28},{5,29},{6,30},{7,31},{8,16},{9,... | collective-permute-start | bytes 1572872 | tf_op jit(solution)/shard_map/ppermute | solution.py:387
  68.8 48.4 %collective-permute-start.20 = (bf16[512,512]{1,0:T(8,128)(2,1)S(1)}, bf16[512,512]{1,0:T(8,128)(2,1)S(1)}, u32[]{:S(2)}, u32[]{:S(2)}) collective-permute-start(bf16[512,512]{1,0:T(8,128)(2,1)S(1)} %copy-done), channel_id=1, source_target_pairs={{0,16},{1,17},{2,18},{3,19},{4,20},{5,21},{6,22},{7,23},{8,24},{9,... | collective-permute-start | bytes 1572872 | tf_op jit(solution)/shard_map/ppermute | solution.py:387
  68.9 48.3 %collective-permute-start.19 = (bf16[1024,512]{1,0:T(8,128)(2,1)S(1)}, bf16[1024,512]{1,0:T(8,128)(2,1)S(1)}, u32[]{:S(2)}, u32[]{:S(2)}) collective-permute-start(bf16[1024,512]{1,0:T(8,128)(2,1)S(1)} %constant_dynamic-update-slice_fusion.refs_14_), channel_id=1, source_target_pairs={{2,6},{3,7},{10,14},{11,15},{18,22},{19,23},{26,30},{27,31}} | collective-permute-start | bytes 3145736 | tf_op jit(solution)/shard_map/ppermute | solution.py:387
  69.6 47.6 %collective-permute-start.18 = (bf16[1024,512]{1,0:T(8,128)(2,1)S(1)}, bf16[1024,512]{1,0:T(8,128)(2,1)S(1)}, u32[]{:S(2)}, u32[]{:S(2)}) collective-permute-start(bf16[1024,512]{1,0:T(8,128)(2,1)S(1)} %constant_dynamic-update-slice_fusion.refs_14_), channel_id=1, source_target_pairs={{2,4},{3,5},{4,6},{5,7},{6,0},{7,1},{10,12},{11,13},{12,14},{13,15... | collective-permute-start | bytes 3145736 | tf_op jit(solution)/shard_map/ppermute | solution.py:387
  71.6 45.7 %collective-permute-start.17 = (bf16[1024,512]{1,0:T(8,128)(2,1)}, bf16[1024,512]{1,0:T(8,128)(2,1)S(1)}, u32[]{:S(2)}, u32[]{:S(2)}) collective-permute-start(bf16[1024,512]{1,0:T(8,128)(2,1)} %collective-permute-done.16.refs_15_), channel_id=1, source_target_pairs={{2,0},{3,1},{4,2},{5,3},{10,8},{11,9},{12,10},{13,11},{18,16},{19,... | collective-permute-start | bytes 3145736 | tf_op jit(solution)/shard_map/ppermute | solution.py:387
  75.1 1.1 copy-start.3
  76.1 41.2 %copy-start.4 = (bf16[528,512]{1,0:T(8,128)(2,1)S(1)}, bf16[528,512]{1,0:T(8,128)(2,1)}, u32[]{:S(2)}) copy-start(bf16[528,512]{1,0:T(8,128)(2,1)} %copy-done.2) | copy-start | bytes 1622020
  76.1 41.2 %copy-start.6 = (bf16[512,512]{1,0:T(8,128)(2,1)S(1)}, bf16[512,512]{1,0:T(8,128)(2,1)}, u32[]{:S(2)}) copy-start(bf16[512,512]{1,0:T(8,128)(2,1)} %copy-done.5) | copy-start | bytes 1572868

commit v4 on v3

--- a/solution.py
+++ b/solution.py
@@ -57,11 +57,13 @@
     for step in range(tiles_count):
         base = SUB * step
         side, inverse = sides[step], inverses[step]
-        columns = [lanes(side, base + b) for b in range(SUB)]
+        if step == 0:
+            columns = [lanes(side, base + b) for b in range(SUB)]
         entry = {(a, b): sublanes(columns[b], a) for b in range(SUB) for a in range(b, SUB)}
         vectors = [[sublanes(side, a) for a in range(SUB)], [sublanes(inverse, a) for a in range(SUB)]]
         if step + 1 < tiles_count:
             vectors.append([lanes(sides[step + 1], base + b) for b in range(SUB)])
+            columns = [lanes(sides[step + 1], base + SUB + b) for b in range(SUB)]
         scale = [None] * SUB
         for m in range(0, SUB, 2):
             n = m + 1
@@ -87,6 +89,12 @@
                 vector[n] = (vector[n] - link * vector[m]) * scale[n]
                 for x in rest:
                     vector[x] = (vector[x] - entry[x, m] * vector[m]) - entry[x, n] * vector[n]
+            if step + 1 < tiles_count:
+                left, right = vectors[2][m], vectors[2][n]
+                columns = [
+                    (column - left * sublanes(left, b)) - right * sublanes(right, b)
+                    for b, column in enumerate(columns)
+                ]
         tops, insides = vectors[:2]
         upper, lower_inverse = tops[0], insides[0]
         for m in range(1, SUB):
@@ -406,7 +414,7 @@
             shared, lambda p, h, s, w: (p, h, s + reach, w), lambda p, h, s, w: s % (2 * reach) == 0
         )
         if reach == SPAN // 2:
-            for turn in reversed(range(ways)):
+            for turn in range(ways):
                 for flip in range(CORES):
                     quarters.append(
                         exchange(offers[flip], lambda p, h, s, w: (w, h ^ flip, s, (p + turn) % ways))

time: 142 us -> 140 us (0.986)
  waiting for transfers between devices: 31.8 us -> 44.6 us
  starting transfers between devices: 35.5 us -> 27.5 us
  Pallas kernels: 63.3 us -> 56.7 us
    ppermute x22, waiting for transfers between devices: 31.8 us -> 44.6 us  [exchange(): return lax.ppermute(value, ('row', 'col'), perm)]
    ppermute x22, starting transfers between devices: 35.5 us -> 27.5 us  [exchange(): return lax.ppermute(value, ('row', 'col'), perm)]
    pallas_call x1, Pallas kernels: 41.1 us -> 34.4 us  [factor_panel(): pl.pallas_call(functools.partial(panel_kernel, views, len(pieces), width)...]
  transfers between devices with their start and end apart: 22 -> 22, of which waited for: 6 -> 7; matrix products, arithmetic and copies ran while one was open for 3% -> 3% of each run, Pallas kernels for 29% -> 25%
where the time goes in v4:
time: 140 us; the launch traced here: 138 us
  Pallas kernels  56.7 us (40%)
  waiting for transfers between devices  44.6 us (32%)
  starting transfers between devices  27.5 us (20%)
  local copies, waits for them, and re-layouts  6.63 us (5%)
  other arithmetic  2.05 us (1%)
    ppermute x22, waiting for transfers between devices, exchange(): return lax.ppermute(value, ('row', 'col'), perm)  44.6 us
    pallas_call x1, Pallas kernels, factor_panel(): pl.pallas_call(functools.partial(panel_kernel, views, len(pieces), width)...  34.4 us
    ppermute x22, starting transfers between devices, exchange(): return lax.ppermute(value, ('row', 'col'), perm)  27.5 us
    pallas_call x1, Pallas kernels, finish_tile(): pl.pallas_call(functools.partial(tile_kernel, (len(panel), len(rows), len...  22.2 us
    unnamed x17, local copies, waits for them, and re-layouts  4.61 us
  transfers between devices with their start and end apart: 22, of which 7 were waited for; matrix products, arithmetic and copies ran while one was open for 3% of the time, Pallas kernels for 25%

profile of v4, /device:TPU:17, one launch (start us, length us, event | category | flops | bytes accessed | tf_op | source)
XLA Modules:
  0.0 137.9 jit_solution(2085672164824600025)
XLA Ops:
  0.0 0.7 reduce-precision_convert_fusion.1
  0.8 1.1 pad_maximum_fusion
  1.9 1.3 collective-permute-start
  3.2 0.0 copy-done
  3.2 0.7 dynamic-slice_bitcast_fusion
  4.0 0.7 collective-permute-start.3
  4.6 1.6 %collective-permute-start.2 = (bf16[256,512]{1,0:T(8,128)(2,1)}, bf16[256,512]{1,0:T(8,128)(2,1)S(1)}, u32[]{:S(2)}, u32[]{:S(2)}) collective-permute-start(bf16[256,512]{1,0:T(8,128)(2,1)} %get-tuple-element.26), channel_id=1, source_target_pairs={{0,0},{1,16},{2,2},{3,18},{4,4},{5,20},{6,6},{7,22},{8,8},{9,24},{... | collective-permute-start | bytes 786440 | tf_op jit(solution)/shard_map/ppermute | solution.py:395
  6.2 11.6 %collective-permute-done = bf16[528,512]{1,0:T(8,128)(2,1)S(1)} collective-permute-done((bf16[528,512]{1,0:T(8,128)(2,1)S(1)}, bf16[528,512]{1,0:T(8,128)(2,1)S(1)}, u32[]{:S(2)}, u32[]{:S(2)}) %collective-permute-start) | collective-permute-done | bytes 540704 | tf_op jit(solution)/shard_map/ppermute | solution.py:395
  17.8 0.1 broadcast_select_fusion
  18.0 2.1 %collective-permute-start.1 = (bf16[528,512]{1,0:T(8,128)(2,1)S(1)}, bf16[528,512]{1,0:T(8,128)(2,1)}, u32[]{:S(2)}, u32[]{:S(2)}) collective-permute-start(bf16[528,512]{1,0:T(8,128)(2,1)S(1)} %broadcast_select_fusion), channel_id=1, source_target_pairs={{0,2},{1,3},{4,6},{5,7},{8,10},{9,11},{12,14},{13,15},{16,18},{17,... | collective-permute-start | bytes 1622024 | tf_op jit(solution)/shard_map/ppermute | solution.py:395
  20.1 1.2 collective-permute-start.4
  21.3 2.9 %collective-permute-start.5 = (bf16[256,512]{1,0:T(8,128)(2,1)S(1)}, bf16[256,512]{1,0:T(8,128)(2,1)}, u32[]{:S(2)}, u32[]{:S(2)}) collective-permute-start(bf16[256,512]{1,0:T(8,128)(2,1)S(1)} %get-tuple-element.25), channel_id=1, source_target_pairs={{0,9},{1,25},{2,11},{3,27},{4,13},{5,29},{6,15},{7,31},{8,1},{9,17... | collective-permute-start | bytes 786440 | tf_op jit(solution)/shard_map/ppermute | solution.py:395
  24.2 0.0 collective-permute-done.2
  24.2 0.0 collective-permute-start.6
  24.3 0.0 collective-permute-done.3
  24.3 1.0 constant_dynamic-update-slice_fusion.2
  25.2 1.4 %collective-permute-done.4 = bf16[256,512]{1,0:T(8,128)(2,1)} collective-permute-done((bf16[256,512]{1,0:T(8,128)(2,1)}, bf16[256,512]{1,0:T(8,128)(2,1)}, u32[]{:S(2)}, u32[]{:S(2)}) %collective-permute-start.4) | collective-permute-done | bytes 262176 | tf_op jit(solution)/shard_map/ppermute | solution.py:395
  26.6 1.0 constant_dynamic-update-slice_fusion.1
  27.6 6.4 %collective-permute-done.5 = bf16[256,512]{1,0:T(8,128)(2,1)} collective-permute-done((bf16[256,512]{1,0:T(8,128)(2,1)S(1)}, bf16[256,512]{1,0:T(8,128)(2,1)}, u32[]{:S(2)}, u32[]{:S(2)}) %collective-permute-start.5) | collective-permute-done | bytes 262176 | tf_op jit(solution)/shard_map/ppermute | solution.py:395
  34.0 1.0 constant_dynamic-update-slice_fusion.refs_14_
  35.0 0.0 collective-permute-done.1
  35.0 0.1 broadcast_select_fusion.1.refs_0_.refs_4_
  35.1 0.0 collective-permute-done.6.refs_20_
  35.1 0.8 copy-done.5
  35.9 1.2 collective-permute-start.10
  37.1 0.0 collective-permute-start.7
  37.1 1.2 collective-permute-start.8
  38.4 1.9 %collective-permute-start.16 = (bf16[1024,512]{1,0:T(8,128)(2,1)S(1)}, bf16[1024,512]{1,0:T(8,128)(2,1)}, u32[]{:S(2)}, u32[]{:S(2)}) collective-permute-start(bf16[1024,512]{1,0:T(8,128)(2,1)S(1)} %constant_dynamic-update-slice_fusion.refs_14_), channel_id=1, source_target_pairs={{2,0},{3,1},{4,2},{5,3},{6,4},{7,5},{10,8},{11,9},{12,10},{13,11},... | collective-permute-start | bytes 3145736 | tf_op jit(solution)/shard_map/ppermute | solution.py:395
  40.3 9.9 %collective-permute-done.10.refs_4_.refs_8_ = bf16[528,512]{1,0:T(8,128)(2,1)S(1)} collective-permute-done((bf16[528,512]{1,0:T(8,128)(2,1)S(1)}, bf16[528,512]{1,0:T(8,128)(2,1)S(1)}, u32[]{:S(2)}, u32[]{:S(2)}) %collective-permute-start.10) | collective-permute-done | bytes 540704 | tf_op jit(solution)/shard_map/ppermute | solution.py:395
  50.2 0.0 collective-permute-done.7.refs_1_.refs_5_
  50.2 0.8 copy-done.2
  51.0 0.5 collective-permute-start.14
  51.5 0.1 collective-permute-start.11
  51.6 0.0 collective-permute-done.8.refs_2_.refs_6_
  51.6 0.5 collective-permute-start.9
  52.0 1.3 collective-permute-start.12
  53.3 5.8 %collective-permute-done.14.refs_8_.refs_12_ = bf16[272,512]{1,0:T(8,128)(2,1)S(1)} collective-permute-done((bf16[272,512]{1,0:T(8,128)(2,1)S(1)}, bf16[272,512]{1,0:T(8,128)(2,1)S(1)}, u32[]{:S(2)}, u32[]{:S(2)}) %collective-permute-start.14) | collective-permute-done | bytes 278560 | tf_op jit(solution)/shard_map/ppermute | solution.py:395
  59.1 1.1 collective-permute-start.15
  60.2 0.0 collective-permute-done.12.refs_6_.refs_10_
  60.2 0.7 collective-permute-start.13
  60.9 0.1 stack.89.place_ref
  61.0 0.2 stack.86.place_ref
  61.2 0.0 copy-start.1
  61.2 3.0 %collective-permute-done.16.refs_15_ = bf16[1024,512]{1,0:T(8,128)(2,1)} collective-permute-done((bf16[1024,512]{1,0:T(8,128)(2,1)S(1)}, bf16[1024,512]{1,0:T(8,128)(2,1)}, u32[]{:S(2)}, u32[]{:S(2)}) %collective-permute-start.16) | collective-permute-done | bytes 1048608 | tf_op jit(solution)/shard_map/ppermute | solution.py:395
  64.2 1.8 %collective-permute-start.21 = (bf16[512,512]{1,0:T(8,128)(2,1)S(1)}, bf16[512,512]{1,0:T(8,128)(2,1)S(1)}, u32[]{:S(2)}, u32[]{:S(2)}) collective-permute-start(bf16[512,512]{1,0:T(8,128)(2,1)S(1)} %copy-done), channel_id=1, source_target_pairs={{0,24},{1,25},{2,26},{3,27},{4,28},{5,29},{6,30},{7,31},{8,16},{9,... | collective-permute-start | bytes 1572872 | tf_op jit(solution)/shard_map/ppermute | solution.py:395
  66.1 0.0 collective-permute-done.13.refs_7_.refs_11_
  66.1 1.2 collective-permute-start.20
  67.3 0.0 collective-permute-done.11.refs_5_.refs_9_
  67.3 0.7 collective-permute-start.19
  68.0 0.0 collective-permute-done.9.refs_3_.refs_7_
  68.0 1.9 %collective-permute-start.18 = (bf16[1024,512]{1,0:T(8,128)(2,1)S(1)}, bf16[1024,512]{1,0:T(8,128)(2,1)S(1)}, u32[]{:S(2)}, u32[]{:S(2)}) collective-permute-start(bf16[1024,512]{1,0:T(8,128)(2,1)S(1)} %constant_dynamic-update-slice_fusion.refs_14_), channel_id=1, source_target_pairs={{2,4},{3,5},{4,6},{5,7},{6,0},{7,1},{10,12},{11,13},{12,14},{13,15... | collective-permute-start | bytes 3145736 | tf_op jit(solution)/shard_map/ppermute | solution.py:395
  69.9 0.0 collective-permute-done.15.refs_9_.refs_13_
  70.0 3.5 %collective-permute-start.17 = (bf16[1024,512]{1,0:T(8,128)(2,1)}, bf16[1024,512]{1,0:T(8,128)(2,1)S(1)}, u32[]{:S(2)}, u32[]{:S(2)}) collective-permute-start(bf16[1024,512]{1,0:T(8,128)(2,1)} %collective-permute-done.16.refs_15_), channel_id=1, source_target_pairs={{2,0},{3,1},{4,2},{5,3},{10,8},{11,9},{12,10},{13,11},{18,16},{19,... | collective-permute-start | bytes 3145736 | tf_op jit(solution)/shard_map/ppermute | solution.py:395
  73.5 0.0 copy-start.3
  73.5 1.0 copy-done.3
  74.5 34.4 %factor_panel.1 = (bf16[1024,1024]{1,0:T(8,128)(2,1)}, bf16[1024,1024]{1,0:T(8,128)(2,1)}, bf16[1024,128]{1,0:T(8,128)(2,1)}, bf16[1024,128]{1,0:T(8,128)(2,1)}) custom-call(s32[24]{0:T(128)S(1)} %stack.89.place_ref, bf16[528,512]{1,0:T(8,128)(2,1)S(1)} %broadcast_select_fusion.1.refs_0_.refs_4_, bf16[528,512]{1,0:T(8,128)(2,1)S(1)} %copy-done.3, ...), custom_call_target="tpu_custom_call" | custom-call | flops 40000000000 | bytes 16777216 | tf_op jit(solution)/shard_map/factor_panel/pallas_call | solution.py:242
  109.0 0.0 collective-permute-done.21.refs_22_
  109.0 0.0 collective-permute-done.20.refs_21_
  109.0 6.5 %collective-permute-done.17.refs_16_ = bf16[1024,512]{1,0:T(8,128)(2,1)S(1)} collective-permute-done((bf16[1024,512]{1,0:T(8,128)(2,1)}, bf16[1024,512]{1,0:T(8,128)(2,1)S(1)}, u32[]{:S(2)}, u32[]{:S(2)}) %collective-permute-start.17) | collective-permute-done | bytes 1048608 | tf_op jit(solution)/shard_map/ppermute | solution.py:395
  115.4 0.0 collective-permute-done.19.refs_18_
  115.4 0.0 collective-permute-done.18.refs_17_
  115.4 0.0 copy-done.1
  115.5 0.0 copy-done.4
  115.5 22.2 %finish_tile.1 = f32[1024,512]{1,0:T(8,128)} custom-call(s32[70]{0:T(128)S(1)} %stack.86.place_ref, f32[1,512]{1,0:T(1,128)S(1)} %bitcast.32, bf16[1024,1024]{1,0:T(8,128)(2,1)} %get-tuple-element.18.refs_0_, bf16[1024,1024]{1,0:T(8,128)(2,1)} %get-tuple-element.19.refs_1_, bf16[1024,128]{1,0:T(8,128)(2,1)} %get-tuple-element.20.refs_2_, ...), custom_call_target="tpu_custom_call" | custom-call | flops 20000000000 | bytes 25165824 | tf_op jit(solution)/shard_map/finish_tile/pallas_call | solution.py:355
  (13 shorter events, 0.1 us)
Async XLA Ops:
  0.0 3.2 %copy-start = (bf16[512,512]{1,0:T(8,128)(2,1)S(1)}, bf16[512,512]{1,0:T(8,128)(2,1)}, u32[]{:S(2)}) copy-start(bf16[512,512]{1,0:T(8,128)(2,1)} %refs_19_.1) | copy-start | bytes 1572868
  1.9 15.9 %collective-permute-start = (bf16[528,512]{1,0:T(8,128)(2,1)S(1)}, bf16[528,512]{1,0:T(8,128)(2,1)S(1)}, u32[]{:S(2)}, u32[]{:S(2)}) collective-permute-start(bf16[528,512]{1,0:T(8,128)(2,1)S(1)} %pad_maximum_fusion), channel_id=1, source_target_pairs={{0,4},{1,5},{8,12},{9,13},{16,20},{17,21},{24,28},{25,29}} | collective-permute-start | bytes 1622024 | tf_op jit(solution)/shard_map/ppermute | solution.py:395
  4.0 20.3 %collective-permute-start.3 = (bf16[256,512]{1,0:T(8,128)(2,1)S(1)}, bf16[256,512]{1,0:T(8,128)(2,1)}, u32[]{:S(2)}, u32[]{:S(2)}) collective-permute-start(bf16[256,512]{1,0:T(8,128)(2,1)S(1)} %get-tuple-element.25), channel_id=1, source_target_pairs={{0,8},{1,24},{2,10},{3,26},{4,12},{5,28},{6,14},{7,30},{8,0},{9,16... | collective-permute-start | bytes 786440 | tf_op jit(solution)/shard_map/ppermute | solution.py:395
  4.6 19.6 %collective-permute-start.2 = (bf16[256,512]{1,0:T(8,128)(2,1)}, bf16[256,512]{1,0:T(8,128)(2,1)S(1)}, u32[]{:S(2)}, u32[]{:S(2)}) collective-permute-start(bf16[256,512]{1,0:T(8,128)(2,1)} %get-tuple-element.26), channel_id=1, source_target_pairs={{0,0},{1,16},{2,2},{3,18},{4,4},{5,20},{6,6},{7,22},{8,8},{9,24},{... | collective-permute-start | bytes 786440 | tf_op jit(solution)/shard_map/ppermute | solution.py:395
  18.0 17.0 %collective-permute-start.1 = (bf16[528,512]{1,0:T(8,128)(2,1)S(1)}, bf16[528,512]{1,0:T(8,128)(2,1)}, u32[]{:S(2)}, u32[]{:S(2)}) collective-permute-start(bf16[528,512]{1,0:T(8,128)(2,1)S(1)} %broadcast_select_fusion), channel_id=1, source_target_pairs={{0,2},{1,3},{4,6},{5,7},{8,10},{9,11},{12,14},{13,15},{16,18},{17,... | collective-permute-start | bytes 1622024 | tf_op jit(solution)/shard_map/ppermute | solution.py:395
  20.1 6.6 %collective-permute-start.4 = (bf16[256,512]{1,0:T(8,128)(2,1)}, bf16[256,512]{1,0:T(8,128)(2,1)}, u32[]{:S(2)}, u32[]{:S(2)}) collective-permute-start(bf16[256,512]{1,0:T(8,128)(2,1)} %get-tuple-element.26), channel_id=1, source_target_pairs={{0,1},{1,17},{2,3},{3,19},{4,5},{5,21},{6,7},{7,23},{8,9},{9,25},{... | collective-permute-start | bytes 786440 | tf_op jit(solution)/shard_map/ppermute | solution.py:395
  21.3 12.7 %collective-permute-start.5 = (bf16[256,512]{1,0:T(8,128)(2,1)S(1)}, bf16[256,512]{1,0:T(8,128)(2,1)}, u32[]{:S(2)}, u32[]{:S(2)}) collective-permute-start(bf16[256,512]{1,0:T(8,128)(2,1)S(1)} %get-tuple-element.25), channel_id=1, source_target_pairs={{0,9},{1,25},{2,11},{3,27},{4,13},{5,29},{6,15},{7,31},{8,1},{9,17... | collective-permute-start | bytes 786440 | tf_op jit(solution)/shard_map/ppermute | solution.py:395
  24.2 10.9 %collective-permute-start.6 = (bf16[512,512]{1,0:T(8,128)(2,1)S(1)}, bf16[512,512]{1,0:T(8,128)(2,1)S(1)}, u32[]{:S(2)}, u32[]{:S(2)}) collective-permute-start(bf16[512,512]{1,0:T(8,128)(2,1)S(1)} %copy-done), channel_id=1, source_target_pairs={{0,8},{1,9},{2,10},{3,11},{4,12},{5,13},{6,14},{7,15},{8,0},{9,1},... | collective-permute-start | bytes 1572872 | tf_op jit(solution)/shard_map/ppermute | solution.py:395
  35.1 0.8 copy-start.5
  35.9 14.3 %collective-permute-start.10 = (bf16[528,512]{1,0:T(8,128)(2,1)S(1)}, bf16[528,512]{1,0:T(8,128)(2,1)S(1)}, u32[]{:S(2)}, u32[]{:S(2)}) collective-permute-start(bf16[528,512]{1,0:T(8,128)(2,1)S(1)} %broadcast_select_fusion.1.refs_0_.refs_4_), channel_id=1, source_target_pairs={{0,1},{1,0},{2,3},{3,2},{4,5},{5,4},{6,7},{7,6},{8,9},{9,8},{10,11... | collective-permute-start | bytes 1622024 | tf_op jit(solution)/shard_map/ppermute | solution.py:395
  37.1 13.1 %collective-permute-start.7 = (bf16[528,512]{1,0:T(8,128)(2,1)S(1)}, bf16[528,512]{1,0:T(8,128)(2,1)S(1)}, u32[]{:S(2)}, u32[]{:S(2)}) collective-permute-start(bf16[528,512]{1,0:T(8,128)(2,1)S(1)} %broadcast_select_fusion.1.refs_0_.refs_4_), channel_id=1, source_target_pairs={{0,8},{1,9},{2,10},{3,11},{4,12},{5,13},{6,14},{7,15},{8,0},{9,1},... | collective-permute-start | bytes 1622024 | tf_op jit(solution)/shard_map/ppermute | solution.py:395
  37.1 14.4 %collective-permute-start.8 = (bf16[528,512]{1,0:T(8,128)(2,1)S(1)}, bf16[528,512]{1,0:T(8,128)(2,1)S(1)}, u32[]{:S(2)}, u32[]{:S(2)}) collective-permute-start(bf16[528,512]{1,0:T(8,128)(2,1)S(1)} %broadcast_select_fusion.1.refs_0_.refs_4_), channel_id=1, source_target_pairs={{0,16},{1,17},{2,18},{3,19},{4,20},{5,21},{6,22},{7,23},{8,24},{9,... | collective-permute-start | bytes 1622024 | tf_op jit(solution)/shard_map/ppermute | solution.py:395
  38.4 25.9 %collective-permute-start.16 = (bf16[1024,512]{1,0:T(8,128)(2,1)S(1)}, bf16[1024,512]{1,0:T(8,128)(2,1)}, u32[]{:S(2)}, u32[]{:S(2)}) collective-permute-start(bf16[1024,512]{1,0:T(8,128)(2,1)S(1)} %constant_dynamic-update-slice_fusion.refs_14_), channel_id=1, source_target_pairs={{2,0},{3,1},{4,2},{5,3},{6,4},{7,5},{10,8},{11,9},{12,10},{13,11},... | collective-permute-start | bytes 3145736 | tf_op jit(solution)/shard_map/ppermute | solution.py:395
  50.2 0.8 copy-start.2
  51.0 8.0 %collective-permute-start.14 = (bf16[272,512]{1,0:T(8,128)(2,1)S(1)}, bf16[272,512]{1,0:T(8,128)(2,1)S(1)}, u32[]{:S(2)}, u32[]{:S(2)}) collective-permute-start(bf16[272,512]{1,0:T(8,128)(2,1)S(1)} %slice.7), channel_id=1, source_target_pairs={{0,16},{1,17},{2,18},{3,19},{4,20},{5,21},{6,22},{7,23},{8,24},{9,... | collective-permute-start | bytes 835592 | tf_op jit(solution)/shard_map/ppermute | solution.py:395
  51.5 15.8 %collective-permute-start.11 = (bf16[528,512]{1,0:T(8,128)(2,1)S(1)}, bf16[528,512]{1,0:T(8,128)(2,1)}, u32[]{:S(2)}, u32[]{:S(2)}) collective-permute-start(bf16[528,512]{1,0:T(8,128)(2,1)S(1)} %collective-permute-done.10.refs_4_.refs_8_), channel_id=1, source_target_pairs={{0,8},{1,9},{2,10},{3,11},{4,12},{5,13},{6,14},{7,15},{8,0},{9,1},... | collective-permute-start | bytes 1622024 | tf_op jit(solution)/shard_map/ppermute | solution.py:395
  51.6 16.4 %collective-permute-start.9 = (bf16[528,512]{1,0:T(8,128)(2,1)S(1)}, bf16[528,512]{1,0:T(8,128)(2,1)}, u32[]{:S(2)}, u32[]{:S(2)}) collective-permute-start(bf16[528,512]{1,0:T(8,128)(2,1)S(1)} %collective-permute-done.8.refs_2_.refs_6_), channel_id=1, source_target_pairs={{0,8},{1,9},{2,10},{3,11},{4,12},{5,13},{6,14},{7,15},{8,0},{9,1},... | collective-permute-start | bytes 1622024 | tf_op jit(solution)/shard_map/ppermute | solution.py:395
  52.0 8.1 %collective-permute-start.12 = (bf16[256,512]{1,0:T(8,128)(2,1)S(1)}, bf16[256,512]{1,0:T(8,128)(2,1)}, u32[]{:S(2)}, u32[]{:S(2)}) collective-permute-start(bf16[256,512]{1,0:T(8,128)(2,1)S(1)} %slice.6), channel_id=1, source_target_pairs={{0,1},{1,0},{2,3},{3,2},{4,5},{5,4},{6,7},{7,6},{8,9},{9,8},{10,11... | collective-permute-start | bytes 786440 | tf_op jit(solution)/shard_map/ppermute | solution.py:395
  59.1 10.9 %collective-permute-start.15 = (bf16[272,512]{1,0:T(8,128)(2,1)S(1)}, bf16[272,512]{1,0:T(8,128)(2,1)}, u32[]{:S(2)}, u32[]{:S(2)}) collective-permute-start(bf16[272,512]{1,0:T(8,128)(2,1)S(1)} %collective-permute-done.14.refs_8_.refs_12_), channel_id=1, source_target_pairs={{0,8},{1,9},{2,10},{3,11},{4,12},{5,13},{6,14},{7,15},{8,0},{9,1},... | collective-permute-start | bytes 835592 | tf_op jit(solution)/shard_map/ppermute | solution.py:395
  60.2 5.9 %collective-permute-start.13 = (bf16[256,512]{1,0:T(8,128)(2,1)}, bf16[256,512]{1,0:T(8,128)(2,1)}, u32[]{:S(2)}, u32[]{:S(2)}) collective-permute-start(bf16[256,512]{1,0:T(8,128)(2,1)} %collective-permute-done.12.refs_6_.refs_10_), channel_id=1, source_target_pairs={{0,8},{1,9},{2,10},{3,11},{4,12},{5,13},{6,14},{7,15},{8,0},{9,1},... | collective-permute-start | bytes 786440 | tf_op jit(solution)/shard_map/ppermute | solution.py:395
  61.2 54.2 %copy-start.1 = (f32[512]{0:T(512)S(1)}, f32[512]{0:T(512)}, u32[]{:S(2)}) copy-start(f32[512]{0:T(512)} %param.3) | copy-start | bytes 6148
  64.2 44.7 %collective-permute-start.21 = (bf16[512,512]{1,0:T(8,128)(2,1)S(1)}, bf16[512,512]{1,0:T(8,128)(2,1)S(1)}, u32[]{:S(2)}, u32[]{:S(2)}) collective-permute-start(bf16[512,512]{1,0:T(8,128)(2,1)S(1)} %copy-done), channel_id=1, source_target_pairs={{0,24},{1,25},{2,26},{3,27},{4,28},{5,29},{6,30},{7,31},{8,16},{9,... | collective-permute-start | bytes 1572872 | tf_op jit(solution)/shard_map/ppermute | solution.py:395
  66.1 42.9 %collective-permute-start.20 = (bf16[512,512]{1,0:T(8,128)(2,1)S(1)}, bf16[512,512]{1,0:T(8,128)(2,1)S(1)}, u32[]{:S(2)}, u32[]{:S(2)}) collective-permute-start(bf16[512,512]{1,0:T(8,128)(2,1)S(1)} %copy-done), channel_id=1, source_target_pairs={{0,16},{1,17},{2,18},{3,19},{4,20},{5,21},{6,22},{7,23},{8,24},{9,... | collective-permute-start | bytes 1572872 | tf_op jit(solution)/shard_map/ppermute | solution.py:395
  67.3 48.2 %collective-permute-start.19 = (bf16[1024,512]{1,0:T(8,128)(2,1)S(1)}, bf16[1024,512]{1,0:T(8,128)(2,1)S(1)}, u32[]{:S(2)}, u32[]{:S(2)}) collective-permute-start(bf16[1024,512]{1,0:T(8,128)(2,1)S(1)} %constant_dynamic-update-slice_fusion.refs_14_), channel_id=1, source_target_pairs={{2,6},{3,7},{10,14},{11,15},{18,22},{19,23},{26,30},{27,31}} | collective-permute-start | bytes 3145736 | tf_op jit(solution)/shard_map/ppermute | solution.py:395
  68.0 47.4 %collective-permute-start.18 = (bf16[1024,512]{1,0:T(8,128)(2,1)S(1)}, bf16[1024,512]{1,0:T(8,128)(2,1)S(1)}, u32[]{:S(2)}, u32[]{:S(2)}) collective-permute-start(bf16[1024,512]{1,0:T(8,128)(2,1)S(1)} %constant_dynamic-update-slice_fusion.refs_14_), channel_id=1, source_target_pairs={{2,4},{3,5},{4,6},{5,7},{6,0},{7,1},{10,12},{11,13},{12,14},{13,15... | collective-permute-start | bytes 3145736 | tf_op jit(solution)/shard_map/ppermute | solution.py:395
  70.0 45.5 %collective-permute-start.17 = (bf16[1024,512]{1,0:T(8,128)(2,1)}, bf16[1024,512]{1,0:T(8,128)(2,1)S(1)}, u32[]{:S(2)}, u32[]{:S(2)}) collective-permute-start(bf16[1024,512]{1,0:T(8,128)(2,1)} %collective-permute-done.16.refs_15_), channel_id=1, source_target_pairs={{2,0},{3,1},{4,2},{5,3},{10,8},{11,9},{12,10},{13,11},{18,16},{19,... | collective-permute-start | bytes 3145736 | tf_op jit(solution)/shard_map/ppermute | solution.py:395
  73.5 1.1 copy-start.3
  74.5 41.0 %copy-start.4 = (bf16[528,512]{1,0:T(8,128)(2,1)S(1)}, bf16[528,512]{1,0:T(8,128)(2,1)}, u32[]{:S(2)}) copy-start(bf16[528,512]{1,0:T(8,128)(2,1)} %copy-done.2) | copy-start | bytes 1622020
  74.5 41.0 %copy-start.6 = (bf16[512,512]{1,0:T(8,128)(2,1)S(1)}, bf16[512,512]{1,0:T(8,128)(2,1)}, u32[]{:S(2)}) copy-start(bf16[512,512]{1,0:T(8,128)(2,1)} %copy-done.5) | copy-start | bytes 1572868

commit v5 on v4

--- a/solution.py
+++ b/solution.py
@@ -278,52 +278,58 @@
     at = pl.ds(pl.multiple_of(slot * width, width), width)
     below, right = pl.ds(0, row_count), pl.ds(row_count, width)
 
-    for wait in waits:
-        wait()
-    step = min(WIDE, width)
-    groups = [(cols_ref, at_row, pl.ds(row_count + at_row, step), step) for at_row in range(0, width, step)]
-    groups += [(rows_ref, at_row, pl.ds(at_row, band), band) for at_row in range(0, row_count, band)]
-
-    def grams(start):
-        block = panel_ref[pl.ds(start, WIDE), :]
-        return [dot_nt(ref[pl.ds(at_row, count), :], block) for ref, at_row, _, count in groups]
-
-    columns = grams(0)
-    for fetch in fetches:
-        fetch.wait()
-
-    for start in range(0, PANEL, WIDE):
-        first, second = pl.ds(start, BLOCK), pl.ds(start + BLOCK, BLOCK)
-        between = dot_nn3((high_ref[second, first], low_ref[second, first]), (inv_high_ref[first, :], inv_low_ref[first, :]))
-        corner = split(-dot_nn3((inv_high_ref[second, :], inv_low_ref[second, :]), split(between)))
-        for wide_ref, inv_ref, part in ((wide_high_ref, inv_high_ref, corner[0]), (wide_low_ref, inv_low_ref, corner[1])):
-            wide_ref[first, pl.ds(0, BLOCK)] = inv_ref[first, :]
-            wide_ref[first, pl.ds(BLOCK, BLOCK)] = jnp.zeros((BLOCK, BLOCK), bf16)
-            wide_ref[second, pl.ds(0, BLOCK)] = part
-            wide_ref[second, pl.ds(BLOCK, BLOCK)] = inv_ref[second, :]
-
-    for start in range(0, PANEL, WIDE):
-        here = pl.ds(start, WIDE)
-        if start > 0:
-            columns = [
-                column
-                - dot_nt3(
-                    (left_high_ref[mine, :start], left_low_ref[mine, :start]), (high_ref[here, :start], low_ref[here, :start])
-                )
-                for column, (_, _, mine, _) in zip(grams(start), groups)
-            ]
-        for column, (_, _, mine, _) in zip(columns, groups):
-            column = dot_nt3(split(column), (wide_high_ref[here, :], wide_low_ref[here, :]))
-            left_high_ref[mine, here], left_low_ref[mine, here] = split(column)
+    def solve(with_cols):
+        for wait in waits:
+            wait()
+        step = min(WIDE, width)
+        groups = [(rows_ref, at_row, pl.ds(at_row, band), band) for at_row in range(0, row_count, band)]
+        if with_cols:
+            groups = [
+                (cols_ref, at_row, pl.ds(row_count + at_row, step), step) for at_row in range(0, width, step)
+            ] + groups
+
+        def grams(start):
+            block = panel_ref[pl.ds(start, WIDE), :]
+            return [dot_nt(ref[pl.ds(at_row, count), :], block) for ref, at_row, _, count in groups]
+
+        columns = grams(0)
+        for fetch in fetches:
+            fetch.wait()
+
+        for start in range(0, PANEL, WIDE):
+            first, second = pl.ds(start, BLOCK), pl.ds(start + BLOCK, BLOCK)
+            between = dot_nn3((high_ref[second, first], low_ref[second, first]), (inv_high_ref[first, :], inv_low_ref[first, :]))
+            corner = split(-dot_nn3((inv_high_ref[second, :], inv_low_ref[second, :]), split(between)))
+            for wide_ref, inv_ref, part in ((wide_high_ref, inv_high_ref, corner[0]), (wide_low_ref, inv_low_ref, corner[1])):
+                wide_ref[first, pl.ds(0, BLOCK)] = inv_ref[first, :]
+                wide_ref[first, pl.ds(BLOCK, BLOCK)] = jnp.zeros((BLOCK, BLOCK), bf16)
+                wide_ref[second, pl.ds(0, BLOCK)] = part
+                wide_ref[second, pl.ds(BLOCK, BLOCK)] = inv_ref[second, :]
+
+        for start in range(0, PANEL, WIDE):
+            here = pl.ds(start, WIDE)
+            if start > 0:
+                columns = [
+                    column
+                    - dot_nt3(
+                        (left_high_ref[mine, :start], left_low_ref[mine, :start]), (high_ref[here, :start], low_ref[here, :start])
+                    )
+                    for column, (_, _, mine, _) in zip(grams(start), groups)
+                ]
+            for column, (_, _, mine, _) in zip(columns, groups):
+                column = dot_nt3(split(column), (wide_high_ref[here, :], wide_low_ref[here, :]))
+                left_high_ref[mine, here], left_low_ref[mine, here] = split(column)
 
     @pl.when(in_panel)
     def _():
+        solve(False)
         mine = pl.ds(pl.multiple_of(row_index * band, band), band)
         out_ref[pl.ds(0, band), :] = high_ref[mine, at].astype(f32) + low_ref[mine, at].astype(f32)
         out_ref[pl.ds(band, row_count), :] = left_high_ref[below, at].astype(f32) + left_low_ref[below, at].astype(f32)
 
     @pl.when(jnp.logical_not(in_panel))
     def _():
+        solve(True)
         out_ref[pl.ds(0, band), :] = jnp.zeros((band, width), f32)
         items = lax.broadcasted_iota(jnp.int32, (band, width), 0) + row_index * band
         columns = lax.broadcasted_iota(jnp.int32, (band, width), 1) + col_index * width
@@ -402,7 +408,8 @@
     parts = jnp.stack([high, middle, regular - high - middle]).astype(bf16)
     parts = jnp.pad(parts, ((0, PARTS - 3), (0, users - width)))
 
-    halves = interactions.reshape(CORES, band, users)
+    raised = exchange(interactions, lambda p, h, s, w: (p, h, 0, w), lambda p, h, s, w: s == SPAN - 1)
+    halves = (jnp.where(slot == 0, raised, interactions) if ways == 2 else interactions).reshape(CORES, band, users)
     offers = [lax.dynamic_index_in_dim(halves, core ^ flip, 0, False) for flip in range(CORES)]
 
     half = width // 2
@@ -469,14 +476,14 @@
         first = exchange(quarters, lambda p, h, s, w: (p, h, s - 1, w), lambda p, h, s, w: s > 0)
         relayed, ready = lax.optimization_barrier((first, quarters, *crossed))[:2]
         second = exchange(relayed, lambda p, h, s, w: (p, h, s - 1, w), lambda p, h, s, w: 0 < s < SPAN - 1)
-        ring = exchange(ready, lambda p, h, s, w: (p, h, (s + 1) % SPAN, w), lambda p, h, s, w: s > 0)
+        ring = exchange(ready, lambda p, h, s, w: (p, h, s + 1, w), lambda p, h, s, w: 0 < s < SPAN - 1)
         leap = exchange(ready, lambda p, h, s, w: (p, h, s + 2, w), lambda p, h, s, w: s == 1)
         rows = [quarters, first, second, ring, leap]
         from_slots = [
-            slot,
+            jnp.where(slot == 0, 3, slot),
             jnp.where(slot < 3, slot + 1, 0),
             jnp.where(slot < 2, slot + 2, 0),
-            jnp.where(slot == 1, 0, (slot + 3) % SPAN),
+            jnp.where(slot > 1, slot - 1, 0),
             jnp.where(slot == 3, 1, 0),
         ]
         for from_slot, piece in enumerate(rows):

time: 140 us -> 144 us (1.029); the launches traced: 138 us -> 144 us
  waiting for transfers between devices: 44.6 us -> 48.4 us
  starting transfers between devices: 27.5 us -> 29.9 us
    ppermute x22 -> x23, waiting for transfers between devices: 44.6 us -> 48.4 us  [exchange(): return lax.ppermute(value, ('row', 'col'), perm)]
    ppermute x22 -> x23, starting transfers between devices: 27.5 us -> 29.9 us  [exchange(): return lax.ppermute(value, ('row', 'col'), perm)]
    unnamed x17 -> x19, local copies, waits for them, and re-layouts: 4.61 us -> 5.32 us
  transfers between devices with their start and end apart: 22 -> 23, of which waited for: 7 -> 8; matrix products, arithmetic and copies ran while one was open for 3% -> 4% of each run, Pallas kernels for 25% -> 24%
where the time goes in v5:
time: 144 us
  Pallas kernels  56.2 us (39%)
  waiting for transfers between devices  48.4 us (34%)
  starting transfers between devices  29.9 us (21%)
  local copies, waits for them, and re-layouts  6.39 us (4%)
  other arithmetic  2.05 us (1%)
    ppermute x23, waiting for transfers between devices, exchange(): return lax.ppermute(value, ('row', 'col'), perm)  48.4 us
    pallas_call x1, Pallas kernels, factor_panel(): pl.pallas_call(functools.partial(panel_kernel, views, len(pieces), width)...  34.4 us
    ppermute x23, starting transfers between devices, exchange(): return lax.ppermute(value, ('row', 'col'), perm)  29.9 us
    pallas_call x1, Pallas kernels, finish_tile(): pl.pallas_call(functools.partial(tile_kernel, (len(panel), len(rows), len...  21.8 us
    unnamed x19, local copies, waits for them, and re-layouts  5.32 us
  transfers between devices with their start and end apart: 23, of which 8 were waited for; matrix products, arithmetic and copies ran while one was open for 4% of the time, Pallas kernels for 24%

profile of v5, /device:TPU:17, one launch (start us, length us, event | category | flops | bytes accessed | tf_op | source)
XLA Modules:
  0.0 143.5 jit_solution(13833048048684311002)
XLA Ops:
  0.0 0.8 collective-permute-start.2
  0.8 0.7 reduce-precision_convert_fusion.1
  1.6 1.1 pad_maximum_fusion
  2.6 1.3 collective-permute-start
  4.0 0.0 collective-permute-done.2
  4.0 0.1 broadcast_select_fusion.2
  4.1 0.7 dynamic-slice_bitcast_fusion
  4.8 0.7 collective-permute-start.4
  5.5 1.6 %collective-permute-start.3 = (bf16[256,512]{1,0:T(8,128)(2,1)}, bf16[256,512]{1,0:T(8,128)(2,1)S(1)}, u32[]{:S(2)}, u32[]{:S(2)}) collective-permute-start(bf16[256,512]{1,0:T(8,128)(2,1)} %get-tuple-element.26), channel_id=1, source_target_pairs={{0,0},{1,16},{2,2},{3,18},{4,4},{5,20},{6,6},{7,22},{8,8},{9,24},{... | collective-permute-start | bytes 786440 | tf_op jit(solution)/shard_map/ppermute | solution.py:401
  7.1 11.5 %collective-permute-done = bf16[528,512]{1,0:T(8,128)(2,1)S(1)} collective-permute-done((bf16[528,512]{1,0:T(8,128)(2,1)S(1)}, bf16[528,512]{1,0:T(8,128)(2,1)S(1)}, u32[]{:S(2)}, u32[]{:S(2)}) %collective-permute-start) | collective-permute-done | bytes 540704 | tf_op jit(solution)/shard_map/ppermute | solution.py:401
  18.6 0.1 broadcast_select_fusion
  18.7 2.1 %collective-permute-start.1 = (bf16[528,512]{1,0:T(8,128)(2,1)S(1)}, bf16[528,512]{1,0:T(8,128)(2,1)}, u32[]{:S(2)}, u32[]{:S(2)}) collective-permute-start(bf16[528,512]{1,0:T(8,128)(2,1)S(1)} %broadcast_select_fusion), channel_id=1, source_target_pairs={{0,2},{1,3},{4,6},{5,7},{8,10},{9,11},{12,14},{13,15},{16,18},{17,... | collective-permute-start | bytes 1622024 | tf_op jit(solution)/shard_map/ppermute | solution.py:401
  20.8 4.0 %collective-permute-start.5 = (bf16[256,512]{1,0:T(8,128)(2,1)}, bf16[256,512]{1,0:T(8,128)(2,1)S(1)}, u32[]{:S(2)}, u32[]{:S(2)}) collective-permute-start(bf16[256,512]{1,0:T(8,128)(2,1)} %get-tuple-element.26), channel_id=1, source_target_pairs={{0,1},{1,17},{2,3},{3,19},{4,5},{5,21},{6,7},{7,23},{8,9},{9,25},{... | collective-permute-start | bytes 786440 | tf_op jit(solution)/shard_map/ppermute | solution.py:401
  24.8 0.0 collective-permute-start.7
  24.8 0.0 collective-permute-done.3
  24.8 0.7 copy-done.7
  25.5 0.4 collective-permute-start.6
  25.9 1.0 constant_dynamic-update-slice_fusion.3
  26.9 0.0 collective-permute-done.4
  26.9 1.0 constant_dynamic-update-slice_fusion.2
  27.8 3.7 %collective-permute-done.5 = bf16[256,512]{1,0:T(8,128)(2,1)S(1)} collective-permute-done((bf16[256,512]{1,0:T(8,128)(2,1)}, bf16[256,512]{1,0:T(8,128)(2,1)S(1)}, u32[]{:S(2)}, u32[]{:S(2)}) %collective-permute-start.5) | collective-permute-done | bytes 262176 | tf_op jit(solution)/shard_map/ppermute | solution.py:401
  31.6 5.3 %collective-permute-done.6 = bf16[256,512]{1,0:T(8,128)(2,1)S(1)} collective-permute-done((bf16[256,512]{1,0:T(8,128)(2,1)S(1)}, bf16[256,512]{1,0:T(8,128)(2,1)S(1)}, u32[]{:S(2)}, u32[]{:S(2)}) %collective-permute-start.6) | collective-permute-done | bytes 262176 | tf_op jit(solution)/shard_map/ppermute | solution.py:401
  36.9 0.0 collective-permute-done.1
  36.9 0.1 broadcast_select_fusion.1.refs_0_.refs_4_
  37.0 0.0 collective-permute-done.7.refs_20_
  37.0 0.8 copy-done.5
  37.8 2.1 %collective-permute-start.11 = (bf16[528,512]{1,0:T(8,128)(2,1)S(1)}, bf16[528,512]{1,0:T(8,128)(2,1)S(1)}, u32[]{:S(2)}, u32[]{:S(2)}) collective-permute-start(bf16[528,512]{1,0:T(8,128)(2,1)S(1)} %broadcast_select_fusion.1.refs_0_.refs_4_), channel_id=1, source_target_pairs={{0,1},{1,0},{2,3},{3,2},{4,5},{5,4},{6,7},{7,6},{8,9},{9,8},{10,11... | collective-permute-start | bytes 1622024 | tf_op jit(solution)/shard_map/ppermute | solution.py:401
  39.8 0.7 collective-permute-start.8
  40.5 0.0 collective-permute-start.9
  40.5 2.2 %collective-permute-start.17 = (bf16[1024,512]{1,0:T(8,128)(2,1)S(1)}, bf16[1024,512]{1,0:T(8,128)(2,1)}, u32[]{:S(2)}, u32[]{:S(2)}) collective-permute-start(bf16[1024,512]{1,0:T(8,128)(2,1)S(1)} %constant_dynamic-update-slice_fusion.refs_14_), channel_id=1, source_target_pairs={{2,0},{3,1},{4,2},{5,3},{6,4},{7,5},{10,8},{11,9},{12,10},{13,11},... | collective-permute-start | bytes 3145736 | tf_op jit(solution)/shard_map/ppermute | solution.py:401
  42.7 9.5 %collective-permute-done.11.refs_4_.refs_8_ = bf16[528,512]{1,0:T(8,128)(2,1)S(1)} collective-permute-done((bf16[528,512]{1,0:T(8,128)(2,1)S(1)}, bf16[528,512]{1,0:T(8,128)(2,1)S(1)}, u32[]{:S(2)}, u32[]{:S(2)}) %collective-permute-start.11) | collective-permute-done | bytes 540704 | tf_op jit(solution)/shard_map/ppermute | solution.py:401
  52.2 0.0 collective-permute-done.8.refs_1_.refs_5_
  52.2 0.8 copy-done.2
  53.1 1.2 collective-permute-start.15
  54.2 1.4 collective-permute-start.12
  55.7 0.0 collective-permute-done.9.refs_2_.refs_6_
  55.7 0.0 collective-permute-start.10
  55.7 0.1 collective-permute-start.13
  55.8 4.8 %collective-permute-done.15.refs_8_.refs_12_ = bf16[272,512]{1,0:T(8,128)(2,1)S(1)} collective-permute-done((bf16[272,512]{1,0:T(8,128)(2,1)S(1)}, bf16[272,512]{1,0:T(8,128)(2,1)S(1)}, u32[]{:S(2)}, u32[]{:S(2)}) %collective-permute-start.15) | collective-permute-done | bytes 278560 | tf_op jit(solution)/shard_map/ppermute | solution.py:401
  60.6 1.6 %collective-permute-start.16 = (bf16[272,512]{1,0:T(8,128)(2,1)S(1)}, bf16[272,512]{1,0:T(8,128)(2,1)}, u32[]{:S(2)}, u32[]{:S(2)}) collective-permute-start(bf16[272,512]{1,0:T(8,128)(2,1)S(1)} %collective-permute-done.15.refs_8_.refs_12_), channel_id=1, source_target_pairs={{0,8},{1,9},{2,10},{3,11},{4,12},{5,13},{6,14},{7,15},{8,0},{9,1},... | collective-permute-start | bytes 835592 | tf_op jit(solution)/shard_map/ppermute | solution.py:401
  62.2 1.0 collective-permute-done.13.refs_6_.refs_10_
  63.2 1.4 collective-permute-start.14
  64.6 0.1 stack.89.place_ref
  64.7 0.2 stack.86.place_ref
  64.9 0.0 copy-start.1
  64.9 5.6 %collective-permute-done.17.refs_15_ = bf16[1024,512]{1,0:T(8,128)(2,1)} collective-permute-done((bf16[1024,512]{1,0:T(8,128)(2,1)S(1)}, bf16[1024,512]{1,0:T(8,128)(2,1)}, u32[]{:S(2)}, u32[]{:S(2)}) %collective-permute-start.17) | collective-permute-done | bytes 1048608 | tf_op jit(solution)/shard_map/ppermute | solution.py:401
  70.5 1.8 %collective-permute-start.22 = (bf16[512,512]{1,0:T(8,128)(2,1)S(1)}, bf16[512,512]{1,0:T(8,128)(2,1)S(1)}, u32[]{:S(2)}, u32[]{:S(2)}) collective-permute-start(bf16[512,512]{1,0:T(8,128)(2,1)S(1)} %copy-done), channel_id=1, source_target_pairs={{0,24},{1,25},{2,26},{3,27},{4,28},{5,29},{6,30},{7,31},{8,16},{9,... | collective-permute-start | bytes 1572872 | tf_op jit(solution)/shard_map/ppermute | solution.py:401
  72.3 0.0 collective-permute-done.14.refs_7_.refs_11_
  72.4 0.3 collective-permute-start.21
  72.7 0.0 collective-permute-done.12.refs_5_.refs_9_
  72.7 0.7 collective-permute-start.20
  73.4 0.0 collective-permute-done.10.refs_3_.refs_7_
  73.4 1.9 %collective-permute-start.19 = (bf16[1024,512]{1,0:T(8,128)(2,1)S(1)}, bf16[1024,512]{1,0:T(8,128)(2,1)S(1)}, u32[]{:S(2)}, u32[]{:S(2)}) collective-permute-start(bf16[1024,512]{1,0:T(8,128)(2,1)S(1)} %constant_dynamic-update-slice_fusion.refs_14_), channel_id=1, source_target_pairs={{2,4},{3,5},{4,6},{5,7},{10,12},{11,13},{12,14},{13,15},{18,20},{1... | collective-permute-start | bytes 3145736 | tf_op jit(solution)/shard_map/ppermute | solution.py:401
  75.3 0.0 collective-permute-done.16.refs_9_.refs_13_
  75.3 3.8 %collective-permute-start.18 = (bf16[1024,512]{1,0:T(8,128)(2,1)}, bf16[1024,512]{1,0:T(8,128)(2,1)S(1)}, u32[]{:S(2)}, u32[]{:S(2)}) collective-permute-start(bf16[1024,512]{1,0:T(8,128)(2,1)} %collective-permute-done.17.refs_15_), channel_id=1, source_target_pairs={{2,0},{3,1},{4,2},{5,3},{10,8},{11,9},{12,10},{13,11},{18,16},{19,... | collective-permute-start | bytes 3145736 | tf_op jit(solution)/shard_map/ppermute | solution.py:401
  79.1 0.0 copy-start.3
  79.1 1.0 copy-done.3
  80.2 34.4 %factor_panel.1 = (bf16[1024,1024]{1,0:T(8,128)(2,1)}, bf16[1024,1024]{1,0:T(8,128)(2,1)}, bf16[1024,128]{1,0:T(8,128)(2,1)}, bf16[1024,128]{1,0:T(8,128)(2,1)}) custom-call(s32[24]{0:T(128)S(1)} %stack.89.place_ref, bf16[528,512]{1,0:T(8,128)(2,1)S(1)} %broadcast_select_fusion.1.refs_0_.refs_4_, bf16[528,512]{1,0:T(8,128)(2,1)S(1)} %copy-done.3, ...), custom_call_target="tpu_custom_call" | custom-call | flops 40000000000 | bytes 16777216 | tf_op jit(solution)/shard_map/factor_panel/pallas_call | solution.py:242
  114.6 0.0 collective-permute-done.22.refs_22_
  114.6 0.0 collective-permute-done.21.refs_21_
  114.6 0.0 collective-permute-done.18.refs_16_
  114.6 0.0 collective-permute-done.20.refs_18_
  114.7 6.9 %collective-permute-done.19.refs_17_ = bf16[1024,512]{1,0:T(8,128)(2,1)S(1)} collective-permute-done((bf16[1024,512]{1,0:T(8,128)(2,1)S(1)}, bf16[1024,512]{1,0:T(8,128)(2,1)S(1)}, u32[]{:S(2)}, u32[]{:S(2)}) %collective-permute-start.19) | collective-permute-done | bytes 1048608 | tf_op jit(solution)/shard_map/ppermute | solution.py:401
  121.6 21.8 %finish_tile.1 = f32[1024,512]{1,0:T(8,128)} custom-call(s32[70]{0:T(128)S(1)} %stack.86.place_ref, f32[1,512]{1,0:T(1,128)S(1)} %bitcast.31, bf16[1024,1024]{1,0:T(8,128)(2,1)} %get-tuple-element.18.refs_0_, bf16[1024,1024]{1,0:T(8,128)(2,1)} %get-tuple-element.19.refs_1_, bf16[1024,128]{1,0:T(8,128)(2,1)} %get-tuple-element.20.refs_2_, ...), custom_call_target="tpu_custom_call" | custom-call | flops 20000000000 | bytes 25165824 | tf_op jit(solution)/shard_map/finish_tile/pallas_call | solution.py:361
  (18 shorter events, 0.1 us)
Async XLA Ops:
  0.0 4.0 %copy-start = (bf16[512,512]{1,0:T(8,128)(2,1)S(1)}, bf16[512,512]{1,0:T(8,128)(2,1)}, u32[]{:S(2)}) copy-start(bf16[512,512]{1,0:T(8,128)(2,1)} %refs_19_.1) | copy-start | bytes 1572868
  0.0 4.0 %collective-permute-start.2 = (bf16[512,512]{1,0:T(8,128)(2,1)}, bf16[512,512]{1,0:T(8,128)(2,1)S(1)}, u32[]{:S(2)}, u32[]{:S(2)}) collective-permute-start(bf16[512,512]{1,0:T(8,128)(2,1)} %refs_19_.1), channel_id=1, source_target_pairs={{6,0},{7,1},{14,8},{15,9},{22,16},{23,17},{30,24},{31,25}} | collective-permute-start | bytes 1572872 | tf_op jit(solution)/shard_map/ppermute | solution.py:401
  2.6 15.9 %collective-permute-start = (bf16[528,512]{1,0:T(8,128)(2,1)S(1)}, bf16[528,512]{1,0:T(8,128)(2,1)S(1)}, u32[]{:S(2)}, u32[]{:S(2)}) collective-permute-start(bf16[528,512]{1,0:T(8,128)(2,1)S(1)} %pad_maximum_fusion), channel_id=1, source_target_pairs={{0,4},{1,5},{8,12},{9,13},{16,20},{17,21},{24,28},{25,29}} | collective-permute-start | bytes 1622024 | tf_op jit(solution)/shard_map/ppermute | solution.py:401
  4.8 22.0 %collective-permute-start.4 = (bf16[256,512]{1,0:T(8,128)(2,1)S(1)}, bf16[256,512]{1,0:T(8,128)(2,1)}, u32[]{:S(2)}, u32[]{:S(2)}) collective-permute-start(bf16[256,512]{1,0:T(8,128)(2,1)S(1)} %get-tuple-element.25), channel_id=1, source_target_pairs={{0,8},{1,24},{2,10},{3,26},{4,12},{5,28},{6,14},{7,30},{8,0},{9,16... | collective-permute-start | bytes 786440 | tf_op jit(solution)/shard_map/ppermute | solution.py:401
  5.5 19.3 %collective-permute-start.3 = (bf16[256,512]{1,0:T(8,128)(2,1)}, bf16[256,512]{1,0:T(8,128)(2,1)S(1)}, u32[]{:S(2)}, u32[]{:S(2)}) collective-permute-start(bf16[256,512]{1,0:T(8,128)(2,1)} %get-tuple-element.26), channel_id=1, source_target_pairs={{0,0},{1,16},{2,2},{3,18},{4,4},{5,20},{6,6},{7,22},{8,8},{9,24},{... | collective-permute-start | bytes 786440 | tf_op jit(solution)/shard_map/ppermute | solution.py:401
  18.7 18.2 %collective-permute-start.1 = (bf16[528,512]{1,0:T(8,128)(2,1)S(1)}, bf16[528,512]{1,0:T(8,128)(2,1)}, u32[]{:S(2)}, u32[]{:S(2)}) collective-permute-start(bf16[528,512]{1,0:T(8,128)(2,1)S(1)} %broadcast_select_fusion), channel_id=1, source_target_pairs={{0,2},{1,3},{4,6},{5,7},{8,10},{9,11},{12,14},{13,15},{16,18},{17,... | collective-permute-start | bytes 1622024 | tf_op jit(solution)/shard_map/ppermute | solution.py:401
  20.8 10.7 %collective-permute-start.5 = (bf16[256,512]{1,0:T(8,128)(2,1)}, bf16[256,512]{1,0:T(8,128)(2,1)S(1)}, u32[]{:S(2)}, u32[]{:S(2)}) collective-permute-start(bf16[256,512]{1,0:T(8,128)(2,1)} %get-tuple-element.26), channel_id=1, source_target_pairs={{0,1},{1,17},{2,3},{3,19},{4,5},{5,21},{6,7},{7,23},{8,9},{9,25},{... | collective-permute-start | bytes 786440 | tf_op jit(solution)/shard_map/ppermute | solution.py:401
  24.8 12.2 %collective-permute-start.7 = (bf16[512,512]{1,0:T(8,128)(2,1)S(1)}, bf16[512,512]{1,0:T(8,128)(2,1)S(1)}, u32[]{:S(2)}, u32[]{:S(2)}) collective-permute-start(bf16[512,512]{1,0:T(8,128)(2,1)S(1)} %copy-done), channel_id=1, source_target_pairs={{0,8},{1,9},{2,10},{3,11},{4,12},{5,13},{6,14},{7,15},{8,0},{9,1},... | collective-permute-start | bytes 1572872 | tf_op jit(solution)/shard_map/ppermute | solution.py:401
  24.8 0.7 copy-start.7
  25.5 11.4 %collective-permute-start.6 = (bf16[256,512]{1,0:T(8,128)(2,1)S(1)}, bf16[256,512]{1,0:T(8,128)(2,1)S(1)}, u32[]{:S(2)}, u32[]{:S(2)}) collective-permute-start(bf16[256,512]{1,0:T(8,128)(2,1)S(1)} %get-tuple-element.25), channel_id=1, source_target_pairs={{0,9},{1,25},{2,11},{3,27},{4,13},{5,29},{6,15},{7,31},{8,1},{9,17... | collective-permute-start | bytes 786440 | tf_op jit(solution)/shard_map/ppermute | solution.py:401
  37.0 0.8 copy-start.5
  37.8 14.5 %collective-permute-start.11 = (bf16[528,512]{1,0:T(8,128)(2,1)S(1)}, bf16[528,512]{1,0:T(8,128)(2,1)S(1)}, u32[]{:S(2)}, u32[]{:S(2)}) collective-permute-start(bf16[528,512]{1,0:T(8,128)(2,1)S(1)} %broadcast_select_fusion.1.refs_0_.refs_4_), channel_id=1, source_target_pairs={{0,1},{1,0},{2,3},{3,2},{4,5},{5,4},{6,7},{7,6},{8,9},{9,8},{10,11... | collective-permute-start | bytes 1622024 | tf_op jit(solution)/shard_map/ppermute | solution.py:401
  39.8 12.4 %collective-permute-start.8 = (bf16[528,512]{1,0:T(8,128)(2,1)S(1)}, bf16[528,512]{1,0:T(8,128)(2,1)S(1)}, u32[]{:S(2)}, u32[]{:S(2)}) collective-permute-start(bf16[528,512]{1,0:T(8,128)(2,1)S(1)} %broadcast_select_fusion.1.refs_0_.refs_4_), channel_id=1, source_target_pairs={{0,8},{1,9},{2,10},{3,11},{4,12},{5,13},{6,14},{7,15},{8,0},{9,1},... | collective-permute-start | bytes 1622024 | tf_op jit(solution)/shard_map/ppermute | solution.py:401
  40.5 15.1 %collective-permute-start.9 = (bf16[528,512]{1,0:T(8,128)(2,1)S(1)}, bf16[528,512]{1,0:T(8,128)(2,1)S(1)}, u32[]{:S(2)}, u32[]{:S(2)}) collective-permute-start(bf16[528,512]{1,0:T(8,128)(2,1)S(1)} %broadcast_select_fusion.1.refs_0_.refs_4_), channel_id=1, source_target_pairs={{0,16},{1,17},{2,18},{3,19},{4,20},{5,21},{6,22},{7,23},{8,24},{9,... | collective-permute-start | bytes 1622024 | tf_op jit(solution)/shard_map/ppermute | solution.py:401
  40.5 30.0 %collective-permute-start.17 = (bf16[1024,512]{1,0:T(8,128)(2,1)S(1)}, bf16[1024,512]{1,0:T(8,128)(2,1)}, u32[]{:S(2)}, u32[]{:S(2)}) collective-permute-start(bf16[1024,512]{1,0:T(8,128)(2,1)S(1)} %constant_dynamic-update-slice_fusion.refs_14_), channel_id=1, source_target_pairs={{2,0},{3,1},{4,2},{5,3},{6,4},{7,5},{10,8},{11,9},{12,10},{13,11},... | collective-permute-start | bytes 3145736 | tf_op jit(solution)/shard_map/ppermute | solution.py:401
  52.2 0.8 copy-start.2
  53.1 7.5 %collective-permute-start.15 = (bf16[272,512]{1,0:T(8,128)(2,1)S(1)}, bf16[272,512]{1,0:T(8,128)(2,1)S(1)}, u32[]{:S(2)}, u32[]{:S(2)}) collective-permute-start(bf16[272,512]{1,0:T(8,128)(2,1)S(1)} %slice.7), channel_id=1, source_target_pairs={{0,16},{1,17},{2,18},{3,19},{4,20},{5,21},{6,22},{7,23},{8,24},{9,... | collective-permute-start | bytes 835592 | tf_op jit(solution)/shard_map/ppermute | solution.py:401
  54.2 18.4 %collective-permute-start.12 = (bf16[528,512]{1,0:T(8,128)(2,1)S(1)}, bf16[528,512]{1,0:T(8,128)(2,1)}, u32[]{:S(2)}, u32[]{:S(2)}) collective-permute-start(bf16[528,512]{1,0:T(8,128)(2,1)S(1)} %collective-permute-done.11.refs_4_.refs_8_), channel_id=1, source_target_pairs={{0,8},{1,9},{2,10},{3,11},{4,12},{5,13},{6,14},{7,15},{8,0},{9,1},... | collective-permute-start | bytes 1622024 | tf_op jit(solution)/shard_map/ppermute | solution.py:401
  55.7 17.7 %collective-permute-start.10 = (bf16[528,512]{1,0:T(8,128)(2,1)S(1)}, bf16[528,512]{1,0:T(8,128)(2,1)}, u32[]{:S(2)}, u32[]{:S(2)}) collective-permute-start(bf16[528,512]{1,0:T(8,128)(2,1)S(1)} %collective-permute-done.9.refs_2_.refs_6_), channel_id=1, source_target_pairs={{0,8},{1,9},{2,10},{3,11},{4,12},{5,13},{6,14},{7,15},{8,0},{9,1},... | collective-permute-start | bytes 1622024 | tf_op jit(solution)/shard_map/ppermute | solution.py:401
  55.7 7.5 %collective-permute-start.13 = (bf16[256,512]{1,0:T(8,128)(2,1)S(1)}, bf16[256,512]{1,0:T(8,128)(2,1)}, u32[]{:S(2)}, u32[]{:S(2)}) collective-permute-start(bf16[256,512]{1,0:T(8,128)(2,1)S(1)} %slice.6), channel_id=1, source_target_pairs={{0,1},{1,0},{2,3},{3,2},{4,5},{5,4},{6,7},{7,6},{8,9},{9,8},{10,11... | collective-permute-start | bytes 786440 | tf_op jit(solution)/shard_map/ppermute | solution.py:401
  60.6 14.7 %collective-permute-start.16 = (bf16[272,512]{1,0:T(8,128)(2,1)S(1)}, bf16[272,512]{1,0:T(8,128)(2,1)}, u32[]{:S(2)}, u32[]{:S(2)}) collective-permute-start(bf16[272,512]{1,0:T(8,128)(2,1)S(1)} %collective-permute-done.15.refs_8_.refs_12_), channel_id=1, source_target_pairs={{0,8},{1,9},{2,10},{3,11},{4,12},{5,13},{6,14},{7,15},{8,0},{9,1},... | collective-permute-start | bytes 835592 | tf_op jit(solution)/shard_map/ppermute | solution.py:401
  63.2 9.1 %collective-permute-start.14 = (bf16[256,512]{1,0:T(8,128)(2,1)}, bf16[256,512]{1,0:T(8,128)(2,1)}, u32[]{:S(2)}, u32[]{:S(2)}) collective-permute-start(bf16[256,512]{1,0:T(8,128)(2,1)} %collective-permute-done.13.refs_6_.refs_10_), channel_id=1, source_target_pairs={{0,8},{1,9},{2,10},{3,11},{4,12},{5,13},{6,14},{7,15},{8,0},{9,1},... | collective-permute-start | bytes 786440 | tf_op jit(solution)/shard_map/ppermute | solution.py:401
  64.9 56.7 %copy-start.1 = (f32[512]{0:T(512)S(1)}, f32[512]{0:T(512)}, u32[]{:S(2)}) copy-start(f32[512]{0:T(512)} %param.3) | copy-start | bytes 6148
  70.5 44.1 %collective-permute-start.22 = (bf16[512,512]{1,0:T(8,128)(2,1)S(1)}, bf16[512,512]{1,0:T(8,128)(2,1)S(1)}, u32[]{:S(2)}, u32[]{:S(2)}) collective-permute-start(bf16[512,512]{1,0:T(8,128)(2,1)S(1)} %copy-done), channel_id=1, source_target_pairs={{0,24},{1,25},{2,26},{3,27},{4,28},{5,29},{6,30},{7,31},{8,16},{9,... | collective-permute-start | bytes 1572872 | tf_op jit(solution)/shard_map/ppermute | solution.py:401
  72.4 42.3 %collective-permute-start.21 = (bf16[512,512]{1,0:T(8,128)(2,1)S(1)}, bf16[512,512]{1,0:T(8,128)(2,1)S(1)}, u32[]{:S(2)}, u32[]{:S(2)}) collective-permute-start(bf16[512,512]{1,0:T(8,128)(2,1)S(1)} %copy-done), channel_id=1, source_target_pairs={{0,16},{1,17},{2,18},{3,19},{4,20},{5,21},{6,22},{7,23},{8,24},{9,... | collective-permute-start | bytes 1572872 | tf_op jit(solution)/shard_map/ppermute | solution.py:401
  72.7 42.0 %collective-permute-start.20 = (bf16[1024,512]{1,0:T(8,128)(2,1)S(1)}, bf16[1024,512]{1,0:T(8,128)(2,1)S(1)}, u32[]{:S(2)}, u32[]{:S(2)}) collective-permute-start(bf16[1024,512]{1,0:T(8,128)(2,1)S(1)} %constant_dynamic-update-slice_fusion.refs_14_), channel_id=1, source_target_pairs={{2,6},{3,7},{10,14},{11,15},{18,22},{19,23},{26,30},{27,31}} | collective-permute-start | bytes 3145736 | tf_op jit(solution)/shard_map/ppermute | solution.py:401
  73.4 48.2 %collective-permute-start.19 = (bf16[1024,512]{1,0:T(8,128)(2,1)S(1)}, bf16[1024,512]{1,0:T(8,128)(2,1)S(1)}, u32[]{:S(2)}, u32[]{:S(2)}) collective-permute-start(bf16[1024,512]{1,0:T(8,128)(2,1)S(1)} %constant_dynamic-update-slice_fusion.refs_14_), channel_id=1, source_target_pairs={{2,4},{3,5},{4,6},{5,7},{10,12},{11,13},{12,14},{13,15},{18,20},{1... | collective-permute-start | bytes 3145736 | tf_op jit(solution)/shard_map/ppermute | solution.py:401
  75.3 39.3 %collective-permute-start.18 = (bf16[1024,512]{1,0:T(8,128)(2,1)}, bf16[1024,512]{1,0:T(8,128)(2,1)S(1)}, u32[]{:S(2)}, u32[]{:S(2)}) collective-permute-start(bf16[1024,512]{1,0:T(8,128)(2,1)} %collective-permute-done.17.refs_15_), channel_id=1, source_target_pairs={{2,0},{3,1},{4,2},{5,3},{10,8},{11,9},{12,10},{13,11},{18,16},{19,... | collective-permute-start | bytes 3145736 | tf_op jit(solution)/shard_map/ppermute | solution.py:401
  79.1 1.1 copy-start.3
  80.1 41.4 %copy-start.4 = (bf16[528,512]{1,0:T(8,128)(2,1)S(1)}, bf16[528,512]{1,0:T(8,128)(2,1)}, u32[]{:S(2)}) copy-start(bf16[528,512]{1,0:T(8,128)(2,1)} %copy-done.2) | copy-start | bytes 1622020
  80.2 41.4 %copy-start.6 = (bf16[512,512]{1,0:T(8,128)(2,1)S(1)}, bf16[512,512]{1,0:T(8,128)(2,1)}, u32[]{:S(2)}) copy-start(bf16[512,512]{1,0:T(8,128)(2,1)} %copy-done.5) | copy-start | bytes 1572868

commit v6 on v5

--- a/solution.py
+++ b/solution.py
@@ -248,19 +248,18 @@
         scratch_shapes=[VMEM(*one) for one in outs + held]
         + [pltpu.SemaphoreType.DMA((len(views),)), pltpu.SemaphoreType.DMA((len(outs), NBLOCKS))],
         compiler_params=pltpu.CompilerParams(vmem_limit_bytes=room(*outs, *held)),
-        cost_estimate=pl.CostEstimate(flops=4 * 10**10, bytes_accessed=16 * 2**20, transcendentals=1024),
+        cost_estimate=pl.CostEstimate(flops=8 * 10**9, bytes_accessed=2**20, transcendentals=1024),
         name="factor_panel",
     )(place, *pieces)
 
 
-def tile_kernel(counts, views, place_ref, regular_ref, *refs):
+def tile_kernel(total, counts, views, place_ref, regular_ref, *refs):
     factors, refs = refs[:4], refs[4:]
-    pieces, refs = refs[: sum(counts)], refs[sum(counts) :]
+    pieces, refs = refs[:total], refs[total:]
     out_ref, refs = refs[0], refs[1:]
     high_ref, low_ref, inv_high_ref, inv_low_ref, left_high_ref, left_low_ref, wide_high_ref, wide_low_ref = refs[:8]
     panel_ref, rows_ref, cols_ref, sem, factor_sem = refs[8:]
-    targets = [panel_ref] * counts[0] + [rows_ref] * counts[1] + [cols_ref] * counts[2]
-    held = [targets[which] for which, *_ in views]
+    held = [ref for ref, count in zip((panel_ref, rows_ref, cols_ref), counts) for _ in range(count)]
     views = [pieces[which].at[pl.ds(start, rows)] for which, start, rows in views]
     fetches = [
         pltpu.make_async_copy(factor, ref, factor_sem.at[i])
@@ -342,7 +341,7 @@
             )
 
 
-def finish_tile(place, regular, factors, panel, rows, cols, views, band, users):
+def finish_tile(place, regular, factors, panel, rows, cols, counts, views, band, users):
     spec = pl.BlockSpec(memory_space=VMEM)
     width = regular.shape[1]
     factors = [pltpu.with_memory_space_constraint(x, pltpu.HBM) for x in factors]
@@ -359,7 +358,7 @@
         ((width, users), bf16),
     ]
     return pl.pallas_call(
-        functools.partial(tile_kernel, (len(panel), len(rows), len(cols)), views),
+        functools.partial(tile_kernel, len(pieces), counts, views),
         out_shape=jax.ShapeDtypeStruct(*out),
         in_specs=[pl.BlockSpec(memory_space=pltpu.SMEM)]
         + [spec]
@@ -408,9 +407,23 @@
     parts = jnp.stack([high, middle, regular - high - middle]).astype(bf16)
     parts = jnp.pad(parts, ((0, PARTS - 3), (0, users - width)))
 
-    raised = exchange(interactions, lambda p, h, s, w: (p, h, 0, w), lambda p, h, s, w: s == SPAN - 1)
-    halves = (jnp.where(slot == 0, raised, interactions) if ways == 2 else interactions).reshape(CORES, band, users)
-    offers = [lax.dynamic_index_in_dim(halves, core ^ flip, 0, False) for flip in range(CORES)]
+    def over_core(value, only=None):
+        return exchange(value, lambda p, h, s, w: (p, 1 - h, s, w), only)
+
+    def over_pair(value):
+        return exchange(value, lambda p, h, s, w: (1 - p, h, s, w))
+
+    def over_way(value):
+        return exchange(value, lambda p, h, s, w: (p, h, s, 1 - w))
+
+    def traded(items, only):
+        halves = items.reshape(CORES, band, users)
+        kept, given = (lax.dynamic_index_in_dim(halves, core ^ flip, 0, False) for flip in range(CORES))
+        return jnp.concatenate([kept, over_core(given, only)], 0)
+
+    paired = traded(interactions, lambda p, h, s, w: s > 0)
+    if ways == 2:
+        raised = exchange(interactions, lambda p, h, s, w: (p, h, 0, w), lambda p, h, s, w: s == SPAN - 1)
 
     half = width // 2
     shared = jnp.concatenate([interactions, parts], 0)
@@ -422,11 +435,14 @@
         )
         if reach == SPAN // 2:
             for turn in range(ways):
-                for flip in range(CORES):
-                    quarters.append(
-                        exchange(offers[flip], lambda p, h, s, w: (w, h ^ flip, s, (p + turn) % ways))
+                quarters.append(
+                    exchange(
+                        paired, lambda p, h, s, w: (w, h, s, (p + turn) % ways), lambda p, h, s, w: s > 0
                     )
-                    quarter_users.append(((way - turn) % ways * CORES + (core ^ flip)) * users)
+                )
+                quarter_users += [((way - turn) % ways * CORES + (core ^ flip)) * users for flip in range(CORES)]
+            if ways == 2:
+                got = after(got, raised)
         shared = jnp.where(slot % (2 * reach) == reach, got, shared)
         reach //= 2
     quarters = jnp.concatenate(quarters, 0)
@@ -438,21 +454,13 @@
     cols, cols_place = [interactions], [0, row_index * users]
     rows, rows_views, rows_place = [], [], []
 
-    def over_core(value):
-        return exchange(value, lambda p, h, s, w: (p, 1 - h, s, w))
-
-    def over_pair(value):
-        return exchange(value, lambda p, h, s, w: (1 - p, h, s, w))
-
-    def over_way(value, only=None):
-        return exchange(value, lambda p, h, s, w: (p, h, s, 1 - w), only)
-
     if ways == 2:
         twin_items = over_core(interactions)
-        shared = after(shared, quarters, twin_items)
+        mixed = jnp.where(slot == 0, traded(raised, lambda p, h, s, w: s == 0), interactions)
+        shared = after(shared, quarters, twin_items, mixed)
         pair_side, way_side = over_pair(shared), over_way(shared)
-        own_twin = over_core(shared)
-        diagonal = [over_way(after(pair_side, own_twin)[:half]), over_pair(after(way_side, own_twin)[half:])]
+        own_twin, way_twin = over_core(shared), over_core(way_side)
+        diagonal = [over_way(after(pair_side, own_twin, way_twin)[:half]), over_pair(after(way_side, own_twin)[half:])]
         for from_pair, from_way, first_row, piece in (
             (pair, way, 0, shared),
             (1 - pair, way, 0, pair_side),
@@ -460,7 +468,7 @@
             (1 - pair, 1 - way, 0, diagonal[0]),
             (1 - pair, 1 - way, half, diagonal[1]),
         ):
-            twin = own_twin if piece is shared else over_core(piece)
+            twin = own_twin if piece is shared else way_twin if piece is way_side else over_core(piece)
             for from_core, value in ((core, piece), (1 - core, twin)):
                 if value is shared or value is way_side:
                     part_views.append((len(panel), width, PARTS, True))
@@ -470,26 +478,36 @@
                 panel_place += [from_way * width + first_row, (from_pair * CORES + from_core) * users]
                 panel.append(value)
         crossed = [pair_side, way_side, *diagonal]
-        held = after(interactions, *crossed)
-        cols += [twin_items, over_pair(held), exchange(held, lambda p, h, s, w: (1 - p, 1 - h, s, w))]
-        cols_place += [0, (row_index ^ 1) * users, 0, (row_index ^ 2) * users, 0, (row_index ^ 3) * users]
-        first = exchange(quarters, lambda p, h, s, w: (p, h, s - 1, w), lambda p, h, s, w: s > 0)
-        relayed, ready = lax.optimization_barrier((first, quarters, *crossed))[:2]
-        second = exchange(relayed, lambda p, h, s, w: (p, h, s - 1, w), lambda p, h, s, w: 0 < s < SPAN - 1)
-        ring = exchange(ready, lambda p, h, s, w: (p, h, s + 1, w), lambda p, h, s, w: 0 < s < SPAN - 1)
-        leap = exchange(ready, lambda p, h, s, w: (p, h, s + 2, w), lambda p, h, s, w: s == 1)
-        rows = [quarters, first, second, ring, leap]
+        down = exchange(quarters, lambda p, h, s, w: (p, h, s - 1, w), lambda p, h, s, w: s > 0)
+        up = exchange(quarters, lambda p, h, s, w: (p, h, s + 1, w), lambda p, h, s, w: 0 < s < SPAN - 1)
+        down_held, up_held, mixed = lax.optimization_barrier(
+            (down, up, mixed, *crossed)
+        )[:3]
+        down_again = exchange(down_held, lambda p, h, s, w: (p, h, s - 1, w), lambda p, h, s, w: 0 < s < SPAN - 1)
+        up_again = exchange(up_held, lambda p, h, s, w: (p, h, s + 1, w), lambda p, h, s, w: s == 2)
+        rows = [quarters, down, down_again, up, up_again]
         from_slots = [
-            jnp.where(slot == 0, 3, slot),
+            slot,
             jnp.where(slot < 3, slot + 1, 0),
             jnp.where(slot < 2, slot + 2, 0),
             jnp.where(slot > 1, slot - 1, 0),
             jnp.where(slot == 3, 1, 0),
         ]
+        cols += [twin_items]
+        cols_place += [0, (row_index ^ 1) * users]
+        for turn in range(ways):
+            mix = exchange(
+                mixed, lambda p, h, s, w: (w, h, s, (p + turn) % ways) if s == 0 else (1 - p, h ^ turn, s, w)
+            )
+            cols.append(mix)
+            cols_place += [jnp.where(slot == 0, -1, 0), (row_index ^ (CORES + turn)) * users]
         for from_slot, piece in enumerate(rows):
             for which, from_users in enumerate(quarter_users):
                 rows_views.append((from_slot, which * band, band))
                 rows_place += [(from_slots[from_slot] - 1) * band, from_users]
+        for which, from_users in enumerate(quarter_users):
+            rows_views.append((len(rows) + 2 + which // CORES, which % CORES * band, band))
+            rows_place += [jnp.where(slot == 0, (SPAN - 2) * band, -1), from_users]
     else:
         groups = [[s * ways + w for w in range(ways)] for s in range(SPAN)]
         shared = lax.all_gather(shared, "col", axis=0, axis_index_groups=groups)
@@ -512,9 +530,10 @@
     views = [view[:3] for view in panel_views]
     views += [(len(panel) + i, start, count) for i, start, count in rows_views]
     views += [(len(panel) + len(rows) + i, 0, width) for i in range(len(cols))]
+    counts = len(panel_views), len(rows_views), len(cols)
     tile = finish_tile(
         numbers([row_index, col_index] + panel_place + rows_place + cols_place),
-        regular[None, :], factors, panel, rows, cols, views, band, all_users,
+        regular[None, :], factors, panel, rows, cols, counts, views, band, all_users,
     )
     return tile.reshape(SPAN, band, width)
 

time: 144 us -> 144 us (level)
  waiting for transfers between devices: 48.4 us -> 32.1 us
  starting transfers between devices: 29.9 us -> 43.4 us
  other arithmetic: 2.05 us -> 3.78 us
    ppermute x23, waiting for transfers between devices: 48.4 us -> 32.1 us  [exchange(): return lax.ppermute(value, ('row', 'col'), perm)]
    ppermute x23, starting transfers between devices: 29.9 us -> 43.4 us  [exchange(): return lax.ppermute(value, ('row', 'col'), perm)]
    unnamed x19 -> x21, local copies, waits for them, and re-layouts: 5.32 us -> 5.56 us
where the time goes in v6:
time: 144 us; the launch traced here: 143 us
  Pallas kernels  56.2 us (39%)
  starting transfers between devices  43.4 us (30%)
  waiting for transfers between devices  32.1 us (22%)
  local copies, waits for them, and re-layouts  7.03 us (5%)
  other arithmetic  3.78 us (3%)
    ppermute x23, starting transfers between devices, exchange(): return lax.ppermute(value, ('row', 'col'), perm)  43.4 us
    pallas_call x1, Pallas kernels, factor_panel(): pl.pallas_call(functools.partial(panel_kernel, views, len(pieces), width)...  34.3 us
    ppermute x23, waiting for transfers between devices, exchange(): return lax.ppermute(value, ('row', 'col'), perm)  32.1 us
    pallas_call x1, Pallas kernels, finish_tile(): pl.pallas_call(functools.partial(tile_kernel, len(pieces), counts, views)...  22 us
    unnamed x21, local copies, waits for them, and re-layouts  5.56 us
  transfers between devices with their start and end apart: 23, of which 8 were waited for; matrix products, arithmetic and copies ran while one was open for 4% of the time, Pallas kernels for 24%

profile of v6, /device:TPU:17, one launch (start us, length us, event | category | flops | bytes accessed | tf_op | source)
XLA Modules:
  0.0 143.1 jit_solution(8333427351395963170)
XLA Ops:
  0.0 0.8 collective-permute-start.1
  0.8 0.7 reduce-precision_convert_fusion.1
  1.6 1.1 pad_maximum_fusion
  2.6 1.3 collective-permute-start
  4.0 2.6 %collective-permute-start.3 = (bf16[256,512]{1,0:T(8,128)(2,1)S(1)}, bf16[256,512]{1,0:T(8,128)(2,1)S(1)}, u32[]{:S(2)}, u32[]{:S(2)}) collective-permute-start(bf16[256,512]{1,0:T(8,128)(2,1)S(1)} %get-tuple-element.30), channel_id=1, source_target_pairs={{2,10},{3,11},{4,12},{5,13},{6,14},{7,15},{10,2},{11,3},{12,4},{13... | collective-permute-start | bytes 786440 | tf_op jit(solution)/shard_map/ppermute | solution.py:400
  6.6 1.1 collective-permute-done.3
  7.8 0.8 pad_maximum_fusion.1
  8.6 5.3 %collective-permute-start.4 = (bf16[512,512]{1,0:T(8,128)(2,1)}, bf16[512,512]{1,0:T(8,128)(2,1)}, u32[]{:S(2)}, u32[]{:S(2)}) collective-permute-start(bf16[512,512]{1,0:T(8,128)(2,1)} %pad_maximum_fusion.1), channel_id=1, source_target_pairs={{2,2},{3,18},{4,4},{5,20},{6,6},{7,22},{10,10},{11,26},{12,12},{13... | collective-permute-start | bytes 1572872 | tf_op jit(solution)/shard_map/ppermute | solution.py:400
  13.9 1.9 %collective-permute-start.5 = (bf16[512,512]{1,0:T(8,128)(2,1)}, bf16[512,512]{1,0:T(8,128)(2,1)}, u32[]{:S(2)}, u32[]{:S(2)}) collective-permute-start(bf16[512,512]{1,0:T(8,128)(2,1)} %pad_maximum_fusion.1), channel_id=1, source_target_pairs={{2,3},{3,19},{4,5},{5,21},{6,7},{7,23},{10,11},{11,27},{12,13},{13... | collective-permute-start | bytes 1572872 | tf_op jit(solution)/shard_map/ppermute | solution.py:400
  15.9 0.0 collective-permute-done.1
  15.9 2.7 %collective-permute-done = bf16[528,512]{1,0:T(8,128)(2,1)S(1)} collective-permute-done((bf16[528,512]{1,0:T(8,128)(2,1)S(1)}, bf16[528,512]{1,0:T(8,128)(2,1)S(1)}, u32[]{:S(2)}, u32[]{:S(2)}) %collective-permute-start) | collective-permute-done | bytes 540704 | tf_op jit(solution)/shard_map/ppermute | solution.py:400
  18.6 0.1 broadcast_select_fusion
  18.7 2.1 %collective-permute-start.2 = (bf16[528,512]{1,0:T(8,128)(2,1)S(1)}, bf16[528,512]{1,0:T(8,128)(2,1)}, u32[]{:S(2)}, u32[]{:S(2)}) collective-permute-start(bf16[528,512]{1,0:T(8,128)(2,1)S(1)} %broadcast_select_fusion), channel_id=1, source_target_pairs={{0,2},{1,3},{4,6},{5,7},{8,10},{9,11},{12,14},{13,15},{16,18},{17,... | collective-permute-start | bytes 1622024 | tf_op jit(solution)/shard_map/ppermute | solution.py:400
  20.9 0.7 collective-permute-start.7
  21.5 1.6 %collective-permute-start.6 = (bf16[512,512]{1,0:T(8,128)(2,1)S(1)}, bf16[512,512]{1,0:T(8,128)(2,1)S(1)}, u32[]{:S(2)}, u32[]{:S(2)}) collective-permute-start(bf16[512,512]{1,0:T(8,128)(2,1)S(1)} %copy-done), channel_id=1, source_target_pairs={{0,8},{1,9},{2,10},{3,11},{4,12},{5,13},{6,14},{7,15},{8,0},{9,1},... | collective-permute-start | bytes 1572872 | tf_op jit(solution)/shard_map/ppermute | solution.py:400
  23.2 0.0 collective-permute-done.4
  23.2 1.1 constant_dynamic-update-slice_fusion.1
  24.2 11.9 %collective-permute-done.5 = bf16[512,512]{1,0:T(8,128)(2,1)} collective-permute-done((bf16[512,512]{1,0:T(8,128)(2,1)}, bf16[512,512]{1,0:T(8,128)(2,1)}, u32[]{:S(2)}, u32[]{:S(2)}) %collective-permute-start.5) | collective-permute-done | bytes 524320 | tf_op jit(solution)/shard_map/ppermute | solution.py:400
  36.2 1.1 constant_dynamic-update-slice_fusion.refs_14_
  37.2 0.0 collective-permute-done.7
  37.2 1.0 maximum_select_fusion
  38.2 0.0 collective-permute-done.2
  38.2 0.1 broadcast_select_fusion.1.refs_0_.refs_4_
  38.3 0.0 collective-permute-done.6.refs_20_
  38.3 0.8 copy-done.8
  39.1 1.9 %collective-permute-start.11 = (bf16[528,512]{1,0:T(8,128)(2,1)S(1)}, bf16[528,512]{1,0:T(8,128)(2,1)S(1)}, u32[]{:S(2)}, u32[]{:S(2)}) collective-permute-start(bf16[528,512]{1,0:T(8,128)(2,1)S(1)} %broadcast_select_fusion.1.refs_0_.refs_4_), channel_id=1, source_target_pairs={{0,1},{1,0},{2,3},{3,2},{4,5},{5,4},{6,7},{7,6},{8,9},{9,8},{10,11... | collective-permute-start | bytes 1622024 | tf_op jit(solution)/shard_map/ppermute | solution.py:400
  41.0 5.1 %collective-permute-start.18 = (bf16[1024,512]{1,0:T(8,128)(2,1)S(1)}, bf16[1024,512]{1,0:T(8,128)(2,1)}, u32[]{:S(2)}, u32[]{:S(2)}) collective-permute-start(bf16[1024,512]{1,0:T(8,128)(2,1)S(1)} %constant_dynamic-update-slice_fusion.refs_14_), channel_id=1, source_target_pairs={{2,4},{3,5},{4,6},{5,7},{10,12},{11,13},{12,14},{13,15},{18,20},{1... | collective-permute-start | bytes 3145736 | tf_op jit(solution)/shard_map/ppermute | solution.py:400
  46.1 1.9 %collective-permute-start.17 = (bf16[1024,512]{1,0:T(8,128)(2,1)S(1)}, bf16[1024,512]{1,0:T(8,128)(2,1)}, u32[]{:S(2)}, u32[]{:S(2)}) collective-permute-start(bf16[1024,512]{1,0:T(8,128)(2,1)S(1)} %constant_dynamic-update-slice_fusion.refs_14_), channel_id=1, source_target_pairs={{2,0},{3,1},{4,2},{5,3},{6,4},{7,5},{10,8},{11,9},{12,10},{13,11},... | collective-permute-start | bytes 3145736 | tf_op jit(solution)/shard_map/ppermute | solution.py:400
  48.0 1.1 collective-permute-start.8
  49.1 0.3 collective-permute-start.9
  49.4 3.2 %collective-permute-done.11.refs_4_.refs_8_ = bf16[528,512]{1,0:T(8,128)(2,1)S(1)} collective-permute-done((bf16[528,512]{1,0:T(8,128)(2,1)S(1)}, bf16[528,512]{1,0:T(8,128)(2,1)S(1)}, u32[]{:S(2)}, u32[]{:S(2)}) %collective-permute-start.11) | collective-permute-done | bytes 540704 | tf_op jit(solution)/shard_map/ppermute | solution.py:400
  52.6 1.6 %collective-permute-start.12 = (bf16[528,512]{1,0:T(8,128)(2,1)S(1)}, bf16[528,512]{1,0:T(8,128)(2,1)S(1)}, u32[]{:S(2)}, u32[]{:S(2)}) collective-permute-start(bf16[528,512]{1,0:T(8,128)(2,1)S(1)} %collective-permute-done.11.refs_4_.refs_8_), channel_id=1, source_target_pairs={{0,8},{1,9},{2,10},{3,11},{4,12},{5,13},{6,14},{7,15},{8,0},{9,1},... | collective-permute-start | bytes 1622024 | tf_op jit(solution)/shard_map/ppermute | solution.py:400
  54.2 0.0 collective-permute-done.8.refs_1_.refs_5_
  54.2 0.8 copy-done.2
  55.0 1.5 %collective-permute-start.15 = (bf16[272,512]{1,0:T(8,128)(2,1)S(1)}, bf16[272,512]{1,0:T(8,128)(2,1)S(1)}, u32[]{:S(2)}, u32[]{:S(2)}) collective-permute-start(bf16[272,512]{1,0:T(8,128)(2,1)S(1)} %slice.7), channel_id=1, source_target_pairs={{0,16},{1,17},{2,18},{3,19},{4,20},{5,21},{6,22},{7,23},{8,24},{9,... | collective-permute-start | bytes 835592 | tf_op jit(solution)/shard_map/ppermute | solution.py:400
  56.5 6.5 %collective-permute-done.9.refs_2_.refs_6_ = bf16[528,512]{1,0:T(8,128)(2,1)S(1)} collective-permute-done((bf16[528,512]{1,0:T(8,128)(2,1)S(1)}, bf16[528,512]{1,0:T(8,128)(2,1)S(1)}, u32[]{:S(2)}, u32[]{:S(2)}) %collective-permute-start.9) | collective-permute-done | bytes 540704 | tf_op jit(solution)/shard_map/ppermute | solution.py:400
  63.0 0.0 collective-permute-done.12.refs_5_.refs_9_
  63.1 0.8 copy-done.5
  63.9 0.4 collective-permute-start.13
  64.3 1.5 %collective-permute-start.10 = (bf16[528,512]{1,0:T(8,128)(2,1)S(1)}, bf16[528,512]{1,0:T(8,128)(2,1)}, u32[]{:S(2)}, u32[]{:S(2)}) collective-permute-start(bf16[528,512]{1,0:T(8,128)(2,1)S(1)} %collective-permute-done.9.refs_2_.refs_6_), channel_id=1, source_target_pairs={{0,8},{1,9},{2,10},{3,11},{4,12},{5,13},{6,14},{7,15},{8,0},{9,1},... | collective-permute-start | bytes 1622024 | tf_op jit(solution)/shard_map/ppermute | solution.py:400
  65.7 2.0 %collective-permute-done.18.refs_17_ = bf16[1024,512]{1,0:T(8,128)(2,1)} collective-permute-done((bf16[1024,512]{1,0:T(8,128)(2,1)S(1)}, bf16[1024,512]{1,0:T(8,128)(2,1)}, u32[]{:S(2)}, u32[]{:S(2)}) %collective-permute-start.18) | collective-permute-done | bytes 1048608 | tf_op jit(solution)/shard_map/ppermute | solution.py:400
  67.8 3.9 %collective-permute-done.17.refs_15_ = bf16[1024,512]{1,0:T(8,128)(2,1)} collective-permute-done((bf16[1024,512]{1,0:T(8,128)(2,1)S(1)}, bf16[1024,512]{1,0:T(8,128)(2,1)}, u32[]{:S(2)}, u32[]{:S(2)}) %collective-permute-start.17) | collective-permute-done | bytes 1048608 | tf_op jit(solution)/shard_map/ppermute | solution.py:400
  71.7 0.0 collective-permute-done.15.refs_8_.refs_12_
  71.7 0.0 collective-permute-done.13.refs_6_.refs_10_
  71.7 3.2 %collective-permute-start.19 = (bf16[1024,512]{1,0:T(8,128)(2,1)}, bf16[1024,512]{1,0:T(8,128)(2,1)}, u32[]{:S(2)}, u32[]{:S(2)}) collective-permute-start(bf16[1024,512]{1,0:T(8,128)(2,1)} %collective-permute-done.17.refs_15_), channel_id=1, source_target_pairs={{2,0},{3,1},{4,2},{5,3},{10,8},{11,9},{12,10},{13,11},{18,16},{19,... | collective-permute-start | bytes 3145736 | tf_op jit(solution)/shard_map/ppermute | solution.py:400
  74.9 3.3 %collective-permute-start.20 = (bf16[1024,512]{1,0:T(8,128)(2,1)}, bf16[1024,512]{1,0:T(8,128)(2,1)}, u32[]{:S(2)}, u32[]{:S(2)}) collective-permute-start(bf16[1024,512]{1,0:T(8,128)(2,1)} %collective-permute-done.18.refs_17_), channel_id=1, source_target_pairs={{4,6},{5,7},{12,14},{13,15},{20,22},{21,23},{28,30},{29,31}} | collective-permute-start | bytes 3145736 | tf_op jit(solution)/shard_map/ppermute | solution.py:400
  78.1 2.3 %collective-permute-start.16 = (bf16[272,512]{1,0:T(8,128)(2,1)S(1)}, bf16[272,512]{1,0:T(8,128)(2,1)}, u32[]{:S(2)}, u32[]{:S(2)}) collective-permute-start(bf16[272,512]{1,0:T(8,128)(2,1)S(1)} %collective-permute-done.15.refs_8_.refs_12_), channel_id=1, source_target_pairs={{0,8},{1,9},{2,10},{3,11},{4,12},{5,13},{6,14},{7,15},{8,0},{9,1},... | collective-permute-start | bytes 835592 | tf_op jit(solution)/shard_map/ppermute | solution.py:400
  80.4 0.0 collective-permute-start.14
  80.4 0.1 stack.95.place_ref
  80.5 0.2 stack.92.place_ref
  80.7 0.0 copy-start.1
  80.7 0.0 collective-permute-done.10.refs_3_.refs_7_
  80.7 0.7 collective-permute-start.22
  81.4 0.7 collective-permute-done.16.refs_9_.refs_13_
  82.1 2.4 %collective-permute-start.21 = (bf16[512,512]{1,0:T(8,128)(2,1)}, bf16[512,512]{1,0:T(8,128)(2,1)S(1)}, u32[]{:S(2)}, u32[]{:S(2)}) collective-permute-start(bf16[512,512]{1,0:T(8,128)(2,1)} %maximum_select_fusion), channel_id=1, source_target_pairs={{0,0},{1,16},{2,18},{3,19},{4,20},{5,21},{6,22},{7,23},{8,8},{9,24... | collective-permute-start | bytes 1572872 | tf_op jit(solution)/shard_map/ppermute | solution.py:400
  84.5 0.0 collective-permute-done.14.refs_7_.refs_11_
  84.5 0.0 copy-start.3
  84.5 1.0 copy-done.3
  85.6 1.0 copy-done.6
  86.6 34.3 %factor_panel.1 = (bf16[1024,1024]{1,0:T(8,128)(2,1)}, bf16[1024,1024]{1,0:T(8,128)(2,1)}, bf16[1024,128]{1,0:T(8,128)(2,1)}, bf16[1024,128]{1,0:T(8,128)(2,1)}) custom-call(s32[24]{0:T(128)S(1)} %stack.95.place_ref, bf16[528,512]{1,0:T(8,128)(2,1)S(1)} %broadcast_select_fusion.1.refs_0_.refs_4_, bf16[528,512]{1,0:T(8,128)(2,1)S(1)} %copy-done.3, ...), custom_call_target="tpu_custom_call" | custom-call | flops 8000000000 | bytes 1048576 | tf_op jit(solution)/shard_map/factor_panel/pallas_call | solution.py:242
  120.9 0.0 collective-permute-done.22.refs_22_
  120.9 0.0 collective-permute-done.21.refs_21_
  121.0 0.0 collective-permute-done.19.refs_16_
  121.0 22.0 %finish_tile.1 = f32[1024,512]{1,0:T(8,128)} custom-call(s32[78]{0:T(128)S(1)} %stack.92.place_ref, f32[1,512]{1,0:T(1,128)S(1)} %bitcast.39, bf16[1024,1024]{1,0:T(8,128)(2,1)} %get-tuple-element.20.refs_0_, bf16[1024,1024]{1,0:T(8,128)(2,1)} %get-tuple-element.21.refs_1_, bf16[1024,128]{1,0:T(8,128)(2,1)} %get-tuple-element.22.refs_2_, ...), custom_call_target="tpu_custom_call" | custom-call | flops 20000000000 | bytes 25165824 | tf_op jit(solution)/shard_map/finish_tile/pallas_call | solution.py:360
  (22 shorter events, 0.2 us)
Async XLA Ops:
  0.0 4.0 %copy-start = (bf16[512,512]{1,0:T(8,128)(2,1)S(1)}, bf16[512,512]{1,0:T(8,128)(2,1)}, u32[]{:S(2)}) copy-start(bf16[512,512]{1,0:T(8,128)(2,1)} %refs_19_.1) | copy-start | bytes 1572868
  0.0 15.9 %collective-permute-start.1 = (bf16[512,512]{1,0:T(8,128)(2,1)}, bf16[512,512]{1,0:T(8,128)(2,1)S(1)}, u32[]{:S(2)}, u32[]{:S(2)}) collective-permute-start(bf16[512,512]{1,0:T(8,128)(2,1)} %refs_19_.1), channel_id=1, source_target_pairs={{6,0},{7,1},{14,8},{15,9},{22,16},{23,17},{30,24},{31,25}} | collective-permute-start | bytes 1572872 | tf_op jit(solution)/shard_map/ppermute | solution.py:400
  2.6 15.9 %collective-permute-start = (bf16[528,512]{1,0:T(8,128)(2,1)S(1)}, bf16[528,512]{1,0:T(8,128)(2,1)S(1)}, u32[]{:S(2)}, u32[]{:S(2)}) collective-permute-start(bf16[528,512]{1,0:T(8,128)(2,1)S(1)} %pad_maximum_fusion), channel_id=1, source_target_pairs={{0,4},{1,5},{8,12},{9,13},{16,20},{17,21},{24,28},{25,29}} | collective-permute-start | bytes 1622024 | tf_op jit(solution)/shard_map/ppermute | solution.py:400
  4.0 3.7 %collective-permute-start.3 = (bf16[256,512]{1,0:T(8,128)(2,1)S(1)}, bf16[256,512]{1,0:T(8,128)(2,1)S(1)}, u32[]{:S(2)}, u32[]{:S(2)}) collective-permute-start(bf16[256,512]{1,0:T(8,128)(2,1)S(1)} %get-tuple-element.30), channel_id=1, source_target_pairs={{2,10},{3,11},{4,12},{5,13},{6,14},{7,15},{10,2},{11,3},{12,4},{13... | collective-permute-start | bytes 786440 | tf_op jit(solution)/shard_map/ppermute | solution.py:400
  8.6 14.6 %collective-permute-start.4 = (bf16[512,512]{1,0:T(8,128)(2,1)}, bf16[512,512]{1,0:T(8,128)(2,1)}, u32[]{:S(2)}, u32[]{:S(2)}) collective-permute-start(bf16[512,512]{1,0:T(8,128)(2,1)} %pad_maximum_fusion.1), channel_id=1, source_target_pairs={{2,2},{3,18},{4,4},{5,20},{6,6},{7,22},{10,10},{11,26},{12,12},{13... | collective-permute-start | bytes 1572872 | tf_op jit(solution)/shard_map/ppermute | solution.py:400
  13.9 22.2 %collective-permute-start.5 = (bf16[512,512]{1,0:T(8,128)(2,1)}, bf16[512,512]{1,0:T(8,128)(2,1)}, u32[]{:S(2)}, u32[]{:S(2)}) collective-permute-start(bf16[512,512]{1,0:T(8,128)(2,1)} %pad_maximum_fusion.1), channel_id=1, source_target_pairs={{2,3},{3,19},{4,5},{5,21},{6,7},{7,23},{10,11},{11,27},{12,13},{13... | collective-permute-start | bytes 1572872 | tf_op jit(solution)/shard_map/ppermute | solution.py:400
  18.7 19.5 %collective-permute-start.2 = (bf16[528,512]{1,0:T(8,128)(2,1)S(1)}, bf16[528,512]{1,0:T(8,128)(2,1)}, u32[]{:S(2)}, u32[]{:S(2)}) collective-permute-start(bf16[528,512]{1,0:T(8,128)(2,1)S(1)} %broadcast_select_fusion), channel_id=1, source_target_pairs={{0,2},{1,3},{4,6},{5,7},{8,10},{9,11},{12,14},{13,15},{16,18},{17,... | collective-permute-start | bytes 1622024 | tf_op jit(solution)/shard_map/ppermute | solution.py:400
  20.9 16.4 %collective-permute-start.7 = (bf16[256,512]{1,0:T(8,128)(2,1)S(1)}, bf16[256,512]{1,0:T(8,128)(2,1)S(1)}, u32[]{:S(2)}, u32[]{:S(2)}) collective-permute-start(bf16[256,512]{1,0:T(8,128)(2,1)S(1)} %get-tuple-element.28), channel_id=1, source_target_pairs={{0,8},{1,9},{8,0},{9,1},{16,24},{17,25},{24,16},{25,17}} | collective-permute-start | bytes 786440 | tf_op jit(solution)/shard_map/ppermute | solution.py:400
  21.5 16.7 %collective-permute-start.6 = (bf16[512,512]{1,0:T(8,128)(2,1)S(1)}, bf16[512,512]{1,0:T(8,128)(2,1)S(1)}, u32[]{:S(2)}, u32[]{:S(2)}) collective-permute-start(bf16[512,512]{1,0:T(8,128)(2,1)S(1)} %copy-done), channel_id=1, source_target_pairs={{0,8},{1,9},{2,10},{3,11},{4,12},{5,13},{6,14},{7,15},{8,0},{9,1},... | collective-permute-start | bytes 1572872 | tf_op jit(solution)/shard_map/ppermute | solution.py:400
  38.3 0.8 copy-start.8
  39.1 13.6 %collective-permute-start.11 = (bf16[528,512]{1,0:T(8,128)(2,1)S(1)}, bf16[528,512]{1,0:T(8,128)(2,1)S(1)}, u32[]{:S(2)}, u32[]{:S(2)}) collective-permute-start(bf16[528,512]{1,0:T(8,128)(2,1)S(1)} %broadcast_select_fusion.1.refs_0_.refs_4_), channel_id=1, source_target_pairs={{0,1},{1,0},{2,3},{3,2},{4,5},{5,4},{6,7},{7,6},{8,9},{9,8},{10,11... | collective-permute-start | bytes 1622024 | tf_op jit(solution)/shard_map/ppermute | solution.py:400
  41.0 26.8 %collective-permute-start.18 = (bf16[1024,512]{1,0:T(8,128)(2,1)S(1)}, bf16[1024,512]{1,0:T(8,128)(2,1)}, u32[]{:S(2)}, u32[]{:S(2)}) collective-permute-start(bf16[1024,512]{1,0:T(8,128)(2,1)S(1)} %constant_dynamic-update-slice_fusion.refs_14_), channel_id=1, source_target_pairs={{2,4},{3,5},{4,6},{5,7},{10,12},{11,13},{12,14},{13,15},{18,20},{1... | collective-permute-start | bytes 3145736 | tf_op jit(solution)/shard_map/ppermute | solution.py:400
  46.1 25.6 %collective-permute-start.17 = (bf16[1024,512]{1,0:T(8,128)(2,1)S(1)}, bf16[1024,512]{1,0:T(8,128)(2,1)}, u32[]{:S(2)}, u32[]{:S(2)}) collective-permute-start(bf16[1024,512]{1,0:T(8,128)(2,1)S(1)} %constant_dynamic-update-slice_fusion.refs_14_), channel_id=1, source_target_pairs={{2,0},{3,1},{4,2},{5,3},{6,4},{7,5},{10,8},{11,9},{12,10},{13,11},... | collective-permute-start | bytes 3145736 | tf_op jit(solution)/shard_map/ppermute | solution.py:400
  48.0 6.2 %collective-permute-start.8 = (bf16[528,512]{1,0:T(8,128)(2,1)S(1)}, bf16[528,512]{1,0:T(8,128)(2,1)S(1)}, u32[]{:S(2)}, u32[]{:S(2)}) collective-permute-start(bf16[528,512]{1,0:T(8,128)(2,1)S(1)} %broadcast_select_fusion.1.refs_0_.refs_4_), channel_id=1, source_target_pairs={{0,8},{1,9},{2,10},{3,11},{4,12},{5,13},{6,14},{7,15},{8,0},{9,1},... | collective-permute-start | bytes 1622024 | tf_op jit(solution)/shard_map/ppermute | solution.py:400
  49.1 14.0 %collective-permute-start.9 = (bf16[528,512]{1,0:T(8,128)(2,1)S(1)}, bf16[528,512]{1,0:T(8,128)(2,1)S(1)}, u32[]{:S(2)}, u32[]{:S(2)}) collective-permute-start(bf16[528,512]{1,0:T(8,128)(2,1)S(1)} %broadcast_select_fusion.1.refs_0_.refs_4_), channel_id=1, source_target_pairs={{0,16},{1,17},{2,18},{3,19},{4,20},{5,21},{6,22},{7,23},{8,24},{9,... | collective-permute-start | bytes 1622024 | tf_op jit(solution)/shard_map/ppermute | solution.py:400
  52.6 10.4 %collective-permute-start.12 = (bf16[528,512]{1,0:T(8,128)(2,1)S(1)}, bf16[528,512]{1,0:T(8,128)(2,1)S(1)}, u32[]{:S(2)}, u32[]{:S(2)}) collective-permute-start(bf16[528,512]{1,0:T(8,128)(2,1)S(1)} %collective-permute-done.11.refs_4_.refs_8_), channel_id=1, source_target_pairs={{0,8},{1,9},{2,10},{3,11},{4,12},{5,13},{6,14},{7,15},{8,0},{9,1},... | collective-permute-start | bytes 1622024 | tf_op jit(solution)/shard_map/ppermute | solution.py:400
  54.2 0.8 copy-start.2
  55.0 16.6 %collective-permute-start.15 = (bf16[272,512]{1,0:T(8,128)(2,1)S(1)}, bf16[272,512]{1,0:T(8,128)(2,1)S(1)}, u32[]{:S(2)}, u32[]{:S(2)}) collective-permute-start(bf16[272,512]{1,0:T(8,128)(2,1)S(1)} %slice.7), channel_id=1, source_target_pairs={{0,16},{1,17},{2,18},{3,19},{4,20},{5,21},{6,22},{7,23},{8,24},{9,... | collective-permute-start | bytes 835592 | tf_op jit(solution)/shard_map/ppermute | solution.py:400
  63.1 0.8 copy-start.5
  63.9 7.8 %collective-permute-start.13 = (bf16[256,512]{1,0:T(8,128)(2,1)S(1)}, bf16[256,512]{1,0:T(8,128)(2,1)}, u32[]{:S(2)}, u32[]{:S(2)}) collective-permute-start(bf16[256,512]{1,0:T(8,128)(2,1)S(1)} %slice.6), channel_id=1, source_target_pairs={{0,1},{1,0},{2,3},{3,2},{4,5},{5,4},{6,7},{7,6},{8,9},{9,8},{10,11... | collective-permute-start | bytes 786440 | tf_op jit(solution)/shard_map/ppermute | solution.py:400
  64.3 16.4 %collective-permute-start.10 = (bf16[528,512]{1,0:T(8,128)(2,1)S(1)}, bf16[528,512]{1,0:T(8,128)(2,1)}, u32[]{:S(2)}, u32[]{:S(2)}) collective-permute-start(bf16[528,512]{1,0:T(8,128)(2,1)S(1)} %collective-permute-done.9.refs_2_.refs_6_), channel_id=1, source_target_pairs={{0,8},{1,9},{2,10},{3,11},{4,12},{5,13},{6,14},{7,15},{8,0},{9,1},... | collective-permute-start | bytes 1622024 | tf_op jit(solution)/shard_map/ppermute | solution.py:400
  71.7 49.3 %collective-permute-start.19 = (bf16[1024,512]{1,0:T(8,128)(2,1)}, bf16[1024,512]{1,0:T(8,128)(2,1)}, u32[]{:S(2)}, u32[]{:S(2)}) collective-permute-start(bf16[1024,512]{1,0:T(8,128)(2,1)} %collective-permute-done.17.refs_15_), channel_id=1, source_target_pairs={{2,0},{3,1},{4,2},{5,3},{10,8},{11,9},{12,10},{13,11},{18,16},{19,... | collective-permute-start | bytes 3145736 | tf_op jit(solution)/shard_map/ppermute | solution.py:400
  74.9 46.1 %collective-permute-start.20 = (bf16[1024,512]{1,0:T(8,128)(2,1)}, bf16[1024,512]{1,0:T(8,128)(2,1)}, u32[]{:S(2)}, u32[]{:S(2)}) collective-permute-start(bf16[1024,512]{1,0:T(8,128)(2,1)} %collective-permute-done.18.refs_17_), channel_id=1, source_target_pairs={{4,6},{5,7},{12,14},{13,15},{20,22},{21,23},{28,30},{29,31}} | collective-permute-start | bytes 3145736 | tf_op jit(solution)/shard_map/ppermute | solution.py:400
  78.1 3.9 %collective-permute-start.16 = (bf16[272,512]{1,0:T(8,128)(2,1)S(1)}, bf16[272,512]{1,0:T(8,128)(2,1)}, u32[]{:S(2)}, u32[]{:S(2)}) collective-permute-start(bf16[272,512]{1,0:T(8,128)(2,1)S(1)} %collective-permute-done.15.refs_8_.refs_12_), channel_id=1, source_target_pairs={{0,8},{1,9},{2,10},{3,11},{4,12},{5,13},{6,14},{7,15},{8,0},{9,1},... | collective-permute-start | bytes 835592 | tf_op jit(solution)/shard_map/ppermute | solution.py:400
  80.4 4.1 %collective-permute-start.14 = (bf16[256,512]{1,0:T(8,128)(2,1)}, bf16[256,512]{1,0:T(8,128)(2,1)}, u32[]{:S(2)}, u32[]{:S(2)}) collective-permute-start(bf16[256,512]{1,0:T(8,128)(2,1)} %collective-permute-done.13.refs_6_.refs_10_), channel_id=1, source_target_pairs={{0,8},{1,9},{2,10},{3,11},{4,12},{5,13},{6,14},{7,15},{8,0},{9,1},... | collective-permute-start | bytes 786440 | tf_op jit(solution)/shard_map/ppermute | solution.py:400
  80.7 40.3 %copy-start.1 = (f32[512]{0:T(512)S(1)}, f32[512]{0:T(512)}, u32[]{:S(2)}) copy-start(f32[512]{0:T(512)} %param.3) | copy-start | bytes 6148
  80.7 40.2 %collective-permute-start.22 = (bf16[512,512]{1,0:T(8,128)(2,1)}, bf16[512,512]{1,0:T(8,128)(2,1)S(1)}, u32[]{:S(2)}, u32[]{:S(2)}) collective-permute-start(bf16[512,512]{1,0:T(8,128)(2,1)} %maximum_select_fusion), channel_id=1, source_target_pairs={{0,1},{1,17},{2,26},{3,27},{4,28},{5,29},{6,30},{7,31},{8,9},{9,25... | collective-permute-start | bytes 1572872 | tf_op jit(solution)/shard_map/ppermute | solution.py:400
  82.1 38.9 %collective-permute-start.21 = (bf16[512,512]{1,0:T(8,128)(2,1)}, bf16[512,512]{1,0:T(8,128)(2,1)S(1)}, u32[]{:S(2)}, u32[]{:S(2)}) collective-permute-start(bf16[512,512]{1,0:T(8,128)(2,1)} %maximum_select_fusion), channel_id=1, source_target_pairs={{0,0},{1,16},{2,18},{3,19},{4,20},{5,21},{6,22},{7,23},{8,8},{9,24... | collective-permute-start | bytes 1572872 | tf_op jit(solution)/shard_map/ppermute | solution.py:400
  84.5 1.1 copy-start.3
  85.6 1.0 copy-start.6
  86.6 34.4 %copy-start.4 = (bf16[528,512]{1,0:T(8,128)(2,1)S(1)}, bf16[528,512]{1,0:T(8,128)(2,1)}, u32[]{:S(2)}) copy-start(bf16[528,512]{1,0:T(8,128)(2,1)} %copy-done.2) | copy-start | bytes 1622020
  86.6 34.4 %copy-start.7 = (bf16[528,512]{1,0:T(8,128)(2,1)S(1)}, bf16[528,512]{1,0:T(8,128)(2,1)}, u32[]{:S(2)}) copy-start(bf16[528,512]{1,0:T(8,128)(2,1)} %copy-done.5) | copy-start | bytes 1622020
  86.6 34.4 %copy-start.9 = (bf16[512,512]{1,0:T(8,128)(2,1)S(1)}, bf16[512,512]{1,0:T(8,128)(2,1)}, u32[]{:S(2)}) copy-start(bf16[512,512]{1,0:T(8,128)(2,1)} %copy-done.8) | copy-start | bytes 1572868

commit v7 on v6

--- a/solution.py
+++ b/solution.py
@@ -421,7 +421,8 @@
         kept, given = (lax.dynamic_index_in_dim(halves, core ^ flip, 0, False) for flip in range(CORES))
         return jnp.concatenate([kept, over_core(given, only)], 0)
 
-    paired = traded(interactions, lambda p, h, s, w: s > 0)
+    halves = interactions.reshape(CORES, band, users)
+    offers = [lax.dynamic_index_in_dim(halves, core ^ flip, 0, False) for flip in range(CORES)]
     if ways == 2:
         raised = exchange(interactions, lambda p, h, s, w: (p, h, 0, w), lambda p, h, s, w: s == SPAN - 1)
 
@@ -435,12 +436,15 @@
         )
         if reach == SPAN // 2:
             for turn in range(ways):
-                quarters.append(
-                    exchange(
-                        paired, lambda p, h, s, w: (w, h, s, (p + turn) % ways), lambda p, h, s, w: s > 0
+                for flip in range(CORES):
+                    quarters.append(
+                        exchange(
+                            offers[flip],
+                            lambda p, h, s, w: (w, h ^ flip, s, (p + turn) % ways),
+                            lambda p, h, s, w: s > 0,
+                        )
                     )
-                )
-                quarter_users += [((way - turn) % ways * CORES + (core ^ flip)) * users for flip in range(CORES)]
+                    quarter_users.append(((way - turn) % ways * CORES + (core ^ flip)) * users)
             if ways == 2:
                 got = after(got, raised)
         shared = jnp.where(slot % (2 * reach) == reach, got, shared)
@@ -455,9 +459,8 @@
     rows, rows_views, rows_place = [], [], []
 
     if ways == 2:
-        twin_items = over_core(interactions)
         mixed = jnp.where(slot == 0, traded(raised, lambda p, h, s, w: s == 0), interactions)
-        shared = after(shared, quarters, twin_items, mixed)
+        shared = after(shared, quarters, mixed)
         pair_side, way_side = over_pair(shared), over_way(shared)
         own_twin, way_twin = over_core(shared), over_core(way_side)
         diagonal = [over_way(after(pair_side, own_twin, way_twin)[:half]), over_pair(after(way_side, own_twin)[half:])]
@@ -493,7 +496,7 @@
             jnp.where(slot > 1, slot - 1, 0),
             jnp.where(slot == 3, 1, 0),
         ]
-        cols += [twin_items]
+        cols += [over_core(after(interactions, *crossed))]
         cols_place += [0, (row_index ^ 1) * users]
         for turn in range(ways):
             mix = exchange(

time: 144 us -> 140 us (0.972)
  waiting for transfers between devices: 32.1 us -> 20.5 us
  starting transfers between devices: 43.4 us -> 51.1 us
    ppermute x23 -> x24, waiting for transfers between devices: 32.1 us -> 20.5 us  [exchange(): return lax.ppermute(value, ('row', 'col'), perm)]
    ppermute x23 -> x24, starting transfers between devices: 43.4 us -> 51.1 us  [exchange(): return lax.ppermute(value, ('row', 'col'), perm)]
    unnamed x21 -> x19, local copies, waits for them, and re-layouts: 5.56 us -> 4.7 us
  transfers between devices with their start and end apart: 23 -> 24, of which waited for: 8 -> 5; matrix products, arithmetic and copies ran while one was open for 4% -> 5% of each run, Pallas kernels for 24% -> 25%
where the time goes in v7:
time: 140 us; the launch traced here: 139 us
  Pallas kernels  56.3 us (40%)
  starting transfers between devices  51.1 us (36%)
  waiting for transfers between devices  20.5 us (15%)
  local copies, waits for them, and re-layouts  7.89 us (6%)
  other arithmetic  2.9 us (2%)
    ppermute x24, starting transfers between devices, exchange(): return lax.ppermute(value, ('row', 'col'), perm)  51.1 us
    pallas_call x1, Pallas kernels, factor_panel(): pl.pallas_call(functools.partial(panel_kernel, views, len(pieces), width)...  34.3 us
    pallas_call x1, Pallas kernels, finish_tile(): pl.pallas_call(functools.partial(tile_kernel, len(pieces), counts, views)...  22 us
    ppermute x24, waiting for transfers between devices, exchange(): return lax.ppermute(value, ('row', 'col'), perm)  20.5 us
    unnamed x19, local copies, waits for them, and re-layouts  4.7 us
  transfers between devices with their start and end apart: 24, of which 5 were waited for; matrix products, arithmetic and copies ran while one was open for 5% of the time, Pallas kernels for 25%

profile of v7, /device:TPU:17, one launch (start us, length us, event | category | flops | bytes accessed | tf_op | source)
XLA Modules:
  0.0 139.2 jit_solution(13395545666181582666)
XLA Ops:
  0.0 1.6 %collective-permute-start.1 = (bf16[512,512]{1,0:T(8,128)(2,1)}, bf16[512,512]{1,0:T(8,128)(2,1)}, u32[]{:S(2)}, u32[]{:S(2)}) collective-permute-start(bf16[512,512]{1,0:T(8,128)(2,1)} %refs_19_.1), channel_id=1, source_target_pairs={{6,0},{7,1},{14,8},{15,9},{22,16},{23,17},{30,24},{31,25}} | collective-permute-start | bytes 1572872 | tf_op jit(solution)/shard_map/ppermute | solution.py:400
  1.6 0.7 reduce-precision_convert_fusion.1
  2.3 1.1 pad_maximum_fusion
  3.4 1.3 collective-permute-start
  4.7 0.8 dynamic-slice_bitcast_fusion.2
  5.6 1.6 %collective-permute-start.3 = (bf16[256,512]{1,0:T(8,128)(2,1)}, bf16[256,512]{1,0:T(8,128)(2,1)S(1)}, u32[]{:S(2)}, u32[]{:S(2)}) collective-permute-start(bf16[256,512]{1,0:T(8,128)(2,1)} %get-tuple-element.32), channel_id=1, source_target_pairs={{2,2},{3,18},{4,4},{5,20},{6,6},{7,22},{10,10},{11,26},{12,12},{13... | collective-permute-start | bytes 786440 | tf_op jit(solution)/shard_map/ppermute | solution.py:400
  7.1 5.5 %collective-permute-start.6 = (bf16[256,512]{1,0:T(8,128)(2,1)}, bf16[256,512]{1,0:T(8,128)(2,1)}, u32[]{:S(2)}, u32[]{:S(2)}) collective-permute-start(bf16[256,512]{1,0:T(8,128)(2,1)} %get-tuple-element.31), channel_id=1, source_target_pairs={{2,11},{3,27},{4,13},{5,29},{6,15},{7,31},{10,3},{11,19},{12,5},{1... | collective-permute-start | bytes 786440 | tf_op jit(solution)/shard_map/ppermute | solution.py:400
  12.6 1.9 %collective-permute-start.4 = (bf16[256,512]{1,0:T(8,128)(2,1)}, bf16[256,512]{1,0:T(8,128)(2,1)}, u32[]{:S(2)}, u32[]{:S(2)}) collective-permute-start(bf16[256,512]{1,0:T(8,128)(2,1)} %get-tuple-element.31), channel_id=1, source_target_pairs={{2,10},{3,26},{4,12},{5,28},{6,14},{7,30},{10,2},{11,18},{12,4},{1... | collective-permute-start | bytes 786440 | tf_op jit(solution)/shard_map/ppermute | solution.py:400
  14.6 0.0 collective-permute-done.3
  14.6 4.3 %collective-permute-start.5 = (bf16[256,512]{1,0:T(8,128)(2,1)}, bf16[256,512]{1,0:T(8,128)(2,1)S(1)}, u32[]{:S(2)}, u32[]{:S(2)}) collective-permute-start(bf16[256,512]{1,0:T(8,128)(2,1)} %get-tuple-element.32), channel_id=1, source_target_pairs={{2,3},{3,19},{4,5},{5,21},{6,7},{7,23},{10,11},{11,27},{12,13},{13... | collective-permute-start | bytes 786440 | tf_op jit(solution)/shard_map/ppermute | solution.py:400
  18.9 0.0 collective-permute-done.1
  18.9 1.1 dynamic-slice_bitcast_fusion.1
  20.0 0.7 collective-permute-start.7
  20.7 0.0 collective-permute-done
  20.7 0.1 broadcast_select_fusion
  20.8 3.5 %collective-permute-start.2 = (bf16[528,512]{1,0:T(8,128)(2,1)S(1)}, bf16[528,512]{1,0:T(8,128)(2,1)S(1)}, u32[]{:S(2)}, u32[]{:S(2)}) collective-permute-start(bf16[528,512]{1,0:T(8,128)(2,1)S(1)} %broadcast_select_fusion), channel_id=1, source_target_pairs={{0,2},{1,3},{4,6},{5,7},{8,10},{9,11},{12,14},{13,15},{16,18},{17,... | collective-permute-start | bytes 1622024 | tf_op jit(solution)/shard_map/ppermute | solution.py:400
  24.3 0.0 collective-permute-done.4
  24.3 1.0 constant_dynamic-update-slice_fusion.2
  25.3 7.4 %collective-permute-done.5 = bf16[256,512]{1,0:T(8,128)(2,1)S(1)} collective-permute-done((bf16[256,512]{1,0:T(8,128)(2,1)}, bf16[256,512]{1,0:T(8,128)(2,1)S(1)}, u32[]{:S(2)}, u32[]{:S(2)}) %collective-permute-start.5) | collective-permute-done | bytes 262176 | tf_op jit(solution)/shard_map/ppermute | solution.py:400
  32.8 0.0 collective-permute-done.6
  32.8 1.0 constant_dynamic-update-slice_fusion.refs_14_
  33.7 0.0 collective-permute-done.7
  33.8 0.9 maximum_select_fusion
  34.7 0.0 collective-permute-done.2
  34.7 0.1 broadcast_select_fusion.1.refs_0_.refs_4_
  34.7 2.2 %collective-permute-start.11 = (bf16[528,512]{1,0:T(8,128)(2,1)S(1)}, bf16[528,512]{1,0:T(8,128)(2,1)S(1)}, u32[]{:S(2)}, u32[]{:S(2)}) collective-permute-start(bf16[528,512]{1,0:T(8,128)(2,1)S(1)} %broadcast_select_fusion.1.refs_0_.refs_4_), channel_id=1, source_target_pairs={{0,1},{1,0},{2,3},{3,2},{4,5},{5,4},{6,7},{7,6},{8,9},{9,8},{10,11... | collective-permute-start | bytes 1622024 | tf_op jit(solution)/shard_map/ppermute | solution.py:400
  36.9 3.8 %collective-permute-start.18 = (bf16[1024,512]{1,0:T(8,128)(2,1)S(1)}, bf16[1024,512]{1,0:T(8,128)(2,1)}, u32[]{:S(2)}, u32[]{:S(2)}) collective-permute-start(bf16[1024,512]{1,0:T(8,128)(2,1)S(1)} %constant_dynamic-update-slice_fusion.refs_14_), channel_id=1, source_target_pairs={{2,4},{3,5},{4,6},{5,7},{10,12},{11,13},{12,14},{13,15},{18,20},{1... | collective-permute-start | bytes 3145736 | tf_op jit(solution)/shard_map/ppermute | solution.py:400
  40.7 2.4 %collective-permute-start.17 = (bf16[1024,512]{1,0:T(8,128)(2,1)S(1)}, bf16[1024,512]{1,0:T(8,128)(2,1)}, u32[]{:S(2)}, u32[]{:S(2)}) collective-permute-start(bf16[1024,512]{1,0:T(8,128)(2,1)S(1)} %constant_dynamic-update-slice_fusion.refs_14_), channel_id=1, source_target_pairs={{2,0},{3,1},{4,2},{5,3},{6,4},{7,5},{10,8},{11,9},{12,10},{13,11},... | collective-permute-start | bytes 3145736 | tf_op jit(solution)/shard_map/ppermute | solution.py:400
  43.2 1.4 %collective-permute-start.8 = (bf16[528,512]{1,0:T(8,128)(2,1)S(1)}, bf16[528,512]{1,0:T(8,128)(2,1)S(1)}, u32[]{:S(2)}, u32[]{:S(2)}) collective-permute-start(bf16[528,512]{1,0:T(8,128)(2,1)S(1)} %broadcast_select_fusion.1.refs_0_.refs_4_), channel_id=1, source_target_pairs={{0,8},{1,9},{2,10},{3,11},{4,12},{5,13},{6,14},{7,15},{8,0},{9,1},... | collective-permute-start | bytes 1622024 | tf_op jit(solution)/shard_map/ppermute | solution.py:400
  44.6 0.9 collective-permute-start.9
  45.5 2.5 %collective-permute-done.11.refs_4_.refs_8_ = bf16[528,512]{1,0:T(8,128)(2,1)S(1)} collective-permute-done((bf16[528,512]{1,0:T(8,128)(2,1)S(1)}, bf16[528,512]{1,0:T(8,128)(2,1)S(1)}, u32[]{:S(2)}, u32[]{:S(2)}) %collective-permute-start.11) | collective-permute-done | bytes 540704 | tf_op jit(solution)/shard_map/ppermute | solution.py:400
  48.0 2.1 %collective-permute-start.12 = (bf16[528,512]{1,0:T(8,128)(2,1)S(1)}, bf16[528,512]{1,0:T(8,128)(2,1)S(1)}, u32[]{:S(2)}, u32[]{:S(2)}) collective-permute-start(bf16[528,512]{1,0:T(8,128)(2,1)S(1)} %collective-permute-done.11.refs_4_.refs_8_), channel_id=1, source_target_pairs={{0,8},{1,9},{2,10},{3,11},{4,12},{5,13},{6,14},{7,15},{8,0},{9,1},... | collective-permute-start | bytes 1622024 | tf_op jit(solution)/shard_map/ppermute | solution.py:400
  50.1 0.0 collective-permute-done.8.refs_1_.refs_5_
  50.1 0.8 copy-done.2
  51.0 1.5 %collective-permute-start.15 = (bf16[272,512]{1,0:T(8,128)(2,1)S(1)}, bf16[272,512]{1,0:T(8,128)(2,1)S(1)}, u32[]{:S(2)}, u32[]{:S(2)}) collective-permute-start(bf16[272,512]{1,0:T(8,128)(2,1)S(1)} %slice.7), channel_id=1, source_target_pairs={{0,16},{1,17},{2,18},{3,19},{4,20},{5,21},{6,22},{7,23},{8,24},{9,... | collective-permute-start | bytes 835592 | tf_op jit(solution)/shard_map/ppermute | solution.py:400
  52.5 6.1 %collective-permute-done.9.refs_2_.refs_6_ = bf16[528,512]{1,0:T(8,128)(2,1)S(1)} collective-permute-done((bf16[528,512]{1,0:T(8,128)(2,1)S(1)}, bf16[528,512]{1,0:T(8,128)(2,1)S(1)}, u32[]{:S(2)}, u32[]{:S(2)}) %collective-permute-start.9) | collective-permute-done | bytes 540704 | tf_op jit(solution)/shard_map/ppermute | solution.py:400
  58.5 0.0 collective-permute-done.12.refs_5_.refs_9_
  58.6 0.8 copy-done.5
  59.4 1.0 collective-permute-start.13
  60.4 1.5 %collective-permute-start.10 = (bf16[528,512]{1,0:T(8,128)(2,1)S(1)}, bf16[528,512]{1,0:T(8,128)(2,1)}, u32[]{:S(2)}, u32[]{:S(2)}) collective-permute-start(bf16[528,512]{1,0:T(8,128)(2,1)S(1)} %collective-permute-done.9.refs_2_.refs_6_), channel_id=1, source_target_pairs={{0,8},{1,9},{2,10},{3,11},{4,12},{5,13},{6,14},{7,15},{8,0},{9,1},... | collective-permute-start | bytes 1622024 | tf_op jit(solution)/shard_map/ppermute | solution.py:400
  61.8 0.9 collective-permute-done.18.refs_17_
  62.8 3.6 %collective-permute-done.17.refs_15_ = bf16[1024,512]{1,0:T(8,128)(2,1)} collective-permute-done((bf16[1024,512]{1,0:T(8,128)(2,1)S(1)}, bf16[1024,512]{1,0:T(8,128)(2,1)}, u32[]{:S(2)}, u32[]{:S(2)}) %collective-permute-start.17) | collective-permute-done | bytes 1048608 | tf_op jit(solution)/shard_map/ppermute | solution.py:400
  66.3 0.0 collective-permute-done.15.refs_8_.refs_12_
  66.3 0.0 collective-permute-done.13.refs_6_.refs_10_
  66.3 3.4 %collective-permute-start.19 = (bf16[1024,512]{1,0:T(8,128)(2,1)}, bf16[1024,512]{1,0:T(8,128)(2,1)}, u32[]{:S(2)}, u32[]{:S(2)}) collective-permute-start(bf16[1024,512]{1,0:T(8,128)(2,1)} %collective-permute-done.17.refs_15_), channel_id=1, source_target_pairs={{2,0},{3,1},{4,2},{5,3},{10,8},{11,9},{12,10},{13,11},{18,16},{19,... | collective-permute-start | bytes 3145736 | tf_op jit(solution)/shard_map/ppermute | solution.py:400
  69.7 3.1 %collective-permute-start.20 = (bf16[1024,512]{1,0:T(8,128)(2,1)}, bf16[1024,512]{1,0:T(8,128)(2,1)}, u32[]{:S(2)}, u32[]{:S(2)}) collective-permute-start(bf16[1024,512]{1,0:T(8,128)(2,1)} %collective-permute-done.18.refs_17_), channel_id=1, source_target_pairs={{4,6},{5,7},{12,14},{13,15},{20,22},{21,23},{28,30},{29,31}} | collective-permute-start | bytes 3145736 | tf_op jit(solution)/shard_map/ppermute | solution.py:400
  72.8 2.3 %collective-permute-start.16 = (bf16[272,512]{1,0:T(8,128)(2,1)S(1)}, bf16[272,512]{1,0:T(8,128)(2,1)}, u32[]{:S(2)}, u32[]{:S(2)}) collective-permute-start(bf16[272,512]{1,0:T(8,128)(2,1)S(1)} %collective-permute-done.15.refs_8_.refs_12_), channel_id=1, source_target_pairs={{0,8},{1,9},{2,10},{3,11},{4,12},{5,13},{6,14},{7,15},{8,0},{9,1},... | collective-permute-start | bytes 835592 | tf_op jit(solution)/shard_map/ppermute | solution.py:400
  75.1 0.0 collective-permute-start.14
  75.1 0.1 stack.95.place_ref
  75.2 0.2 stack.92.place_ref
  75.3 0.0 copy-start.1
  75.3 0.0 collective-permute-done.10.refs_3_.refs_7_
  75.4 1.7 %collective-permute-start.23 = (bf16[512,512]{1,0:T(8,128)(2,1)}, bf16[512,512]{1,0:T(8,128)(2,1)S(1)}, u32[]{:S(2)}, u32[]{:S(2)}) collective-permute-start(bf16[512,512]{1,0:T(8,128)(2,1)} %maximum_select_fusion), channel_id=1, source_target_pairs={{0,1},{1,17},{2,26},{3,27},{4,28},{5,29},{6,30},{7,31},{8,9},{9,25... | collective-permute-start | bytes 1572872 | tf_op jit(solution)/shard_map/ppermute | solution.py:400
  77.0 0.0 collective-permute-done.16.refs_9_.refs_13_
  77.0 2.8 %collective-permute-start.22 = (bf16[512,512]{1,0:T(8,128)(2,1)}, bf16[512,512]{1,0:T(8,128)(2,1)S(1)}, u32[]{:S(2)}, u32[]{:S(2)}) collective-permute-start(bf16[512,512]{1,0:T(8,128)(2,1)} %maximum_select_fusion), channel_id=1, source_target_pairs={{0,0},{1,16},{2,18},{3,19},{4,20},{5,21},{6,22},{7,23},{8,8},{9,24... | collective-permute-start | bytes 1572872 | tf_op jit(solution)/shard_map/ppermute | solution.py:400
  79.9 0.0 collective-permute-done.14.refs_7_.refs_11_
  79.9 0.7 collective-permute-start.21
  80.6 1.0 copy-done.3
  81.7 1.0 copy-done.6
  82.7 34.3 %factor_panel.1 = (bf16[1024,1024]{1,0:T(8,128)(2,1)}, bf16[1024,1024]{1,0:T(8,128)(2,1)}, bf16[1024,128]{1,0:T(8,128)(2,1)}, bf16[1024,128]{1,0:T(8,128)(2,1)}) custom-call(s32[24]{0:T(128)S(1)} %stack.95.place_ref, bf16[528,512]{1,0:T(8,128)(2,1)S(1)} %broadcast_select_fusion.1.refs_0_.refs_4_, bf16[528,512]{1,0:T(8,128)(2,1)S(1)} %copy-done.3, ...), custom_call_target="tpu_custom_call" | custom-call | flops 8000000000 | bytes 1048576 | tf_op jit(solution)/shard_map/factor_panel/pallas_call | solution.py:242
  117.0 0.0 collective-permute-done.21.refs_20_
  117.0 0.0 collective-permute-done.23.refs_22_
  117.0 0.0 collective-permute-done.22.refs_21_
  117.1 22.0 %finish_tile.1 = f32[1024,512]{1,0:T(8,128)} custom-call(s32[78]{0:T(128)S(1)} %stack.92.place_ref, f32[1,512]{1,0:T(1,128)S(1)} %bitcast.39, bf16[1024,1024]{1,0:T(8,128)(2,1)} %get-tuple-element.21.refs_0_, bf16[1024,1024]{1,0:T(8,128)(2,1)} %get-tuple-element.22.refs_1_, bf16[1024,128]{1,0:T(8,128)(2,1)} %get-tuple-element.23.refs_2_, ...), custom_call_target="tpu_custom_call" | custom-call | flops 20000000000 | bytes 25165824 | tf_op jit(solution)/shard_map/finish_tile/pallas_call | solution.py:360
  (21 shorter events, 0.1 us)
Async XLA Ops:
  0.0 4.7 %copy-start = (bf16[512,512]{1,0:T(8,128)(2,1)S(1)}, bf16[512,512]{1,0:T(8,128)(2,1)}, u32[]{:S(2)}) copy-start(bf16[512,512]{1,0:T(8,128)(2,1)} %refs_19_.1) | copy-start | bytes 1572868
  0.0 18.9 %collective-permute-start.1 = (bf16[512,512]{1,0:T(8,128)(2,1)}, bf16[512,512]{1,0:T(8,128)(2,1)}, u32[]{:S(2)}, u32[]{:S(2)}) collective-permute-start(bf16[512,512]{1,0:T(8,128)(2,1)} %refs_19_.1), channel_id=1, source_target_pairs={{6,0},{7,1},{14,8},{15,9},{22,16},{23,17},{30,24},{31,25}} | collective-permute-start | bytes 1572872 | tf_op jit(solution)/shard_map/ppermute | solution.py:400
  3.4 17.3 %collective-permute-start = (bf16[528,512]{1,0:T(8,128)(2,1)S(1)}, bf16[528,512]{1,0:T(8,128)(2,1)S(1)}, u32[]{:S(2)}, u32[]{:S(2)}) collective-permute-start(bf16[528,512]{1,0:T(8,128)(2,1)S(1)} %pad_maximum_fusion), channel_id=1, source_target_pairs={{0,4},{1,5},{8,12},{9,13},{16,20},{17,21},{24,28},{25,29}} | collective-permute-start | bytes 1622024 | tf_op jit(solution)/shard_map/ppermute | solution.py:400
  5.6 9.0 %collective-permute-start.3 = (bf16[256,512]{1,0:T(8,128)(2,1)}, bf16[256,512]{1,0:T(8,128)(2,1)S(1)}, u32[]{:S(2)}, u32[]{:S(2)}) collective-permute-start(bf16[256,512]{1,0:T(8,128)(2,1)} %get-tuple-element.32), channel_id=1, source_target_pairs={{2,2},{3,18},{4,4},{5,20},{6,6},{7,22},{10,10},{11,26},{12,12},{13... | collective-permute-start | bytes 786440 | tf_op jit(solution)/shard_map/ppermute | solution.py:400
  7.1 25.6 %collective-permute-start.6 = (bf16[256,512]{1,0:T(8,128)(2,1)}, bf16[256,512]{1,0:T(8,128)(2,1)}, u32[]{:S(2)}, u32[]{:S(2)}) collective-permute-start(bf16[256,512]{1,0:T(8,128)(2,1)} %get-tuple-element.31), channel_id=1, source_target_pairs={{2,11},{3,27},{4,13},{5,29},{6,15},{7,31},{10,3},{11,19},{12,5},{1... | collective-permute-start | bytes 786440 | tf_op jit(solution)/shard_map/ppermute | solution.py:400
  12.6 11.7 %collective-permute-start.4 = (bf16[256,512]{1,0:T(8,128)(2,1)}, bf16[256,512]{1,0:T(8,128)(2,1)}, u32[]{:S(2)}, u32[]{:S(2)}) collective-permute-start(bf16[256,512]{1,0:T(8,128)(2,1)} %get-tuple-element.31), channel_id=1, source_target_pairs={{2,10},{3,26},{4,12},{5,28},{6,14},{7,30},{10,2},{11,18},{12,4},{1... | collective-permute-start | bytes 786440 | tf_op jit(solution)/shard_map/ppermute | solution.py:400
  14.6 18.1 %collective-permute-start.5 = (bf16[256,512]{1,0:T(8,128)(2,1)}, bf16[256,512]{1,0:T(8,128)(2,1)S(1)}, u32[]{:S(2)}, u32[]{:S(2)}) collective-permute-start(bf16[256,512]{1,0:T(8,128)(2,1)} %get-tuple-element.32), channel_id=1, source_target_pairs={{2,3},{3,19},{4,5},{5,21},{6,7},{7,23},{10,11},{11,27},{12,13},{13... | collective-permute-start | bytes 786440 | tf_op jit(solution)/shard_map/ppermute | solution.py:400
  20.0 13.7 %collective-permute-start.7 = (bf16[256,512]{1,0:T(8,128)(2,1)S(1)}, bf16[256,512]{1,0:T(8,128)(2,1)S(1)}, u32[]{:S(2)}, u32[]{:S(2)}) collective-permute-start(bf16[256,512]{1,0:T(8,128)(2,1)S(1)} %get-tuple-element.30), channel_id=1, source_target_pairs={{0,8},{1,9},{8,0},{9,1},{16,24},{17,25},{24,16},{25,17}} | collective-permute-start | bytes 786440 | tf_op jit(solution)/shard_map/ppermute | solution.py:400
  20.8 13.8 %collective-permute-start.2 = (bf16[528,512]{1,0:T(8,128)(2,1)S(1)}, bf16[528,512]{1,0:T(8,128)(2,1)S(1)}, u32[]{:S(2)}, u32[]{:S(2)}) collective-permute-start(bf16[528,512]{1,0:T(8,128)(2,1)S(1)} %broadcast_select_fusion), channel_id=1, source_target_pairs={{0,2},{1,3},{4,6},{5,7},{8,10},{9,11},{12,14},{13,15},{16,18},{17,... | collective-permute-start | bytes 1622024 | tf_op jit(solution)/shard_map/ppermute | solution.py:400
  34.7 13.3 %collective-permute-start.11 = (bf16[528,512]{1,0:T(8,128)(2,1)S(1)}, bf16[528,512]{1,0:T(8,128)(2,1)S(1)}, u32[]{:S(2)}, u32[]{:S(2)}) collective-permute-start(bf16[528,512]{1,0:T(8,128)(2,1)S(1)} %broadcast_select_fusion.1.refs_0_.refs_4_), channel_id=1, source_target_pairs={{0,1},{1,0},{2,3},{3,2},{4,5},{5,4},{6,7},{7,6},{8,9},{9,8},{10,11... | collective-permute-start | bytes 1622024 | tf_op jit(solution)/shard_map/ppermute | solution.py:400
  36.9 25.9 %collective-permute-start.18 = (bf16[1024,512]{1,0:T(8,128)(2,1)S(1)}, bf16[1024,512]{1,0:T(8,128)(2,1)}, u32[]{:S(2)}, u32[]{:S(2)}) collective-permute-start(bf16[1024,512]{1,0:T(8,128)(2,1)S(1)} %constant_dynamic-update-slice_fusion.refs_14_), channel_id=1, source_target_pairs={{2,4},{3,5},{4,6},{5,7},{10,12},{11,13},{12,14},{13,15},{18,20},{1... | collective-permute-start | bytes 3145736 | tf_op jit(solution)/shard_map/ppermute | solution.py:400
  40.7 25.6 %collective-permute-start.17 = (bf16[1024,512]{1,0:T(8,128)(2,1)S(1)}, bf16[1024,512]{1,0:T(8,128)(2,1)}, u32[]{:S(2)}, u32[]{:S(2)}) collective-permute-start(bf16[1024,512]{1,0:T(8,128)(2,1)S(1)} %constant_dynamic-update-slice_fusion.refs_14_), channel_id=1, source_target_pairs={{2,0},{3,1},{4,2},{5,3},{6,4},{7,5},{10,8},{11,9},{12,10},{13,11},... | collective-permute-start | bytes 3145736 | tf_op jit(solution)/shard_map/ppermute | solution.py:400
  43.2 7.0 %collective-permute-start.8 = (bf16[528,512]{1,0:T(8,128)(2,1)S(1)}, bf16[528,512]{1,0:T(8,128)(2,1)S(1)}, u32[]{:S(2)}, u32[]{:S(2)}) collective-permute-start(bf16[528,512]{1,0:T(8,128)(2,1)S(1)} %broadcast_select_fusion.1.refs_0_.refs_4_), channel_id=1, source_target_pairs={{0,8},{1,9},{2,10},{3,11},{4,12},{5,13},{6,14},{7,15},{8,0},{9,1},... | collective-permute-start | bytes 1622024 | tf_op jit(solution)/shard_map/ppermute | solution.py:400
  44.6 14.0 %collective-permute-start.9 = (bf16[528,512]{1,0:T(8,128)(2,1)S(1)}, bf16[528,512]{1,0:T(8,128)(2,1)S(1)}, u32[]{:S(2)}, u32[]{:S(2)}) collective-permute-start(bf16[528,512]{1,0:T(8,128)(2,1)S(1)} %broadcast_select_fusion.1.refs_0_.refs_4_), channel_id=1, source_target_pairs={{0,16},{1,17},{2,18},{3,19},{4,20},{5,21},{6,22},{7,23},{8,24},{9,... | collective-permute-start | bytes 1622024 | tf_op jit(solution)/shard_map/ppermute | solution.py:400
  48.0 10.5 %collective-permute-start.12 = (bf16[528,512]{1,0:T(8,128)(2,1)S(1)}, bf16[528,512]{1,0:T(8,128)(2,1)S(1)}, u32[]{:S(2)}, u32[]{:S(2)}) collective-permute-start(bf16[528,512]{1,0:T(8,128)(2,1)S(1)} %collective-permute-done.11.refs_4_.refs_8_), channel_id=1, source_target_pairs={{0,8},{1,9},{2,10},{3,11},{4,12},{5,13},{6,14},{7,15},{8,0},{9,1},... | collective-permute-start | bytes 1622024 | tf_op jit(solution)/shard_map/ppermute | solution.py:400
  50.1 0.8 copy-start.2
  51.0 15.4 %collective-permute-start.15 = (bf16[272,512]{1,0:T(8,128)(2,1)S(1)}, bf16[272,512]{1,0:T(8,128)(2,1)S(1)}, u32[]{:S(2)}, u32[]{:S(2)}) collective-permute-start(bf16[272,512]{1,0:T(8,128)(2,1)S(1)} %slice.7), channel_id=1, source_target_pairs={{0,16},{1,17},{2,18},{3,19},{4,20},{5,21},{6,22},{7,23},{8,24},{9,... | collective-permute-start | bytes 835592 | tf_op jit(solution)/shard_map/ppermute | solution.py:400
  58.5 0.8 copy-start.5
  59.4 7.0 %collective-permute-start.13 = (bf16[256,512]{1,0:T(8,128)(2,1)S(1)}, bf16[256,512]{1,0:T(8,128)(2,1)}, u32[]{:S(2)}, u32[]{:S(2)}) collective-permute-start(bf16[256,512]{1,0:T(8,128)(2,1)S(1)} %slice.6), channel_id=1, source_target_pairs={{0,1},{1,0},{2,3},{3,2},{4,5},{5,4},{6,7},{7,6},{8,9},{9,8},{10,11... | collective-permute-start | bytes 786440 | tf_op jit(solution)/shard_map/ppermute | solution.py:400
  60.4 15.0 %collective-permute-start.10 = (bf16[528,512]{1,0:T(8,128)(2,1)S(1)}, bf16[528,512]{1,0:T(8,128)(2,1)}, u32[]{:S(2)}, u32[]{:S(2)}) collective-permute-start(bf16[528,512]{1,0:T(8,128)(2,1)S(1)} %collective-permute-done.9.refs_2_.refs_6_), channel_id=1, source_target_pairs={{0,8},{1,9},{2,10},{3,11},{4,12},{5,13},{6,14},{7,15},{8,0},{9,1},... | collective-permute-start | bytes 1622024 | tf_op jit(solution)/shard_map/ppermute | solution.py:400
  66.3 50.7 %collective-permute-start.19 = (bf16[1024,512]{1,0:T(8,128)(2,1)}, bf16[1024,512]{1,0:T(8,128)(2,1)}, u32[]{:S(2)}, u32[]{:S(2)}) collective-permute-start(bf16[1024,512]{1,0:T(8,128)(2,1)} %collective-permute-done.17.refs_15_), channel_id=1, source_target_pairs={{2,0},{3,1},{4,2},{5,3},{10,8},{11,9},{12,10},{13,11},{18,16},{19,... | collective-permute-start | bytes 3145736 | tf_op jit(solution)/shard_map/ppermute | solution.py:400
  69.7 47.4 %collective-permute-start.20 = (bf16[1024,512]{1,0:T(8,128)(2,1)}, bf16[1024,512]{1,0:T(8,128)(2,1)}, u32[]{:S(2)}, u32[]{:S(2)}) collective-permute-start(bf16[1024,512]{1,0:T(8,128)(2,1)} %collective-permute-done.18.refs_17_), channel_id=1, source_target_pairs={{4,6},{5,7},{12,14},{13,15},{20,22},{21,23},{28,30},{29,31}} | collective-permute-start | bytes 3145736 | tf_op jit(solution)/shard_map/ppermute | solution.py:400
  72.8 4.2 %collective-permute-start.16 = (bf16[272,512]{1,0:T(8,128)(2,1)S(1)}, bf16[272,512]{1,0:T(8,128)(2,1)}, u32[]{:S(2)}, u32[]{:S(2)}) collective-permute-start(bf16[272,512]{1,0:T(8,128)(2,1)S(1)} %collective-permute-done.15.refs_8_.refs_12_), channel_id=1, source_target_pairs={{0,8},{1,9},{2,10},{3,11},{4,12},{5,13},{6,14},{7,15},{8,0},{9,1},... | collective-permute-start | bytes 835592 | tf_op jit(solution)/shard_map/ppermute | solution.py:400
  75.1 4.8 %collective-permute-start.14 = (bf16[256,512]{1,0:T(8,128)(2,1)}, bf16[256,512]{1,0:T(8,128)(2,1)}, u32[]{:S(2)}, u32[]{:S(2)}) collective-permute-start(bf16[256,512]{1,0:T(8,128)(2,1)} %collective-permute-done.13.refs_6_.refs_10_), channel_id=1, source_target_pairs={{0,8},{1,9},{2,10},{3,11},{4,12},{5,13},{6,14},{7,15},{8,0},{9,1},... | collective-permute-start | bytes 786440 | tf_op jit(solution)/shard_map/ppermute | solution.py:400
  75.3 41.7 %copy-start.1 = (f32[512]{0:T(512)S(1)}, f32[512]{0:T(512)}, u32[]{:S(2)}) copy-start(f32[512]{0:T(512)} %param.3) | copy-start | bytes 6148
  75.4 41.7 %collective-permute-start.23 = (bf16[512,512]{1,0:T(8,128)(2,1)}, bf16[512,512]{1,0:T(8,128)(2,1)S(1)}, u32[]{:S(2)}, u32[]{:S(2)}) collective-permute-start(bf16[512,512]{1,0:T(8,128)(2,1)} %maximum_select_fusion), channel_id=1, source_target_pairs={{0,1},{1,17},{2,26},{3,27},{4,28},{5,29},{6,30},{7,31},{8,9},{9,25... | collective-permute-start | bytes 1572872 | tf_op jit(solution)/shard_map/ppermute | solution.py:400
  77.0 40.0 %collective-permute-start.22 = (bf16[512,512]{1,0:T(8,128)(2,1)}, bf16[512,512]{1,0:T(8,128)(2,1)S(1)}, u32[]{:S(2)}, u32[]{:S(2)}) collective-permute-start(bf16[512,512]{1,0:T(8,128)(2,1)} %maximum_select_fusion), channel_id=1, source_target_pairs={{0,0},{1,16},{2,18},{3,19},{4,20},{5,21},{6,22},{7,23},{8,8},{9,24... | collective-permute-start | bytes 1572872 | tf_op jit(solution)/shard_map/ppermute | solution.py:400
  79.9 37.1 %collective-permute-start.21 = (bf16[512,512]{1,0:T(8,128)(2,1)S(1)}, bf16[512,512]{1,0:T(8,128)(2,1)S(1)}, u32[]{:S(2)}, u32[]{:S(2)}) collective-permute-start(bf16[512,512]{1,0:T(8,128)(2,1)S(1)} %copy-done), channel_id=1, source_target_pairs={{0,8},{1,9},{2,10},{3,11},{4,12},{5,13},{6,14},{7,15},{8,0},{9,1},... | collective-permute-start | bytes 1572872 | tf_op jit(solution)/shard_map/ppermute | solution.py:400
  80.6 1.0 copy-start.3
  81.7 1.0 copy-start.6
  82.7 34.4 %copy-start.4 = (bf16[528,512]{1,0:T(8,128)(2,1)S(1)}, bf16[528,512]{1,0:T(8,128)(2,1)}, u32[]{:S(2)}) copy-start(bf16[528,512]{1,0:T(8,128)(2,1)} %copy-done.2) | copy-start | bytes 1622020
  82.7 34.4 %copy-start.7 = (bf16[528,512]{1,0:T(8,128)(2,1)S(1)}, bf16[528,512]{1,0:T(8,128)(2,1)}, u32[]{:S(2)}) copy-start(bf16[528,512]{1,0:T(8,128)(2,1)} %copy-done.5) | copy-start | bytes 1622020

commit v8 on v7

--- a/solution.py
+++ b/solution.py
@@ -482,12 +482,13 @@
                 panel.append(value)
         crossed = [pair_side, way_side, *diagonal]
         down = exchange(quarters, lambda p, h, s, w: (p, h, s - 1, w), lambda p, h, s, w: s > 0)
-        up = exchange(quarters, lambda p, h, s, w: (p, h, s + 1, w), lambda p, h, s, w: 0 < s < SPAN - 1)
-        down_held, up_held, mixed = lax.optimization_barrier(
-            (down, up, mixed, *crossed)
-        )[:3]
+        up = exchange(
+            after(quarters, pair_side, way_side), lambda p, h, s, w: (p, h, s + 1, w), lambda p, h, s, w: 0 < s < SPAN - 1
+        )
+        own_core = over_core(after(interactions, pair_side, way_side))
+        down_held, ready, mixed = lax.optimization_barrier((down, quarters, mixed, own_core, *crossed))[:3]
         down_again = exchange(down_held, lambda p, h, s, w: (p, h, s - 1, w), lambda p, h, s, w: 0 < s < SPAN - 1)
-        up_again = exchange(up_held, lambda p, h, s, w: (p, h, s + 1, w), lambda p, h, s, w: s == 2)
+        up_again = exchange(ready, lambda p, h, s, w: (p, h, s + 2, w), lambda p, h, s, w: s == 1)
         rows = [quarters, down, down_again, up, up_again]
         from_slots = [
             slot,
@@ -496,7 +497,7 @@
             jnp.where(slot > 1, slot - 1, 0),
             jnp.where(slot == 3, 1, 0),
         ]
-        cols += [over_core(after(interactions, *crossed))]
+        cols += [own_core]
         cols_place += [0, (row_index ^ 1) * users]
         for turn in range(ways):
             mix = exchange(

time: 140 us -> 141 us (level)
  local copies, waits for them, and re-layouts: 7.89 us -> 10.6 us
  starting transfers between devices: 51.1 us -> 49.5 us
    unnamed x19 -> x29, local copies, waits for them, and re-layouts: 4.7 us -> 7.42 us
    ppermute x24, starting transfers between devices: 51.1 us -> 49.5 us  [exchange(): return lax.ppermute(value, ('row', 'col'), perm)]
  transfers between devices with their start and end apart: 24 -> 24, of which waited for: 5 -> 4; matrix products, arithmetic and copies ran while one was open for 5% -> 5% of each run, Pallas kernels for 25% -> 24%
where the time goes in v8:
time: 141 us
  Pallas kernels  56.2 us (40%)
  starting transfers between devices  49.5 us (35%)
  waiting for transfers between devices  20.7 us (15%)
  local copies, waits for them, and re-layouts  10.6 us (8%)
  other arithmetic  2.92 us (2%)
    ppermute x24, starting transfers between devices, exchange(): return lax.ppermute(value, ('row', 'col'), perm)  49.5 us
    pallas_call x1, Pallas kernels, factor_panel(): pl.pallas_call(functools.partial(panel_kernel, views, len(pieces), width)...  34.3 us
    pallas_call x1, Pallas kernels, finish_tile(): pl.pallas_call(functools.partial(tile_kernel, len(pieces), counts, views)...  21.8 us
    ppermute x24, waiting for transfers between devices, exchange(): return lax.ppermute(value, ('row', 'col'), perm)  20.7 us
    unnamed x29, local copies, waits for them, and re-layouts  7.42 us
  transfers between devices with their start and end apart: 24, of which 4 were waited for; matrix products, arithmetic and copies ran while one was open for 5% of the time, Pallas kernels for 24%

profile of v8, /device:TPU:17, one launch (start us, length us, event | category | flops | bytes accessed | tf_op | source)
XLA Modules:
  0.0 140.5 jit_solution(10148380634269028108)
XLA Ops:
  0.0 1.6 %collective-permute-start.1 = (bf16[512,512]{1,0:T(8,128)(2,1)}, bf16[512,512]{1,0:T(8,128)(2,1)}, u32[]{:S(2)}, u32[]{:S(2)}) collective-permute-start(bf16[512,512]{1,0:T(8,128)(2,1)} %refs_19_.1), channel_id=1, source_target_pairs={{6,0},{7,1},{14,8},{15,9},{22,16},{23,17},{30,24},{31,25}} | collective-permute-start | bytes 1572872 | tf_op jit(solution)/shard_map/ppermute | solution.py:400
  1.6 0.7 reduce-precision_convert_fusion.1
  2.3 1.1 pad_maximum_fusion
  3.4 1.3 collective-permute-start
  4.7 0.8 dynamic-slice_bitcast_fusion.2
  5.6 1.6 %collective-permute-start.3 = (bf16[256,512]{1,0:T(8,128)(2,1)}, bf16[256,512]{1,0:T(8,128)(2,1)S(1)}, u32[]{:S(2)}, u32[]{:S(2)}) collective-permute-start(bf16[256,512]{1,0:T(8,128)(2,1)} %get-tuple-element.34), channel_id=1, source_target_pairs={{2,2},{3,18},{4,4},{5,20},{6,6},{7,22},{10,10},{11,26},{12,12},{13... | collective-permute-start | bytes 786440 | tf_op jit(solution)/shard_map/ppermute | solution.py:400
  7.2 5.5 %collective-permute-start.6 = (bf16[256,512]{1,0:T(8,128)(2,1)}, bf16[256,512]{1,0:T(8,128)(2,1)}, u32[]{:S(2)}, u32[]{:S(2)}) collective-permute-start(bf16[256,512]{1,0:T(8,128)(2,1)} %get-tuple-element.33), channel_id=1, source_target_pairs={{2,11},{3,27},{4,13},{5,29},{6,15},{7,31},{10,3},{11,19},{12,5},{1... | collective-permute-start | bytes 786440 | tf_op jit(solution)/shard_map/ppermute | solution.py:400
  12.6 1.9 %collective-permute-start.4 = (bf16[256,512]{1,0:T(8,128)(2,1)}, bf16[256,512]{1,0:T(8,128)(2,1)}, u32[]{:S(2)}, u32[]{:S(2)}) collective-permute-start(bf16[256,512]{1,0:T(8,128)(2,1)} %get-tuple-element.33), channel_id=1, source_target_pairs={{2,10},{3,26},{4,12},{5,28},{6,14},{7,30},{10,2},{11,18},{12,4},{1... | collective-permute-start | bytes 786440 | tf_op jit(solution)/shard_map/ppermute | solution.py:400
  14.6 0.0 collective-permute-done.3
  14.6 4.3 %collective-permute-start.5 = (bf16[256,512]{1,0:T(8,128)(2,1)}, bf16[256,512]{1,0:T(8,128)(2,1)S(1)}, u32[]{:S(2)}, u32[]{:S(2)}) collective-permute-start(bf16[256,512]{1,0:T(8,128)(2,1)} %get-tuple-element.34), channel_id=1, source_target_pairs={{2,3},{3,19},{4,5},{5,21},{6,7},{7,23},{10,11},{11,27},{12,13},{13... | collective-permute-start | bytes 786440 | tf_op jit(solution)/shard_map/ppermute | solution.py:400
  18.9 0.0 collective-permute-done.1
  19.0 1.1 dynamic-slice_bitcast_fusion.1
  20.0 0.7 collective-permute-start.7
  20.7 0.0 collective-permute-done
  20.7 0.1 broadcast_select_fusion
  20.9 3.5 %collective-permute-start.2 = (bf16[528,512]{1,0:T(8,128)(2,1)S(1)}, bf16[528,512]{1,0:T(8,128)(2,1)S(1)}, u32[]{:S(2)}, u32[]{:S(2)}) collective-permute-start(bf16[528,512]{1,0:T(8,128)(2,1)S(1)} %broadcast_select_fusion), channel_id=1, source_target_pairs={{0,2},{1,3},{4,6},{5,7},{8,10},{9,11},{12,14},{13,15},{16,18},{17,... | collective-permute-start | bytes 1622024 | tf_op jit(solution)/shard_map/ppermute | solution.py:400
  24.4 0.0 collective-permute-done.4
  24.4 1.0 constant_dynamic-update-slice_fusion.2
  25.3 7.4 %collective-permute-done.5 = bf16[256,512]{1,0:T(8,128)(2,1)S(1)} collective-permute-done((bf16[256,512]{1,0:T(8,128)(2,1)}, bf16[256,512]{1,0:T(8,128)(2,1)S(1)}, u32[]{:S(2)}, u32[]{:S(2)}) %collective-permute-start.5) | collective-permute-done | bytes 262176 | tf_op jit(solution)/shard_map/ppermute | solution.py:400
  32.8 0.0 collective-permute-done.6
  32.8 1.0 constant_dynamic-update-slice_fusion.refs_14_
  33.8 0.0 collective-permute-done.7
  33.8 0.9 maximum_select_fusion
  34.7 0.1 broadcast_select_fusion.1.refs_0_.refs_4_
  34.8 2.2 %collective-permute-start.11 = (bf16[528,512]{1,0:T(8,128)(2,1)S(1)}, bf16[528,512]{1,0:T(8,128)(2,1)S(1)}, u32[]{:S(2)}, u32[]{:S(2)}) collective-permute-start(bf16[528,512]{1,0:T(8,128)(2,1)S(1)} %broadcast_select_fusion.1.refs_0_.refs_4_), channel_id=1, source_target_pairs={{0,1},{1,0},{2,3},{3,2},{4,5},{5,4},{6,7},{7,6},{8,9},{9,8},{10,11... | collective-permute-start | bytes 1622024 | tf_op jit(solution)/shard_map/ppermute | solution.py:400
  36.9 0.1 collective-permute-start.9
  37.0 1.9 %collective-permute-start.17 = (bf16[1024,512]{1,0:T(8,128)(2,1)S(1)}, bf16[1024,512]{1,0:T(8,128)(2,1)}, u32[]{:S(2)}, u32[]{:S(2)}) collective-permute-start(bf16[1024,512]{1,0:T(8,128)(2,1)S(1)} %constant_dynamic-update-slice_fusion.refs_14_), channel_id=1, source_target_pairs={{2,0},{3,1},{4,2},{5,3},{6,4},{7,5},{10,8},{11,9},{12,10},{13,11},... | collective-permute-start | bytes 3145736 | tf_op jit(solution)/shard_map/ppermute | solution.py:400
  38.9 2.9 %collective-permute-start.8 = (bf16[528,512]{1,0:T(8,128)(2,1)S(1)}, bf16[528,512]{1,0:T(8,128)(2,1)S(1)}, u32[]{:S(2)}, u32[]{:S(2)}) collective-permute-start(bf16[528,512]{1,0:T(8,128)(2,1)S(1)} %broadcast_select_fusion.1.refs_0_.refs_4_), channel_id=1, source_target_pairs={{0,8},{1,9},{2,10},{3,11},{4,12},{5,13},{6,14},{7,15},{8,0},{9,1},... | collective-permute-start | bytes 1622024 | tf_op jit(solution)/shard_map/ppermute | solution.py:400
  41.8 6.2 %collective-permute-done.11.refs_4_.refs_8_ = bf16[528,512]{1,0:T(8,128)(2,1)S(1)} collective-permute-done((bf16[528,512]{1,0:T(8,128)(2,1)S(1)}, bf16[528,512]{1,0:T(8,128)(2,1)S(1)}, u32[]{:S(2)}, u32[]{:S(2)}) %collective-permute-start.11) | collective-permute-done | bytes 540704 | tf_op jit(solution)/shard_map/ppermute | solution.py:400
  48.1 2.1 %collective-permute-start.12 = (bf16[528,512]{1,0:T(8,128)(2,1)S(1)}, bf16[528,512]{1,0:T(8,128)(2,1)S(1)}, u32[]{:S(2)}, u32[]{:S(2)}) collective-permute-start(bf16[528,512]{1,0:T(8,128)(2,1)S(1)} %collective-permute-done.11.refs_4_.refs_8_), channel_id=1, source_target_pairs={{0,8},{1,9},{2,10},{3,11},{4,12},{5,13},{6,14},{7,15},{8,0},{9,1},... | collective-permute-start | bytes 1622024 | tf_op jit(solution)/shard_map/ppermute | solution.py:400
  50.2 1.5 %collective-permute-start.18 = (bf16[512,512]{1,0:T(8,128)(2,1)S(1)}, bf16[512,512]{1,0:T(8,128)(2,1)S(1)}, u32[]{:S(2)}, u32[]{:S(2)}) collective-permute-start(bf16[512,512]{1,0:T(8,128)(2,1)S(1)} %copy-done), channel_id=1, source_target_pairs={{0,8},{1,9},{2,10},{3,11},{4,12},{5,13},{6,14},{7,15},{8,0},{9,1},... | collective-permute-start | bytes 1572872 | tf_op jit(solution)/shard_map/ppermute | solution.py:400
  51.6 0.0 collective-permute-start.10
  51.6 0.0 collective-permute-done.8.refs_1_.refs_5_
  51.6 0.8 copy-done.2
  52.5 0.6 collective-permute-start.15
  53.0 0.0 collective-permute-done.12.refs_5_.refs_9_
  53.0 0.8 copy-done.5
  53.9 1.0 collective-permute-start.13
  54.9 6.8 %collective-permute-done.17.refs_15_ = bf16[1024,512]{1,0:T(8,128)(2,1)} collective-permute-done((bf16[1024,512]{1,0:T(8,128)(2,1)S(1)}, bf16[1024,512]{1,0:T(8,128)(2,1)}, u32[]{:S(2)}, u32[]{:S(2)}) %collective-permute-start.17) | collective-permute-done | bytes 1048608 | tf_op jit(solution)/shard_map/ppermute | solution.py:400
  61.7 1.9 %collective-permute-start.20 = (bf16[1024,512]{1,0:T(8,128)(2,1)S(1)}, bf16[1024,512]{1,0:T(8,128)(2,1)}, u32[]{:S(2)}, u32[]{:S(2)}) collective-permute-start(bf16[1024,512]{1,0:T(8,128)(2,1)S(1)} %constant_dynamic-update-slice_fusion.refs_14_), channel_id=1, source_target_pairs={{2,4},{3,5},{4,6},{5,7},{10,12},{11,13},{12,14},{13,15},{18,20},{1... | collective-permute-start | bytes 3145736 | tf_op jit(solution)/shard_map/ppermute | solution.py:400
  63.7 0.0 collective-permute-done.15.refs_8_.refs_12_
  63.7 0.0 collective-permute-done.18.refs_20_
  63.7 0.8 copy-done.11
  64.5 0.0 collective-permute-done.13.refs_6_.refs_10_
  64.5 5.3 %collective-permute-start.19 = (bf16[1024,512]{1,0:T(8,128)(2,1)}, bf16[1024,512]{1,0:T(8,128)(2,1)}, u32[]{:S(2)}, u32[]{:S(2)}) collective-permute-start(bf16[1024,512]{1,0:T(8,128)(2,1)} %collective-permute-done.17.refs_15_), channel_id=1, source_target_pairs={{2,0},{3,1},{4,2},{5,3},{10,8},{11,9},{12,10},{13,11},{18,16},{19,... | collective-permute-start | bytes 3145736 | tf_op jit(solution)/shard_map/ppermute | solution.py:400
  69.8 1.7 %collective-permute-start.21 = (bf16[1024,512]{1,0:T(8,128)(2,1)S(1)}, bf16[1024,512]{1,0:T(8,128)(2,1)}, u32[]{:S(2)}, u32[]{:S(2)}) collective-permute-start(bf16[1024,512]{1,0:T(8,128)(2,1)S(1)} %constant_dynamic-update-slice_fusion.refs_14_), channel_id=1, source_target_pairs={{2,6},{3,7},{10,14},{11,15},{18,22},{19,23},{26,30},{27,31}} | collective-permute-start | bytes 3145736 | tf_op jit(solution)/shard_map/ppermute | solution.py:400
  71.5 3.4 %collective-permute-start.16 = (bf16[272,512]{1,0:T(8,128)(2,1)S(1)}, bf16[272,512]{1,0:T(8,128)(2,1)}, u32[]{:S(2)}, u32[]{:S(2)}) collective-permute-start(bf16[272,512]{1,0:T(8,128)(2,1)S(1)} %collective-permute-done.15.refs_8_.refs_12_), channel_id=1, source_target_pairs={{0,8},{1,9},{2,10},{3,11},{4,12},{5,13},{6,14},{7,15},{8,0},{9,1},... | collective-permute-start | bytes 835592 | tf_op jit(solution)/shard_map/ppermute | solution.py:400
  74.9 0.0 collective-permute-done.10.refs_3_.refs_7_
  75.0 0.8 copy-done.8
  75.8 0.0 collective-permute-start.14
  75.8 0.1 stack.95.place_ref
  75.9 0.2 stack.92.place_ref
  76.0 0.0 copy-start.1
  76.0 0.2 collective-permute-done.16.refs_9_.refs_13_
  76.3 1.7 %collective-permute-start.23 = (bf16[512,512]{1,0:T(8,128)(2,1)}, bf16[512,512]{1,0:T(8,128)(2,1)S(1)}, u32[]{:S(2)}, u32[]{:S(2)}) collective-permute-start(bf16[512,512]{1,0:T(8,128)(2,1)} %maximum_select_fusion), channel_id=1, source_target_pairs={{0,1},{1,17},{2,26},{3,27},{4,28},{5,29},{6,30},{7,31},{8,9},{9,25... | collective-permute-start | bytes 1572872 | tf_op jit(solution)/shard_map/ppermute | solution.py:400
  77.9 3.0 %collective-permute-start.22 = (bf16[512,512]{1,0:T(8,128)(2,1)}, bf16[512,512]{1,0:T(8,128)(2,1)S(1)}, u32[]{:S(2)}, u32[]{:S(2)}) collective-permute-start(bf16[512,512]{1,0:T(8,128)(2,1)} %maximum_select_fusion), channel_id=1, source_target_pairs={{0,0},{1,16},{2,18},{3,19},{4,20},{5,21},{6,22},{7,23},{8,8},{9,24... | collective-permute-start | bytes 1572872 | tf_op jit(solution)/shard_map/ppermute | solution.py:400
  80.9 0.0 copy-start.3
  81.0 1.0 copy-done.3
  82.0 1.0 copy-done.6
  83.0 1.0 copy-done.9
  84.1 34.3 %factor_panel.1 = (bf16[1024,1024]{1,0:T(8,128)(2,1)}, bf16[1024,1024]{1,0:T(8,128)(2,1)}, bf16[1024,128]{1,0:T(8,128)(2,1)}, bf16[1024,128]{1,0:T(8,128)(2,1)}) custom-call(s32[24]{0:T(128)S(1)} %stack.95.place_ref, bf16[528,512]{1,0:T(8,128)(2,1)S(1)} %broadcast_select_fusion.1.refs_0_.refs_4_, bf16[528,512]{1,0:T(8,128)(2,1)S(1)} %copy-done.3, ...), custom_call_target="tpu_custom_call" | custom-call | flops 8000000000 | bytes 1048576 | tf_op jit(solution)/shard_map/factor_panel/pallas_call | solution.py:242
  118.4 0.0 collective-permute-done.20.refs_17_
  118.5 0.0 collective-permute-done.19.refs_16_
  118.5 21.8 %finish_tile.1 = f32[1024,512]{1,0:T(8,128)} custom-call(s32[78]{0:T(128)S(1)} %stack.92.place_ref, f32[1,512]{1,0:T(1,128)S(1)} %bitcast.39, bf16[1024,1024]{1,0:T(8,128)(2,1)} %get-tuple-element.22.refs_0_, bf16[1024,1024]{1,0:T(8,128)(2,1)} %get-tuple-element.23.refs_1_, bf16[1024,128]{1,0:T(8,128)(2,1)} %get-tuple-element.24.refs_2_, ...), custom_call_target="tpu_custom_call" | custom-call | flops 20000000000 | bytes 25165824 | tf_op jit(solution)/shard_map/finish_tile/pallas_call | solution.py:360
  (31 shorter events, 0.1 us)
Async XLA Ops:
  0.0 4.7 %copy-start = (bf16[512,512]{1,0:T(8,128)(2,1)S(1)}, bf16[512,512]{1,0:T(8,128)(2,1)}, u32[]{:S(2)}) copy-start(bf16[512,512]{1,0:T(8,128)(2,1)} %refs_19_.1) | copy-start | bytes 1572868
  0.0 18.9 %collective-permute-start.1 = (bf16[512,512]{1,0:T(8,128)(2,1)}, bf16[512,512]{1,0:T(8,128)(2,1)}, u32[]{:S(2)}, u32[]{:S(2)}) collective-permute-start(bf16[512,512]{1,0:T(8,128)(2,1)} %refs_19_.1), channel_id=1, source_target_pairs={{6,0},{7,1},{14,8},{15,9},{22,16},{23,17},{30,24},{31,25}} | collective-permute-start | bytes 1572872 | tf_op jit(solution)/shard_map/ppermute | solution.py:400
  3.4 17.3 %collective-permute-start = (bf16[528,512]{1,0:T(8,128)(2,1)S(1)}, bf16[528,512]{1,0:T(8,128)(2,1)S(1)}, u32[]{:S(2)}, u32[]{:S(2)}) collective-permute-start(bf16[528,512]{1,0:T(8,128)(2,1)S(1)} %pad_maximum_fusion), channel_id=1, source_target_pairs={{0,4},{1,5},{8,12},{9,13},{16,20},{17,21},{24,28},{25,29}} | collective-permute-start | bytes 1622024 | tf_op jit(solution)/shard_map/ppermute | solution.py:400
  5.6 9.0 %collective-permute-start.3 = (bf16[256,512]{1,0:T(8,128)(2,1)}, bf16[256,512]{1,0:T(8,128)(2,1)S(1)}, u32[]{:S(2)}, u32[]{:S(2)}) collective-permute-start(bf16[256,512]{1,0:T(8,128)(2,1)} %get-tuple-element.34), channel_id=1, source_target_pairs={{2,2},{3,18},{4,4},{5,20},{6,6},{7,22},{10,10},{11,26},{12,12},{13... | collective-permute-start | bytes 786440 | tf_op jit(solution)/shard_map/ppermute | solution.py:400
  7.2 25.6 %collective-permute-start.6 = (bf16[256,512]{1,0:T(8,128)(2,1)}, bf16[256,512]{1,0:T(8,128)(2,1)}, u32[]{:S(2)}, u32[]{:S(2)}) collective-permute-start(bf16[256,512]{1,0:T(8,128)(2,1)} %get-tuple-element.33), channel_id=1, source_target_pairs={{2,11},{3,27},{4,13},{5,29},{6,15},{7,31},{10,3},{11,19},{12,5},{1... | collective-permute-start | bytes 786440 | tf_op jit(solution)/shard_map/ppermute | solution.py:400
  12.6 11.7 %collective-permute-start.4 = (bf16[256,512]{1,0:T(8,128)(2,1)}, bf16[256,512]{1,0:T(8,128)(2,1)}, u32[]{:S(2)}, u32[]{:S(2)}) collective-permute-start(bf16[256,512]{1,0:T(8,128)(2,1)} %get-tuple-element.33), channel_id=1, source_target_pairs={{2,10},{3,26},{4,12},{5,28},{6,14},{7,30},{10,2},{11,18},{12,4},{1... | collective-permute-start | bytes 786440 | tf_op jit(solution)/shard_map/ppermute | solution.py:400
  14.6 18.1 %collective-permute-start.5 = (bf16[256,512]{1,0:T(8,128)(2,1)}, bf16[256,512]{1,0:T(8,128)(2,1)S(1)}, u32[]{:S(2)}, u32[]{:S(2)}) collective-permute-start(bf16[256,512]{1,0:T(8,128)(2,1)} %get-tuple-element.34), channel_id=1, source_target_pairs={{2,3},{3,19},{4,5},{5,21},{6,7},{7,23},{10,11},{11,27},{12,13},{13... | collective-permute-start | bytes 786440 | tf_op jit(solution)/shard_map/ppermute | solution.py:400
  20.0 13.7 %collective-permute-start.7 = (bf16[256,512]{1,0:T(8,128)(2,1)S(1)}, bf16[256,512]{1,0:T(8,128)(2,1)S(1)}, u32[]{:S(2)}, u32[]{:S(2)}) collective-permute-start(bf16[256,512]{1,0:T(8,128)(2,1)S(1)} %get-tuple-element.32), channel_id=1, source_target_pairs={{0,8},{1,9},{8,0},{9,1},{16,24},{17,25},{24,16},{25,17}} | collective-permute-start | bytes 786440 | tf_op jit(solution)/shard_map/ppermute | solution.py:400
  20.9 13.8 %collective-permute-start.2 = (bf16[528,512]{1,0:T(8,128)(2,1)S(1)}, bf16[528,512]{1,0:T(8,128)(2,1)S(1)}, u32[]{:S(2)}, u32[]{:S(2)}) collective-permute-start(bf16[528,512]{1,0:T(8,128)(2,1)S(1)} %broadcast_select_fusion), channel_id=1, source_target_pairs={{0,2},{1,3},{4,6},{5,7},{8,10},{9,11},{12,14},{13,15},{16,18},{17,... | collective-permute-start | bytes 1622024 | tf_op jit(solution)/shard_map/ppermute | solution.py:400
  34.8 13.3 %collective-permute-start.11 = (bf16[528,512]{1,0:T(8,128)(2,1)S(1)}, bf16[528,512]{1,0:T(8,128)(2,1)S(1)}, u32[]{:S(2)}, u32[]{:S(2)}) collective-permute-start(bf16[528,512]{1,0:T(8,128)(2,1)S(1)} %broadcast_select_fusion.1.refs_0_.refs_4_), channel_id=1, source_target_pairs={{0,1},{1,0},{2,3},{3,2},{4,5},{5,4},{6,7},{7,6},{8,9},{9,8},{10,11... | collective-permute-start | bytes 1622024 | tf_op jit(solution)/shard_map/ppermute | solution.py:400
  36.9 13.2 %collective-permute-start.9 = (bf16[528,512]{1,0:T(8,128)(2,1)S(1)}, bf16[528,512]{1,0:T(8,128)(2,1)S(1)}, u32[]{:S(2)}, u32[]{:S(2)}) collective-permute-start(bf16[528,512]{1,0:T(8,128)(2,1)S(1)} %broadcast_select_fusion.1.refs_0_.refs_4_), channel_id=1, source_target_pairs={{0,16},{1,17},{2,18},{3,19},{4,20},{5,21},{6,22},{7,23},{8,24},{9,... | collective-permute-start | bytes 1622024 | tf_op jit(solution)/shard_map/ppermute | solution.py:400
  37.0 24.7 %collective-permute-start.17 = (bf16[1024,512]{1,0:T(8,128)(2,1)S(1)}, bf16[1024,512]{1,0:T(8,128)(2,1)}, u32[]{:S(2)}, u32[]{:S(2)}) collective-permute-start(bf16[1024,512]{1,0:T(8,128)(2,1)S(1)} %constant_dynamic-update-slice_fusion.refs_14_), channel_id=1, source_target_pairs={{2,0},{3,1},{4,2},{5,3},{6,4},{7,5},{10,8},{11,9},{12,10},{13,11},... | collective-permute-start | bytes 3145736 | tf_op jit(solution)/shard_map/ppermute | solution.py:400
  38.9 12.7 %collective-permute-start.8 = (bf16[528,512]{1,0:T(8,128)(2,1)S(1)}, bf16[528,512]{1,0:T(8,128)(2,1)S(1)}, u32[]{:S(2)}, u32[]{:S(2)}) collective-permute-start(bf16[528,512]{1,0:T(8,128)(2,1)S(1)} %broadcast_select_fusion.1.refs_0_.refs_4_), channel_id=1, source_target_pairs={{0,8},{1,9},{2,10},{3,11},{4,12},{5,13},{6,14},{7,15},{8,0},{9,1},... | collective-permute-start | bytes 1622024 | tf_op jit(solution)/shard_map/ppermute | solution.py:400
  48.1 5.0 %collective-permute-start.12 = (bf16[528,512]{1,0:T(8,128)(2,1)S(1)}, bf16[528,512]{1,0:T(8,128)(2,1)S(1)}, u32[]{:S(2)}, u32[]{:S(2)}) collective-permute-start(bf16[528,512]{1,0:T(8,128)(2,1)S(1)} %collective-permute-done.11.refs_4_.refs_8_), channel_id=1, source_target_pairs={{0,8},{1,9},{2,10},{3,11},{4,12},{5,13},{6,14},{7,15},{8,0},{9,1},... | collective-permute-start | bytes 1622024 | tf_op jit(solution)/shard_map/ppermute | solution.py:400
  50.2 13.5 %collective-permute-start.18 = (bf16[512,512]{1,0:T(8,128)(2,1)S(1)}, bf16[512,512]{1,0:T(8,128)(2,1)S(1)}, u32[]{:S(2)}, u32[]{:S(2)}) collective-permute-start(bf16[512,512]{1,0:T(8,128)(2,1)S(1)} %copy-done), channel_id=1, source_target_pairs={{0,8},{1,9},{2,10},{3,11},{4,12},{5,13},{6,14},{7,15},{8,0},{9,1},... | collective-permute-start | bytes 1572872 | tf_op jit(solution)/shard_map/ppermute | solution.py:400
  51.6 23.3 %collective-permute-start.10 = (bf16[528,512]{1,0:T(8,128)(2,1)S(1)}, bf16[528,512]{1,0:T(8,128)(2,1)S(1)}, u32[]{:S(2)}, u32[]{:S(2)}) collective-permute-start(bf16[528,512]{1,0:T(8,128)(2,1)S(1)} %collective-permute-done.9.refs_2_.refs_6_), channel_id=1, source_target_pairs={{0,8},{1,9},{2,10},{3,11},{4,12},{5,13},{6,14},{7,15},{8,0},{9,1},... | collective-permute-start | bytes 1622024 | tf_op jit(solution)/shard_map/ppermute | solution.py:400
  51.6 0.8 copy-start.2
  52.5 11.2 %collective-permute-start.15 = (bf16[272,512]{1,0:T(8,128)(2,1)S(1)}, bf16[272,512]{1,0:T(8,128)(2,1)S(1)}, u32[]{:S(2)}, u32[]{:S(2)}) collective-permute-start(bf16[272,512]{1,0:T(8,128)(2,1)S(1)} %slice.7), channel_id=1, source_target_pairs={{0,16},{1,17},{2,18},{3,19},{4,20},{5,21},{6,22},{7,23},{8,24},{9,... | collective-permute-start | bytes 835592 | tf_op jit(solution)/shard_map/ppermute | solution.py:400
  53.0 0.8 copy-start.5
  53.9 10.6 %collective-permute-start.13 = (bf16[256,512]{1,0:T(8,128)(2,1)S(1)}, bf16[256,512]{1,0:T(8,128)(2,1)}, u32[]{:S(2)}, u32[]{:S(2)}) collective-permute-start(bf16[256,512]{1,0:T(8,128)(2,1)S(1)} %slice.6), channel_id=1, source_target_pairs={{0,1},{1,0},{2,3},{3,2},{4,5},{5,4},{6,7},{7,6},{8,9},{9,8},{10,11... | collective-permute-start | bytes 786440 | tf_op jit(solution)/shard_map/ppermute | solution.py:400
  61.7 56.7 %collective-permute-start.20 = (bf16[1024,512]{1,0:T(8,128)(2,1)S(1)}, bf16[1024,512]{1,0:T(8,128)(2,1)}, u32[]{:S(2)}, u32[]{:S(2)}) collective-permute-start(bf16[1024,512]{1,0:T(8,128)(2,1)S(1)} %constant_dynamic-update-slice_fusion.refs_14_), channel_id=1, source_target_pairs={{2,4},{3,5},{4,6},{5,7},{10,12},{11,13},{12,14},{13,15},{18,20},{1... | collective-permute-start | bytes 3145736 | tf_op jit(solution)/shard_map/ppermute | solution.py:400
  63.7 0.8 copy-start.11
  64.5 54.0 %collective-permute-start.19 = (bf16[1024,512]{1,0:T(8,128)(2,1)}, bf16[1024,512]{1,0:T(8,128)(2,1)}, u32[]{:S(2)}, u32[]{:S(2)}) collective-permute-start(bf16[1024,512]{1,0:T(8,128)(2,1)} %collective-permute-done.17.refs_15_), channel_id=1, source_target_pairs={{2,0},{3,1},{4,2},{5,3},{10,8},{11,9},{12,10},{13,11},{18,16},{19,... | collective-permute-start | bytes 3145736 | tf_op jit(solution)/shard_map/ppermute | solution.py:400
  69.8 48.7 %collective-permute-start.21 = (bf16[1024,512]{1,0:T(8,128)(2,1)S(1)}, bf16[1024,512]{1,0:T(8,128)(2,1)}, u32[]{:S(2)}, u32[]{:S(2)}) collective-permute-start(bf16[1024,512]{1,0:T(8,128)(2,1)S(1)} %constant_dynamic-update-slice_fusion.refs_14_), channel_id=1, source_target_pairs={{2,6},{3,7},{10,14},{11,15},{18,22},{19,23},{26,30},{27,31}} | collective-permute-start | bytes 3145736 | tf_op jit(solution)/shard_map/ppermute | solution.py:400
  71.5 4.7 %collective-permute-start.16 = (bf16[272,512]{1,0:T(8,128)(2,1)S(1)}, bf16[272,512]{1,0:T(8,128)(2,1)}, u32[]{:S(2)}, u32[]{:S(2)}) collective-permute-start(bf16[272,512]{1,0:T(8,128)(2,1)S(1)} %collective-permute-done.15.refs_8_.refs_12_), channel_id=1, source_target_pairs={{0,8},{1,9},{2,10},{3,11},{4,12},{5,13},{6,14},{7,15},{8,0},{9,1},... | collective-permute-start | bytes 835592 | tf_op jit(solution)/shard_map/ppermute | solution.py:400
  74.9 0.8 copy-start.8
  75.8 2.2 %collective-permute-start.14 = (bf16[256,512]{1,0:T(8,128)(2,1)}, bf16[256,512]{1,0:T(8,128)(2,1)}, u32[]{:S(2)}, u32[]{:S(2)}) collective-permute-start(bf16[256,512]{1,0:T(8,128)(2,1)} %collective-permute-done.13.refs_6_.refs_10_), channel_id=1, source_target_pairs={{0,8},{1,9},{2,10},{3,11},{4,12},{5,13},{6,14},{7,15},{8,0},{9,1},... | collective-permute-start | bytes 786440 | tf_op jit(solution)/shard_map/ppermute | solution.py:400
  76.0 42.5 %copy-start.1 = (f32[512]{0:T(512)S(1)}, f32[512]{0:T(512)}, u32[]{:S(2)}) copy-start(f32[512]{0:T(512)} %param.3) | copy-start | bytes 6148
  76.3 42.2 %collective-permute-start.23 = (bf16[512,512]{1,0:T(8,128)(2,1)}, bf16[512,512]{1,0:T(8,128)(2,1)S(1)}, u32[]{:S(2)}, u32[]{:S(2)}) collective-permute-start(bf16[512,512]{1,0:T(8,128)(2,1)} %maximum_select_fusion), channel_id=1, source_target_pairs={{0,1},{1,17},{2,26},{3,27},{4,28},{5,29},{6,30},{7,31},{8,9},{9,25... | collective-permute-start | bytes 1572872 | tf_op jit(solution)/shard_map/ppermute | solution.py:400
  77.9 40.5 %collective-permute-start.22 = (bf16[512,512]{1,0:T(8,128)(2,1)}, bf16[512,512]{1,0:T(8,128)(2,1)S(1)}, u32[]{:S(2)}, u32[]{:S(2)}) collective-permute-start(bf16[512,512]{1,0:T(8,128)(2,1)} %maximum_select_fusion), channel_id=1, source_target_pairs={{0,0},{1,16},{2,18},{3,19},{4,20},{5,21},{6,22},{7,23},{8,8},{9,24... | collective-permute-start | bytes 1572872 | tf_op jit(solution)/shard_map/ppermute | solution.py:400
  80.9 1.1 copy-start.3
  82.0 1.0 copy-start.6
  83.0 1.0 copy-start.9
  84.1 34.4 %copy-start.4 = (bf16[528,512]{1,0:T(8,128)(2,1)S(1)}, bf16[528,512]{1,0:T(8,128)(2,1)}, u32[]{:S(2)}) copy-start(bf16[528,512]{1,0:T(8,128)(2,1)} %copy-done.2) | copy-start | bytes 1622020
  84.1 34.4 %copy-start.7 = (bf16[528,512]{1,0:T(8,128)(2,1)S(1)}, bf16[528,512]{1,0:T(8,128)(2,1)}, u32[]{:S(2)}) copy-start(bf16[528,512]{1,0:T(8,128)(2,1)} %copy-done.5) | copy-start | bytes 1622020
  84.1 34.4 %copy-start.10 = (bf16[528,512]{1,0:T(8,128)(2,1)S(1)}, bf16[528,512]{1,0:T(8,128)(2,1)}, u32[]{:S(2)}) copy-start(bf16[528,512]{1,0:T(8,128)(2,1)} %copy-done.8) | copy-start | bytes 1622020
  84.1 34.4 %copy-start.12 = (bf16[512,512]{1,0:T(8,128)(2,1)S(1)}, bf16[512,512]{1,0:T(8,128)(2,1)}, u32[]{:S(2)}) copy-start(bf16[512,512]{1,0:T(8,128)(2,1)} %copy-done.11) | copy-start | bytes 1572868

commit v9 on v7

--- a/solution.py
+++ b/solution.py
@@ -463,13 +463,15 @@
         shared = after(shared, quarters, mixed)
         pair_side, way_side = over_pair(shared), over_way(shared)
         own_twin, way_twin = over_core(shared), over_core(way_side)
-        diagonal = [over_way(after(pair_side, own_twin, way_twin)[:half]), over_pair(after(way_side, own_twin)[half:])]
+        diagonal = exchange(
+            jnp.where(core == 0, after(pair_side, own_twin), after(way_side, own_twin)),
+            lambda p, h, s, w: (p, h, s, 1 - w) if h == 0 else (1 - p, h, s, w),
+        )
         for from_pair, from_way, first_row, piece in (
             (pair, way, 0, shared),
             (1 - pair, way, 0, pair_side),
             (pair, 1 - way, 0, way_side),
-            (1 - pair, 1 - way, 0, diagonal[0]),
-            (1 - pair, 1 - way, half, diagonal[1]),
+            (1 - pair, 1 - way, 0, diagonal),
         ):
             twin = own_twin if piece is shared else way_twin if piece is way_side else over_core(piece)
             for from_core, value in ((core, piece), (1 - core, twin)):
@@ -480,7 +482,7 @@
                 panel_views.append((len(panel), 0, count, False))
                 panel_place += [from_way * width + first_row, (from_pair * CORES + from_core) * users]
                 panel.append(value)
-        crossed = [pair_side, way_side, *diagonal]
+        crossed = [pair_side, way_side, diagonal]
         down = exchange(quarters, lambda p, h, s, w: (p, h, s - 1, w), lambda p, h, s, w: s > 0)
         up = exchange(quarters, lambda p, h, s, w: (p, h, s + 1, w), lambda p, h, s, w: 0 < s < SPAN - 1)
         down_held, up_held, mixed = lax.optimization_barrier(

time: 140 us -> 136 us (0.971)
  waiting for transfers between devices: 20.5 us -> 27.9 us
  starting transfers between devices: 51.1 us -> 44.2 us
  local copies, waits for them, and re-layouts: 7.89 us -> 3.37 us
    ppermute x24 -> x22, waiting for transfers between devices: 20.5 us -> 27.9 us  [exchange(): return lax.ppermute(value, ('row', 'col'), perm)]
    ppermute x24 -> x22, starting transfers between devices: 51.1 us -> 44.2 us  [exchange(): return lax.ppermute(value, ('row', 'col'), perm)]
    unnamed x19 -> x7, local copies, waits for them, and re-layouts: 4.7 us -> 1.02 us
  transfers between devices with their start and end apart: 24 -> 22, of which waited for: 5 -> 6; matrix products, arithmetic and copies ran while one was open for 5% -> 5% of each run, Pallas kernels for 25% -> 25%
where the time goes in v9:
time: 136 us
  Pallas kernels  56.8 us (42%)
  starting transfers between devices  44.2 us (32%)
  waiting for transfers between devices  27.9 us (21%)
  local copies, waits for them, and re-layouts  3.37 us (2%)
  other arithmetic  2.97 us (2%)
    ppermute x22, starting transfers between devices, exchange(): return lax.ppermute(value, ('row', 'col'), perm)  44.2 us
    pallas_call x1, Pallas kernels, factor_panel(): pl.pallas_call(functools.partial(panel_kernel, views, len(pieces), width)...  34.5 us
    ppermute x22, waiting for transfers between devices, exchange(): return lax.ppermute(value, ('row', 'col'), perm)  27.9 us
    pallas_call x1, Pallas kernels, finish_tile(): pl.pallas_call(functools.partial(tile_kernel, len(pieces), counts, views)...  22.3 us
  transfers between devices with their start and end apart: 22, of which 6 were waited for; matrix products, arithmetic and copies ran while one was open for 5% of the time, Pallas kernels for 25%

profile of v9, /device:TPU:17, one launch (start us, length us, event | category | flops | bytes accessed | tf_op | source)
XLA Modules:
  0.0 135.8 jit_solution(12823455249025597086)
XLA Ops:
  0.0 0.0 copy-start
  0.0 1.6 %collective-permute-start.1 = (bf16[512,512]{1,0:T(8,128)(2,1)}, bf16[512,512]{1,0:T(8,128)(2,1)}, u32[]{:S(2)}, u32[]{:S(2)}) collective-permute-start(bf16[512,512]{1,0:T(8,128)(2,1)} %refs_17_.1), channel_id=1, source_target_pairs={{6,0},{7,1},{14,8},{15,9},{22,16},{23,17},{30,24},{31,25}} | collective-permute-start | bytes 1572872 | tf_op jit(solution)/shard_map/ppermute | solution.py:400
  1.6 0.7 reduce-precision_convert_fusion.1
  2.3 1.1 pad_maximum_fusion
  3.4 1.3 collective-permute-start
  4.7 0.0 copy-done
  4.8 0.7 collective-permute-start.3
  5.5 6.4 %collective-permute-start.6 = (bf16[256,512]{1,0:T(8,128)(2,1)S(1)}, bf16[256,512]{1,0:T(8,128)(2,1)}, u32[]{:S(2)}, u32[]{:S(2)}) collective-permute-start(bf16[256,512]{1,0:T(8,128)(2,1)S(1)} %get-tuple-element.31), channel_id=1, source_target_pairs={{2,11},{3,27},{4,13},{5,29},{6,15},{7,31},{10,3},{11,19},{12,5},{1... | collective-permute-start | bytes 786440 | tf_op jit(solution)/shard_map/ppermute | solution.py:400
  11.9 1.9 %collective-permute-start.4 = (bf16[256,512]{1,0:T(8,128)(2,1)S(1)}, bf16[256,512]{1,0:T(8,128)(2,1)}, u32[]{:S(2)}, u32[]{:S(2)}) collective-permute-start(bf16[256,512]{1,0:T(8,128)(2,1)S(1)} %get-tuple-element.31), channel_id=1, source_target_pairs={{2,10},{3,26},{4,12},{5,28},{6,14},{7,30},{10,2},{11,18},{12,4},{1... | collective-permute-start | bytes 786440 | tf_op jit(solution)/shard_map/ppermute | solution.py:400
  13.8 0.0 collective-permute-done.3
  13.9 4.1 %collective-permute-start.5 = (bf16[256,512]{1,0:T(8,128)(2,1)S(1)}, bf16[256,512]{1,0:T(8,128)(2,1)S(1)}, u32[]{:S(2)}, u32[]{:S(2)}) collective-permute-start(bf16[256,512]{1,0:T(8,128)(2,1)S(1)} %get-tuple-element.32), channel_id=1, source_target_pairs={{2,3},{3,19},{4,5},{5,21},{6,7},{7,23},{10,11},{11,27},{12,13},{13... | collective-permute-start | bytes 786440 | tf_op jit(solution)/shard_map/ppermute | solution.py:400
  18.0 0.0 collective-permute-done.1
  18.0 1.1 dynamic-slice_bitcast_fusion.1
  19.1 0.7 collective-permute-start.7
  19.7 0.0 collective-permute-done
  19.7 0.1 broadcast_select_fusion.1
  19.9 3.5 %collective-permute-start.2 = (bf16[528,512]{1,0:T(8,128)(2,1)S(1)}, bf16[528,512]{1,0:T(8,128)(2,1)S(1)}, u32[]{:S(2)}, u32[]{:S(2)}) collective-permute-start(bf16[528,512]{1,0:T(8,128)(2,1)S(1)} %broadcast_select_fusion.1), channel_id=1, source_target_pairs={{0,2},{1,3},{4,6},{5,7},{8,10},{9,11},{12,14},{13,15},{16,18},{17,... | collective-permute-start | bytes 1622024 | tf_op jit(solution)/shard_map/ppermute | solution.py:400
  23.4 0.0 collective-permute-done.4
  23.4 1.0 constant_dynamic-update-slice_fusion.2
  24.4 7.5 %collective-permute-done.5 = bf16[256,512]{1,0:T(8,128)(2,1)S(1)} collective-permute-done((bf16[256,512]{1,0:T(8,128)(2,1)S(1)}, bf16[256,512]{1,0:T(8,128)(2,1)S(1)}, u32[]{:S(2)}, u32[]{:S(2)}) %collective-permute-start.5) | collective-permute-done | bytes 262176 | tf_op jit(solution)/shard_map/ppermute | solution.py:400
  31.9 0.0 collective-permute-done.6
  31.9 1.0 constant_dynamic-update-slice_fusion.refs_12_
  32.8 0.0 collective-permute-done.7
  32.8 0.9 maximum_select_fusion
  33.8 0.0 collective-permute-done.2
  33.8 0.1 broadcast_select_fusion.2.refs_0_.refs_4_
  33.8 2.2 %collective-permute-start.11 = (bf16[528,512]{1,0:T(8,128)(2,1)S(1)}, bf16[528,512]{1,0:T(8,128)(2,1)S(1)}, u32[]{:S(2)}, u32[]{:S(2)}) collective-permute-start(bf16[528,512]{1,0:T(8,128)(2,1)S(1)} %broadcast_select_fusion.2.refs_0_.refs_4_), channel_id=1, source_target_pairs={{0,1},{1,0},{2,3},{3,2},{4,5},{5,4},{6,7},{7,6},{8,9},{9,8},{10,11... | collective-permute-start | bytes 1622024 | tf_op jit(solution)/shard_map/ppermute | solution.py:400
  36.1 0.7 collective-permute-start.8
  36.7 0.9 collective-permute-start.9
  37.7 4.1 %collective-permute-start.16 = (bf16[1024,512]{1,0:T(8,128)(2,1)S(1)}, bf16[1024,512]{1,0:T(8,128)(2,1)}, u32[]{:S(2)}, u32[]{:S(2)}) collective-permute-start(bf16[1024,512]{1,0:T(8,128)(2,1)S(1)} %constant_dynamic-update-slice_fusion.refs_12_), channel_id=1, source_target_pairs={{2,4},{3,5},{4,6},{5,7},{10,12},{11,13},{12,14},{13,15},{18,20},{1... | collective-permute-start | bytes 3145736 | tf_op jit(solution)/shard_map/ppermute | solution.py:400
  41.8 2.1 %collective-permute-start.15 = (bf16[1024,512]{1,0:T(8,128)(2,1)S(1)}, bf16[1024,512]{1,0:T(8,128)(2,1)}, u32[]{:S(2)}, u32[]{:S(2)}) collective-permute-start(bf16[1024,512]{1,0:T(8,128)(2,1)S(1)} %constant_dynamic-update-slice_fusion.refs_12_), channel_id=1, source_target_pairs={{2,0},{3,1},{4,2},{5,3},{6,4},{7,5},{10,8},{11,9},{12,10},{13,11},... | collective-permute-start | bytes 3145736 | tf_op jit(solution)/shard_map/ppermute | solution.py:400
  43.9 3.4 %collective-permute-done.11.refs_4_.refs_8_ = bf16[528,512]{1,0:T(8,128)(2,1)S(1)} collective-permute-done((bf16[528,512]{1,0:T(8,128)(2,1)S(1)}, bf16[528,512]{1,0:T(8,128)(2,1)S(1)}, u32[]{:S(2)}, u32[]{:S(2)}) %collective-permute-start.11) | collective-permute-done | bytes 540704 | tf_op jit(solution)/shard_map/ppermute | solution.py:400
  47.3 0.0 collective-permute-done.8.refs_1_.refs_5_
  47.3 3.4 %collective-permute-done.9.refs_2_.refs_6_ = bf16[528,512]{1,0:T(8,128)(2,1)S(1)} collective-permute-done((bf16[528,512]{1,0:T(8,128)(2,1)S(1)}, bf16[528,512]{1,0:T(8,128)(2,1)S(1)}, u32[]{:S(2)}, u32[]{:S(2)}) %collective-permute-start.9) | collective-permute-done | bytes 540704 | tf_op jit(solution)/shard_map/ppermute | solution.py:400
  50.8 0.1 broadcast_select_fusion
  50.8 1.0 collective-permute-start.13
  51.8 1.0 collective-permute-start.12
  52.8 0.0 collective-permute-start.10
  52.8 6.7 %collective-permute-done.13.refs_6_.refs_10_ = bf16[528,512]{1,0:T(8,128)(2,1)} collective-permute-done((bf16[528,512]{1,0:T(8,128)(2,1)S(1)}, bf16[528,512]{1,0:T(8,128)(2,1)}, u32[]{:S(2)}, u32[]{:S(2)}) %collective-permute-start.13) | collective-permute-done | bytes 540704 | tf_op jit(solution)/shard_map/ppermute | solution.py:400
  59.5 1.5 %collective-permute-start.14 = (bf16[528,512]{1,0:T(8,128)(2,1)}, bf16[528,512]{1,0:T(8,128)(2,1)}, u32[]{:S(2)}, u32[]{:S(2)}) collective-permute-start(bf16[528,512]{1,0:T(8,128)(2,1)} %collective-permute-done.13.refs_6_.refs_10_), channel_id=1, source_target_pairs={{0,8},{1,9},{2,10},{3,11},{4,12},{5,13},{6,14},{7,15},{8,0},{9,1},... | collective-permute-start | bytes 1622024 | tf_op jit(solution)/shard_map/ppermute | solution.py:400
  61.0 3.1 %collective-permute-done.16.refs_15_ = bf16[1024,512]{1,0:T(8,128)(2,1)} collective-permute-done((bf16[1024,512]{1,0:T(8,128)(2,1)S(1)}, bf16[1024,512]{1,0:T(8,128)(2,1)}, u32[]{:S(2)}, u32[]{:S(2)}) %collective-permute-start.16) | collective-permute-done | bytes 1048608 | tf_op jit(solution)/shard_map/ppermute | solution.py:400
  64.1 3.8 %collective-permute-done.15.refs_13_ = bf16[1024,512]{1,0:T(8,128)(2,1)} collective-permute-done((bf16[1024,512]{1,0:T(8,128)(2,1)S(1)}, bf16[1024,512]{1,0:T(8,128)(2,1)}, u32[]{:S(2)}, u32[]{:S(2)}) %collective-permute-start.15) | collective-permute-done | bytes 1048608 | tf_op jit(solution)/shard_map/ppermute | solution.py:400
  67.9 3.1 %collective-permute-start.17 = (bf16[1024,512]{1,0:T(8,128)(2,1)}, bf16[1024,512]{1,0:T(8,128)(2,1)}, u32[]{:S(2)}, u32[]{:S(2)}) collective-permute-start(bf16[1024,512]{1,0:T(8,128)(2,1)} %collective-permute-done.15.refs_13_), channel_id=1, source_target_pairs={{2,0},{3,1},{4,2},{5,3},{10,8},{11,9},{12,10},{13,11},{18,16},{19,... | collective-permute-start | bytes 3145736 | tf_op jit(solution)/shard_map/ppermute | solution.py:400
  71.0 2.4 %collective-permute-start.18 = (bf16[1024,512]{1,0:T(8,128)(2,1)}, bf16[1024,512]{1,0:T(8,128)(2,1)}, u32[]{:S(2)}, u32[]{:S(2)}) collective-permute-start(bf16[1024,512]{1,0:T(8,128)(2,1)} %collective-permute-done.16.refs_15_), channel_id=1, source_target_pairs={{4,6},{5,7},{12,14},{13,15},{20,22},{21,23},{28,30},{29,31}} | collective-permute-start | bytes 3145736 | tf_op jit(solution)/shard_map/ppermute | solution.py:400
  73.4 0.1 stack.92.place_ref
  73.5 0.2 stack.89.place_ref
  73.6 0.0 copy-start.1
  73.7 0.0 collective-permute-done.12.refs_5_.refs_9_
  73.7 2.2 %collective-permute-start.21 = (bf16[512,512]{1,0:T(8,128)(2,1)}, bf16[512,512]{1,0:T(8,128)(2,1)S(1)}, u32[]{:S(2)}, u32[]{:S(2)}) collective-permute-start(bf16[512,512]{1,0:T(8,128)(2,1)} %maximum_select_fusion), channel_id=1, source_target_pairs={{0,1},{1,17},{2,26},{3,27},{4,28},{5,29},{6,30},{7,31},{8,9},{9,25... | collective-permute-start | bytes 1572872 | tf_op jit(solution)/shard_map/ppermute | solution.py:400
  75.8 0.0 collective-permute-done.10.refs_3_.refs_7_
  75.8 2.8 %collective-permute-start.20 = (bf16[512,512]{1,0:T(8,128)(2,1)}, bf16[512,512]{1,0:T(8,128)(2,1)S(1)}, u32[]{:S(2)}, u32[]{:S(2)}) collective-permute-start(bf16[512,512]{1,0:T(8,128)(2,1)} %maximum_select_fusion), channel_id=1, source_target_pairs={{0,0},{1,16},{2,18},{3,19},{4,20},{5,21},{6,22},{7,23},{8,8},{9,24... | collective-permute-start | bytes 1572872 | tf_op jit(solution)/shard_map/ppermute | solution.py:400
  78.7 0.0 collective-permute-done.14.refs_7_.refs_11_
  78.7 0.1 collective-permute-start.19
  78.8 34.5 %factor_panel.1 = (bf16[1024,1024]{1,0:T(8,128)(2,1)}, bf16[1024,1024]{1,0:T(8,128)(2,1)}, bf16[1024,128]{1,0:T(8,128)(2,1)}, bf16[1024,128]{1,0:T(8,128)(2,1)}) custom-call(s32[20]{0:T(128)S(1)} %stack.92.place_ref, bf16[528,512]{1,0:T(8,128)(2,1)S(1)} %broadcast_select_fusion.2.refs_0_.refs_4_, bf16[528,512]{1,0:T(8,128)(2,1)} %collective-permute-done.8.refs_1_.refs_5_, ...), custom_call_target="tpu_custom_call" | custom-call | flops 8000000000 | bytes 1048576 | tf_op jit(solution)/shard_map/factor_panel/pallas_call | solution.py:242
  113.3 0.0 collective-permute-done.19.refs_18_
  113.3 0.0 collective-permute-done.21.refs_20_
  113.3 0.0 collective-permute-done.20.refs_19_
  113.3 0.0 collective-permute-done.17.refs_14_
  113.3 0.0 collective-permute-done.18.refs_16_
  113.3 0.0 copy-done.1
  113.4 22.3 %finish_tile.1 = f32[1024,512]{1,0:T(8,128)} custom-call(s32[74]{0:T(128)S(1)} %stack.89.place_ref, f32[1,512]{1,0:T(1,128)S(1)} %bitcast.38, bf16[1024,1024]{1,0:T(8,128)(2,1)} %get-tuple-element.21.refs_0_, bf16[1024,1024]{1,0:T(8,128)(2,1)} %get-tuple-element.22.refs_1_, bf16[1024,128]{1,0:T(8,128)(2,1)} %get-tuple-element.23.refs_2_, ...), custom_call_target="tpu_custom_call" | custom-call | flops 20000000000 | bytes 25165824 | tf_op jit(solution)/shard_map/finish_tile/pallas_call | solution.py:360
  (7 shorter events, 0.1 us)
Async XLA Ops:
  0.0 4.7 %copy-start = (bf16[512,512]{1,0:T(8,128)(2,1)S(1)}, bf16[512,512]{1,0:T(8,128)(2,1)}, u32[]{:S(2)}) copy-start(bf16[512,512]{1,0:T(8,128)(2,1)} %refs_17_.1) | copy-start | bytes 1572868
  0.0 18.0 %collective-permute-start.1 = (bf16[512,512]{1,0:T(8,128)(2,1)}, bf16[512,512]{1,0:T(8,128)(2,1)}, u32[]{:S(2)}, u32[]{:S(2)}) collective-permute-start(bf16[512,512]{1,0:T(8,128)(2,1)} %refs_17_.1), channel_id=1, source_target_pairs={{6,0},{7,1},{14,8},{15,9},{22,16},{23,17},{30,24},{31,25}} | collective-permute-start | bytes 1572872 | tf_op jit(solution)/shard_map/ppermute | solution.py:400
  3.4 16.3 %collective-permute-start = (bf16[528,512]{1,0:T(8,128)(2,1)S(1)}, bf16[528,512]{1,0:T(8,128)(2,1)S(1)}, u32[]{:S(2)}, u32[]{:S(2)}) collective-permute-start(bf16[528,512]{1,0:T(8,128)(2,1)S(1)} %pad_maximum_fusion), channel_id=1, source_target_pairs={{0,4},{1,5},{8,12},{9,13},{16,20},{17,21},{24,28},{25,29}} | collective-permute-start | bytes 1622024 | tf_op jit(solution)/shard_map/ppermute | solution.py:400
  4.8 9.0 %collective-permute-start.3 = (bf16[256,512]{1,0:T(8,128)(2,1)S(1)}, bf16[256,512]{1,0:T(8,128)(2,1)S(1)}, u32[]{:S(2)}, u32[]{:S(2)}) collective-permute-start(bf16[256,512]{1,0:T(8,128)(2,1)S(1)} %get-tuple-element.32), channel_id=1, source_target_pairs={{2,2},{3,18},{4,4},{5,20},{6,6},{7,22},{10,10},{11,26},{12,12},{13... | collective-permute-start | bytes 786440 | tf_op jit(solution)/shard_map/ppermute | solution.py:400
  5.5 26.4 %collective-permute-start.6 = (bf16[256,512]{1,0:T(8,128)(2,1)S(1)}, bf16[256,512]{1,0:T(8,128)(2,1)}, u32[]{:S(2)}, u32[]{:S(2)}) collective-permute-start(bf16[256,512]{1,0:T(8,128)(2,1)S(1)} %get-tuple-element.31), channel_id=1, source_target_pairs={{2,11},{3,27},{4,13},{5,29},{6,15},{7,31},{10,3},{11,19},{12,5},{1... | collective-permute-start | bytes 786440 | tf_op jit(solution)/shard_map/ppermute | solution.py:400
  11.9 11.5 %collective-permute-start.4 = (bf16[256,512]{1,0:T(8,128)(2,1)S(1)}, bf16[256,512]{1,0:T(8,128)(2,1)}, u32[]{:S(2)}, u32[]{:S(2)}) collective-permute-start(bf16[256,512]{1,0:T(8,128)(2,1)S(1)} %get-tuple-element.31), channel_id=1, source_target_pairs={{2,10},{3,26},{4,12},{5,28},{6,14},{7,30},{10,2},{11,18},{12,4},{1... | collective-permute-start | bytes 786440 | tf_op jit(solution)/shard_map/ppermute | solution.py:400
  13.9 18.0 %collective-permute-start.5 = (bf16[256,512]{1,0:T(8,128)(2,1)S(1)}, bf16[256,512]{1,0:T(8,128)(2,1)S(1)}, u32[]{:S(2)}, u32[]{:S(2)}) collective-permute-start(bf16[256,512]{1,0:T(8,128)(2,1)S(1)} %get-tuple-element.32), channel_id=1, source_target_pairs={{2,3},{3,19},{4,5},{5,21},{6,7},{7,23},{10,11},{11,27},{12,13},{13... | collective-permute-start | bytes 786440 | tf_op jit(solution)/shard_map/ppermute | solution.py:400
  19.1 13.8 %collective-permute-start.7 = (bf16[256,512]{1,0:T(8,128)(2,1)S(1)}, bf16[256,512]{1,0:T(8,128)(2,1)S(1)}, u32[]{:S(2)}, u32[]{:S(2)}) collective-permute-start(bf16[256,512]{1,0:T(8,128)(2,1)S(1)} %get-tuple-element.30), channel_id=1, source_target_pairs={{0,8},{1,9},{8,0},{9,1},{16,24},{17,25},{24,16},{25,17}} | collective-permute-start | bytes 786440 | tf_op jit(solution)/shard_map/ppermute | solution.py:400
  19.9 13.9 %collective-permute-start.2 = (bf16[528,512]{1,0:T(8,128)(2,1)S(1)}, bf16[528,512]{1,0:T(8,128)(2,1)S(1)}, u32[]{:S(2)}, u32[]{:S(2)}) collective-permute-start(bf16[528,512]{1,0:T(8,128)(2,1)S(1)} %broadcast_select_fusion.1), channel_id=1, source_target_pairs={{0,2},{1,3},{4,6},{5,7},{8,10},{9,11},{12,14},{13,15},{16,18},{17,... | collective-permute-start | bytes 1622024 | tf_op jit(solution)/shard_map/ppermute | solution.py:400
  33.8 13.5 %collective-permute-start.11 = (bf16[528,512]{1,0:T(8,128)(2,1)S(1)}, bf16[528,512]{1,0:T(8,128)(2,1)S(1)}, u32[]{:S(2)}, u32[]{:S(2)}) collective-permute-start(bf16[528,512]{1,0:T(8,128)(2,1)S(1)} %broadcast_select_fusion.2.refs_0_.refs_4_), channel_id=1, source_target_pairs={{0,1},{1,0},{2,3},{3,2},{4,5},{5,4},{6,7},{7,6},{8,9},{9,8},{10,11... | collective-permute-start | bytes 1622024 | tf_op jit(solution)/shard_map/ppermute | solution.py:400
  36.1 11.3 %collective-permute-start.8 = (bf16[528,512]{1,0:T(8,128)(2,1)S(1)}, bf16[528,512]{1,0:T(8,128)(2,1)}, u32[]{:S(2)}, u32[]{:S(2)}) collective-permute-start(bf16[528,512]{1,0:T(8,128)(2,1)S(1)} %broadcast_select_fusion.2.refs_0_.refs_4_), channel_id=1, source_target_pairs={{0,8},{1,9},{2,10},{3,11},{4,12},{5,13},{6,14},{7,15},{8,0},{9,1},... | collective-permute-start | bytes 1622024 | tf_op jit(solution)/shard_map/ppermute | solution.py:400
  36.7 14.0 %collective-permute-start.9 = (bf16[528,512]{1,0:T(8,128)(2,1)S(1)}, bf16[528,512]{1,0:T(8,128)(2,1)S(1)}, u32[]{:S(2)}, u32[]{:S(2)}) collective-permute-start(bf16[528,512]{1,0:T(8,128)(2,1)S(1)} %broadcast_select_fusion.2.refs_0_.refs_4_), channel_id=1, source_target_pairs={{0,16},{1,17},{2,18},{3,19},{4,20},{5,21},{6,22},{7,23},{8,24},{9,... | collective-permute-start | bytes 1622024 | tf_op jit(solution)/shard_map/ppermute | solution.py:400
  37.7 26.5 %collective-permute-start.16 = (bf16[1024,512]{1,0:T(8,128)(2,1)S(1)}, bf16[1024,512]{1,0:T(8,128)(2,1)}, u32[]{:S(2)}, u32[]{:S(2)}) collective-permute-start(bf16[1024,512]{1,0:T(8,128)(2,1)S(1)} %constant_dynamic-update-slice_fusion.refs_12_), channel_id=1, source_target_pairs={{2,4},{3,5},{4,6},{5,7},{10,12},{11,13},{12,14},{13,15},{18,20},{1... | collective-permute-start | bytes 3145736 | tf_op jit(solution)/shard_map/ppermute | solution.py:400
  41.8 26.2 %collective-permute-start.15 = (bf16[1024,512]{1,0:T(8,128)(2,1)S(1)}, bf16[1024,512]{1,0:T(8,128)(2,1)}, u32[]{:S(2)}, u32[]{:S(2)}) collective-permute-start(bf16[1024,512]{1,0:T(8,128)(2,1)S(1)} %constant_dynamic-update-slice_fusion.refs_12_), channel_id=1, source_target_pairs={{2,0},{3,1},{4,2},{5,3},{6,4},{7,5},{10,8},{11,9},{12,10},{13,11},... | collective-permute-start | bytes 3145736 | tf_op jit(solution)/shard_map/ppermute | solution.py:400
  50.8 8.7 %collective-permute-start.13 = (bf16[528,512]{1,0:T(8,128)(2,1)S(1)}, bf16[528,512]{1,0:T(8,128)(2,1)}, u32[]{:S(2)}, u32[]{:S(2)}) collective-permute-start(bf16[528,512]{1,0:T(8,128)(2,1)S(1)} %broadcast_select_fusion), channel_id=1, source_target_pairs={{0,1},{1,0},{2,3},{3,2},{4,5},{5,4},{6,7},{7,6},{8,24},{9,25},{10,... | collective-permute-start | bytes 1622024 | tf_op jit(solution)/shard_map/ppermute | solution.py:400
  51.8 21.9 %collective-permute-start.12 = (bf16[528,512]{1,0:T(8,128)(2,1)S(1)}, bf16[528,512]{1,0:T(8,128)(2,1)}, u32[]{:S(2)}, u32[]{:S(2)}) collective-permute-start(bf16[528,512]{1,0:T(8,128)(2,1)S(1)} %collective-permute-done.11.refs_4_.refs_8_), channel_id=1, source_target_pairs={{0,8},{1,9},{2,10},{3,11},{4,12},{5,13},{6,14},{7,15},{8,0},{9,1},... | collective-permute-start | bytes 1622024 | tf_op jit(solution)/shard_map/ppermute | solution.py:400
  52.8 23.0 %collective-permute-start.10 = (bf16[528,512]{1,0:T(8,128)(2,1)S(1)}, bf16[528,512]{1,0:T(8,128)(2,1)}, u32[]{:S(2)}, u32[]{:S(2)}) collective-permute-start(bf16[528,512]{1,0:T(8,128)(2,1)S(1)} %collective-permute-done.9.refs_2_.refs_6_), channel_id=1, source_target_pairs={{0,8},{1,9},{2,10},{3,11},{4,12},{5,13},{6,14},{7,15},{8,0},{9,1},... | collective-permute-start | bytes 1622024 | tf_op jit(solution)/shard_map/ppermute | solution.py:400
  59.5 19.2 %collective-permute-start.14 = (bf16[528,512]{1,0:T(8,128)(2,1)}, bf16[528,512]{1,0:T(8,128)(2,1)}, u32[]{:S(2)}, u32[]{:S(2)}) collective-permute-start(bf16[528,512]{1,0:T(8,128)(2,1)} %collective-permute-done.13.refs_6_.refs_10_), channel_id=1, source_target_pairs={{0,8},{1,9},{2,10},{3,11},{4,12},{5,13},{6,14},{7,15},{8,0},{9,1},... | collective-permute-start | bytes 1622024 | tf_op jit(solution)/shard_map/ppermute | solution.py:400
  67.9 45.4 %collective-permute-start.17 = (bf16[1024,512]{1,0:T(8,128)(2,1)}, bf16[1024,512]{1,0:T(8,128)(2,1)}, u32[]{:S(2)}, u32[]{:S(2)}) collective-permute-start(bf16[1024,512]{1,0:T(8,128)(2,1)} %collective-permute-done.15.refs_13_), channel_id=1, source_target_pairs={{2,0},{3,1},{4,2},{5,3},{10,8},{11,9},{12,10},{13,11},{18,16},{19,... | collective-permute-start | bytes 3145736 | tf_op jit(solution)/shard_map/ppermute | solution.py:400
  71.0 42.3 %collective-permute-start.18 = (bf16[1024,512]{1,0:T(8,128)(2,1)}, bf16[1024,512]{1,0:T(8,128)(2,1)}, u32[]{:S(2)}, u32[]{:S(2)}) collective-permute-start(bf16[1024,512]{1,0:T(8,128)(2,1)} %collective-permute-done.16.refs_15_), channel_id=1, source_target_pairs={{4,6},{5,7},{12,14},{13,15},{20,22},{21,23},{28,30},{29,31}} | collective-permute-start | bytes 3145736 | tf_op jit(solution)/shard_map/ppermute | solution.py:400
  73.6 39.7 %copy-start.1 = (f32[512]{0:T(512)S(1)}, f32[512]{0:T(512)}, u32[]{:S(2)}) copy-start(f32[512]{0:T(512)} %param.3) | copy-start | bytes 6148
  73.7 39.6 %collective-permute-start.21 = (bf16[512,512]{1,0:T(8,128)(2,1)}, bf16[512,512]{1,0:T(8,128)(2,1)S(1)}, u32[]{:S(2)}, u32[]{:S(2)}) collective-permute-start(bf16[512,512]{1,0:T(8,128)(2,1)} %maximum_select_fusion), channel_id=1, source_target_pairs={{0,1},{1,17},{2,26},{3,27},{4,28},{5,29},{6,30},{7,31},{8,9},{9,25... | collective-permute-start | bytes 1572872 | tf_op jit(solution)/shard_map/ppermute | solution.py:400
  75.8 37.5 %collective-permute-start.20 = (bf16[512,512]{1,0:T(8,128)(2,1)}, bf16[512,512]{1,0:T(8,128)(2,1)S(1)}, u32[]{:S(2)}, u32[]{:S(2)}) collective-permute-start(bf16[512,512]{1,0:T(8,128)(2,1)} %maximum_select_fusion), channel_id=1, source_target_pairs={{0,0},{1,16},{2,18},{3,19},{4,20},{5,21},{6,22},{7,23},{8,8},{9,24... | collective-permute-start | bytes 1572872 | tf_op jit(solution)/shard_map/ppermute | solution.py:400
  78.7 34.6 %collective-permute-start.19 = (bf16[512,512]{1,0:T(8,128)(2,1)S(1)}, bf16[512,512]{1,0:T(8,128)(2,1)S(1)}, u32[]{:S(2)}, u32[]{:S(2)}) collective-permute-start(bf16[512,512]{1,0:T(8,128)(2,1)S(1)} %copy-done), channel_id=1, source_target_pairs={{0,8},{1,9},{2,10},{3,11},{4,12},{5,13},{6,14},{7,15},{8,0},{9,1},... | collective-permute-start | bytes 1572872 | tf_op jit(solution)/shard_map/ppermute | solution.py:400

commit v10 on v9

--- a/solution.py
+++ b/solution.py
@@ -484,7 +484,7 @@
                 panel.append(value)
         crossed = [pair_side, way_side, diagonal]
         down = exchange(quarters, lambda p, h, s, w: (p, h, s - 1, w), lambda p, h, s, w: s > 0)
-        up = exchange(quarters, lambda p, h, s, w: (p, h, s + 1, w), lambda p, h, s, w: 0 < s < SPAN - 1)
+        up = exchange(after(quarters, own_twin), lambda p, h, s, w: (p, h, s + 1, w), lambda p, h, s, w: 0 < s < SPAN - 1)
         down_held, up_held, mixed = lax.optimization_barrier(
             (down, up, mixed, *crossed)
         )[:3]

time: 136 us -> 137 us (level)
  waiting for transfers between devices: 27.9 us -> 25.9 us
  local copies, waits for them, and re-layouts: 3.37 us -> 5.21 us
    ppermute x22, waiting for transfers between devices: 27.9 us -> 25.9 us  [exchange(): return lax.ppermute(value, ('row', 'col'), perm)]
    unnamed x7 -> x13, local copies, waits for them, and re-layouts: 1.02 us -> 2.86 us
where the time goes in v10:
time: 137 us
  Pallas kernels  56.7 us (41%)
  starting transfers between devices  45.5 us (33%)
  waiting for transfers between devices  25.9 us (19%)
  local copies, waits for them, and re-layouts  5.21 us (4%)
  other arithmetic  2.98 us (2%)
    ppermute x22, starting transfers between devices, exchange(): return lax.ppermute(value, ('row', 'col'), perm)  45.5 us
    pallas_call x1, Pallas kernels, factor_panel(): pl.pallas_call(functools.partial(panel_kernel, views, len(pieces), width)...  34.5 us
    ppermute x22, waiting for transfers between devices, exchange(): return lax.ppermute(value, ('row', 'col'), perm)  25.9 us
    pallas_call x1, Pallas kernels, finish_tile(): pl.pallas_call(functools.partial(tile_kernel, len(pieces), counts, views)...  22.2 us
    unnamed x13, local copies, waits for them, and re-layouts  2.86 us
  transfers between devices with their start and end apart: 22, of which 6 were waited for; matrix products, arithmetic and copies ran while one was open for 5% of the time, Pallas kernels for 25%

profile of v10, /device:TPU:17, one launch (start us, length us, event | category | flops | bytes accessed | tf_op | source)
XLA Modules:
  0.0 136.8 jit_solution(3468900534211625830)
XLA Ops:
  0.0 1.6 %collective-permute-start.1 = (bf16[512,512]{1,0:T(8,128)(2,1)}, bf16[512,512]{1,0:T(8,128)(2,1)}, u32[]{:S(2)}, u32[]{:S(2)}) collective-permute-start(bf16[512,512]{1,0:T(8,128)(2,1)} %refs_17_.1), channel_id=1, source_target_pairs={{6,0},{7,1},{14,8},{15,9},{22,16},{23,17},{30,24},{31,25}} | collective-permute-start | bytes 1572872 | tf_op jit(solution)/shard_map/ppermute | solution.py:400
  1.6 0.7 reduce-precision_convert_fusion.1
  2.3 1.1 pad_maximum_fusion
  3.4 1.3 collective-permute-start
  4.8 0.0 copy-done
  4.8 0.7 collective-permute-start.3
  5.5 6.4 %collective-permute-start.6 = (bf16[256,512]{1,0:T(8,128)(2,1)S(1)}, bf16[256,512]{1,0:T(8,128)(2,1)}, u32[]{:S(2)}, u32[]{:S(2)}) collective-permute-start(bf16[256,512]{1,0:T(8,128)(2,1)S(1)} %get-tuple-element.33), channel_id=1, source_target_pairs={{2,11},{3,27},{4,13},{5,29},{6,15},{7,31},{10,3},{11,19},{12,5},{1... | collective-permute-start | bytes 786440 | tf_op jit(solution)/shard_map/ppermute | solution.py:400
  11.9 1.9 %collective-permute-start.4 = (bf16[256,512]{1,0:T(8,128)(2,1)S(1)}, bf16[256,512]{1,0:T(8,128)(2,1)}, u32[]{:S(2)}, u32[]{:S(2)}) collective-permute-start(bf16[256,512]{1,0:T(8,128)(2,1)S(1)} %get-tuple-element.33), channel_id=1, source_target_pairs={{2,10},{3,26},{4,12},{5,28},{6,14},{7,30},{10,2},{11,18},{12,4},{1... | collective-permute-start | bytes 786440 | tf_op jit(solution)/shard_map/ppermute | solution.py:400
  13.9 0.0 collective-permute-done.3
  13.9 4.1 %collective-permute-start.5 = (bf16[256,512]{1,0:T(8,128)(2,1)S(1)}, bf16[256,512]{1,0:T(8,128)(2,1)S(1)}, u32[]{:S(2)}, u32[]{:S(2)}) collective-permute-start(bf16[256,512]{1,0:T(8,128)(2,1)S(1)} %get-tuple-element.34), channel_id=1, source_target_pairs={{2,3},{3,19},{4,5},{5,21},{6,7},{7,23},{10,11},{11,27},{12,13},{13... | collective-permute-start | bytes 786440 | tf_op jit(solution)/shard_map/ppermute | solution.py:400
  18.0 0.0 collective-permute-done.1
  18.0 1.1 dynamic-slice_bitcast_fusion.1
  19.1 0.7 collective-permute-start.7
  19.8 0.0 collective-permute-done
  19.8 0.1 broadcast_select_fusion.1
  19.9 3.5 %collective-permute-start.2 = (bf16[528,512]{1,0:T(8,128)(2,1)S(1)}, bf16[528,512]{1,0:T(8,128)(2,1)S(1)}, u32[]{:S(2)}, u32[]{:S(2)}) collective-permute-start(bf16[528,512]{1,0:T(8,128)(2,1)S(1)} %broadcast_select_fusion.1), channel_id=1, source_target_pairs={{0,2},{1,3},{4,6},{5,7},{8,10},{9,11},{12,14},{13,15},{16,18},{17,... | collective-permute-start | bytes 1622024 | tf_op jit(solution)/shard_map/ppermute | solution.py:400
  23.4 0.0 collective-permute-done.4
  23.4 1.0 constant_dynamic-update-slice_fusion.2
  24.4 7.5 %collective-permute-done.5 = bf16[256,512]{1,0:T(8,128)(2,1)S(1)} collective-permute-done((bf16[256,512]{1,0:T(8,128)(2,1)S(1)}, bf16[256,512]{1,0:T(8,128)(2,1)S(1)}, u32[]{:S(2)}, u32[]{:S(2)}) %collective-permute-start.5) | collective-permute-done | bytes 262176 | tf_op jit(solution)/shard_map/ppermute | solution.py:400
  31.9 0.0 collective-permute-done.6
  31.9 1.0 constant_dynamic-update-slice_fusion.refs_12_
  32.8 0.0 collective-permute-done.7
  32.9 0.9 maximum_select_fusion
  33.8 0.0 collective-permute-done.2
  33.8 0.1 broadcast_select_fusion.2.refs_0_.refs_4_
  33.9 2.1 %collective-permute-start.8 = (bf16[528,512]{1,0:T(8,128)(2,1)S(1)}, bf16[528,512]{1,0:T(8,128)(2,1)S(1)}, u32[]{:S(2)}, u32[]{:S(2)}) collective-permute-start(bf16[528,512]{1,0:T(8,128)(2,1)S(1)} %broadcast_select_fusion.2.refs_0_.refs_4_), channel_id=1, source_target_pairs={{0,8},{1,9},{2,10},{3,11},{4,12},{5,13},{6,14},{7,15},{8,0},{9,1},... | collective-permute-start | bytes 1622024 | tf_op jit(solution)/shard_map/ppermute | solution.py:400
  36.0 0.5 collective-permute-start.11
  36.5 0.9 collective-permute-start.9
  37.4 3.5 %collective-permute-start.15 = (bf16[1024,512]{1,0:T(8,128)(2,1)S(1)}, bf16[1024,512]{1,0:T(8,128)(2,1)}, u32[]{:S(2)}, u32[]{:S(2)}) collective-permute-start(bf16[1024,512]{1,0:T(8,128)(2,1)S(1)} %constant_dynamic-update-slice_fusion.refs_12_), channel_id=1, source_target_pairs={{2,0},{3,1},{4,2},{5,3},{6,4},{7,5},{10,8},{11,9},{12,10},{13,11},... | collective-permute-start | bytes 3145736 | tf_op jit(solution)/shard_map/ppermute | solution.py:400
  41.0 0.0 collective-permute-done.8.refs_1_.refs_5_
  41.0 0.0 copy-start.2
  41.0 0.8 copy-done.2
  41.8 2.8 %collective-permute-start.16 = (bf16[1024,512]{1,0:T(8,128)(2,1)S(1)}, bf16[1024,512]{1,0:T(8,128)(2,1)}, u32[]{:S(2)}, u32[]{:S(2)}) collective-permute-start(bf16[1024,512]{1,0:T(8,128)(2,1)S(1)} %constant_dynamic-update-slice_fusion.refs_12_), channel_id=1, source_target_pairs={{2,4},{3,5},{4,6},{5,7},{10,12},{11,13},{12,14},{13,15},{18,20},{1... | collective-permute-start | bytes 3145736 | tf_op jit(solution)/shard_map/ppermute | solution.py:400
  44.6 5.3 %collective-permute-done.11.refs_4_.refs_8_ = bf16[528,512]{1,0:T(8,128)(2,1)S(1)} collective-permute-done((bf16[528,512]{1,0:T(8,128)(2,1)S(1)}, bf16[528,512]{1,0:T(8,128)(2,1)S(1)}, u32[]{:S(2)}, u32[]{:S(2)}) %collective-permute-start.11) | collective-permute-done | bytes 540704 | tf_op jit(solution)/shard_map/ppermute | solution.py:400
  49.9 0.1 collective-permute-done.9.refs_2_.refs_6_
  50.0 0.1 broadcast_select_fusion
  50.1 1.1 collective-permute-start.13
  51.2 1.4 %collective-permute-start.12 = (bf16[528,512]{1,0:T(8,128)(2,1)S(1)}, bf16[528,512]{1,0:T(8,128)(2,1)}, u32[]{:S(2)}, u32[]{:S(2)}) collective-permute-start(bf16[528,512]{1,0:T(8,128)(2,1)S(1)} %collective-permute-done.11.refs_4_.refs_8_), channel_id=1, source_target_pairs={{0,8},{1,9},{2,10},{3,11},{4,12},{5,13},{6,14},{7,15},{8,0},{9,1},... | collective-permute-start | bytes 1622024 | tf_op jit(solution)/shard_map/ppermute | solution.py:400
  52.5 0.0 collective-permute-start.10
  52.5 6.2 %collective-permute-done.13.refs_6_.refs_10_ = bf16[528,512]{1,0:T(8,128)(2,1)} collective-permute-done((bf16[528,512]{1,0:T(8,128)(2,1)S(1)}, bf16[528,512]{1,0:T(8,128)(2,1)}, u32[]{:S(2)}, u32[]{:S(2)}) %collective-permute-start.13) | collective-permute-done | bytes 540704 | tf_op jit(solution)/shard_map/ppermute | solution.py:400
  58.8 2.0 %collective-permute-start.14 = (bf16[528,512]{1,0:T(8,128)(2,1)}, bf16[528,512]{1,0:T(8,128)(2,1)}, u32[]{:S(2)}, u32[]{:S(2)}) collective-permute-start(bf16[528,512]{1,0:T(8,128)(2,1)} %collective-permute-done.13.refs_6_.refs_10_), channel_id=1, source_target_pairs={{0,8},{1,9},{2,10},{3,11},{4,12},{5,13},{6,14},{7,15},{8,0},{9,1},... | collective-permute-start | bytes 1622024 | tf_op jit(solution)/shard_map/ppermute | solution.py:400
  60.8 3.0 %collective-permute-done.15.refs_13_ = bf16[1024,512]{1,0:T(8,128)(2,1)} collective-permute-done((bf16[1024,512]{1,0:T(8,128)(2,1)S(1)}, bf16[1024,512]{1,0:T(8,128)(2,1)}, u32[]{:S(2)}, u32[]{:S(2)}) %collective-permute-start.15) | collective-permute-done | bytes 1048608 | tf_op jit(solution)/shard_map/ppermute | solution.py:400
  63.7 3.8 %collective-permute-done.16.refs_15_ = bf16[1024,512]{1,0:T(8,128)(2,1)} collective-permute-done((bf16[1024,512]{1,0:T(8,128)(2,1)S(1)}, bf16[1024,512]{1,0:T(8,128)(2,1)}, u32[]{:S(2)}, u32[]{:S(2)}) %collective-permute-start.16) | collective-permute-done | bytes 1048608 | tf_op jit(solution)/shard_map/ppermute | solution.py:400
  67.5 2.3 %collective-permute-start.17 = (bf16[1024,512]{1,0:T(8,128)(2,1)}, bf16[1024,512]{1,0:T(8,128)(2,1)}, u32[]{:S(2)}, u32[]{:S(2)}) collective-permute-start(bf16[1024,512]{1,0:T(8,128)(2,1)} %collective-permute-done.15.refs_13_), channel_id=1, source_target_pairs={{2,0},{3,1},{4,2},{5,3},{10,8},{11,9},{12,10},{13,11},{18,16},{19,... | collective-permute-start | bytes 3145736 | tf_op jit(solution)/shard_map/ppermute | solution.py:400
  69.8 3.4 %collective-permute-start.18 = (bf16[1024,512]{1,0:T(8,128)(2,1)}, bf16[1024,512]{1,0:T(8,128)(2,1)}, u32[]{:S(2)}, u32[]{:S(2)}) collective-permute-start(bf16[1024,512]{1,0:T(8,128)(2,1)} %collective-permute-done.16.refs_15_), channel_id=1, source_target_pairs={{4,6},{5,7},{12,14},{13,15},{20,22},{21,23},{28,30},{29,31}} | collective-permute-start | bytes 3145736 | tf_op jit(solution)/shard_map/ppermute | solution.py:400
  73.2 0.1 stack.92.place_ref
  73.3 0.2 stack.89.place_ref
  73.5 0.0 copy-start.1
  73.5 0.0 collective-permute-done.12.refs_5_.refs_9_
  73.5 2.0 %collective-permute-start.19 = (bf16[512,512]{1,0:T(8,128)(2,1)S(1)}, bf16[512,512]{1,0:T(8,128)(2,1)S(1)}, u32[]{:S(2)}, u32[]{:S(2)}) collective-permute-start(bf16[512,512]{1,0:T(8,128)(2,1)S(1)} %copy-done), channel_id=1, source_target_pairs={{0,8},{1,9},{2,10},{3,11},{4,12},{5,13},{6,14},{7,15},{8,0},{9,1},... | collective-permute-start | bytes 1572872 | tf_op jit(solution)/shard_map/ppermute | solution.py:400
  75.5 0.0 collective-permute-done.10.refs_3_.refs_7_
  75.5 0.4 collective-permute-start.21
  75.9 0.0 collective-permute-done.14.refs_7_.refs_11_
  75.9 2.9 %collective-permute-start.20 = (bf16[512,512]{1,0:T(8,128)(2,1)}, bf16[512,512]{1,0:T(8,128)(2,1)S(1)}, u32[]{:S(2)}, u32[]{:S(2)}) collective-permute-start(bf16[512,512]{1,0:T(8,128)(2,1)} %maximum_select_fusion), channel_id=1, source_target_pairs={{0,0},{1,16},{2,18},{3,19},{4,20},{5,21},{6,22},{7,23},{8,8},{9,24... | collective-permute-start | bytes 1572872 | tf_op jit(solution)/shard_map/ppermute | solution.py:400
  78.8 0.0 copy-start.3
  78.9 1.0 copy-done.3
  79.9 34.5 %factor_panel.1 = (bf16[1024,1024]{1,0:T(8,128)(2,1)}, bf16[1024,1024]{1,0:T(8,128)(2,1)}, bf16[1024,128]{1,0:T(8,128)(2,1)}, bf16[1024,128]{1,0:T(8,128)(2,1)}) custom-call(s32[20]{0:T(128)S(1)} %stack.92.place_ref, bf16[528,512]{1,0:T(8,128)(2,1)S(1)} %broadcast_select_fusion.2.refs_0_.refs_4_, bf16[528,512]{1,0:T(8,128)(2,1)S(1)} %copy-done.3, ...), custom_call_target="tpu_custom_call" | custom-call | flops 8000000000 | bytes 1048576 | tf_op jit(solution)/shard_map/factor_panel/pallas_call | solution.py:242
  114.4 0.0 collective-permute-done.19.refs_18_
  114.4 0.0 collective-permute-done.21.refs_20_
  114.4 0.0 collective-permute-done.20.refs_19_
  114.5 0.0 collective-permute-done.17.refs_14_
  114.5 0.0 collective-permute-done.18.refs_16_
  114.5 0.0 copy-done.1
  114.5 22.2 %finish_tile.1 = f32[1024,512]{1,0:T(8,128)} custom-call(s32[74]{0:T(128)S(1)} %stack.89.place_ref, f32[1,512]{1,0:T(1,128)S(1)} %bitcast.38, bf16[1024,1024]{1,0:T(8,128)(2,1)} %get-tuple-element.22.refs_0_, bf16[1024,1024]{1,0:T(8,128)(2,1)} %get-tuple-element.23.refs_1_, bf16[1024,128]{1,0:T(8,128)(2,1)} %get-tuple-element.24.refs_2_, ...), custom_call_target="tpu_custom_call" | custom-call | flops 20000000000 | bytes 25165824 | tf_op jit(solution)/shard_map/finish_tile/pallas_call | solution.py:360
  (10 shorter events, 0.1 us)
Async XLA Ops:
  0.0 4.8 %copy-start = (bf16[512,512]{1,0:T(8,128)(2,1)S(1)}, bf16[512,512]{1,0:T(8,128)(2,1)}, u32[]{:S(2)}) copy-start(bf16[512,512]{1,0:T(8,128)(2,1)} %refs_17_.1) | copy-start | bytes 1572868
  0.0 18.0 %collective-permute-start.1 = (bf16[512,512]{1,0:T(8,128)(2,1)}, bf16[512,512]{1,0:T(8,128)(2,1)}, u32[]{:S(2)}, u32[]{:S(2)}) collective-permute-start(bf16[512,512]{1,0:T(8,128)(2,1)} %refs_17_.1), channel_id=1, source_target_pairs={{6,0},{7,1},{14,8},{15,9},{22,16},{23,17},{30,24},{31,25}} | collective-permute-start | bytes 1572872 | tf_op jit(solution)/shard_map/ppermute | solution.py:400
  3.4 16.3 %collective-permute-start = (bf16[528,512]{1,0:T(8,128)(2,1)S(1)}, bf16[528,512]{1,0:T(8,128)(2,1)S(1)}, u32[]{:S(2)}, u32[]{:S(2)}) collective-permute-start(bf16[528,512]{1,0:T(8,128)(2,1)S(1)} %pad_maximum_fusion), channel_id=1, source_target_pairs={{0,4},{1,5},{8,12},{9,13},{16,20},{17,21},{24,28},{25,29}} | collective-permute-start | bytes 1622024 | tf_op jit(solution)/shard_map/ppermute | solution.py:400
  4.8 9.0 %collective-permute-start.3 = (bf16[256,512]{1,0:T(8,128)(2,1)S(1)}, bf16[256,512]{1,0:T(8,128)(2,1)S(1)}, u32[]{:S(2)}, u32[]{:S(2)}) collective-permute-start(bf16[256,512]{1,0:T(8,128)(2,1)S(1)} %get-tuple-element.34), channel_id=1, source_target_pairs={{2,2},{3,18},{4,4},{5,20},{6,6},{7,22},{10,10},{11,26},{12,12},{13... | collective-permute-start | bytes 786440 | tf_op jit(solution)/shard_map/ppermute | solution.py:400
  5.5 26.4 %collective-permute-start.6 = (bf16[256,512]{1,0:T(8,128)(2,1)S(1)}, bf16[256,512]{1,0:T(8,128)(2,1)}, u32[]{:S(2)}, u32[]{:S(2)}) collective-permute-start(bf16[256,512]{1,0:T(8,128)(2,1)S(1)} %get-tuple-element.33), channel_id=1, source_target_pairs={{2,11},{3,27},{4,13},{5,29},{6,15},{7,31},{10,3},{11,19},{12,5},{1... | collective-permute-start | bytes 786440 | tf_op jit(solution)/shard_map/ppermute | solution.py:400
  11.9 11.5 %collective-permute-start.4 = (bf16[256,512]{1,0:T(8,128)(2,1)S(1)}, bf16[256,512]{1,0:T(8,128)(2,1)}, u32[]{:S(2)}, u32[]{:S(2)}) collective-permute-start(bf16[256,512]{1,0:T(8,128)(2,1)S(1)} %get-tuple-element.33), channel_id=1, source_target_pairs={{2,10},{3,26},{4,12},{5,28},{6,14},{7,30},{10,2},{11,18},{12,4},{1... | collective-permute-start | bytes 786440 | tf_op jit(solution)/shard_map/ppermute | solution.py:400
  13.9 18.0 %collective-permute-start.5 = (bf16[256,512]{1,0:T(8,128)(2,1)S(1)}, bf16[256,512]{1,0:T(8,128)(2,1)S(1)}, u32[]{:S(2)}, u32[]{:S(2)}) collective-permute-start(bf16[256,512]{1,0:T(8,128)(2,1)S(1)} %get-tuple-element.34), channel_id=1, source_target_pairs={{2,3},{3,19},{4,5},{5,21},{6,7},{7,23},{10,11},{11,27},{12,13},{13... | collective-permute-start | bytes 786440 | tf_op jit(solution)/shard_map/ppermute | solution.py:400
  19.1 13.8 %collective-permute-start.7 = (bf16[256,512]{1,0:T(8,128)(2,1)S(1)}, bf16[256,512]{1,0:T(8,128)(2,1)S(1)}, u32[]{:S(2)}, u32[]{:S(2)}) collective-permute-start(bf16[256,512]{1,0:T(8,128)(2,1)S(1)} %get-tuple-element.32), channel_id=1, source_target_pairs={{0,8},{1,9},{8,0},{9,1},{16,24},{17,25},{24,16},{25,17}} | collective-permute-start | bytes 786440 | tf_op jit(solution)/shard_map/ppermute | solution.py:400
  19.9 13.9 %collective-permute-start.2 = (bf16[528,512]{1,0:T(8,128)(2,1)S(1)}, bf16[528,512]{1,0:T(8,128)(2,1)S(1)}, u32[]{:S(2)}, u32[]{:S(2)}) collective-permute-start(bf16[528,512]{1,0:T(8,128)(2,1)S(1)} %broadcast_select_fusion.1), channel_id=1, source_target_pairs={{0,2},{1,3},{4,6},{5,7},{8,10},{9,11},{12,14},{13,15},{16,18},{17,... | collective-permute-start | bytes 1622024 | tf_op jit(solution)/shard_map/ppermute | solution.py:400
  33.9 7.1 %collective-permute-start.8 = (bf16[528,512]{1,0:T(8,128)(2,1)S(1)}, bf16[528,512]{1,0:T(8,128)(2,1)S(1)}, u32[]{:S(2)}, u32[]{:S(2)}) collective-permute-start(bf16[528,512]{1,0:T(8,128)(2,1)S(1)} %broadcast_select_fusion.2.refs_0_.refs_4_), channel_id=1, source_target_pairs={{0,8},{1,9},{2,10},{3,11},{4,12},{5,13},{6,14},{7,15},{8,0},{9,1},... | collective-permute-start | bytes 1622024 | tf_op jit(solution)/shard_map/ppermute | solution.py:400
  36.0 14.0 %collective-permute-start.11 = (bf16[528,512]{1,0:T(8,128)(2,1)S(1)}, bf16[528,512]{1,0:T(8,128)(2,1)S(1)}, u32[]{:S(2)}, u32[]{:S(2)}) collective-permute-start(bf16[528,512]{1,0:T(8,128)(2,1)S(1)} %broadcast_select_fusion.2.refs_0_.refs_4_), channel_id=1, source_target_pairs={{0,1},{1,0},{2,3},{3,2},{4,5},{5,4},{6,7},{7,6},{8,9},{9,8},{10,11... | collective-permute-start | bytes 1622024 | tf_op jit(solution)/shard_map/ppermute | solution.py:400
  36.5 13.5 %collective-permute-start.9 = (bf16[528,512]{1,0:T(8,128)(2,1)S(1)}, bf16[528,512]{1,0:T(8,128)(2,1)S(1)}, u32[]{:S(2)}, u32[]{:S(2)}) collective-permute-start(bf16[528,512]{1,0:T(8,128)(2,1)S(1)} %broadcast_select_fusion.2.refs_0_.refs_4_), channel_id=1, source_target_pairs={{0,16},{1,17},{2,18},{3,19},{4,20},{5,21},{6,22},{7,23},{8,24},{9,... | collective-permute-start | bytes 1622024 | tf_op jit(solution)/shard_map/ppermute | solution.py:400
  37.4 26.3 %collective-permute-start.15 = (bf16[1024,512]{1,0:T(8,128)(2,1)S(1)}, bf16[1024,512]{1,0:T(8,128)(2,1)}, u32[]{:S(2)}, u32[]{:S(2)}) collective-permute-start(bf16[1024,512]{1,0:T(8,128)(2,1)S(1)} %constant_dynamic-update-slice_fusion.refs_12_), channel_id=1, source_target_pairs={{2,0},{3,1},{4,2},{5,3},{6,4},{7,5},{10,8},{11,9},{12,10},{13,11},... | collective-permute-start | bytes 3145736 | tf_op jit(solution)/shard_map/ppermute | solution.py:400
  41.0 0.8 copy-start.2
  41.8 25.8 %collective-permute-start.16 = (bf16[1024,512]{1,0:T(8,128)(2,1)S(1)}, bf16[1024,512]{1,0:T(8,128)(2,1)}, u32[]{:S(2)}, u32[]{:S(2)}) collective-permute-start(bf16[1024,512]{1,0:T(8,128)(2,1)S(1)} %constant_dynamic-update-slice_fusion.refs_12_), channel_id=1, source_target_pairs={{2,4},{3,5},{4,6},{5,7},{10,12},{11,13},{12,14},{13,15},{18,20},{1... | collective-permute-start | bytes 3145736 | tf_op jit(solution)/shard_map/ppermute | solution.py:400
  50.1 8.7 %collective-permute-start.13 = (bf16[528,512]{1,0:T(8,128)(2,1)S(1)}, bf16[528,512]{1,0:T(8,128)(2,1)}, u32[]{:S(2)}, u32[]{:S(2)}) collective-permute-start(bf16[528,512]{1,0:T(8,128)(2,1)S(1)} %broadcast_select_fusion), channel_id=1, source_target_pairs={{0,1},{1,0},{2,3},{3,2},{4,5},{5,4},{6,7},{7,6},{8,24},{9,25},{10,... | collective-permute-start | bytes 1622024 | tf_op jit(solution)/shard_map/ppermute | solution.py:400
  51.2 22.3 %collective-permute-start.12 = (bf16[528,512]{1,0:T(8,128)(2,1)S(1)}, bf16[528,512]{1,0:T(8,128)(2,1)}, u32[]{:S(2)}, u32[]{:S(2)}) collective-permute-start(bf16[528,512]{1,0:T(8,128)(2,1)S(1)} %collective-permute-done.11.refs_4_.refs_8_), channel_id=1, source_target_pairs={{0,8},{1,9},{2,10},{3,11},{4,12},{5,13},{6,14},{7,15},{8,0},{9,1},... | collective-permute-start | bytes 1622024 | tf_op jit(solution)/shard_map/ppermute | solution.py:400
  52.5 23.0 %collective-permute-start.10 = (bf16[528,512]{1,0:T(8,128)(2,1)S(1)}, bf16[528,512]{1,0:T(8,128)(2,1)}, u32[]{:S(2)}, u32[]{:S(2)}) collective-permute-start(bf16[528,512]{1,0:T(8,128)(2,1)S(1)} %collective-permute-done.9.refs_2_.refs_6_), channel_id=1, source_target_pairs={{0,8},{1,9},{2,10},{3,11},{4,12},{5,13},{6,14},{7,15},{8,0},{9,1},... | collective-permute-start | bytes 1622024 | tf_op jit(solution)/shard_map/ppermute | solution.py:400
  58.8 17.1 %collective-permute-start.14 = (bf16[528,512]{1,0:T(8,128)(2,1)}, bf16[528,512]{1,0:T(8,128)(2,1)}, u32[]{:S(2)}, u32[]{:S(2)}) collective-permute-start(bf16[528,512]{1,0:T(8,128)(2,1)} %collective-permute-done.13.refs_6_.refs_10_), channel_id=1, source_target_pairs={{0,8},{1,9},{2,10},{3,11},{4,12},{5,13},{6,14},{7,15},{8,0},{9,1},... | collective-permute-start | bytes 1622024 | tf_op jit(solution)/shard_map/ppermute | solution.py:400
  67.5 46.9 %collective-permute-start.17 = (bf16[1024,512]{1,0:T(8,128)(2,1)}, bf16[1024,512]{1,0:T(8,128)(2,1)}, u32[]{:S(2)}, u32[]{:S(2)}) collective-permute-start(bf16[1024,512]{1,0:T(8,128)(2,1)} %collective-permute-done.15.refs_13_), channel_id=1, source_target_pairs={{2,0},{3,1},{4,2},{5,3},{10,8},{11,9},{12,10},{13,11},{18,16},{19,... | collective-permute-start | bytes 3145736 | tf_op jit(solution)/shard_map/ppermute | solution.py:400
  69.8 44.7 %collective-permute-start.18 = (bf16[1024,512]{1,0:T(8,128)(2,1)}, bf16[1024,512]{1,0:T(8,128)(2,1)}, u32[]{:S(2)}, u32[]{:S(2)}) collective-permute-start(bf16[1024,512]{1,0:T(8,128)(2,1)} %collective-permute-done.16.refs_15_), channel_id=1, source_target_pairs={{4,6},{5,7},{12,14},{13,15},{20,22},{21,23},{28,30},{29,31}} | collective-permute-start | bytes 3145736 | tf_op jit(solution)/shard_map/ppermute | solution.py:400
  73.5 41.0 %copy-start.1 = (f32[512]{0:T(512)S(1)}, f32[512]{0:T(512)}, u32[]{:S(2)}) copy-start(f32[512]{0:T(512)} %param.3) | copy-start | bytes 6148
  73.5 40.9 %collective-permute-start.19 = (bf16[512,512]{1,0:T(8,128)(2,1)S(1)}, bf16[512,512]{1,0:T(8,128)(2,1)S(1)}, u32[]{:S(2)}, u32[]{:S(2)}) collective-permute-start(bf16[512,512]{1,0:T(8,128)(2,1)S(1)} %copy-done), channel_id=1, source_target_pairs={{0,8},{1,9},{2,10},{3,11},{4,12},{5,13},{6,14},{7,15},{8,0},{9,1},... | collective-permute-start | bytes 1572872 | tf_op jit(solution)/shard_map/ppermute | solution.py:400
  75.5 38.9 %collective-permute-start.21 = (bf16[512,512]{1,0:T(8,128)(2,1)}, bf16[512,512]{1,0:T(8,128)(2,1)S(1)}, u32[]{:S(2)}, u32[]{:S(2)}) collective-permute-start(bf16[512,512]{1,0:T(8,128)(2,1)} %maximum_select_fusion), channel_id=1, source_target_pairs={{0,1},{1,17},{2,26},{3,27},{4,28},{5,29},{6,30},{7,31},{8,9},{9,25... | collective-permute-start | bytes 1572872 | tf_op jit(solution)/shard_map/ppermute | solution.py:400
  75.9 38.6 %collective-permute-start.20 = (bf16[512,512]{1,0:T(8,128)(2,1)}, bf16[512,512]{1,0:T(8,128)(2,1)S(1)}, u32[]{:S(2)}, u32[]{:S(2)}) collective-permute-start(bf16[512,512]{1,0:T(8,128)(2,1)} %maximum_select_fusion), channel_id=1, source_target_pairs={{0,0},{1,16},{2,18},{3,19},{4,20},{5,21},{6,22},{7,23},{8,8},{9,24... | collective-permute-start | bytes 1572872 | tf_op jit(solution)/shard_map/ppermute | solution.py:400
  78.8 1.1 copy-start.3
  79.9 34.6 %copy-start.4 = (bf16[528,512]{1,0:T(8,128)(2,1)S(1)}, bf16[528,512]{1,0:T(8,128)(2,1)}, u32[]{:S(2)}) copy-start(bf16[528,512]{1,0:T(8,128)(2,1)} %copy-done.2) | copy-start | bytes 1622020
